TPU v7x, 32 devices: a whole 2x2x4 slice. The times are simulated.
32 devices in a mesh: seq: 4 (over z), tp: 8 (over y, x, core).
Axes of the slice: x: 2, y: 2, z: 4, core: 2. Of those that a mesh axis runs over, the one named last changes fastest.
Arguments:
- inputs: bfloat16 [4096, 4096], P('seq'), may hold values from -6 to 6
- cotangent: bfloat16 [4096, 4096], P('seq'), may hold values from -6 to 6
- w_in: bfloat16 [4096, 5120], P(None, 'tp'), may hold values from -0.125 to 0.125
- conv_w: float32 [3, 5120], P(None, 'tp'), may hold values from -3.5 to 3.5
- norm_gain: float32 [4096], P('tp'), may hold values from 0.25 to 1.75
- w_out: bfloat16 [4096, 4096], P('tp'), may hold values from -0.125 to 0.125
- keep_flags: int32 [32], P('tp'), may hold values 0 or 1
Outputs:
- layer_out: bfloat16 [4096, 4096], P('seq', 'tp')
- input_grad: bfloat16 [4096, 4096], P('seq', 'tp')
All inputs are finite; a program needn't handle non-finite values. No bound on the sum of `keep_flags` on one device may be relied on, other than what follows from the above.
Results may differ from a plain program's by a relative error of at most 0.0071.
Values may be sent and summed in bfloat16 or wider, within the bound.
No kernel may reach another device: no remote copies, remote signals or barrier semaphores. Data moves between devices by JAX's collectives and lax.ppermute only.
A program may use at most 192 MiB of HBM per device.

v0:
```python
import functools

import jax
import jax.numpy as jnp
import numpy as np
from jax import lax
from jax.experimental import pallas as pl
from jax.experimental.pallas import tpu as pltpu
from jax.sharding import PartitionSpec as P

FEAT = 16
DV = 128
HW = 2 * FEAT + DV
EP = 256
ES = 160
CH = 256
EPS = 1e-06
BF = jnp.bfloat16
F32 = jnp.float32
VMEM = 40 * 1024 * 1024


def mm(a, b):
    return lax.dot_general(a, b, (((1,), (0,)), ((), ())), preferred_element_type=F32)


def mm_nt(a, b):
    return lax.dot_general(a, b, (((1,), (1,)), ((), ())), preferred_element_type=F32)


def mm_tn(a, b):
    return lax.dot_general(a, b, (((0,), (0,)), ((), ())), preferred_element_type=F32)


def selectors(heads):
    sel = np.zeros((heads, 128, 4 * EP + 256), np.float32)
    bias = np.zeros((8, EP), np.float32)
    bias[1, :FEAT] = 1.0
    bias[0, FEAT] = bias[1, FEAT] = 1.0
    for h in range(heads):
        q0 = (HW * h) % 128
        k0 = q0 + FEAT
        for i in range(FEAT):
            sel[h, q0 + i, i] = 0.5
            sel[h, k0 + i, 2 * EP + i] = 0.5
            sel[h, k0 + i, 4 * EP + q0 + i] = 0.25
            sel[h, q0 + i, 4 * EP + 128 + k0 + i] = 0.25
        col = FEAT + 1
        for i in range(FEAT):
            for j in range(i, FEAT):
                sel[h, q0 + i, col] = 0.25 if i == j else 0.5
                sel[h, q0 + j, EP + col] = 0.5
                sel[h, k0 + i, 2 * EP + col] = 0.5
                sel[h, k0 + j, 3 * EP + col] = 0.5
                col += 1
    return jnp.asarray(sel, BF), jnp.asarray(bias, F32)


def window(h):
    t = (HW * h) // 128
    return slice(128 * t, 128 * t + 128)


def value_place(h):
    start = HW * h + 2 * FEAT
    return start // 128, start % 128


def lane_iota():
    return lax.broadcasted_iota(jnp.int32, (CH, 128), 1)


def take_values(conv, h):
    tile, off = value_place(h)
    first = conv[:, 128 * tile : 128 * tile + 128]
    if off == 0:
        return first
    second = conv[:, 128 * tile + 128 : min(128 * tile + 256, conv.shape[1])]
    if second.shape[1] < 128:
        second = jnp.concatenate([second, jnp.zeros((CH, 128 - second.shape[1]), second.dtype)], 1)
    a = pltpu.roll(first, 128 - off, 1)
    b = pltpu.roll(second, 128 - off, 1)
    return jnp.where(lane_iota() < 128 - off, a, b)


def causal():
    r = lax.broadcasted_iota(jnp.int32, (CH, CH), 0)
    c = lax.broadcasted_iota(jnp.int32, (CH, CH), 1)
    return r >= c


def params():
    return pltpu.CompilerParams(dimension_semantics=("arbitrary",), vmem_limit_bytes=VMEM)


def whole(shape):
    return pl.BlockSpec(shape, lambda c: (0,) * len(shape))


def project_kernel(heads, x_ref, halo_ref, w_ref, cw_ref, sel_ref, bias_ref,
                   cv_ref, v_ref, pq_ref, pk_ref, loc_ref, state_ref, ext, run):
    c = pl.program_id(0)

    @pl.when(c == 0)
    def _():
        before = mm(halo_ref[...], w_ref[...]).astype(BF).astype(F32)
        ext[0:8, :] = before[8:16]
        run[...] = jnp.zeros_like(run)

    ext[8:, :] = mm(x_ref[...], w_ref[...]).astype(BF).astype(F32)
    conv = (cw_ref[0:1] * ext[8 : 8 + CH, :] + cw_ref[1:2] * ext[7 : 7 + CH, :]
            + cw_ref[2:3] * ext[6 : 6 + CH, :])
    ext[0:8, :] = ext[CH : CH + 8, :]
    conv_b = conv.astype(BF)
    cv_ref[...] = conv_b
    conv = conv_b.astype(F32)
    b0 = bias_ref[0:1]
    b1 = bias_ref[1:2]
    for h in range(heads):
        u = mm(conv_b[:, window(h)], sel_ref[h, :, : 4 * EP])
        pq_ref[h] = ((u[:, :EP] + b0) * (u[:, EP : 2 * EP] + b1)).astype(BF)
        pk = ((u[:, 2 * EP : 3 * EP] + b0) * (u[:, 3 * EP :] + b1)).astype(BF)
        pk_ref[h] = pk
        v = take_values(conv, h).astype(BF)
        v_ref[:, DV * h : DV * h + DV] = v
        loc_ref[0, h] = run[h].astype(BF)
        run[h] = run[h] + mm_tn(v, pk)

    @pl.when(c == pl.num_programs(0) - 1)
    def _():
        for h in range(heads):
            state_ref[h] = run[h].T[:ES].astype(BF)


def project(x, halo, w_in, conv_w, sel, bias, heads):
    rows, d = x.shape
    width = w_in.shape[1]
    n = rows // CH
    return pl.pallas_call(
        functools.partial(project_kernel, heads),
        grid=(n,),
        in_specs=[
            pl.BlockSpec((CH, d), lambda c: (c, 0)),
            whole((16, d)),
            whole((d, width)),
            whole((3, width)),
            whole(sel.shape),
            whole(bias.shape),
        ],
        out_specs=[
            pl.BlockSpec((CH, width), lambda c: (c, 0)),
            pl.BlockSpec((CH, heads * DV), lambda c: (c, 0)),
            pl.BlockSpec((heads, CH, EP), lambda c: (0, c, 0)),
            pl.BlockSpec((heads, CH, EP), lambda c: (0, c, 0)),
            pl.BlockSpec((1, heads, DV, EP), lambda c: (c, 0, 0, 0)),
            whole((heads, ES, DV)),
        ],
        out_shape=[
            jax.ShapeDtypeStruct((rows, width), BF),
            jax.ShapeDtypeStruct((rows, heads * DV), BF),
            jax.ShapeDtypeStruct((heads, rows, EP), BF),
            jax.ShapeDtypeStruct((heads, rows, EP), BF),
            jax.ShapeDtypeStruct((n, heads, DV, EP), BF),
            jax.ShapeDtypeStruct((heads, ES, DV), BF),
        ],
        scratch_shapes=[pltpu.VMEM((CH + 8, width), F32), pltpu.VMEM((heads, DV, EP), F32)],
        compiler_params=params(),
        cost_estimate=pl.CostEstimate(flops=2 * rows * d * width, bytes_accessed=20 << 20, transcendentals=0),
        name="project",
    )(x, halo, w_in, conv_w, sel, bias)


def local_kernel(heads, ct_ref, wo_ref, gain_ref, v_ref, pq_ref, pk_ref, loc_ref, g_ref, num_ref):
    g_ref[...] = mm_nt(ct_ref[...], wo_ref[...]) * gain_ref[...]
    mask = causal()
    for h in range(heads):
        pq = pq_ref[h]
        logits = mm_nt(pq[:, :FEAT], pk_ref[h, :, :FEAT])
        weights = jnp.where(mask, 1.0 + logits + 0.5 * logits * logits, 0.0).astype(BF)
        at = slice(DV * h, DV * h + DV)
        num_ref[:, at] = mm(weights, v_ref[:, at]) + mm_nt(pq, loc_ref[0, h])


def local_part(ct, w_out, gain, v, pq, pk, loc, heads):
    rows, d = ct.shape
    n = rows // CH
    wide = heads * DV
    row = pl.BlockSpec((CH, wide), lambda c: (c, 0))
    feat = pl.BlockSpec((heads, CH, EP), lambda c: (0, c, 0))
    return pl.pallas_call(
        functools.partial(local_kernel, heads),
        grid=(n,),
        in_specs=[
            pl.BlockSpec((CH, d), lambda c: (c, 0)),
            whole((wide, d)),
            whole((1, wide)),
            row,
            feat,
            feat,
            pl.BlockSpec((1, heads, DV, EP), lambda c: (c, 0, 0, 0)),
        ],
        out_specs=[row, row],
        out_shape=[jax.ShapeDtypeStruct((rows, wide), F32)] * 2,
        compiler_params=params(),
        cost_estimate=pl.CostEstimate(flops=2 * rows * d * wide, bytes_accessed=20 << 20, transcendentals=0),
        name="local_part",
    )(ct, w_out, gain, v, pq, pk, loc)


def norm_kernel(heads, g_ref, num_ref, gain_ref, pq_ref, pre_ref, ho_ref, dn_ref, loc_ref, state_ref, run):
    c = pl.program_id(0)

    @pl.when(c == 0)
    def _():
        run[...] = jnp.zeros_like(run)

    for h in range(heads):
        at = slice(DV * h, DV * h + DV)
        pq = pq_ref[h]
        num = num_ref[:, at] + mm(pq[:, :ES], pre_ref[h])
        inv = lax.rsqrt(jnp.mean(num * num, 1, keepdims=True) + EPS)
        normed = num * inv
        ho_ref[:, at] = (normed * gain_ref[:, at]).astype(BF)
        g = g_ref[:, at]
        dn = ((g - normed * jnp.mean(g * normed, 1, keepdims=True)) * inv).astype(BF)
        dn_ref[:, at] = dn
        loc_ref[0, h] = run[h].astype(BF)
        run[h] = run[h] + mm_tn(dn, pq)

    @pl.when(c == pl.num_programs(0) - 1)
    def _():
        for h in range(heads):
            state_ref[h] = run[h].T[:ES].astype(BF)


def norm_part(g, num, gain, pq, pre, heads):
    rows, wide = g.shape
    n = rows // CH
    row = pl.BlockSpec((CH, wide), lambda c: (n - 1 - c, 0))
    return pl.pallas_call(
        functools.partial(norm_kernel, heads),
        grid=(n,),
        in_specs=[
            row,
            row,
            whole((1, wide)),
            pl.BlockSpec((heads, CH, EP), lambda c: (0, n - 1 - c, 0)),
            whole((heads, ES, DV)),
        ],
        out_specs=[
            row,
            row,
            pl.BlockSpec((1, heads, DV, EP), lambda c: (n - 1 - c, 0, 0, 0)),
            whole((heads, ES, DV)),
        ],
        out_shape=[
            jax.ShapeDtypeStruct((rows, wide), BF),
            jax.ShapeDtypeStruct((rows, wide), BF),
            jax.ShapeDtypeStruct((n, heads, DV, EP), BF),
            jax.ShapeDtypeStruct((heads, ES, DV), BF),
        ],
        scratch_shapes=[pltpu.VMEM((heads, DV, EP), F32)],
        compiler_params=params(),
        cost_estimate=pl.CostEstimate(flops=1 << 30, bytes_accessed=8 << 20, transcendentals=0),
        name="norm_part",
    )(g, num, gain, pq, pre)


def inner_kernel(heads, cv_ref, v_ref, pq_ref, pk_ref, dn_ref, loc_ref, pre_ref, sel_ref, bias_ref,
                 dqk_ref, dv_ref, pre_t):
    @pl.when(pl.program_id(0) == 0)
    def _():
        pre_t[...] = jnp.zeros_like(pre_t)
        for h in range(heads):
            pre_t[h, :, :ES] = pre_ref[h].astype(F32).T

    mask = causal()
    b0 = bias_ref[0:1]
    b1 = bias_ref[1:2]
    for h in range(heads):
        at = slice(DV * h, DV * h + DV)
        dn = dn_ref[:, at]
        logits = mm_nt(pq_ref[h, :, :FEAT], pk_ref[h, :, :FEAT])
        weights = jnp.where(mask, 1.0 + logits + 0.5 * logits * logits, 0.0).astype(BF)
        dv_ref[:, at] = mm_tn(weights, dn)
        dl = jnp.where(mask, mm_nt(dn, v_ref[:, at]) * (1.0 + logits), 0.0).astype(BF)
        state = (loc_ref[0, h].astype(F32) + pre_t[h]).astype(BF)
        dphi = mm(dn, state)
        cw = cv_ref[:, window(h)]
        u = mm(cw, sel_ref[h, :, : 2 * EP])
        da = (dphi * (u[:, EP:] + b1)).astype(BF)
        db = (dphi * (u[:, :EP] + b0)).astype(BF)
        moved = mm(cw, sel_ref[h, :, 4 * EP :]).astype(BF)
        dqk_ref[h] = (
            mm_nt(da, sel_ref[h, :, :EP])
            + mm_nt(db, sel_ref[h, :, EP : 2 * EP])
            + mm(dl, moved[:, :128])
            + mm_tn(dl, moved[:, 128:])
        )


def inner_part(cv, v, pq, pk, dn, loc, pre, sel, bias, heads):
    rows, width = cv.shape
    n = rows // CH
    wide = heads * DV
    row = pl.BlockSpec((CH, wide), lambda c: (c, 0))
    feat = pl.BlockSpec((heads, CH, EP), lambda c: (0, c, 0))
    return pl.pallas_call(
        functools.partial(inner_kernel, heads),
        grid=(n,),
        in_specs=[
            pl.BlockSpec((CH, width), lambda c: (c, 0)),
            row,
            feat,
            feat,
            row,
            pl.BlockSpec((1, heads, DV, EP), lambda c: (c, 0, 0, 0)),
            whole((heads, ES, DV)),
            whole(sel.shape),
            whole(bias.shape),
        ],
        out_specs=[pl.BlockSpec((heads, CH, 128), lambda c: (0, c, 0)), row],
        out_shape=[
            jax.ShapeDtypeStruct((heads, rows, 128), F32),
            jax.ShapeDtypeStruct((rows, wide), F32),
        ],
        scratch_shapes=[pltpu.VMEM((heads, DV, EP), F32)],
        compiler_params=params(),
        cost_estimate=pl.CostEstimate(flops=12 << 30, bytes_accessed=14 << 20, transcendentals=0),
        name="inner_part",
    )(cv, v, pq, pk, dn, loc, pre, sel, bias)


def outer_kernel(heads, cv_ref, v_ref, pk_ref, dqk_ref, dv_ref, loc_ref, suf_ref, sel_ref, bias_ref, cw_ref,
                 dp_ref, first_ref, last_ref, ext, suf_t):
    c = pl.program_id(0)
    width = cv_ref.shape[1]

    @pl.when(c == 0)
    def _():
        suf_t[...] = jnp.zeros_like(suf_t)
        for h in range(heads):
            suf_t[h, :, :ES] = suf_ref[h].astype(F32).T
        ext[CH:, :] = jnp.zeros((8, width), F32)

    b0 = bias_ref[0:1]
    b1 = bias_ref[1:2]
    lane = lane_iota()
    tiles = [None] * (-(-width // 128))

    def put(t, piece):
        tiles[t] = piece if tiles[t] is None else tiles[t] + piece

    for h in range(heads):
        at = slice(DV * h, DV * h + DV)
        state = (loc_ref[0, h].astype(F32) + suf_t[h]).astype(BF)
        dphi = mm(v_ref[:, at], state)
        u = mm(cv_ref[:, window(h)], sel_ref[h, :, 2 * EP : 4 * EP])
        da = (dphi * (u[:, EP:] + b1)).astype(BF)
        db = (dphi * (u[:, :EP] + b0)).astype(BF)
        dqk = (
            dqk_ref[h]
            + mm_nt(da, sel_ref[h, :, 2 * EP : 3 * EP])
            + mm_nt(db, sel_ref[h, :, 3 * EP : 4 * EP])
        )
        put((HW * h) // 128, dqk)
        dv = dv_ref[:, at] + mm_nt(pk_ref[h], state)
        tile, off = value_place(h)
        if off == 0:
            put(tile, dv)
        else:
            moved = pltpu.roll(dv, off, 1)
            put(tile, jnp.where(lane >= off, moved, 0.0))
            put(tile + 1, jnp.where(lane < off, moved, 0.0))
    for t, tile in enumerate(tiles):
        end = min(128 * t + 128, width)
        ext[:CH, 128 * t : end] = tile[:, : end - 128 * t]
    dp = (cw_ref[0:1] * ext[:CH, :] + cw_ref[1:2] * ext[1 : CH + 1, :]
          + cw_ref[2:3] * ext[2 : CH + 2, :])
    dp_ref[...] = dp.astype(BF)

    @pl.when(c == 0)
    def _():
        last_ref[...] = dp[CH - 16 :]

    ext[CH:, :] = ext[0:8, :]
    first_ref[...] = ext[0:8, :]


def outer_part(cv, v, pk, dqk, dv, loc, suf, sel, bias, conv_w, heads):
    rows, width = cv.shape
    n = rows // CH
    wide = heads * DV
    row = pl.BlockSpec((CH, wide), lambda c: (n - 1 - c, 0))
    full_row = pl.BlockSpec((CH, width), lambda c: (n - 1 - c, 0))
    return pl.pallas_call(
        functools.partial(outer_kernel, heads),
        grid=(n,),
        in_specs=[
            full_row,
            row,
            pl.BlockSpec((heads, CH, EP), lambda c: (0, n - 1 - c, 0)),
            pl.BlockSpec((heads, CH, 128), lambda c: (0, n - 1 - c, 0)),
            row,
            pl.BlockSpec((1, heads, DV, EP), lambda c: (n - 1 - c, 0, 0, 0)),
            whole((heads, ES, DV)),
            whole(sel.shape),
            whole(bias.shape),
            whole((3, width)),
        ],
        out_specs=[full_row, whole((8, width)), whole((16, width))],
        out_shape=[
            jax.ShapeDtypeStruct((rows, width), BF),
            jax.ShapeDtypeStruct((8, width), F32),
            jax.ShapeDtypeStruct((16, width), F32),
        ],
        scratch_shapes=[pltpu.VMEM((CH + 8, width), F32), pltpu.VMEM((heads, DV, EP), F32)],
        compiler_params=params(),
        cost_estimate=pl.CostEstimate(flops=6 << 30, bytes_accessed=12 << 20, transcendentals=0),
        name="outer_part",
    )(cv, v, pk, dqk, dv, loc, suf, sel, bias, conv_w)


def shifted(array, by):
    count = lax.axis_size("seq")
    pairs = [(i, i + by) for i in range(count) if 0 <= i + by < count]
    return lax.ppermute(array, "seq", pairs)


def summed_before(part, sign):
    count = lax.axis_size("seq")
    total = None
    for step in range(1, count):
        got = shifted(part, sign * step).astype(F32)
        total = got if total is None else total + got
    return total.astype(BF)


def per_device(inputs, cotangent, w_in, conv_w, norm_gain, w_out, keep_flags):
    heads = keep_flags.shape[0]
    rows = inputs.shape[0]
    sel, bias = selectors(heads)
    slice_width = inputs.shape[1] // lax.axis_size("tp")
    column = lax.axis_index("tp") * slice_width
    gain = (norm_gain.reshape(heads, DV) * keep_flags.astype(F32)[:, None]).reshape(1, heads * DV)
    halo = shifted(inputs[-16:], 1)
    cv, v, pq, pk, loc, state = project(inputs, halo, w_in, conv_w, sel, bias, heads)
    pre = summed_before(state, 1)
    g, num = local_part(cotangent, w_out, gain, v, pq, pk, loc, heads)
    ho, dn, gloc, gstate = norm_part(g, num, gain, pq, pre, heads)
    suf = summed_before(gstate, -1)
    out_term = jnp.dot(ho, w_out, preferred_element_type=F32).astype(BF)
    dqk, dv = inner_part(cv, v, pq, pk, dn, loc, pre, sel, bias, heads)
    dp, first, last = outer_part(cv, v, pk, dqk, dv, gloc, suf, sel, bias, conv_w, heads)
    after = shifted(first, -1)
    tail = last[14:] + jnp.stack(
        [conv_w[2] * after[0], conv_w[1] * after[0] + conv_w[2] * after[1]]
    )
    dp = lax.dynamic_update_slice(dp, tail.astype(BF), (rows - 2, 0))
    grad = lax.dot_general(dp, w_in, (((1,), (1,)), ((), ())), preferred_element_type=F32).astype(BF)
    out_sum = lax.psum_scatter(out_term, "tp", scatter_dimension=1, tiled=True)
    grad_sum = lax.psum_scatter(grad, "tp", scatter_dimension=1, tiled=True)
    x_own = lax.dynamic_slice_in_dim(inputs, column, slice_width, 1).astype(F32)
    c_own = lax.dynamic_slice_in_dim(cotangent, column, slice_width, 1).astype(F32)
    return (x_own + out_sum).astype(BF), (c_own + grad_sum).astype(BF)


def solution(mesh):
    placed = (
        P("seq", None),
        P("seq", None),
        P(None, "tp"),
        P(None, "tp"),
        P("tp"),
        P("tp", None),
        P("tp"),
    )
    return jax.shard_map(
        per_device,
        mesh=mesh,
        in_specs=placed,
        out_specs=(P("seq", "tp"), P("seq", "tp")),
        check_vma=False,
    )
```

profile of v0, /device:TPU:0, one launch (start us, length us, event | category | flops | bytes accessed | tf_op | source)
XLA Modules:
  0.0 228.8 jit_solution(11855024069199740651)
XLA Ops:
  7.2 0.0 reduce-scatter.3.cloned.1.call-start
  7.2 0.9 slice.20
  8.1 4.9 %collective-permute-start = (bf16[16,4096]{1,0:T(8,128)(2,1)S(1)}, bf16[16,4096]{1,0:T(8,128)(2,1)S(1)}, u32[]{:S(2)}, u32[]{:S(2)}) collective-permute-start(bf16[16,4096]{1,0:T(8,128)(2,1)S(1)} %slice.20), channel_id=1, source_target_pairs={{0,8},{8,16},{16,24},{1,9},{9,17},{17,25},{2,10},{10,18},{18,26},{... | collective-permute-start | bytes 393224 | tf_op jit(solution)/shard_map/ppermute | solution.py:427
  13.1 0.7 convert_element_type.55
  13.7 0.8 bitcast_multiply_fusion
  14.5 1.3 collective-permute-done.halo_ref
  15.8 0.7 copy-done.5
  16.5 2.5 %copy-done.7 = bf16[4096,640]{1,0:T(8,128)(2,1)S(1)} copy-done((bf16[4096,640]{1,0:T(8,128)(2,1)S(1)}, bf16[4096,640]{1,0:T(8,128)(2,1)}, u32[]{:S(2)}) %copy-start.7) | copy-done | bytes 5242904
  19.0 1.3 copy-done.12
  20.3 0.7 copy-done.15
  21.0 15.3 %project.1 = (bf16[1024,640]{1,0:T(8,128)(2,1)S(1)}, bf16[1024,512]{1,0:T(8,128)(2,1)S(1)}, bf16[4,1024,256]{2,1,0:T(8,128)(2,1)S(1)}, bf16[4,1024,256]{2,1,0:T(...) custom-call(bf16[1024,4096]{1,0:T(8,128)(2,1)} %x_ref.1, ...), custom_call_target="tpu_custom_call" | custom-call | flops 5368709120 | bytes 20971520 | tf_op jit(solution)/shard_map/project/pallas_call | solution.py:139
  36.3 0.0 copy-start
  36.3 0.0 copy-start.3
  36.3 0.0 copy-start.17
  36.3 4.4 %collective-permute-start.1 = (bf16[4,160,128]{2,1,0:T(8,128)(2,1)S(1)}, bf16[4,160,128]{2,1,0:T(8,128)(2,1)S(1)}, u32[]{:S(2)}, u32[]{:S(2)}) collective-permute-start(bf16[4,160,128]{2,1,0:T(8,128)(2,1)S(1)} %get-tuple-element.25), channel_id=1, source_target_pairs={{0,8},{8,16},{16,24},{1,9},{9,17},{17,25},{2,10},{10,18},{18,26},{... | collective-permute-start | bytes 491528 | tf_op jit(solution)/shard_map/ppermute | solution.py:427
  40.7 4.5 %collective-permute-start.2 = (bf16[4,160,128]{2,1,0:T(8,128)(2,1)S(1)}, bf16[4,160,128]{2,1,0:T(8,128)(2,1)S(1)}, u32[]{:S(2)}, u32[]{:S(2)}) collective-permute-start(bf16[4,160,128]{2,1,0:T(8,128)(2,1)S(1)} %get-tuple-element.25), channel_id=1, source_target_pairs={{0,16},{8,24},{1,17},{9,25},{2,18},{10,26},{3,19},{11,27},{4,20},{... | collective-permute-start | bytes 491528 | tf_op jit(solution)/shard_map/ppermute | solution.py:427
  45.2 1.3 collective-permute-start.3
  46.5 10.3 %local_part.1 = (f32[1024,512]{1,0:T(8,128)S(1)}, f32[1024,512]{1,0:T(8,128)S(1)}) custom-call(bf16[1024,4096]{1,0:T(8,128)(2,1)} %ct_ref.1, bf16[512,4096]{1,0:T(8,128)(2,1)} %wo_ref.1, f32[1,512]{1,0:T(1,128)S(1)} %bitcast.7, bf16[1024,512]{1,0:T(8,128)(2,1)S(1)} %get-tuple-element.19.v_ref, bf16[4,1024,256]{2,1,0:T(8,128)(2,1)S(1)} %get-tuple-element.20.pq_ref, ...), custom_call_target="tpu_custom_call" | custom-call | flops 4294967296 | bytes 20971520 | tf_op jit(solution)/shard_map/local_part/pallas_call | solution.py:190
  56.8 0.0 copy-done
  56.8 0.0 copy-done.3
  56.8 0.0 copy-done.17
  56.9 0.0 collective-permute-done.1
  56.9 0.0 collective-permute-done.2
  56.9 0.0 collective-permute-done.3
  56.9 0.1 add_convert_fusion.3.pre_ref
  57.0 0.0 copy-start.20
  57.0 7.7 %norm_part.1 = (bf16[1024,512]{1,0:T(8,128)(2,1)S(1)}, bf16[1024,512]{1,0:T(8,128)(2,1)S(1)}, bf16[4,4,128,256]{3,2,1,0:T(8,128)(2,1)S(1)}, bf16[4,160,128]{2,1,0:T(8,128)(2,1)S(1)}) custom-call(f32[1024,512]{1,0:T(8,128)S(1)} %get-tuple-element.23.g_ref, f32[1024,512]{1,0:T(8,128)S(1)} %get-tuple-element.24.num_ref, f32[1,512]{1,0:T(1,128)S(1)} %bitcast.8, ...), custom_call_target="tpu_custom_call" | custom-call | flops 1073741824 | bytes 8388608 | tf_op jit(solution)/shard_map/norm_part/pallas_call | solution.py:240
  64.7 0.0 copy-start.8
  64.7 1.0 copy-done.8
  65.7 1.0 copy-done.10
  66.7 0.0 copy-done.20
  66.7 6.7 %convolution_convert_fusion.1 = bf16[1024,4096]{1,0:T(8,128)(2,1)} fusion(bf16[1024,512]{1,0:T(8,128)(2,1)S(1)} %get-tuple-element.26, bf16[512,4096]{1,0:T(8,128)(2,1)S(1)} %copy-done.20), kind=kOutput, calls=%fused_computation.1 | convolution fusion | flops 4299161600 | bytes 13631488 | tf_op jit(solution)/shard_map/dot_general | solution.py:452
  73.4 0.0 reduce-scatter.3.cloned.1.call-update
  73.4 0.0 reduce-scatter.5.cloned.1.call-start
  73.4 1.3 collective-permute-start.4
  74.7 1.3 collective-permute-start.5
  76.0 1.5 collective-permute-start.6
  77.5 0.0 copy-done.16
  77.5 0.0 copy-start.1
  77.5 2.0 copy-done.1
  79.5 1.3 copy-done.4
  80.8 1.4 copy-done.11
  82.3 1.6 copy-done.13
  83.8 1.5 copy-done.18
  85.4 0.0 copy-start.19
  85.4 11.1 %inner_part.1 = (f32[4,1024,128]{2,1,0:T(8,128)S(1)}, f32[1024,512]{1,0:T(8,128)S(1)}) custom-call(bf16[1024,640]{1,0:T(8,128)(2,1)S(1)} %copy-done.18, bf16[1024,512]{1,0:T(8,128)(2,1)S(1)} %get-tuple-element.19.v_ref, bf16[4,1024,256]{2,1,0:T(8,128)(2,1)S(1)} %get-tuple-element.20.pq_ref, bf16[4,1024,256]{2,1,0:T(8,128)(2,1)S(1)} %copy-done.1, ...), custom_call_target="tpu_custom_call" | custom-call | flops 12884901888 | bytes 14680064 | tf_op jit(solution)/shard_map/inner_part/pallas_call | solution.py:308
  96.5 0.0 collective-permute-done.4
  96.5 0.0 collective-permute-done.5
  96.5 0.0 collective-permute-done.6
  96.5 0.1 add_convert_fusion.2.suf_ref
  96.6 0.0 copy-done.2
  96.6 0.0 copy-done.6
  96.6 0.0 copy-done.9
  96.6 0.0 copy-done.14
  96.6 0.0 copy-done.19
  96.7 5.7 %outer_part.1 = (bf16[1024,640]{1,0:T(8,128)(2,1)S(1)}, f32[8,640]{1,0:T(8,128)S(1)}, f32[16,640]{1,0:T(8,128)S(1)}) custom-call(bf16[1024,640]{1,0:T(8,128)(2,1)S(1)} %copy-done.19, bf16[1024,512]{1,0:T(8,128)(2,1)S(1)} %get-tuple-element.19.v_ref, bf16[4,1024,256]{2,1,0:T(8,128)(2,1)S(1)} %copy-done.2, f32[4,1024,128]{2,1,0:T(8,128)S(1)} %get-tuple-element.29.dqk_ref, ...), custom_call_target="tpu_custom_call" | custom-call | flops 6442450944 | bytes 12582912 | tf_op jit(solution)/shard_map/outer_part/pallas_call | solution.py:396
  102.4 1.3 collective-permute-start.7
  103.7 4.4 %collective-permute-done.7 = f32[8,640]{1,0:T(8,128)S(1)} collective-permute-done((f32[8,640]{1,0:T(8,128)S(1)}, f32[8,640]{1,0:T(8,128)S(1)}, u32[]{:S(2)}, u32[]{:S(2)}) %collective-permute-start.7) | collective-permute-done | bytes 20512 | tf_op jit(solution)/shard_map/ppermute | solution.py:427
  108.1 11.6 %convolution_convert_fusion = bf16[1024,4096]{1,0:T(8,128)(2,1)} fusion(bf16[1024,640]{1,0:T(8,128)(2,1)S(1)} %fusion.1, bf16[4096,640]{1,0:T(8,128)(2,1)} %w_ref.1), kind=kOutput, calls=%fused_computation | convolution fusion | flops 5372903424 | bytes 14942208 | tf_op jit(solution)/shard_map/dot_general | solution.py:460
  119.7 0.0 reduce-scatter.5.cloned.1.call-update
  119.7 24.3 %reduce-scatter.3.cloned.1.call-done = bf16[1024,512]{1,0:T(8,128)(2,1)} async-done(((bf16[1024,4096]{1,0:T(8,128)(2,1)}), bf16[1024,512]{1,0:T(8,128)(2,1)}) %reduce-scatter.3.cloned.1.call-update) | async-done | bytes 1048592 | tf_op jit(solution)/shard_map/reduce_scatter | solution.py:461
  144.0 2.8 %add_convert_fusion.1 = bf16[1024,512]{1,0:T(8,128)(2,1)} fusion(bf16[1024,512]{1,0:T(8,128)(2,1)} %reduce-scatter.3.cloned.1.call-done, bf16[1024,4096]{1,0:T(8,128)(2,1)} %x_ref.1, s32[]{:T(128)S(6)} %select_n.4), kind=kLoop, calls=%fused_computation.3 | loop fusion | flops 2097152 | bytes 3145732 | tf_op jit(solution)/shard_map/convert_element_type | solution.py:465
  146.8 72.4 %reduce-scatter.5.cloned.1.call-done = bf16[1024,512]{1,0:T(8,128)(2,1)} async-done(((bf16[1024,4096]{1,0:T(8,128)(2,1)}), bf16[1024,512]{1,0:T(8,128)(2,1)}) %reduce-scatter.5.cloned.1.call-update) | async-done | bytes 1048592 | tf_op jit(solution)/shard_map/reduce_scatter | solution.py:462
  219.2 2.8 %add_convert_fusion = bf16[1024,512]{1,0:T(8,128)(2,1)} fusion(bf16[1024,512]{1,0:T(8,128)(2,1)} %reduce-scatter.5.cloned.1.call-done, bf16[1024,4096]{1,0:T(8,128)(2,1)} %ct_ref.1, s32[]{:T(128)S(6)} %select_n.4), kind=kLoop, calls=%fused_computation.2 | loop fusion | flops 2097152 | bytes 3145732 | tf_op jit(solution)/shard_map/convert_element_type | solution.py:465
  (16 shorter events, 0.1 us)
Async XLA Ops:
  7.2 136.9 %reduce-scatter.3.cloned.1.call-start = ((), (), s32[]{:S(2)}) async-start(), calls=%async_computation.2 | async-start | bytes 9437184 | tf_op jit(solution)/shard_map/reduce_scatter | solution.py:461
  8.1 7.7 %collective-permute-start = (bf16[16,4096]{1,0:T(8,128)(2,1)S(1)}, bf16[16,4096]{1,0:T(8,128)(2,1)S(1)}, u32[]{:S(2)}, u32[]{:S(2)}) collective-permute-start(bf16[16,4096]{1,0:T(8,128)(2,1)S(1)} %slice.20), channel_id=1, source_target_pairs={{0,8},{8,16},{16,24},{1,9},{9,17},{17,25},{2,10},{10,18},{18,26},{... | collective-permute-start | bytes 393224 | tf_op jit(solution)/shard_map/ppermute | solution.py:427
  15.8 0.7 copy-start.5
  16.5 2.5 %copy-start.7 = (bf16[4096,640]{1,0:T(8,128)(2,1)S(1)}, bf16[4096,640]{1,0:T(8,128)(2,1)}, u32[]{:S(2)}) copy-start(bf16[4096,640]{1,0:T(8,128)(2,1)} %w_ref.1) | copy-start | bytes 15728644
  19.0 1.3 copy-start.12
  20.3 0.7 copy-start.15
  36.3 20.5 %copy-start = (bf16[4,1024,256]{2,1,0:T(8,128)(2,1)}, bf16[4,1024,256]{2,1,0:T(8,128)(2,1)S(1)}, u32[]{:S(2)}) copy-start(bf16[4,1024,256]{2,1,0:T(8,128)(2,1)S(1)} %get-tuple-element.21.pk_ref) | copy-start | bytes 6291460
  36.3 20.5 %copy-start.3 = (bf16[4,4,128,256]{3,2,1,0:T(8,128)(2,1)}, bf16[4,4,128,256]{3,2,1,0:T(8,128)(2,1)S(1)}, u32[]{:S(2)}) copy-start(bf16[4,4,128,256]{3,2,1,0:T(8,128)(2,1)S(1)} %get-tuple-element.22.loc_ref) | copy-start | bytes 3145732
  36.3 20.5 %copy-start.17 = (bf16[1024,640]{1,0:T(8,128)(2,1)}, bf16[1024,640]{1,0:T(8,128)(2,1)S(1)}, u32[]{:S(2)}) copy-start(bf16[1024,640]{1,0:T(8,128)(2,1)S(1)} %get-tuple-element.27.cv_ref) | copy-start | bytes 3932164
  36.3 20.5 %collective-permute-start.1 = (bf16[4,160,128]{2,1,0:T(8,128)(2,1)S(1)}, bf16[4,160,128]{2,1,0:T(8,128)(2,1)S(1)}, u32[]{:S(2)}, u32[]{:S(2)}) collective-permute-start(bf16[4,160,128]{2,1,0:T(8,128)(2,1)S(1)} %get-tuple-element.25), channel_id=1, source_target_pairs={{0,8},{8,16},{16,24},{1,9},{9,17},{17,25},{2,10},{10,18},{18,26},{... | collective-permute-start | bytes 491528 | tf_op jit(solution)/shard_map/ppermute | solution.py:427
  40.7 16.2 %collective-permute-start.2 = (bf16[4,160,128]{2,1,0:T(8,128)(2,1)S(1)}, bf16[4,160,128]{2,1,0:T(8,128)(2,1)S(1)}, u32[]{:S(2)}, u32[]{:S(2)}) collective-permute-start(bf16[4,160,128]{2,1,0:T(8,128)(2,1)S(1)} %get-tuple-element.25), channel_id=1, source_target_pairs={{0,16},{8,24},{1,17},{9,25},{2,18},{10,26},{3,19},{11,27},{4,20},{... | collective-permute-start | bytes 491528 | tf_op jit(solution)/shard_map/ppermute | solution.py:427
  45.2 11.7 %collective-permute-start.3 = (bf16[4,160,128]{2,1,0:T(8,128)(2,1)S(1)}, bf16[4,160,128]{2,1,0:T(8,128)(2,1)S(1)}, u32[]{:S(2)}, u32[]{:S(2)}) collective-permute-start(bf16[4,160,128]{2,1,0:T(8,128)(2,1)S(1)} %get-tuple-element.25), channel_id=1, source_target_pairs={{0,24},{1,25},{2,26},{3,27},{4,28},{5,29},{6,30},{7,31}} | collective-permute-start | bytes 491528 | tf_op jit(solution)/shard_map/ppermute | solution.py:427
  57.0 9.7 %copy-start.20 = (bf16[512,4096]{1,0:T(8,128)(2,1)S(1)}, bf16[512,4096]{1,0:T(8,128)(2,1)}, u32[]{:S(2)}) copy-start(bf16[512,4096]{1,0:T(8,128)(2,1)} %wo_ref.1) | copy-start | bytes 12582916
  64.7 1.0 copy-start.8
  65.7 1.0 copy-start.10
  73.4 4.2 %copy-start.16 = (f32[8,256]{1,0:T(8,128)S(1)}, f32[8,256]{1,0:T(8,128)}, u32[]{:S(2)}) copy-start(f32[8,256]{1,0:T(8,128)} %constant.17.clone.bias_ref) | copy-start | bytes 24580
  73.4 145.8 %reduce-scatter.5.cloned.1.call-start = ((), (), s32[]{:S(2)}) async-start(), calls=%async_computation.3 | async-start | bytes 9437184 | tf_op jit(solution)/shard_map/reduce_scatter | solution.py:462
  73.4 23.1 %collective-permute-start.4 = (bf16[4,160,128]{2,1,0:T(8,128)(2,1)S(1)}, bf16[4,160,128]{2,1,0:T(8,128)(2,1)S(1)}, u32[]{:S(2)}, u32[]{:S(2)}) collective-permute-start(bf16[4,160,128]{2,1,0:T(8,128)(2,1)S(1)} %get-tuple-element.32), channel_id=1, source_target_pairs={{8,0},{16,8},{24,16},{9,1},{17,9},{25,17},{10,2},{18,10},{26,18},{... | collective-permute-start | bytes 491528 | tf_op jit(solution)/shard_map/ppermute | solution.py:427
  74.7 21.8 %collective-permute-start.5 = (bf16[4,160,128]{2,1,0:T(8,128)(2,1)S(1)}, bf16[4,160,128]{2,1,0:T(8,128)(2,1)S(1)}, u32[]{:S(2)}, u32[]{:S(2)}) collective-permute-start(bf16[4,160,128]{2,1,0:T(8,128)(2,1)S(1)} %get-tuple-element.32), channel_id=1, source_target_pairs={{16,0},{24,8},{17,1},{25,9},{18,2},{26,10},{19,3},{27,11},{20,4},{... | collective-permute-start | bytes 491528 | tf_op jit(solution)/shard_map/ppermute | solution.py:427
  76.0 20.5 %collective-permute-start.6 = (bf16[4,160,128]{2,1,0:T(8,128)(2,1)S(1)}, bf16[4,160,128]{2,1,0:T(8,128)(2,1)S(1)}, u32[]{:S(2)}, u32[]{:S(2)}) collective-permute-start(bf16[4,160,128]{2,1,0:T(8,128)(2,1)S(1)} %get-tuple-element.32), channel_id=1, source_target_pairs={{24,0},{25,1},{26,2},{27,3},{28,4},{29,5},{30,6},{31,7}} | collective-permute-start | bytes 491528 | tf_op jit(solution)/shard_map/ppermute | solution.py:427
  77.5 2.0 copy-start.1
  79.5 1.3 copy-start.4
  80.8 1.4 copy-start.11
  82.3 1.6 copy-start.13
  83.8 1.5 copy-start.18
  85.3 11.3 %copy-start.2 = (bf16[4,1024,256]{2,1,0:T(8,128)(2,1)S(1)}, bf16[4,1024,256]{2,1,0:T(8,128)(2,1)}, u32[]{:S(2)}) copy-start(bf16[4,1024,256]{2,1,0:T(8,128)(2,1)} %copy-done) | copy-start | bytes 6291460
  85.3 11.3 %copy-start.6 = (f32[3,640]{1,0:T(4,128)S(1)}, f32[3,640]{1,0:T(4,128)}, u32[]{:S(2)}) copy-start(f32[3,640]{1,0:T(4,128)} %cw_ref.3) | copy-start | bytes 23044
  85.4 11.3 %copy-start.9 = (bf16[4,4,128,256]{3,2,1,0:T(8,128)(2,1)S(1)}, bf16[4,4,128,256]{3,2,1,0:T(8,128)(2,1)}, u32[]{:S(2)}) copy-start(bf16[4,4,128,256]{3,2,1,0:T(8,128)(2,1)} %copy-done.8) | copy-start | bytes 3145732
  85.4 11.3 %copy-start.14 = (bf16[4,128,1280]{2,1,0:T(8,128)(2,1)S(1)}, bf16[4,128,1280]{2,1,0:T(8,128)(2,1)}, u32[]{:S(2)}) copy-start(bf16[4,128,1280]{2,1,0:T(8,128)(2,1)} %constant.16.clone.sel_ref) | copy-start | bytes 3932164
  85.4 11.3 %copy-start.19 = (bf16[1024,640]{1,0:T(8,128)(2,1)S(1)}, bf16[1024,640]{1,0:T(8,128)(2,1)}, u32[]{:S(2)}) copy-start(bf16[1024,640]{1,0:T(8,128)(2,1)} %copy-done.17) | copy-start | bytes 3932164
  102.4 5.7 %collective-permute-start.7 = (f32[8,640]{1,0:T(8,128)S(1)}, f32[8,640]{1,0:T(8,128)S(1)}, u32[]{:S(2)}, u32[]{:S(2)}) collective-permute-start(f32[8,640]{1,0:T(8,128)S(1)} %get-tuple-element.35), channel_id=1, source_target_pairs={{8,0},{16,8},{24,16},{9,1},{17,9},{25,17},{10,2},{18,10},{26,18},{... | collective-permute-start | bytes 61448 | tf_op jit(solution)/shard_map/ppermute | solution.py:427
Sparse Core Ops, SparseCore 0:
  73.5 70.4 reduce-scatter.2
  147.9 71.2 reduce-scatter.4
where the time goes:
time: 230 us; the launch traced here: 229 us
  waiting for transfers between devices  102 us (44%)
  Pallas kernels  50.1 us (22%)
  starting transfers between devices  20.6 us (9%)
  matrix products  18.3 us (8%)
  local copies, waits for them, and re-layouts  16 us (7%)
  between operations  14.4 us (6%)
  other arithmetic  7.17 us (3%)
    reduce_scatter x1, waiting for transfers between devices, per_device(): grad_sum = lax.psum_scatter(grad, 'tp', scatter_dimension=1, tiled=True)  72.4 us
    reduce_scatter x1, waiting for transfers between devices, per_device(): out_sum = lax.psum_scatter(out_term, 'tp', scatter_dimension=1, tiled=True)  24.3 us
    ppermute x8, starting transfers between devices, shifted(): return lax.ppermute(array, 'seq', pairs)  20.5 us
    pallas_call x1, Pallas kernels, project(): pl.pallas_call(functools.partial(project_kernel, heads), grid=(n,), in_sp...  15.3 us
    unnamed x42, local copies, waits for them, and re-layouts  15 us
    dot_general x1, matrix products, per_device(): lax.dot_general(dp, w_in, (((1,), (1,)), ((), ())), preferred_element_typ...  11.6 us
    pallas_call x1, Pallas kernels, inner_part(): pl.pallas_call(functools.partial(inner_kernel, heads), grid=(n,), in_spec...  11.1 us
    pallas_call x1, Pallas kernels, local_part(): pl.pallas_call(functools.partial(local_kernel, heads), grid=(n,), in_spec...  10.3 us
  transfers between devices with their start and end apart: 10, of which 4 were waited for; matrix products, arithmetic and copies ran while one was open for 7% of the time, Pallas kernels for 12%

commit v1 on v0

v1 whole, which is shorter than its diff:
```python
import functools

import jax
import jax.numpy as jnp
import numpy as np
from jax import lax
from jax.experimental import pallas as pl
from jax.experimental.pallas import tpu as pltpu
from jax.sharding import PartitionSpec as P

FEAT = 16
DV = 128
HW = 2 * FEAT + DV
EP = 256
ES = 160
CH = 256
EPS = 1e-06
BF = jnp.bfloat16
F32 = jnp.float32
VMEM = 16 * 1024 * 1024


def mm(a, b):
    return lax.dot_general(a, b, (((1,), (0,)), ((), ())), preferred_element_type=F32)


def mm_nt(a, b):
    return lax.dot_general(a, b, (((1,), (1,)), ((), ())), preferred_element_type=F32)


def mm_tn(a, b):
    return lax.dot_general(a, b, (((0,), (0,)), ((), ())), preferred_element_type=F32)


def selectors(heads):
    sel = np.zeros((heads, 128, 4 * EP + 256), np.float32)
    bias = np.zeros((8, EP), np.float32)
    bias[1, :FEAT] = 1.0
    bias[0, FEAT] = bias[1, FEAT] = 1.0
    for h in range(heads):
        q0 = (HW * h) % 128
        k0 = q0 + FEAT
        for i in range(FEAT):
            sel[h, q0 + i, i] = 0.5
            sel[h, k0 + i, 2 * EP + i] = 0.5
            sel[h, k0 + i, 4 * EP + q0 + i] = 0.25
            sel[h, q0 + i, 4 * EP + 128 + k0 + i] = 0.25
        col = FEAT + 1
        for i in range(FEAT):
            for j in range(i, FEAT):
                sel[h, q0 + i, col] = 0.25 if i == j else 0.5
                sel[h, q0 + j, EP + col] = 0.5
                sel[h, k0 + i, 2 * EP + col] = 0.5
                sel[h, k0 + j, 3 * EP + col] = 0.5
                col += 1
    return jnp.asarray(sel, BF), jnp.asarray(bias, F32)


def window(h):
    t = (HW * h) // 128
    return slice(128 * t, 128 * t + 128)


def value_place(h):
    start = HW * h + 2 * FEAT
    return start // 128, start % 128


def lane_iota():
    return lax.broadcasted_iota(jnp.int32, (CH, 128), 1)


def take_values(conv, h):
    tile, off = value_place(h)
    first = conv[:, 128 * tile : 128 * tile + 128]
    if off == 0:
        return first
    second = conv[:, 128 * tile + 128 : min(128 * tile + 256, conv.shape[1])]
    if second.shape[1] < 128:
        second = jnp.concatenate([second, jnp.zeros((CH, 128 - second.shape[1]), second.dtype)], 1)
    a = pltpu.roll(first, 128 - off, 1)
    b = pltpu.roll(second, 128 - off, 1)
    return jnp.where(lane_iota() < 128 - off, a, b)


def causal():
    r = lax.broadcasted_iota(jnp.int32, (CH, CH), 0)
    c = lax.broadcasted_iota(jnp.int32, (CH, CH), 1)
    return r >= c


def params():
    return pltpu.CompilerParams(dimension_semantics=("arbitrary",), vmem_limit_bytes=VMEM)


def whole(shape):
    return pl.BlockSpec(shape, lambda c, *_: (0,) * len(shape))


KEPT = pl.BlockSpec(memory_space=pltpu.VMEM)


def kept(shape, dtype):
    return pltpu.VMEM(shape, dtype)


def keep(array):
    return pltpu.with_memory_space_constraint(array, pltpu.VMEM)


def stay(array):
    return pltpu.with_memory_space_constraint(array, pltpu.HBM)


def cost(flops):
    return pl.CostEstimate(flops=int(flops), bytes_accessed=1 << 20, transcendentals=0)


LIGHT = cost(1000)


def rows_at(c):
    return pl.ds(pl.multiple_of(c * CH, CH), CH)


def project_kernel(heads, x_ref, halo_ref, w_ref, cw_ref, sel_ref, bias_ref,
                   cv_ref, v_ref, pq_ref, pk_ref, loc_ref, state_ref, ext, run):
    c = pl.program_id(0)
    at = rows_at(c)

    @pl.when(c == 0)
    def _():
        before = mm(halo_ref[...], w_ref[...]).astype(BF).astype(F32)
        ext[0:8, :] = before[8:16]
        run[...] = jnp.zeros_like(run)

    ext[8:, :] = mm(x_ref[...], w_ref[...]).astype(BF).astype(F32)
    conv = (cw_ref[0:1] * ext[8 : 8 + CH, :] + cw_ref[1:2] * ext[7 : 7 + CH, :]
            + cw_ref[2:3] * ext[6 : 6 + CH, :])
    ext[0:8, :] = ext[CH : CH + 8, :]
    conv_b = conv.astype(BF)
    cv_ref[at, :] = conv_b
    conv = conv_b.astype(F32)
    b0 = bias_ref[0:1]
    b1 = bias_ref[1:2]
    for h in range(heads):
        u = mm(conv_b[:, window(h)], sel_ref[h, :, : 4 * EP])
        pq_ref[h, at, :] = ((u[:, :EP] + b0) * (u[:, EP : 2 * EP] + b1)).astype(BF)
        pk = ((u[:, 2 * EP : 3 * EP] + b0) * (u[:, 3 * EP :] + b1)).astype(BF)
        pk_ref[h, at, :] = pk
        v = take_values(conv, h).astype(BF)
        v_ref[at, DV * h : DV * h + DV] = v
        loc_ref[c, h] = run[h].astype(BF)
        run[h] = run[h] + mm_tn(v, pk)

    @pl.when(c == pl.num_programs(0) - 1)
    def _():
        for h in range(heads):
            state_ref[h] = run[h].T[:ES].astype(BF)


def project(x, halo, w_in, conv_w, sel, bias, heads):
    rows, d = x.shape
    width = w_in.shape[1]
    n = rows // CH
    return pl.pallas_call(
        functools.partial(project_kernel, heads),
        grid=(n,),
        in_specs=[
            pl.BlockSpec((CH, d), lambda c: (c, 0)),
            whole((16, d)),
            KEPT,
            whole((3, width)),
            KEPT,
            whole(bias.shape),
        ],
        out_specs=[KEPT] * 5 + [whole((heads, ES, DV))],
        out_shape=[
            kept((rows, width), BF),
            kept((rows, heads * DV), BF),
            kept((heads, rows, EP), BF),
            kept((heads, rows, EP), BF),
            kept((n, heads, DV, EP), BF),
            jax.ShapeDtypeStruct((heads, ES, DV), BF),
        ],
        scratch_shapes=[pltpu.VMEM((CH + 8, width), F32), pltpu.VMEM((heads, DV, EP), F32)],
        compiler_params=params(),
        cost_estimate=cost(100 << 30),
        name="project",
    )(stay(x), halo, keep(w_in), conv_w, keep(sel), bias)


def local_kernel(heads, ct_ref, wo_ref, gain_ref, v_ref, pq_ref, pk_ref, loc_ref, cv_ref, sel_ref, g_ref, num_ref):
    c = pl.program_id(0)
    at = rows_at(c)
    g_ref[at, :] = mm_nt(ct_ref[...], wo_ref[...]) * gain_ref[...]
    mask = causal()
    for h in range(heads):
        pq = pq_ref[h, at, :]
        logits = mm_nt(pq[:, :FEAT], pk_ref[h, at, :FEAT])
        weights = jnp.where(mask, 1.0 + logits + 0.5 * logits * logits, 0.0).astype(BF)
        lanes = slice(DV * h, DV * h + DV)
        num_ref[at, lanes] = mm(weights, v_ref[at, lanes]) + mm_nt(pq, loc_ref[c, h])


def local_part(ct, w_out, gain, v, pq, pk, loc, cv, sel, heads):
    rows, d = ct.shape
    n = rows // CH
    wide = heads * DV
    return pl.pallas_call(
        functools.partial(local_kernel, heads),
        grid=(n,),
        in_specs=[pl.BlockSpec((CH, d), lambda c: (c, 0)), KEPT, whole((1, wide))] + [KEPT] * 6,
        out_specs=[KEPT, KEPT],
        out_shape=[kept((rows, wide), F32)] * 2,
        compiler_params=params(),
        cost_estimate=LIGHT,
        name="local_part",
    )(stay(ct), keep(w_out), gain, *map(keep, (v, pq, pk, loc, cv, sel)))


def norm_kernel(heads, parts, g_ref, num_ref, gain_ref, pq_ref, *refs):
    got = refs[:parts]
    ho_ref, dn_ref, loc_ref, pre_ref, state_ref, run = refs[parts + 5 :]
    step = pl.program_id(0)
    c = pl.num_programs(0) - 1 - step
    at = rows_at(c)

    @pl.when(step == 0)
    def _():
        run[...] = jnp.zeros_like(run)
        total = got[0][...].astype(F32)
        for one in got[1:]:
            total = total + one[...].astype(F32)
        pre_ref[...] = total.astype(BF)

    for h in range(heads):
        lanes = slice(DV * h, DV * h + DV)
        pq = pq_ref[h, at, :]
        num = num_ref[at, lanes] + mm(pq[:, :ES], pre_ref[h])
        inv = lax.rsqrt(jnp.mean(num * num, 1, keepdims=True) + EPS)
        normed = num * inv
        ho_ref[at, lanes] = (normed * gain_ref[:, lanes]).astype(BF)
        g = g_ref[at, lanes]
        dn = ((g - normed * jnp.mean(g * normed, 1, keepdims=True)) * inv).astype(BF)
        dn_ref[at, lanes] = dn
        loc_ref[c, h] = run[h].astype(BF)
        run[h] = run[h] + mm_tn(dn, pq)

    @pl.when(step == pl.num_programs(0) - 1)
    def _():
        for h in range(heads):
            state_ref[h] = run[h].T[:ES].astype(BF)


def norm_part(g, num, gain, pq, got, later, heads):
    rows, wide = g.shape
    n = rows // CH
    return pl.pallas_call(
        functools.partial(norm_kernel, heads, len(got)),
        grid=(n,),
        in_specs=[KEPT, KEPT, whole((1, wide)), KEPT] + [whole((heads, ES, DV))] * len(got) + [KEPT] * 5,
        out_specs=[KEPT] * 4 + [whole((heads, ES, DV))],
        out_shape=[
            kept((rows, wide), BF),
            kept((rows, wide), BF),
            kept((n, heads, DV, EP), BF),
            kept((heads, ES, DV), BF),
            jax.ShapeDtypeStruct((heads, ES, DV), BF),
        ],
        scratch_shapes=[pltpu.VMEM((heads, DV, EP), F32)],
        compiler_params=params(),
        cost_estimate=LIGHT,
        name="norm_part",
    )(keep(g), keep(num), gain, keep(pq), *got, *map(keep, later))


def inner_kernel(heads, cv_ref, v_ref, pq_ref, pk_ref, dn_ref, loc_ref, pre_ref, sel_ref, gloc_ref, bias_ref,
                 dqk_ref, dv_ref, pre_t):
    c = pl.program_id(0)
    at = rows_at(c)

    @pl.when(c == 0)
    def _():
        pre_t[...] = jnp.zeros_like(pre_t)
        for h in range(heads):
            pre_t[h, :, :ES] = pre_ref[h].astype(F32).T

    mask = causal()
    b0 = bias_ref[0:1]
    b1 = bias_ref[1:2]
    dqk = None
    for h in range(heads):
        lanes = slice(DV * h, DV * h + DV)
        dn = dn_ref[at, lanes]
        logits = mm_nt(pq_ref[h, at, :FEAT], pk_ref[h, at, :FEAT])
        weights = jnp.where(mask, 1.0 + logits + 0.5 * logits * logits, 0.0).astype(BF)
        dv_ref[at, lanes] = mm_tn(weights, dn)
        dl = jnp.where(mask, mm_nt(dn, v_ref[at, lanes]) * (1.0 + logits), 0.0).astype(BF)
        state = (loc_ref[c, h].astype(F32) + pre_t[h]).astype(BF)
        dphi = mm(dn, state)
        cw = cv_ref[at, window(h)]
        u = mm(cw, sel_ref[h, :, : 2 * EP])
        da = (dphi * (u[:, EP:] + b1)).astype(BF)
        db = (dphi * (u[:, :EP] + b0)).astype(BF)
        moved = mm(cw, sel_ref[h, :, 4 * EP :]).astype(BF)
        part = (
            mm_nt(da, sel_ref[h, :, :EP])
            + mm_nt(db, sel_ref[h, :, EP : 2 * EP])
            + mm(dl, moved[:, :128])
            + mm_tn(dl, moved[:, 128:])
        )
        dqk = part if dqk is None else dqk + part
    dqk_ref[at, :] = dqk


def inner_part(cv, v, pq, pk, dn, loc, pre, sel, gloc, bias, heads):
    rows = cv.shape[0]
    n = rows // CH
    return pl.pallas_call(
        functools.partial(inner_kernel, heads),
        grid=(n,),
        in_specs=[KEPT] * 9 + [whole(bias.shape)],
        out_specs=[KEPT, KEPT],
        out_shape=[kept((rows, 128), F32), kept((rows, heads * DV), F32)],
        scratch_shapes=[pltpu.VMEM((heads, DV, EP), F32)],
        compiler_params=params(),
        cost_estimate=LIGHT,
        name="inner_part",
    )(*map(keep, (cv, v, pq, pk, dn, loc, pre, sel, gloc)), bias)


def outer_kernel(heads, parts, cv_ref, v_ref, pk_ref, dqk_ref, dv_ref, loc_ref, sel_ref, bias_ref, cw_ref, *refs):
    got = refs[:parts]
    dp_ref, first_ref, last_ref, ext, suf_t = refs[parts:]
    step = pl.program_id(0)
    c = pl.num_programs(0) - 1 - step
    at = rows_at(c)
    width = cv_ref.shape[1]

    @pl.when(step == 0)
    def _():
        suf_t[...] = jnp.zeros_like(suf_t)
        for h in range(heads):
            total = got[0][h].astype(F32)
            for one in got[1:]:
                total = total + one[h].astype(F32)
            suf_t[h, :, :ES] = total.T
        ext[CH:, :] = jnp.zeros((8, width), F32)

    b0 = bias_ref[0:1]
    b1 = bias_ref[1:2]
    lane = lane_iota()
    tiles = [None] * (-(-width // 128))

    def put(t, piece):
        tiles[t] = piece if tiles[t] is None else tiles[t] + piece

    dqk = dqk_ref[at, :]
    for h in range(heads):
        lanes = slice(DV * h, DV * h + DV)
        state = (loc_ref[c, h].astype(F32) + suf_t[h]).astype(BF)
        dphi = mm(v_ref[at, lanes], state)
        u = mm(cv_ref[at, window(h)], sel_ref[h, :, 2 * EP : 4 * EP])
        da = (dphi * (u[:, EP:] + b1)).astype(BF)
        db = (dphi * (u[:, :EP] + b0)).astype(BF)
        own = (
            dqk
            + mm_nt(da, sel_ref[h, :, 2 * EP : 3 * EP])
            + mm_nt(db, sel_ref[h, :, 3 * EP : 4 * EP])
        )
        q0 = (HW * h) % 128
        put((HW * h) // 128, jnp.where((lane >= q0) & (lane < q0 + 2 * FEAT), own, 0.0))
        dv = dv_ref[at, lanes] + mm_nt(pk_ref[h, at, :], state)
        tile, off = value_place(h)
        if off == 0:
            put(tile, dv)
        else:
            moved = pltpu.roll(dv, off, 1)
            put(tile, jnp.where(lane >= off, moved, 0.0))
            put(tile + 1, jnp.where(lane < off, moved, 0.0))
    for t, tile in enumerate(tiles):
        end = min(128 * t + 128, width)
        ext[:CH, 128 * t : end] = tile[:, : end - 128 * t]
    dp = (cw_ref[0:1] * ext[:CH, :] + cw_ref[1:2] * ext[1 : CH + 1, :]
          + cw_ref[2:3] * ext[2 : CH + 2, :])
    dp_ref[at, :] = dp.astype(BF)

    @pl.when(step == 0)
    def _():
        last_ref[...] = dp[CH - 16 :]

    ext[CH:, :] = ext[0:8, :]
    first_ref[...] = ext[0:8, :]


def outer_part(cv, v, pk, dqk, dv, loc, got, sel, bias, conv_w, heads):
    rows, width = cv.shape
    n = rows // CH
    return pl.pallas_call(
        functools.partial(outer_kernel, heads, len(got)),
        grid=(n,),
        in_specs=[KEPT] * 7
        + [whole(bias.shape), whole((3, width))]
        + [whole((heads, ES, DV))] * len(got),
        out_specs=[KEPT, whole((8, width)), KEPT],
        out_shape=[
            kept((rows, width), BF),
            jax.ShapeDtypeStruct((8, width), F32),
            kept((16, width), F32),
        ],
        scratch_shapes=[pltpu.VMEM((CH + 8, width), F32), pltpu.VMEM((heads, DV, EP), F32)],
        compiler_params=params(),
        cost_estimate=LIGHT,
        name="outer_part",
    )(*map(keep, (cv, v, pk, dqk, dv, loc, sel)), bias, conv_w, *got)


def columns_kernel(count, place_ref, w_ref, *refs):
    outs, sems = refs[: count - 1], refs[-1]
    wide = outs[0].shape[1]
    copies = []
    for m in range(1, count):
        start = pl.multiple_of(lax.bitwise_xor(place_ref[0], m) * wide, wide)
        copies.append(
            pltpu.make_async_copy(w_ref.at[:, pl.ds(start, wide)], outs[m - 1], sems.at[m - 1])
        )
    for copy in copies:
        copy.start()
    for copy in copies:
        copy.wait()


def columns(place, w_out, count):
    rows, d = w_out.shape
    anywhere = pl.BlockSpec(memory_space=pltpu.HBM)
    return pl.pallas_call(
        functools.partial(columns_kernel, count),
        grid_spec=pltpu.PrefetchScalarGridSpec(
            num_scalar_prefetch=1,
            grid=(1,),
            in_specs=[anywhere],
            out_specs=[anywhere] * (count - 1),
            scratch_shapes=[pltpu.SemaphoreType.DMA((count - 1,))],
        ),
        out_shape=[jax.ShapeDtypeStruct((rows, d // count), w_out.dtype)] * (count - 1),
        compiler_params=pltpu.CompilerParams(vmem_limit_bytes=VMEM),
        cost_estimate=LIGHT,
        name="columns",
    )(place, stay(w_out))


def shifted(array, by):
    count = lax.axis_size("seq")
    pairs = [(i, i + by) for i in range(count) if 0 <= i + by < count]
    return lax.ppermute(array, "seq", pairs)


def from_others(part, sign):
    return [shifted(part, sign * step) for step in range(1, lax.axis_size("seq"))]


def out_kernel(count, sw, place_ref, *refs):
    tops, lows, ws = refs[:count], refs[count : 2 * count], refs[2 * count : 3 * count]
    send_ref, keep_ref = refs[3 * count :]
    c = pl.program_id(0)
    half_chunks = pl.num_programs(0) // 2
    odd = place_ref[1] == 1

    def product(parts):
        total = None
        for part, w in zip(parts, ws):
            one = mm(part[...], w[...])
            total = one if total is None else total + one
        first, second = total[:, :sw], total[:, sw:]
        send_ref[...] = jnp.where(odd, first, second).astype(BF)
        keep_ref[...] = jnp.where(odd, second, first)

    @pl.when(c < half_chunks)
    def _():
        product(tops)

    @pl.when(c >= half_chunks)
    def _():
        product(lows)


def out_part(place, tops, lows, ws):
    count = len(ws)
    rows = 2 * CH * (lows[0][1] // CH)
    wide = tops[0][0].shape[1]
    sw = ws[1].shape[1] // 2
    part = rows // (2 * CH)
    row = pl.BlockSpec((CH, sw), lambda c, place: (c, 0))
    operands, specs = [], []
    for array, start in tops:
        operands.append(array)
        specs.append(
            pl.BlockSpec((CH, wide), lambda c, place, s=start // CH: (s + jnp.minimum(c, part - 1), 0))
        )
    for array, start in lows:
        operands.append(array)
        specs.append(
            pl.BlockSpec((CH, wide), lambda c, place, s=start // CH: (s + jnp.maximum(c - part, 0), 0))
        )
    return pl.pallas_call(
        functools.partial(out_kernel, count, sw),
        grid_spec=pltpu.PrefetchScalarGridSpec(
            num_scalar_prefetch=1,
            grid=(rows // CH,),
            in_specs=specs
            + [pl.BlockSpec((wide, 2 * sw), lambda c, place: (0, place[0]))]
            + [pl.BlockSpec((wide, 2 * sw), lambda c, place: (0, 0))] * (count - 1),
            out_specs=[row, row],
        ),
        out_shape=[jax.ShapeDtypeStruct((rows, sw), BF), jax.ShapeDtypeStruct((rows, sw), F32)],
        compiler_params=params(),
        cost_estimate=LIGHT,
        name="out_part",
    )(place, *operands, *map(stay, ws))


def grad_top_kernel(place_ref, dp_ref, w_ref, out_ref):
    half, sw = out_ref.shape[1:]
    block = 2 * lax.bitwise_xor(place_ref[0], pl.program_id(0)) + 1 - place_ref[1]
    w = w_ref[pl.ds(pl.multiple_of(block * sw, sw), sw), :]
    out_ref[0] = mm_nt(dp_ref[:half, :], w).astype(BF)


def grad_low_kernel(place_ref, dp_ref, w_ref, last_ref, after_ref, cw_ref, x_ref, y_ref,
                    out_ref, low_ref, x_top_ref, y_low_ref):
    half, sw = out_ref.shape[1:]
    r = pl.program_id(0)

    @pl.when(r == 0)
    def _():
        low_ref[...] = dp_ref[half:, :]
        row = lax.broadcasted_iota(jnp.int32, last_ref.shape, 0)
        a0, a1 = after_ref[0:1], after_ref[1:2]
        one = cw_ref[2:3] * a0
        two = cw_ref[1:2] * a0 + cw_ref[2:3] * a1
        tail = last_ref[...] + jnp.where(row == 14, one, 0.0) + jnp.where(row == 15, two, 0.0)
        low_ref[half - 16 :, :] = tail.astype(BF)
        x_top_ref[...] = x_ref[:half, :]
        y_low_ref[...] = y_ref[half:, :]

    block = 2 * lax.bitwise_xor(place_ref[0], r) + 1 - place_ref[1]
    w = w_ref[pl.ds(pl.multiple_of(block * sw, sw), sw), :]
    out_ref[0] = mm_nt(low_ref[...], w).astype(BF)


def grad_send(place, dp, w_in, count, halo=None):
    rows, width = dp.shape
    half = rows // 2
    sw = w_in.shape[0] // (2 * count)
    out_spec = pl.BlockSpec((1, half, sw), lambda r, place: (r, 0, 0))
    out_shape = jax.ShapeDtypeStruct((count, half, sw), BF)
    args = [keep(dp), keep(w_in)]
    in_specs = [KEPT, KEPT]
    if halo is not None:
        last, after, conv_w, x_got, y_got = halo
        args += [keep(last), after, conv_w, keep(x_got), keep(y_got)]
        in_specs += [KEPT, whole((8, width)), whole((3, width)), KEPT, KEPT]
        out_spec = [out_spec, KEPT, KEPT, KEPT]
        out_shape = [out_shape, kept((half, width), BF)] + [kept((half, x_got.shape[1]), BF)] * 2
    return pl.pallas_call(
        grad_top_kernel if halo is None else grad_low_kernel,
        grid_spec=pltpu.PrefetchScalarGridSpec(
            num_scalar_prefetch=1, grid=(count,), in_specs=in_specs, out_specs=out_spec
        ),
        out_shape=out_shape,
        compiler_params=params(),
        cost_estimate=LIGHT,
        name="grad_top" if halo is None else "grad_low",
    )(place, *args)


def grad_keep_kernel(count, low_first, place_ref, dp_ref, w_ref, got_ref, send_ref, keep_ref):
    r = pl.program_id(0)
    half, sw = got_ref.shape[1:]
    block = 2 * lax.bitwise_xor(place_ref[0], r) + place_ref[1]
    w = w_ref[pl.ds(pl.multiple_of(block * sw, sw), sw), :]
    total = (mm_nt(dp_ref[:half, :], w) + got_ref[0].astype(F32)).astype(BF)
    leaves = (r % 2 == 1) if low_first else (r >= count // 2)

    @pl.when(leaves)
    def _():
        send_ref[0] = total

    @pl.when(jnp.logical_not(leaves))
    def _():
        keep_ref[0] = total


def grad_keep(place, dp, w_in, got, low_first):
    width = dp.shape[1]
    count, half, sw = got.shape
    part = count // 2
    blk = (1, half, sw)
    if low_first:
        specs = [pl.BlockSpec(blk, lambda r, place: (r // 2, 0, 0))] * 2
    else:
        specs = [
            pl.BlockSpec(blk, lambda r, place: (jnp.maximum(r - part, 0), 0, 0)),
            pl.BlockSpec(blk, lambda r, place: (jnp.minimum(r, part - 1), 0, 0)),
        ]
    return pl.pallas_call(
        functools.partial(grad_keep_kernel, count, low_first),
        grid_spec=pltpu.PrefetchScalarGridSpec(
            num_scalar_prefetch=1,
            grid=(count,),
            in_specs=[KEPT, KEPT, pl.BlockSpec(blk, lambda r, place: (r, 0, 0))],
            out_specs=specs,
        ),
        out_shape=[jax.ShapeDtypeStruct((part, half, sw), BF)] * 2,
        compiler_params=params(),
        cost_estimate=LIGHT,
        name="grad_keep",
    )(place, keep(dp), keep(w_in), got)


def swapped(array, distance):
    count = lax.axis_size("tp")
    return lax.ppermute(array, "tp", [(i, i ^ distance) for i in range(count)])


def summed(a, b):
    return a.astype(F32) + b.astype(F32)


def reduce_both(a_send, a_keep, b_send, b_keep, a_own, b_own, meanwhile):
    pairs = lax.axis_size("tp") // 2
    a_step, b_step = 1, pairs // 2
    while True:
        a_got = swapped(a_send, 2 * a_step)
        b_got = swapped(b_send, 2 * b_step)
        left = a_keep.shape[0]
        a_keep, b_keep = meanwhile(a_keep, b_keep)
        if left == 1:
            return a_keep[0], a_got[0], b_keep[0], b_got[0]
        a_send = summed(a_keep[1::2], a_got[1::2]).astype(BF)
        b_send = summed(b_keep[left // 2 :], b_got[left // 2 :]).astype(BF)
        a_keep = summed(a_keep[0::2], a_got[0::2])
        b_keep = summed(b_keep[: left // 2], b_got[: left // 2])
        if left == 2:
            a_keep = a_keep + a_own
            b_keep = b_keep + b_own
        a_step, b_step = a_step * 2, b_step // 2


def finish_kernel(half, ak_ref, ag_ref, bk_ref, bg_ref, out_ref):
    out_ref[:half, :] = (ak_ref[...] + ag_ref[...].astype(F32)).astype(BF)
    out_ref[half:, :] = (bk_ref[...] + bg_ref[...].astype(F32)).astype(BF)


def finish(a_keep, a_got, b_keep, b_got):
    half, sw = a_keep.shape
    return pl.pallas_call(
        functools.partial(finish_kernel, half),
        out_shape=jax.ShapeDtypeStruct((2 * half, sw), BF),
        compiler_params=pltpu.CompilerParams(vmem_limit_bytes=VMEM),
        cost_estimate=LIGHT,
        name="finish",
    )(a_keep, a_got, b_keep, b_got)


def per_device(inputs, cotangent, w_in, conv_w, norm_gain, w_out, keep_flags):
    heads = keep_flags.shape[0]
    sel, bias = selectors(heads)
    tp = lax.axis_size("tp")
    pairs = tp // 2
    me = lax.axis_index("tp")
    pair = me // 2
    place = jnp.stack([pair, me % 2]).astype(jnp.int32)
    slice_width = inputs.shape[1] // tp
    column = me * slice_width
    gain = (norm_gain.reshape(heads, DV) * keep_flags.astype(F32)[:, None]).reshape(1, heads * DV)
    halo = shifted(inputs[-16:], 1)

    half = inputs.shape[0] // 2
    far = list(columns(place, w_out, pairs))
    near = [swapped(far.pop(0), 2 * m) for m in (1, 2)]
    halo, place, gain = lax.optimization_barrier((halo, place, gain))
    cv, v, pq, pk, loc, state = project(inputs, halo, w_in, conv_w, sel, bias, heads)
    state, near, far = lax.optimization_barrier((state, near, far))
    far = [swapped(columns, 2 * m) for m, columns in enumerate(far, 3)]
    before = from_others(state, 1)
    g, num = local_part(cotangent, w_out, gain, v, pq, pk, loc, cv, sel, heads)
    ho, dn, gloc, pre, gstate = norm_part(g, num, gain, pq, before, (cv, v, pk, loc, sel), heads)
    step = pairs // 2
    got = {r: swapped(ho, 2 * r) for r in range(1, pairs) if r != 1 + step}
    later = from_others(gstate, -1)
    bias_, far = lax.optimization_barrier((bias, far))
    dqk, dv = inner_part(cv, v, pq, pk, dn, loc, pre, sel, gloc, bias_, heads)
    dp, first, last = outer_part(cv, v, pk, dqk, dv, gloc, later, sel, bias, conv_w, heads)
    after = shifted(first, -1)
    got_top = swapped(grad_send(place, dp, w_in, pairs), 1)
    sent_low, dp_low, x_top, y_low = grad_send(
        place, dp, w_in, pairs, (last, after, conv_w, got[1], got[step])
    )
    got_low = swapped(sent_low, 1)
    tops = [(ho, 0)] + [(got.get(r), 0) for r in range(1, pairs)]
    lows = [(ho, half)] + [(got.get(r), half) for r in range(1, pairs)]
    x_top, y_low = swapped(x_top, 2 * step), swapped(y_low, 2)
    w_cols = [w_out] + near + far
    a_send, a_keep = grad_keep(place, dp, w_in, got_top, True)
    b_send, b_keep = grad_keep(place, dp_low, w_in, got_low, False)
    b_send, x_top, y_low = lax.optimization_barrier((b_send, x_top, y_low))
    tops[1 + step], lows[1 + step] = (x_top, 0), (y_low, 0)

    x_own = lax.dynamic_slice_in_dim(inputs, column, slice_width, 1).astype(F32)
    c_own = lax.dynamic_slice_in_dim(cotangent, column, slice_width, 1).astype(F32)
    stage = []

    def meanwhile(a, b):
        if not stage:
            out_send, out_keep = out_part(place, tops, lows, w_cols)
            stage.append(x_own + out_keep)
            stage.append(out_send)
            a, b, stage[1] = lax.optimization_barrier((a, b, stage[1]))
            stage.append(swapped(stage[1], 1))
        elif len(stage) == 3:
            stage.append((stage[0] + stage[2].astype(F32)).astype(BF))
            a, b, stage[3] = lax.optimization_barrier((a, b, stage[3]))
        return a, b

    halves = reduce_both(a_send, a_keep, b_send, b_keep, c_own[None, :half], c_own[None, half:], meanwhile)
    return stage[3], finish(*halves)


def solution(mesh):
    placed = (
        P("seq", None),
        P("seq", None),
        P(None, "tp"),
        P(None, "tp"),
        P("tp"),
        P("tp", None),
        P("tp"),
    )
    return jax.shard_map(
        per_device,
        mesh=mesh,
        in_specs=placed,
        out_specs=(P("seq", "tp"), P("seq", "tp")),
        check_vma=False,
    )
```

time: 230 us -> 149 us (0.65)
  waiting for transfers between devices: 102 us -> 33.8 us
  Pallas kernels: 50.1 us -> 73.1 us
  matrix products: 18.3 us -> 0 us
  between operations: 14.4 us -> 0.97 us
  local copies, waits for them, and re-layouts: 16 us -> 3.45 us
  starting transfers between devices: 20.6 us -> 30.2 us
    reduce_scatter x2 -> x0, waiting for transfers between devices: 96.7 us -> none  [the longest x1 72.4 us: per_device(): grad_sum = lax.psum_scatter(grad, 'tp', scatter_dimension=1, tiled=True)]
    ppermute x0 -> x14, waiting for transfers between devices: none -> 30.6 us  [swapped(): return lax.ppermute(array, 'tp', [(i, i ^ distance) for i in range(count)])]
    pallas_call x2 -> x9, Pallas kernels: 13.4 us -> 39.2 us  [the longest x1 8.63 us: out_part(): pl.pallas_call(functools.partial(out_kernel, count, sw), grid_spec=pltpu....]
    dot_general x2 -> x0, matrix products: 18.3 us -> none  [the longest x1 11.6 us: per_device(): lax.dot_general(dp, w_in, (((1,), (1,)), ((), ())), preferred_element_typ...]
    unnamed x42 -> x28, local copies, waits for them, and re-layouts: 15 us -> 2.53 us
    ppermute x0 -> x14, starting transfers between devices: none -> 12.2 us  [swapped(): return lax.ppermute(array, 'tp', [(i, i ^ distance) for i in range(count)])]
    ppermute x8, waiting for transfers between devices: 5.71 us -> 3.14 us  [shifted(): return lax.ppermute(array, 'seq', pairs)]
    ppermute x8, starting transfers between devices: 20.5 us -> 18 us  [shifted(): return lax.ppermute(array, 'seq', pairs)]
  transfers between devices with their start and end apart: 10 -> 22, of which waited for: 4 -> 10; matrix products, arithmetic and copies ran while one was open for 7% -> 5% of each run, Pallas kernels for 12% -> 48%
where the time goes in v1:
time: 149 us
  Pallas kernels  73.1 us (49%)
  waiting for transfers between devices  33.8 us (23%)
  starting transfers between devices  30.2 us (20%)
  other arithmetic  7.13 us (5%)
  local copies, waits for them, and re-layouts  3.45 us (2%)
    ppermute x14, waiting for transfers between devices, swapped(): return lax.ppermute(array, 'tp', [(i, i ^ distance) for i in range(count)])  30.6 us
    ppermute x8, starting transfers between devices, shifted(): return lax.ppermute(array, 'seq', pairs)  18 us
    pallas_call x1, Pallas kernels, project(): pl.pallas_call(functools.partial(project_kernel, heads), grid=(n,), in_sp...  14.8 us
    ppermute x14, starting transfers between devices, swapped(): return lax.ppermute(array, 'tp', [(i, i ^ distance) for i in range(count)])  12.2 us
    pallas_call x1, Pallas kernels, inner_part(): pl.pallas_call(functools.partial(inner_kernel, heads), grid=(n,), in_spec...  10.2 us
    pallas_call x1, Pallas kernels, local_part(): pl.pallas_call(functools.partial(local_kernel, heads), grid=(n,), in_spec...  8.89 us
    pallas_call x1, Pallas kernels, out_part(): pl.pallas_call(functools.partial(out_kernel, count, sw), grid_spec=pltpu....  8.63 us
    pallas_call x2, Pallas kernels, grad_keep(): pl.pallas_call(functools.partial(grad_keep_kernel, count, low_first), gri...  8.24 us
  transfers between devices with their start and end apart: 22, of which 10 were waited for; matrix products, arithmetic and copies ran while one was open for 5% of the time, Pallas kernels for 48%

profile of v1, /device:TPU:0, one launch (start us, length us, event | category | flops | bytes accessed | tf_op | source)
XLA Modules:
  0.0 148.6 jit_solution(6709730992383320470)
XLA Ops:
  0.6 0.9 slice.37
  1.5 4.9 %collective-permute-start = (bf16[16,4096]{1,0:T(8,128)(2,1)S(1)}, bf16[16,4096]{1,0:T(8,128)(2,1)S(1)}, u32[]{:S(2)}, u32[]{:S(2)}) collective-permute-start(bf16[16,4096]{1,0:T(8,128)(2,1)S(1)} %slice.37), channel_id=1, source_target_pairs={{0,8},{8,16},{16,24},{1,9},{9,17},{17,25},{2,10},{10,18},{18,26},{... | collective-permute-start | bytes 393224 | tf_op jit(solution)/shard_map/ppermute | solution.py:456
  6.5 0.1 pad_add_fusion.place_ref
  6.6 0.0 copy-start.6
  6.6 2.4 %columns.1 = (bf16[512,1024]{1,0:T(8,128)(2,1)S(1)}, bf16[512,1024]{1,0:T(8,128)(2,1)S(1)}, bf16[512,1024]{1,0:T(8,128)(2,1)S(1)}) custom-call(s32[2]{0:T(128)S(1)} %pad_add_fusion.place_ref, bf16[512,4096]{1,0:T(8,128)(2,1)} %refs_8_.1), custom_call_target="tpu_custom_call" | custom-call | flops 1000 | bytes 1048576 | tf_op jit(solution)/shard_map/columns/pallas_call | solution.py:437
  9.1 1.6 %collective-permute-start.1 = (bf16[512,1024]{1,0:T(8,128)(2,1)S(1)}, bf16[512,1024]{1,0:T(8,128)(2,1)S(1)}, u32[]{:S(2)}, u32[]{:S(2)}) collective-permute-start(bf16[512,1024]{1,0:T(8,128)(2,1)S(1)} %get-tuple-element.62), channel_id=1, source_target_pairs={{0,2},{1,3},{2,0},{3,1},{4,6},{5,7},{6,4},{7,5},{8,10},{9,11},{10,... | collective-permute-start | bytes 3145736 | tf_op jit(solution)/shard_map/ppermute | solution.py:624
  10.6 1.5 %collective-permute-start.2 = (bf16[512,1024]{1,0:T(8,128)(2,1)S(1)}, bf16[512,1024]{1,0:T(8,128)(2,1)S(1)}, u32[]{:S(2)}, u32[]{:S(2)}) collective-permute-start(bf16[512,1024]{1,0:T(8,128)(2,1)S(1)} %get-tuple-element.63), channel_id=1, source_target_pairs={{0,4},{1,5},{2,6},{3,7},{4,0},{5,1},{6,2},{7,3},{8,12},{9,13},{10,... | collective-permute-start | bytes 3145736 | tf_op jit(solution)/shard_map/ppermute | solution.py:624
  12.1 0.1 bitcast_multiply_fusion
  12.2 0.0 collective-permute-done.halo_ref
  12.2 0.0 copy-start
  12.2 2.5 %copy-done = bf16[4096,640]{1,0:T(8,128)(2,1)S(1)} copy-done((bf16[4096,640]{1,0:T(8,128)(2,1)S(1)}, bf16[4096,640]{1,0:T(8,128)(2,1)}, u32[]{:S(2)}) %copy-start) | copy-done | bytes 5242904
  14.7 14.8 %project.1 = (bf16[1024,640]{1,0:T(8,128)(2,1)S(1)}, bf16[1024,512]{1,0:T(8,128)(2,1)S(1)}, bf16[4,1024,256]{2,1,0:T(8,128)(2,1)S(1)}, bf16[4,1024,256]{2,1,0:T(...) custom-call(bf16[1024,4096]{1,0:T(8,128)(2,1)} %x_ref.1, ...), custom_call_target="tpu_custom_call" | custom-call | flops 107374182400 | bytes 1048576 | tf_op jit(solution)/shard_map/project/pallas_call | solution.py:166
  29.6 4.2 %collective-permute-done.1.refs_9_ = bf16[512,1024]{1,0:T(8,128)(2,1)S(1)} collective-permute-done((bf16[512,1024]{1,0:T(8,128)(2,1)S(1)}, bf16[512,1024]{1,0:T(8,128)(2,1)S(1)}, u32[]{:S(2)}, u32[]{:S(2)}) %collective-permute-start.1) | collective-permute-done | bytes 1048608 | tf_op jit(solution)/shard_map/ppermute | solution.py:624
  33.7 1.2 collective-permute-done.2.refs_10_
  35.0 1.5 %collective-permute-start.6 = (bf16[512,1024]{1,0:T(8,128)(2,1)S(1)}, bf16[512,1024]{1,0:T(8,128)(2,1)S(1)}, u32[]{:S(2)}, u32[]{:S(2)}) collective-permute-start(bf16[512,1024]{1,0:T(8,128)(2,1)S(1)} %get-tuple-element.69), channel_id=1, source_target_pairs={{0,6},{1,7},{2,4},{3,5},{4,2},{5,3},{6,0},{7,1},{8,14},{9,15},{10,... | collective-permute-start | bytes 3145736 | tf_op jit(solution)/shard_map/ppermute | solution.py:624
  36.4 3.5 %collective-permute-start.3 = (bf16[4,160,128]{2,1,0:T(8,128)(2,1)S(1)}, bf16[4,160,128]{2,1,0:T(8,128)(2,1)S(1)}, u32[]{:S(2)}, u32[]{:S(2)}) collective-permute-start(bf16[4,160,128]{2,1,0:T(8,128)(2,1)S(1)} %get-tuple-element.65), channel_id=1, source_target_pairs={{0,8},{8,16},{16,24},{1,9},{9,17},{17,25},{2,10},{10,18},{18,26},{... | collective-permute-start | bytes 491528 | tf_op jit(solution)/shard_map/ppermute | solution.py:456
  39.9 2.9 %collective-permute-start.4 = (bf16[4,160,128]{2,1,0:T(8,128)(2,1)S(1)}, bf16[4,160,128]{2,1,0:T(8,128)(2,1)S(1)}, u32[]{:S(2)}, u32[]{:S(2)}) collective-permute-start(bf16[4,160,128]{2,1,0:T(8,128)(2,1)S(1)} %get-tuple-element.65), channel_id=1, source_target_pairs={{0,16},{8,24},{1,17},{9,25},{2,18},{10,26},{3,19},{11,27},{4,20},{... | collective-permute-start | bytes 491528 | tf_op jit(solution)/shard_map/ppermute | solution.py:456
  42.9 1.3 collective-permute-start.5
  44.2 8.9 %local_part.1 = (f32[1024,512]{1,0:T(8,128)S(1)}, f32[1024,512]{1,0:T(8,128)S(1)}) custom-call(bf16[1024,4096]{1,0:T(8,128)(2,1)} %ct_ref.1, bf16[512,4096]{1,0:T(8,128)(2,1)S(1)} %copy-done.1, f32[1,512]{1,0:T(1,128)S(1)} %bitcast.23, bf16[1024,512]{1,0:T(8,128)(2,1)S(1)} %get-tuple-element.54.v_ref.refs_4_, ...), custom_call_target="tpu_custom_call" | custom-call | flops 1000 | bytes 1048576 | tf_op jit(solution)/shard_map/local_part/pallas_call | solution.py:210
  53.1 0.0 collective-permute-done.3.refs_0_
  53.1 0.0 collective-permute-done.4.refs_1_
  53.1 0.0 collective-permute-done.5.refs_2_
  53.1 7.6 %norm_part.1 = (bf16[1024,512]{1,0:T(8,128)(2,1)S(1)}, bf16[1024,512]{1,0:T(8,128)(2,1)S(1)}, bf16[4,4,128,256]{3,2,1,0:T(8,128)(2,1)S(1)}, bf16[4,160,128]{2,1,0:T(8,128)(2,1)S(1)}, bf16[4,160,128]{2,1,0:T(8,128)(2,1)S(1)}) custom-call(f32[1024,512]{1,0:T(8,128)S(1)} %get-tuple-element.59.g_ref, f32[1024,512]{1,0:T(8,128)S(1)} %get-tuple-element.60.num_ref, ...), custom_call_target="tpu_custom_call" | custom-call | flops 1000 | bytes 1048576 | tf_op jit(solution)/shard_map/norm_part/pallas_call | solution.py:259
  60.7 1.6 %collective-permute-start.12 = (bf16[1024,512]{1,0:T(8,128)(2,1)S(1)}, bf16[1024,512]{1,0:T(8,128)(2,1)S(1)}, u32[]{:S(2)}, u32[]{:S(2)}) collective-permute-start(bf16[1024,512]{1,0:T(8,128)(2,1)S(1)} %get-tuple-element.78.refs_0_.refs_4_), channel_id=1, source_target_pairs={{0,2},{1,3},{2,0},{3,1},{4,6},{5,7},{6,4},{7,5},{8,10},{9,11},{10,... | collective-permute-start | bytes 3145736 | tf_op jit(solution)/shard_map/ppermute | solution.py:624
  62.3 0.5 collective-permute-start.13
  62.8 1.3 collective-permute-start.7
  64.1 1.3 collective-permute-start.8
  65.4 0.0 collective-permute-done.6.refs_11_
  65.4 1.3 collective-permute-start.9
  66.7 10.2 %inner_part.1 = (f32[1024,128]{1,0:T(8,128)S(1)}, f32[1024,512]{1,0:T(8,128)S(1)}) custom-call(bf16[1024,640]{1,0:T(8,128)(2,1)S(1)} %get-tuple-element.53.cv_ref.refs_3_, bf16[1024,512]{1,0:T(8,128)(2,1)S(1)} %get-tuple-element.54.v_ref.refs_4_, bf16[4,1024,256]{2,1,0:T(8,128)(2,1)S(1)} %get-tuple-element.56.pq_ref, ...), custom_call_target="tpu_custom_call" | custom-call | flops 1000 | bytes 1048576 | tf_op jit(solution)/shard_map/inner_part/pallas_call | solution.py:320
  76.9 0.0 collective-permute-done.7.refs_0_
  76.9 2.1 %collective-permute-done.8.refs_1_ = bf16[4,160,128]{2,1,0:T(8,128)(2,1)S(1)} collective-permute-done((bf16[4,160,128]{2,1,0:T(8,128)(2,1)S(1)}, bf16[4,160,128]{2,1,0:T(8,128)(2,1)S(1)}, u32[]{:S(2)}, u32[]{:S(2)}) %collective-permute-start.8) | collective-permute-done | bytes 163872 | tf_op jit(solution)/shard_map/ppermute | solution.py:456
  79.0 0.0 collective-permute-done.9.refs_2_
  79.0 4.9 %outer_part.1 = (bf16[1024,640]{1,0:T(8,128)(2,1)S(1)}, f32[8,640]{1,0:T(8,128)S(1)}, f32[16,640]{1,0:T(8,128)S(1)}) custom-call(bf16[1024,640]{1,0:T(8,128)(2,1)S(1)} %get-tuple-element.53.cv_ref.refs_3_, bf16[1024,512]{1,0:T(8,128)(2,1)S(1)} %get-tuple-element.54.v_ref.refs_4_, bf16[4,1024,256]{2,1,0:T(8,128)(2,1)S(1)} %get-tuple-element.55.pk_ref.refs_5_, ...), custom_call_target="tpu_custom_call" | custom-call | flops 1000 | bytes 1048576 | tf_op jit(solution)/shard_map/outer_part/pallas_call | solution.py:400
  83.9 1.5 collective-permute-start.11
  85.4 3.0 %grad_top.1 = bf16[4,512,512]{2,1,0:T(8,128)(2,1)S(1)} custom-call(s32[2]{0:T(128)S(1)} %pad_add_fusion.place_ref, bf16[1024,640]{1,0:T(8,128)(2,1)S(1)} %get-tuple-element.74.dp_ref, bf16[4096,640]{1,0:T(8,128)(2,1)S(1)} %bitcast.18), custom_call_target="tpu_custom_call" | custom-call | flops 1000 | bytes 1048576 | tf_op jit(solution)/shard_map/grad_top/pallas_call | solution.py:566
  88.4 0.1 collective-permute-start.10
  88.5 1.1 collective-permute-done.11.after_ref
  89.6 0.0 collective-permute-done.12.x_ref.refs_1_.refs_5_
  89.6 0.0 collective-permute-done.13.y_ref.refs_2_.refs_6_
  89.6 3.2 %grad_low.1 = (bf16[4,512,512]{2,1,0:T(8,128)(2,1)S(1)}, bf16[512,640]{1,0:T(8,128)(2,1)S(1)}, bf16[512,512]{1,0:T(8,128)(2,1)S(1)}, bf16[512,512]{1,0:T(8,128)(2,1)S(1)}) custom-call(s32[2]{0:T(128)S(1)} %pad_add_fusion.place_ref, bf16[1024,640]{1,0:T(8,128)(2,1)S(1)} %get-tuple-element.74.dp_ref, bf16[4096,640]{1,0:T(8,128)(2,1)S(1)} %bitcast.18, ...), custom_call_target="tpu_custom_call" | custom-call | flops 1000 | bytes 1048576 | tf_op jit(solution)/shard_map/grad_low/pallas_call | solution.py:566
  92.8 0.1 collective-permute-start.14
  92.8 1.6 %collective-permute-start.15 = (bf16[512,512]{1,0:T(8,128)(2,1)S(1)}, bf16[512,512]{1,0:T(8,128)(2,1)S(1)}, u32[]{:S(2)}, u32[]{:S(2)}) collective-permute-start(bf16[512,512]{1,0:T(8,128)(2,1)S(1)} %get-tuple-element.83), channel_id=1, source_target_pairs={{0,4},{1,5},{2,6},{3,7},{4,0},{5,1},{6,2},{7,3},{8,12},{9,13},{10,... | collective-permute-start | bytes 1572872 | tf_op jit(solution)/shard_map/ppermute | solution.py:624
  94.4 0.6 collective-permute-start.16
  95.1 0.0 collective-permute-done.10.got_ref
  95.1 4.2 %grad_keep.2 = (bf16[2,512,512]{2,1,0:T(8,128)(2,1)}, bf16[2,512,512]{2,1,0:T(8,128)(2,1)S(1)}) custom-call(s32[2]{0:T(128)S(1)} %pad_add_fusion.place_ref, bf16[1024,640]{1,0:T(8,128)(2,1)S(1)} %get-tuple-element.74.dp_ref, bf16[4096,640]{1,0:T(8,128)(2,1)S(1)} %bitcast.18, bf16[4,512,512]{2,1,0:T(8,128)(2,1)S(1)} %collective-permute-done.10.got_ref), custom_call_target="tpu_custom_call" | custom-call | flops 1000 | bytes 1048576 | tf_op jit(solution)/shard_map/grad_keep/pallas_call | solution.py:607
  99.3 1.4 collective-permute-start.17
  100.7 0.0 collective-permute-done.14.got_ref
  100.7 4.1 %grad_keep.3 = (bf16[2,512,512]{2,1,0:T(8,128)(2,1)}, bf16[2,512,512]{2,1,0:T(8,128)(2,1)S(1)}) custom-call(s32[2]{0:T(128)S(1)} %pad_add_fusion.place_ref, bf16[512,640]{1,0:T(8,128)(2,1)S(1)} %get-tuple-element.79.dp_ref, bf16[4096,640]{1,0:T(8,128)(2,1)S(1)} %bitcast.18, bf16[4,512,512]{2,1,0:T(8,128)(2,1)S(1)} %collective-permute-done.14.got_ref), custom_call_target="tpu_custom_call" | custom-call | flops 1000 | bytes 1048576 | tf_op jit(solution)/shard_map/grad_keep/pallas_call | solution.py:607
  104.7 2.5 %collective-permute-done.15.refs_3_ = bf16[512,512]{1,0:T(8,128)(2,1)S(1)} collective-permute-done((bf16[512,512]{1,0:T(8,128)(2,1)S(1)}, bf16[512,512]{1,0:T(8,128)(2,1)S(1)}, u32[]{:S(2)}, u32[]{:S(2)}) %collective-permute-start.15) | collective-permute-done | bytes 524320 | tf_op jit(solution)/shard_map/ppermute | solution.py:624
  107.2 2.0 %collective-permute-done.16.refs_7_ = bf16[512,512]{1,0:T(8,128)(2,1)S(1)} collective-permute-done((bf16[512,512]{1,0:T(8,128)(2,1)S(1)}, bf16[512,512]{1,0:T(8,128)(2,1)S(1)}, u32[]{:S(2)}, u32[]{:S(2)}) %collective-permute-start.16) | collective-permute-done | bytes 524320 | tf_op jit(solution)/shard_map/ppermute | solution.py:624
  109.2 0.5 collective-permute-start.18
  109.7 8.6 %out_part.1 = (bf16[1024,512]{1,0:T(8,128)(2,1)}, f32[1024,512]{1,0:T(8,128)S(1)}) custom-call(s32[2]{0:T(128)S(1)} %pad_add_fusion.place_ref, bf16[1024,512]{1,0:T(8,128)(2,1)S(1)} %get-tuple-element.78.refs_0_.refs_4_, bf16[1024,512]{1,0:T(8,128)(2,1)S(1)} %collective-permute-done.12.x_ref.refs_1_.refs_5_, ...), custom_call_target="tpu_custom_call" | custom-call | flops 1000 | bytes 1048576 | tf_op jit(solution)/shard_map/out_part/pallas_call | solution.py:506
  118.3 1.6 %dynamic-slice_convert_fusion = f32[1024,512]{1,0:T(8,128)S(1)} fusion(bf16[1024,4096]{1,0:T(8,128)(2,1)} %ct_ref.1, s32[]{:T(128)S(6)} %select_n.17), kind=kLoop, calls=%fused_computation.7 | loop fusion | flops 524288 | bytes 3145732 | tf_op jit(solution)/shard_map/convert_element_type | solution.py:712
  119.9 11.1 %collective-permute-done.17 = bf16[2,512,512]{2,1,0:T(8,128)(2,1)} collective-permute-done((bf16[2,512,512]{2,1,0:T(8,128)(2,1)}, bf16[2,512,512]{2,1,0:T(8,128)(2,1)}, u32[]{:S(2)}, u32[]{:S(2)}) %collective-permute-start.17) | collective-permute-done | bytes 1048608 | tf_op jit(solution)/shard_map/ppermute | solution.py:624
  131.0 2.1 %collective-permute-done.18 = bf16[2,512,512]{2,1,0:T(8,128)(2,1)} collective-permute-done((bf16[2,512,512]{2,1,0:T(8,128)(2,1)}, bf16[2,512,512]{2,1,0:T(8,128)(2,1)}, u32[]{:S(2)}, u32[]{:S(2)}) %collective-permute-start.18) | collective-permute-done | bytes 1048608 | tf_op jit(solution)/shard_map/ppermute | solution.py:624
  133.1 2.3 %add_convert_fusion.1 = (bf16[1,512,512]{2,1,0:T(8,128)(2,1)S(1)}, f32[1,512,512]{2,1,0:T(8,128)S(1)}, f32[1,512,512]{2,1,0:T(8,128)S(1)}, bf16[1,512,512]{2,1,0:T(8,128)(2,1)S(1)}) fusion(bf16[2,512,512]{2,1,0:T(8,128)(2,1)} %collective-permute-done.18, bf16[2,512,512]{2,1,0:T(8,128)(2,1)S(1)} %copy-done.4, f32[1024,512]{1,0:T(8,128)S(1)} %dynamic-slice_convert_fusion, ...), kind=kLoop, calls=%fused_computation.5 | loop fusion | flops 4194304 | bytes 9437184 | tf_op jit(solution)/shard_map/convert_element_type | solution.py:642
  135.4 0.7 collective-permute-start.20
  136.1 0.6 collective-permute-start.21
  136.8 0.0 collective-permute-done.19
  136.8 3.1 %add_convert_fusion = bf16[1024,512]{1,0:T(8,128)(2,1)} fusion(bf16[1024,512]{1,0:T(8,128)(2,1)} %collective-permute-done.19, f32[1024,512]{1,0:T(8,128)S(1)} %get-tuple-element.95, bf16[1024,4096]{1,0:T(8,128)(2,1)} %x_ref.1, s32[]{:T(128)S(6)} %select_n.17), kind=kLoop, calls=%fused_computation | loop fusion | flops 2621440 | bytes 5242884 | tf_op jit(solution)/shard_map/convert_element_type | solution.py:723
  139.9 7.1 %collective-permute-done.20 = bf16[1,512,512]{2,1,0:T(8,128)(2,1)S(1)} collective-permute-done((bf16[1,512,512]{2,1,0:T(8,128)(2,1)S(1)}, bf16[1,512,512]{2,1,0:T(8,128)(2,1)S(1)}, u32[]{:S(2)}, u32[]{:S(2)}) %collective-permute-start.20) | collective-permute-done | bytes 524320 | tf_op jit(solution)/shard_map/ppermute | solution.py:624
  147.0 0.4 collective-permute-done.21
  147.4 1.2 finish.1
  (28 shorter events, 0.1 us)
Async XLA Ops:
  1.5 10.7 %collective-permute-start = (bf16[16,4096]{1,0:T(8,128)(2,1)S(1)}, bf16[16,4096]{1,0:T(8,128)(2,1)S(1)}, u32[]{:S(2)}, u32[]{:S(2)}) collective-permute-start(bf16[16,4096]{1,0:T(8,128)(2,1)S(1)} %slice.37), channel_id=1, source_target_pairs={{0,8},{8,16},{16,24},{1,9},{9,17},{17,25},{2,10},{10,18},{18,26},{... | collective-permute-start | bytes 393224 | tf_op jit(solution)/shard_map/ppermute | solution.py:456
  6.6 5.5 %copy-start.11 = (s32[4]{0:T(128)S(1)}, s32[4]{0:T(128)}, u32[]{:S(2)}) copy-start(s32[4]{0:T(128)} %param.15) | copy-start | bytes 52
  6.6 5.6 %copy-start.10 = (f32[512]{0:T(512)S(1)}, f32[512]{0:T(512)}, u32[]{:S(2)}) copy-start(f32[512]{0:T(512)} %param.13) | copy-start | bytes 6148
  6.6 5.6 %copy-start.2 = (bf16[4,128,1280]{2,1,0:T(8,128)(2,1)S(1)}, bf16[4,128,1280]{2,1,0:T(8,128)(2,1)}, u32[]{:S(2)}) copy-start(bf16[4,128,1280]{2,1,0:T(8,128)(2,1)} %constant.37.clone.sel_ref.refs_7_) | copy-start | bytes 3932164
  6.6 5.6 %copy-start.5 = (f32[3,640]{1,0:T(4,128)S(1)}, f32[3,640]{1,0:T(4,128)}, u32[]{:S(2)}) copy-start(f32[3,640]{1,0:T(4,128)} %cw_ref.5) | copy-start | bytes 23044
  6.6 5.6 %copy-start.6 = (f32[8,256]{1,0:T(8,128)S(1)}, f32[8,256]{1,0:T(8,128)}, u32[]{:S(2)}) copy-start(f32[8,256]{1,0:T(8,128)} %constant.38.clone.bias_ref) | copy-start | bytes 24580
  9.1 24.7 %collective-permute-start.1 = (bf16[512,1024]{1,0:T(8,128)(2,1)S(1)}, bf16[512,1024]{1,0:T(8,128)(2,1)S(1)}, u32[]{:S(2)}, u32[]{:S(2)}) collective-permute-start(bf16[512,1024]{1,0:T(8,128)(2,1)S(1)} %get-tuple-element.62), channel_id=1, source_target_pairs={{0,2},{1,3},{2,0},{3,1},{4,6},{5,7},{6,4},{7,5},{8,10},{9,11},{10,... | collective-permute-start | bytes 3145736 | tf_op jit(solution)/shard_map/ppermute | solution.py:624
  10.6 24.3 %collective-permute-start.2 = (bf16[512,1024]{1,0:T(8,128)(2,1)S(1)}, bf16[512,1024]{1,0:T(8,128)(2,1)S(1)}, u32[]{:S(2)}, u32[]{:S(2)}) collective-permute-start(bf16[512,1024]{1,0:T(8,128)(2,1)S(1)} %get-tuple-element.63), channel_id=1, source_target_pairs={{0,4},{1,5},{2,6},{3,7},{4,0},{5,1},{6,2},{7,3},{8,12},{9,13},{10,... | collective-permute-start | bytes 3145736 | tf_op jit(solution)/shard_map/ppermute | solution.py:624
  12.2 2.5 %copy-start = (bf16[4096,640]{1,0:T(8,128)(2,1)S(1)}, bf16[4096,640]{1,0:T(8,128)(2,1)}, u32[]{:S(2)}) copy-start(bf16[4096,640]{1,0:T(8,128)(2,1)} %w_ref.11) | copy-start | bytes 15728644
  14.7 29.5 %copy-start.1 = (bf16[512,4096]{1,0:T(8,128)(2,1)S(1)}, bf16[512,4096]{1,0:T(8,128)(2,1)}, u32[]{:S(2)}) copy-start(bf16[512,4096]{1,0:T(8,128)(2,1)} %refs_8_.1) | copy-start | bytes 12582916
  33.7 19.3 %copy-start.7 = (bf16[512,1024]{1,0:T(8,128)(2,1)}, bf16[512,1024]{1,0:T(8,128)(2,1)S(1)}, u32[]{:S(2)}) copy-start(bf16[512,1024]{1,0:T(8,128)(2,1)S(1)} %collective-permute-done.1.refs_9_) | copy-start | bytes 3145732
  35.0 18.1 %copy-start.8 = (bf16[512,1024]{1,0:T(8,128)(2,1)}, bf16[512,1024]{1,0:T(8,128)(2,1)S(1)}, u32[]{:S(2)}) copy-start(bf16[512,1024]{1,0:T(8,128)(2,1)S(1)} %collective-permute-done.2.refs_10_) | copy-start | bytes 3145732
  35.0 30.4 %collective-permute-start.6 = (bf16[512,1024]{1,0:T(8,128)(2,1)S(1)}, bf16[512,1024]{1,0:T(8,128)(2,1)S(1)}, u32[]{:S(2)}, u32[]{:S(2)}) collective-permute-start(bf16[512,1024]{1,0:T(8,128)(2,1)S(1)} %get-tuple-element.69), channel_id=1, source_target_pairs={{0,6},{1,7},{2,4},{3,5},{4,2},{5,3},{6,0},{7,1},{8,14},{9,15},{10,... | collective-permute-start | bytes 3145736 | tf_op jit(solution)/shard_map/ppermute | solution.py:624
  36.4 16.7 %collective-permute-start.3 = (bf16[4,160,128]{2,1,0:T(8,128)(2,1)S(1)}, bf16[4,160,128]{2,1,0:T(8,128)(2,1)S(1)}, u32[]{:S(2)}, u32[]{:S(2)}) collective-permute-start(bf16[4,160,128]{2,1,0:T(8,128)(2,1)S(1)} %get-tuple-element.65), channel_id=1, source_target_pairs={{0,8},{8,16},{16,24},{1,9},{9,17},{17,25},{2,10},{10,18},{18,26},{... | collective-permute-start | bytes 491528 | tf_op jit(solution)/shard_map/ppermute | solution.py:456
  39.9 13.2 %collective-permute-start.4 = (bf16[4,160,128]{2,1,0:T(8,128)(2,1)S(1)}, bf16[4,160,128]{2,1,0:T(8,128)(2,1)S(1)}, u32[]{:S(2)}, u32[]{:S(2)}) collective-permute-start(bf16[4,160,128]{2,1,0:T(8,128)(2,1)S(1)} %get-tuple-element.65), channel_id=1, source_target_pairs={{0,16},{8,24},{1,17},{9,25},{2,18},{10,26},{3,19},{11,27},{4,20},{... | collective-permute-start | bytes 491528 | tf_op jit(solution)/shard_map/ppermute | solution.py:456
  42.9 10.3 %collective-permute-start.5 = (bf16[4,160,128]{2,1,0:T(8,128)(2,1)S(1)}, bf16[4,160,128]{2,1,0:T(8,128)(2,1)S(1)}, u32[]{:S(2)}, u32[]{:S(2)}) collective-permute-start(bf16[4,160,128]{2,1,0:T(8,128)(2,1)S(1)} %get-tuple-element.65), channel_id=1, source_target_pairs={{0,24},{1,25},{2,26},{3,27},{4,28},{5,29},{6,30},{7,31}} | collective-permute-start | bytes 491528 | tf_op jit(solution)/shard_map/ppermute | solution.py:456
  60.7 28.9 %collective-permute-start.12 = (bf16[1024,512]{1,0:T(8,128)(2,1)S(1)}, bf16[1024,512]{1,0:T(8,128)(2,1)S(1)}, u32[]{:S(2)}, u32[]{:S(2)}) collective-permute-start(bf16[1024,512]{1,0:T(8,128)(2,1)S(1)} %get-tuple-element.78.refs_0_.refs_4_), channel_id=1, source_target_pairs={{0,2},{1,3},{2,0},{3,1},{4,6},{5,7},{6,4},{7,5},{8,10},{9,11},{10,... | collective-permute-start | bytes 3145736 | tf_op jit(solution)/shard_map/ppermute | solution.py:624
  62.3 27.3 %collective-permute-start.13 = (bf16[1024,512]{1,0:T(8,128)(2,1)S(1)}, bf16[1024,512]{1,0:T(8,128)(2,1)S(1)}, u32[]{:S(2)}, u32[]{:S(2)}) collective-permute-start(bf16[1024,512]{1,0:T(8,128)(2,1)S(1)} %get-tuple-element.78.refs_0_.refs_4_), channel_id=1, source_target_pairs={{0,4},{1,5},{2,6},{3,7},{4,0},{5,1},{6,2},{7,3},{8,12},{9,13},{10,... | collective-permute-start | bytes 3145736 | tf_op jit(solution)/shard_map/ppermute | solution.py:624
  62.8 14.1 %collective-permute-start.7 = (bf16[4,160,128]{2,1,0:T(8,128)(2,1)S(1)}, bf16[4,160,128]{2,1,0:T(8,128)(2,1)S(1)}, u32[]{:S(2)}, u32[]{:S(2)}) collective-permute-start(bf16[4,160,128]{2,1,0:T(8,128)(2,1)S(1)} %get-tuple-element.73), channel_id=1, source_target_pairs={{8,0},{16,8},{24,16},{9,1},{17,9},{25,17},{10,2},{18,10},{26,18},{... | collective-permute-start | bytes 491528 | tf_op jit(solution)/shard_map/ppermute | solution.py:456
  64.1 14.9 %collective-permute-start.8 = (bf16[4,160,128]{2,1,0:T(8,128)(2,1)S(1)}, bf16[4,160,128]{2,1,0:T(8,128)(2,1)S(1)}, u32[]{:S(2)}, u32[]{:S(2)}) collective-permute-start(bf16[4,160,128]{2,1,0:T(8,128)(2,1)S(1)} %get-tuple-element.73), channel_id=1, source_target_pairs={{16,0},{24,8},{17,1},{25,9},{18,2},{26,10},{19,3},{27,11},{20,4},{... | collective-permute-start | bytes 491528 | tf_op jit(solution)/shard_map/ppermute | solution.py:456
  65.4 11.5 %copy-start.9 = (bf16[512,1024]{1,0:T(8,128)(2,1)}, bf16[512,1024]{1,0:T(8,128)(2,1)S(1)}, u32[]{:S(2)}) copy-start(bf16[512,1024]{1,0:T(8,128)(2,1)S(1)} %collective-permute-done.6.refs_11_) | copy-start | bytes 3145732
  65.4 13.6 %collective-permute-start.9 = (bf16[4,160,128]{2,1,0:T(8,128)(2,1)S(1)}, bf16[4,160,128]{2,1,0:T(8,128)(2,1)S(1)}, u32[]{:S(2)}, u32[]{:S(2)}) collective-permute-start(bf16[4,160,128]{2,1,0:T(8,128)(2,1)S(1)} %get-tuple-element.73), channel_id=1, source_target_pairs={{24,0},{25,1},{26,2},{27,3},{28,4},{29,5},{30,6},{31,7}} | collective-permute-start | bytes 491528 | tf_op jit(solution)/shard_map/ppermute | solution.py:456
  79.0 6.4 %slice-start = ((s8[5242880]{0:T(1024)(128)(4,1)}), s8[4194304]{0:T(1024)(128)(4,1)S(1)}, s32[]{:S(2)}) async-start(s8[5242880]{0:T(1024)(128)(4,1)} %bitcast.17), calls=%async_computation | async-start | bytes 8388608
  79.0 6.4 %slice-start.1 = ((s8[5242880]{0:T(1024)(128)(4,1)}), s8[1048576]{0:T(1024)(128)(4,1)S(1)}, s32[]{:S(2)}) async-start(s8[5242880]{0:T(1024)(128)(4,1)} %bitcast.17), calls=%async_computation.1 | async-start | bytes 2097152
  83.9 5.7 %collective-permute-start.11 = (f32[8,640]{1,0:T(8,128)S(1)}, f32[8,640]{1,0:T(8,128)S(1)}, u32[]{:S(2)}, u32[]{:S(2)}) collective-permute-start(f32[8,640]{1,0:T(8,128)S(1)} %get-tuple-element.77), channel_id=1, source_target_pairs={{8,0},{16,8},{24,16},{9,1},{17,9},{25,17},{10,2},{18,10},{26,18},{... | collective-permute-start | bytes 61448 | tf_op jit(solution)/shard_map/ppermute | solution.py:456
  88.4 6.6 %collective-permute-start.10 = (bf16[4,512,512]{2,1,0:T(8,128)(2,1)S(1)}, bf16[4,512,512]{2,1,0:T(8,128)(2,1)S(1)}, u32[]{:S(2)}, u32[]{:S(2)}) collective-permute-start(bf16[4,512,512]{2,1,0:T(8,128)(2,1)S(1)} %grad_top.1), channel_id=1, source_target_pairs={{0,1},{1,0},{2,3},{3,2},{4,5},{5,4},{6,7},{7,6},{8,9},{9,8},{10,11... | collective-permute-start | bytes 6291464 | tf_op jit(solution)/shard_map/ppermute | solution.py:624
  92.8 7.9 %collective-permute-start.14 = (bf16[4,512,512]{2,1,0:T(8,128)(2,1)S(1)}, bf16[4,512,512]{2,1,0:T(8,128)(2,1)S(1)}, u32[]{:S(2)}, u32[]{:S(2)}) collective-permute-start(bf16[4,512,512]{2,1,0:T(8,128)(2,1)S(1)} %get-tuple-element.80), channel_id=1, source_target_pairs={{0,1},{1,0},{2,3},{3,2},{4,5},{5,4},{6,7},{7,6},{8,9},{9,8},{10,11... | collective-permute-start | bytes 6291464 | tf_op jit(solution)/shard_map/ppermute | solution.py:624
  92.8 14.3 %collective-permute-start.15 = (bf16[512,512]{1,0:T(8,128)(2,1)S(1)}, bf16[512,512]{1,0:T(8,128)(2,1)S(1)}, u32[]{:S(2)}, u32[]{:S(2)}) collective-permute-start(bf16[512,512]{1,0:T(8,128)(2,1)S(1)} %get-tuple-element.83), channel_id=1, source_target_pairs={{0,4},{1,5},{2,6},{3,7},{4,0},{5,1},{6,2},{7,3},{8,12},{9,13},{10,... | collective-permute-start | bytes 1572872 | tf_op jit(solution)/shard_map/ppermute | solution.py:624
  94.4 14.8 %collective-permute-start.16 = (bf16[512,512]{1,0:T(8,128)(2,1)S(1)}, bf16[512,512]{1,0:T(8,128)(2,1)S(1)}, u32[]{:S(2)}, u32[]{:S(2)}) collective-permute-start(bf16[512,512]{1,0:T(8,128)(2,1)S(1)} %get-tuple-element.84), channel_id=1, source_target_pairs={{0,2},{1,3},{2,0},{3,1},{4,6},{5,7},{6,4},{7,5},{8,10},{9,11},{10,... | collective-permute-start | bytes 1572872 | tf_op jit(solution)/shard_map/ppermute | solution.py:624
  99.3 31.7 %collective-permute-start.17 = (bf16[2,512,512]{2,1,0:T(8,128)(2,1)}, bf16[2,512,512]{2,1,0:T(8,128)(2,1)}, u32[]{:S(2)}, u32[]{:S(2)}) collective-permute-start(bf16[2,512,512]{2,1,0:T(8,128)(2,1)} %get-tuple-element.92), channel_id=1, source_target_pairs={{0,2},{1,3},{2,0},{3,1},{4,6},{5,7},{6,4},{7,5},{8,10},{9,11},{10,... | collective-permute-start | bytes 3145736 | tf_op jit(solution)/shard_map/ppermute | solution.py:624
  104.7 13.6 %copy-start.3 = (bf16[2,512,512]{2,1,0:T(8,128)(2,1)}, bf16[2,512,512]{2,1,0:T(8,128)(2,1)S(1)}, u32[]{:S(2)}) copy-start(bf16[2,512,512]{2,1,0:T(8,128)(2,1)S(1)} %get-tuple-element.93) | copy-start | bytes 3145732
  109.2 23.9 %collective-permute-start.18 = (bf16[2,512,512]{2,1,0:T(8,128)(2,1)}, bf16[2,512,512]{2,1,0:T(8,128)(2,1)}, u32[]{:S(2)}, u32[]{:S(2)}) collective-permute-start(bf16[2,512,512]{2,1,0:T(8,128)(2,1)} %get-tuple-element.94), channel_id=1, source_target_pairs={{0,4},{1,5},{2,6},{3,7},{4,0},{5,1},{6,2},{7,3},{8,12},{9,13},{10,... | collective-permute-start | bytes 3145736 | tf_op jit(solution)/shard_map/ppermute | solution.py:624
  118.3 18.4 %collective-permute-start.19 = (bf16[1024,512]{1,0:T(8,128)(2,1)}, bf16[1024,512]{1,0:T(8,128)(2,1)}, u32[]{:S(2)}, u32[]{:S(2)}) collective-permute-start(bf16[1024,512]{1,0:T(8,128)(2,1)} %get-tuple-element.96), channel_id=1, source_target_pairs={{0,1},{1,0},{2,3},{3,2},{4,5},{5,4},{6,7},{7,6},{8,9},{9,8},{10,11... | collective-permute-start | bytes 3145736 | tf_op jit(solution)/shard_map/ppermute | solution.py:624
  118.3 14.8 %copy-start.4 = (bf16[2,512,512]{2,1,0:T(8,128)(2,1)S(1)}, bf16[2,512,512]{2,1,0:T(8,128)(2,1)}, u32[]{:S(2)}) copy-start(bf16[2,512,512]{2,1,0:T(8,128)(2,1)} %copy-done.3) | copy-start | bytes 3145732
  135.4 11.5 %collective-permute-start.20 = (bf16[1,512,512]{2,1,0:T(8,128)(2,1)S(1)}, bf16[1,512,512]{2,1,0:T(8,128)(2,1)S(1)}, u32[]{:S(2)}, u32[]{:S(2)}) collective-permute-start(bf16[1,512,512]{2,1,0:T(8,128)(2,1)S(1)} %get-tuple-element.103), channel_id=1, source_target_pairs={{0,4},{1,5},{2,6},{3,7},{4,0},{5,1},{6,2},{7,3},{8,12},{9,13},{10,... | collective-permute-start | bytes 1572872 | tf_op jit(solution)/shard_map/ppermute | solution.py:624
  136.1 11.3 %collective-permute-start.21 = (bf16[1,512,512]{2,1,0:T(8,128)(2,1)S(1)}, bf16[1,512,512]{2,1,0:T(8,128)(2,1)S(1)}, u32[]{:S(2)}, u32[]{:S(2)}) collective-permute-start(bf16[1,512,512]{2,1,0:T(8,128)(2,1)S(1)} %get-tuple-element.100), channel_id=1, source_target_pairs={{0,2},{1,3},{2,0},{3,1},{4,6},{5,7},{6,4},{7,5},{8,10},{9,11},{10,... | collective-permute-start | bytes 1572872 | tf_op jit(solution)/shard_map/ppermute | solution.py:624

commit v2 on v1

v2 whole, which is shorter than its diff:
```python
import functools

import jax
import jax.numpy as jnp
import numpy as np
from jax import lax
from jax.experimental import pallas as pl
from jax.experimental.pallas import tpu as pltpu
from jax.sharding import PartitionSpec as P

FEAT = 16
DV = 128
HW = 2 * FEAT + DV
EP = 256
ES = 160
CH = 256
EPS = 1e-06
BF = jnp.bfloat16
F32 = jnp.float32
VMEM = 16 * 1024 * 1024


def mm(a, b):
    return lax.dot_general(a, b, (((1,), (0,)), ((), ())), preferred_element_type=F32)


def mm_nt(a, b):
    return lax.dot_general(a, b, (((1,), (1,)), ((), ())), preferred_element_type=F32)


def mm_tn(a, b):
    return lax.dot_general(a, b, (((0,), (0,)), ((), ())), preferred_element_type=F32)


def selectors(heads):
    sel = np.zeros((heads, 128, 4 * EP), np.float32)
    bias = np.zeros((8, EP), np.float32)
    bias[1, :FEAT] = 1.0
    bias[0, FEAT] = bias[1, FEAT] = 1.0
    for h in range(heads):
        q0 = (HW * h) % 128
        k0 = q0 + FEAT
        for i in range(FEAT):
            sel[h, q0 + i, i] = 0.5
            sel[h, k0 + i, 2 * EP + i] = 0.5
        col = FEAT + 1
        for i in range(FEAT):
            for j in range(i, FEAT):
                sel[h, q0 + i, col] = 0.25 if i == j else 0.5
                sel[h, q0 + j, EP + col] = 0.5
                sel[h, k0 + i, 2 * EP + col] = 0.5
                sel[h, k0 + j, 3 * EP + col] = 0.5
                col += 1
    return jnp.asarray(sel, BF), jnp.asarray(bias, F32)


def window(h):
    t = (HW * h) // 128
    return slice(128 * t, 128 * t + 128)


def value_place(h):
    start = HW * h + 2 * FEAT
    return start // 128, start % 128


def lane_iota():
    return lax.broadcasted_iota(jnp.int32, (CH, 128), 1)


def take_values(conv, h):
    tile, off = value_place(h)
    first = conv[:, 128 * tile : 128 * tile + 128]
    if off == 0:
        return first
    second = conv[:, 128 * tile + 128 : min(128 * tile + 256, conv.shape[1])]
    if second.shape[1] < 128:
        second = jnp.concatenate([second, jnp.zeros((CH, 128 - second.shape[1]), second.dtype)], 1)
    a = pltpu.roll(first, 128 - off, 1)
    b = pltpu.roll(second, 128 - off, 1)
    return jnp.where(lane_iota() < 128 - off, a, b)


def causal():
    r = lax.broadcasted_iota(jnp.int32, (CH, CH), 0)
    c = lax.broadcasted_iota(jnp.int32, (CH, CH), 1)
    return r >= c


def params():
    return pltpu.CompilerParams(dimension_semantics=("arbitrary",), vmem_limit_bytes=VMEM)


def whole(shape):
    return pl.BlockSpec(shape, lambda c, *_: (0,) * len(shape))


KEPT = pl.BlockSpec(memory_space=pltpu.VMEM)


def kept(shape, dtype):
    return pltpu.VMEM(shape, dtype)


def keep(array):
    return pltpu.with_memory_space_constraint(array, pltpu.VMEM)


def stay(array):
    return pltpu.with_memory_space_constraint(array, pltpu.HBM)


def cost(flops):
    return pl.CostEstimate(flops=int(flops), bytes_accessed=1 << 20, transcendentals=0)


LIGHT = cost(1000)


def rows_at(c):
    return pl.ds(pl.multiple_of(c * CH, CH), CH)


def biased(u, bias):
    return jnp.concatenate([u[:, :128] + bias[:, :128], u[:, 128:]], 1)


def project_kernel(heads, x_ref, halo_ref, w_ref, cw_ref, sel_ref, bias_ref,
                   v_ref, pq_ref, pk_ref, fq_ref, fk_ref, loc_ref, state_ref, ext, run):
    c = pl.program_id(0)
    at = rows_at(c)

    @pl.when(c == 0)
    def _():
        before = mm(halo_ref[...], w_ref[...]).astype(BF).astype(F32)
        ext[0:8, :] = before[8:16]
        run[...] = jnp.zeros_like(run)

    ext[8:, :] = mm(x_ref[...], w_ref[...]).astype(BF).astype(F32)
    conv = (cw_ref[0:1] * ext[8 : 8 + CH, :] + cw_ref[1:2] * ext[7 : 7 + CH, :]
            + cw_ref[2:3] * ext[6 : 6 + CH, :])
    ext[0:8, :] = ext[CH : CH + 8, :]
    conv_b = conv.astype(BF)
    conv = conv_b.astype(F32)
    b0 = bias_ref[0:1]
    b1 = bias_ref[1:2]
    for h in range(heads):
        u = mm(conv_b[:, window(h)], sel_ref[h])
        first, second = biased(u[:, :EP], b0), biased(u[:, EP : 2 * EP], b1)
        pq_ref[h, at, :] = (first * second).astype(BF)
        fq_ref[h, at, :EP] = first.astype(BF)
        fq_ref[h, at, EP:] = second.astype(BF)
        first, second = biased(u[:, 2 * EP : 3 * EP], b0), biased(u[:, 3 * EP :], b1)
        pk = (first * second).astype(BF)
        pk_ref[h, at, :] = pk
        fk_ref[h, at, :EP] = first.astype(BF)
        fk_ref[h, at, EP:] = second.astype(BF)
        v = take_values(conv, h).astype(BF)
        v_ref[at, DV * h : DV * h + DV] = v
        loc_ref[c, h] = run[h].astype(BF)
        run[h] = run[h] + mm_tn(v, pk)

    @pl.when(c == pl.num_programs(0) - 1)
    def _():
        for h in range(heads):
            state_ref[h] = run[h].T[:ES].astype(BF)


def project(x, halo, w_in, conv_w, sel, bias, heads):
    rows, d = x.shape
    width = w_in.shape[1]
    n = rows // CH
    return pl.pallas_call(
        functools.partial(project_kernel, heads),
        grid=(n,),
        in_specs=[
            pl.BlockSpec((CH, d), lambda c: (c, 0)),
            whole((16, d)),
            KEPT,
            whole((3, width)),
            KEPT,
            whole(bias.shape),
        ],
        out_specs=[KEPT] * 6 + [whole((heads, ES, DV))],
        out_shape=[
            kept((rows, heads * DV), BF),
            kept((heads, rows, EP), BF),
            kept((heads, rows, EP), BF),
            kept((heads, rows, 2 * EP), BF),
            kept((heads, rows, 2 * EP), BF),
            kept((n, heads, DV, EP), BF),
            jax.ShapeDtypeStruct((heads, ES, DV), BF),
        ],
        scratch_shapes=[pltpu.VMEM((CH + 8, width), F32), pltpu.VMEM((heads, DV, EP), F32)],
        compiler_params=params(),
        cost_estimate=cost(100 << 30),
        name="project",
    )(stay(x), halo, keep(w_in), conv_w, keep(sel), bias)


def local_kernel(heads, ct_ref, wo_ref, gain_ref, v_ref, pq_ref, pk_ref, loc_ref, fq_ref, fk_ref, sel_ref,
                 g_ref, num_ref, wt_ref, slope_ref):
    c = pl.program_id(0)
    at = rows_at(c)
    g_ref[at, :] = mm_nt(ct_ref[...], wo_ref[...]) * gain_ref[...]
    mask = causal()
    for h in range(heads):
        pq = pq_ref[h, at, :]
        logits = mm_nt(pq[:, :FEAT], pk_ref[h, at, :FEAT])
        slope = 1.0 + logits
        weights = jnp.where(mask, 0.5 + 0.5 * slope * slope, 0.0).astype(BF)
        wt_ref[h, at, :] = weights
        slope_ref[h, at, :] = jnp.where(mask, slope, 0.0).astype(BF)
        lanes = slice(DV * h, DV * h + DV)
        num_ref[at, lanes] = mm(weights, v_ref[at, lanes]) + mm_nt(pq, loc_ref[c, h])


def local_part(ct, w_out, gain, v, pq, pk, loc, fq, fk, sel, heads):
    rows, d = ct.shape
    n = rows // CH
    wide = heads * DV
    return pl.pallas_call(
        functools.partial(local_kernel, heads),
        grid=(n,),
        in_specs=[pl.BlockSpec((CH, d), lambda c: (c, 0)), KEPT, whole((1, wide))] + [KEPT] * 7,
        out_specs=[KEPT] * 4,
        out_shape=[kept((rows, wide), F32)] * 2 + [kept((heads, rows, CH), BF)] * 2,
        compiler_params=params(),
        cost_estimate=LIGHT,
        name="local_part",
    )(stay(ct), keep(w_out), gain, *map(keep, (v, pq, pk, loc, fq, fk, sel)))


def norm_kernel(heads, parts, passed, g_ref, num_ref, gain_ref, pq_ref, ones_ref, *refs):
    got = refs[:parts]
    ho_ref, dn_ref, loc_ref, pre_ref, state_ref, run = refs[parts + passed :]
    step = pl.program_id(0)
    c = pl.num_programs(0) - 1 - step
    at = rows_at(c)

    @pl.when(step == 0)
    def _():
        run[...] = jnp.zeros_like(run)
        total = got[0][...].astype(F32)
        for one in got[1:]:
            total = total + one[...].astype(F32)
        pre_ref[...] = total.astype(BF)

    for h in range(0, heads, 2):
        lanes = slice(DV * h, DV * h + 2 * DV)
        pqs = [pq_ref[h, at, :], pq_ref[h + 1, at, :]]
        num = num_ref[at, lanes] + jnp.concatenate(
            [mm(pqs[0][:, :ES], pre_ref[h]), mm(pqs[1][:, :ES], pre_ref[h + 1])], 1
        )
        inv = lax.rsqrt(mm((num * num).astype(BF), ones_ref[...]) + EPS)
        normed = num * inv
        ho_ref[at, lanes] = (normed * gain_ref[:, lanes]).astype(BF)
        g = g_ref[at, lanes]
        dn = ((g - normed * mm((g * normed).astype(BF), ones_ref[...])) * inv).astype(BF)
        dn_ref[at, lanes] = dn
        for i in range(2):
            loc_ref[c, h + i] = run[h + i].astype(BF)
            run[h + i] = run[h + i] + mm_tn(dn[:, DV * i : DV * i + DV], pqs[i])

    @pl.when(step == pl.num_programs(0) - 1)
    def _():
        for h in range(heads):
            state_ref[h] = run[h].T[:ES].astype(BF)


def norm_part(g, num, gain, pq, got, later, heads):
    ones = jnp.asarray(np.kron(np.eye(2), np.full((DV, DV), 1.0 / DV)), BF)
    rows, wide = g.shape
    n = rows // CH
    return pl.pallas_call(
        functools.partial(norm_kernel, heads, len(got), len(later)),
        grid=(n,),
        in_specs=[KEPT, KEPT, whole((1, wide)), KEPT, whole((2 * DV, 2 * DV))]
        + [whole((heads, ES, DV))] * len(got)
        + [KEPT] * len(later),
        out_specs=[KEPT] * 4 + [whole((heads, ES, DV))],
        out_shape=[
            kept((rows, wide), BF),
            kept((rows, wide), BF),
            kept((n, heads, DV, EP), BF),
            kept((heads, ES, DV), BF),
            jax.ShapeDtypeStruct((heads, ES, DV), BF),
        ],
        scratch_shapes=[pltpu.VMEM((heads, DV, EP), F32)],
        compiler_params=params(),
        cost_estimate=cost(16 << 30),
        name="norm_part",
    )(keep(g), keep(num), gain, keep(pq), ones, *got, *map(keep, later))


def inner_kernel(heads, v_ref, pq_ref, pk_ref, fq_ref, wt_ref, slope_ref, dn_ref, loc_ref, pre_ref, sel_ref,
                 fk_ref, gloc_ref, dqk_ref, dv_ref, xk_ref, pre_t):
    c = pl.program_id(0)
    at = rows_at(c)

    @pl.when(c == 0)
    def _():
        pre_t[...] = jnp.zeros_like(pre_t)
        for h in range(heads):
            pre_t[h, :, :ES] = pre_ref[h].astype(F32).T

    linear = lane_iota() < FEAT
    dqk = None
    for h in range(heads):
        lanes = slice(DV * h, DV * h + DV)
        dn = dn_ref[at, lanes]
        dv_ref[at, lanes] = mm_tn(wt_ref[h, at, :], dn)
        dl = (mm_nt(dn, v_ref[at, lanes]) * slope_ref[h, at, :].astype(F32)).astype(BF)
        xk_ref[h, at, :] = mm_tn(dl, pq_ref[h, at, :128])
        state = (loc_ref[c, h].astype(F32) + pre_t[h]).astype(BF)
        dphi = mm(dn, state)
        dphi = jnp.concatenate(
            [dphi[:, :128] + jnp.where(linear, mm(dl, pk_ref[h, at, :128]), 0.0), dphi[:, 128:]], 1
        )
        da = (dphi * fq_ref[h, at, EP:].astype(F32)).astype(BF)
        db = (dphi * fq_ref[h, at, :EP].astype(F32)).astype(BF)
        part = mm_nt(da, sel_ref[h, :, :EP]) + mm_nt(db, sel_ref[h, :, EP : 2 * EP])
        dqk = part if dqk is None else dqk + part
    dqk_ref[at, :] = dqk


def inner_part(v, pq, pk, fq, wt, slope, dn, loc, pre, sel, fk, gloc, heads):
    rows = v.shape[0]
    n = rows // CH
    return pl.pallas_call(
        functools.partial(inner_kernel, heads),
        grid=(n,),
        in_specs=[KEPT] * 12,
        out_specs=[KEPT] * 3,
        out_shape=[
            kept((rows, 128), F32),
            kept((rows, heads * DV), F32),
            kept((heads, rows, 128), F32),
        ],
        scratch_shapes=[pltpu.VMEM((heads, DV, EP), F32)],
        compiler_params=params(),
        cost_estimate=LIGHT,
        name="inner_part",
    )(*map(keep, (v, pq, pk, fq, wt, slope, dn, loc, pre, sel, fk, gloc)))


def outer_kernel(heads, parts, v_ref, pk_ref, fk_ref, dqk_ref, dv_ref, xk_ref, loc_ref, sel_ref, cw_ref, *refs):
    got = refs[:parts]
    top_ref, dp_ref, first_ref, last_ref, ext, suf_t = refs[parts:]
    half_chunks = pl.num_programs(0) // 2
    step = pl.program_id(0)
    c = pl.num_programs(0) - 1 - step
    at = rows_at(c)
    width = cw_ref.shape[1]

    @pl.when(step == 0)
    def _():
        suf_t[...] = jnp.zeros_like(suf_t)
        for h in range(heads):
            total = got[0][h].astype(F32)
            for one in got[1:]:
                total = total + one[h].astype(F32)
            suf_t[h, :, :ES] = total.T
        ext[CH:, :] = jnp.zeros((8, width), F32)

    lane = lane_iota()
    tiles = [None] * (-(-width // 128))

    def put(t, piece):
        tiles[t] = piece if tiles[t] is None else tiles[t] + piece

    dqk = dqk_ref[at, :]
    for h in range(heads):
        lanes = slice(DV * h, DV * h + DV)
        state = (loc_ref[c, h].astype(F32) + suf_t[h]).astype(BF)
        dphi = mm(v_ref[at, lanes], state)
        dphi = jnp.concatenate(
            [dphi[:, :128] + jnp.where(lane < FEAT, xk_ref[h, at, :], 0.0), dphi[:, 128:]], 1
        )
        da = (dphi * fk_ref[h, at, EP:].astype(F32)).astype(BF)
        db = (dphi * fk_ref[h, at, :EP].astype(F32)).astype(BF)
        own = (
            dqk
            + mm_nt(da, sel_ref[h, :, 2 * EP : 3 * EP])
            + mm_nt(db, sel_ref[h, :, 3 * EP : 4 * EP])
        )
        q0 = (HW * h) % 128
        put((HW * h) // 128, jnp.where((lane >= q0) & (lane < q0 + 2 * FEAT), own, 0.0))
        dv = dv_ref[at, lanes] + mm_nt(pk_ref[h, at, :], state)
        tile, off = value_place(h)
        if off == 0:
            put(tile, dv)
        else:
            moved = pltpu.roll(dv, off, 1)
            put(tile, jnp.where(lane >= off, moved, 0.0))
            put(tile + 1, jnp.where(lane < off, moved, 0.0))
    for t, tile in enumerate(tiles):
        end = min(128 * t + 128, width)
        ext[:CH, 128 * t : end] = tile[:, : end - 128 * t]
    dp = (cw_ref[0:1] * ext[:CH, :] + cw_ref[1:2] * ext[1 : CH + 1, :]
          + cw_ref[2:3] * ext[2 : CH + 2, :])
    dp_ref[at, :] = dp.astype(BF)

    @pl.when(c < half_chunks)
    def _():
        top_ref[at, :] = dp.astype(BF)

    @pl.when(step == 0)
    def _():
        last_ref[...] = dp[CH - 16 :]

    ext[CH:, :] = ext[0:8, :]
    first_ref[...] = ext[0:8, :]


def outer_part(v, pk, fk, dqk, dv, xk, loc, got, sel, conv_w, heads):
    rows, width = v.shape[0], conv_w.shape[1]
    n = rows // CH
    return pl.pallas_call(
        functools.partial(outer_kernel, heads, len(got)),
        grid=(n,),
        in_specs=[KEPT] * 8 + [whole((3, width))] + [whole((heads, ES, DV))] * len(got),
        out_specs=[KEPT, KEPT, whole((8, width)), KEPT],
        out_shape=[
            kept((rows // 2, width), BF),
            kept((rows, width), BF),
            jax.ShapeDtypeStruct((8, width), F32),
            kept((16, width), F32),
        ],
        scratch_shapes=[pltpu.VMEM((CH + 8, width), F32), pltpu.VMEM((heads, DV, EP), F32)],
        compiler_params=params(),
        cost_estimate=cost(16 << 30),
        name="outer_part",
    )(*map(keep, (v, pk, fk, dqk, dv, xk, loc, sel)), conv_w, *got)


def columns_kernel(which, place_ref, w_ref, *refs):
    outs, sems = refs[-1 - len(which) : -1], refs[-1]
    wide = outs[0].shape[1]
    copies = []
    for i, m in enumerate(which):
        start = pl.multiple_of(lax.bitwise_xor(place_ref[0], m) * wide, wide)
        copies.append(pltpu.make_async_copy(w_ref.at[:, pl.ds(start, wide)], outs[i], sems.at[i]))
    if len(refs) > len(which) + 1:
        x_ref, wi_ref, tail_ref, wi_out_ref = refs[:4]
        rows = tail_ref.shape[0]
        copies.append(
            pltpu.make_async_copy(x_ref.at[pl.ds(x_ref.shape[0] - rows, rows), :], tail_ref, sems.at[len(which)])
        )
        count, sw = wi_out_ref.shape[:2]
        for r in range(count):
            block = 2 * lax.bitwise_xor(place_ref[0], r) + 1 - place_ref[1]
            copies.append(
                pltpu.make_async_copy(
                    wi_ref.at[pl.ds(pl.multiple_of(block * sw, sw), sw), :],
                    wi_out_ref.at[r],
                    sems.at[len(which) + 1 + r],
                )
            )
    for copy in copies:
        copy.start()
    for copy in copies:
        copy.wait()


def columns(place, w_out, which, count, x=None, w_in=None):
    rows, d = w_out.shape
    anywhere = pl.BlockSpec(memory_space=pltpu.HBM)
    out_shape = [jax.ShapeDtypeStruct((rows, d // count), w_out.dtype)] * len(which)
    args = [stay(w_out)]
    if x is not None:
        args += [stay(x), stay(w_in)]
        out_shape = [
            jax.ShapeDtypeStruct((16, x.shape[1]), x.dtype),
            jax.ShapeDtypeStruct((count, w_in.shape[0] // (2 * count), w_in.shape[1]), w_in.dtype),
        ] + out_shape
    return pl.pallas_call(
        functools.partial(columns_kernel, which),
        grid_spec=pltpu.PrefetchScalarGridSpec(
            num_scalar_prefetch=1,
            grid=(1,),
            in_specs=[anywhere] * len(args),
            out_specs=[anywhere] * len(out_shape),
            scratch_shapes=[pltpu.SemaphoreType.DMA((len(which) + 1 + count,))],
        ),
        out_shape=out_shape,
        compiler_params=pltpu.CompilerParams(vmem_limit_bytes=VMEM),
        cost_estimate=LIGHT,
        name="columns",
    )(place, *args)


def shifted(array, by):
    count = lax.axis_size("seq")
    pairs = [(i, i + by) for i in range(count) if 0 <= i + by < count]
    return lax.ppermute(array, "seq", pairs)


def from_others(part, sign):
    return [shifted(part, sign * step) for step in range(1, lax.axis_size("seq"))]


def out_kernel(count, sw, place_ref, *refs):
    tops, lows, ws = refs[:count], refs[count : 2 * count], refs[2 * count : 3 * count]
    send_ref, keep_ref = refs[3 * count :]
    c = pl.program_id(0)
    half_chunks = pl.num_programs(0) // 2
    odd = place_ref[1] == 1

    def product(parts):
        total = None
        for part, w in zip(parts, ws):
            one = mm(part[...], w[...])
            total = one if total is None else total + one
        first, second = total[:, :sw], total[:, sw:]
        send_ref[...] = jnp.where(odd, first, second).astype(BF)
        keep_ref[...] = jnp.where(odd, second, first)

    @pl.when(c < half_chunks)
    def _():
        product(tops)

    @pl.when(c >= half_chunks)
    def _():
        product(lows)


def out_part(place, tops, lows, ws):
    count = len(ws)
    rows = 2 * CH * (lows[0][1] // CH)
    wide = tops[0][0].shape[1]
    sw = ws[1].shape[1] // 2
    part = rows // (2 * CH)
    row = pl.BlockSpec((CH, sw), lambda c, place: (c, 0))
    operands, specs = [], []
    for array, start in tops:
        operands.append(array)
        specs.append(
            pl.BlockSpec((CH, wide), lambda c, place, s=start // CH: (s + jnp.minimum(c, part - 1), 0))
        )
    for array, start in lows:
        operands.append(array)
        specs.append(
            pl.BlockSpec((CH, wide), lambda c, place, s=start // CH: (s + jnp.maximum(c - part, 0), 0))
        )
    return pl.pallas_call(
        functools.partial(out_kernel, count, sw),
        grid_spec=pltpu.PrefetchScalarGridSpec(
            num_scalar_prefetch=1,
            grid=(rows // CH,),
            in_specs=specs
            + [pl.BlockSpec((wide, 2 * sw), lambda c, place: (0, place[0]))]
            + [pl.BlockSpec((wide, 2 * sw), lambda c, place: (0, 0))] * (count - 1),
            out_specs=[row, row],
        ),
        out_shape=[jax.ShapeDtypeStruct((rows, sw), BF), jax.ShapeDtypeStruct((rows, sw), F32)],
        compiler_params=params(),
        cost_estimate=cost(16 << 30),
        name="out_part",
    )(place, *operands, *map(stay, ws))


def complete_kernel(dp_ref, last_ref, after_ref, cw_ref, low_ref):
    half = low_ref.shape[0]
    low_ref[...] = dp_ref[half:, :]
    row = lax.broadcasted_iota(jnp.int32, last_ref.shape, 0)
    a0, a1 = after_ref[0:1], after_ref[1:2]
    one = cw_ref[2:3] * a0
    two = cw_ref[1:2] * a0 + cw_ref[2:3] * a1
    tail = last_ref[...] + jnp.where(row == 14, one, 0.0) + jnp.where(row == 15, two, 0.0)
    low_ref[half - 16 :, :] = tail.astype(BF)


def complete(dp, last, after, conv_w):
    rows, width = dp.shape
    return pl.pallas_call(
        complete_kernel,
        in_specs=[KEPT] * 4,
        out_specs=KEPT,
        out_shape=kept((rows // 2, width), BF),
        compiler_params=pltpu.CompilerParams(vmem_limit_bytes=VMEM),
        cost_estimate=LIGHT,
        name="complete",
    )(keep(dp), keep(last), after, conv_w)


def grad_kernel(count, low_first, place_ref, dp_ref, other_ref, w_ref, w_other_ref, send_ref, keep_ref, both):
    r = pl.program_id(0)
    half, sw = send_ref.shape[1:]
    width = w_ref.shape[1]

    @pl.when(r == 0)
    def _():
        both[:, :width] = dp_ref[...]
        both[:, width:] = other_ref[...]

    block = 2 * lax.bitwise_xor(place_ref[0], r) + place_ref[1]
    w = w_ref[pl.ds(pl.multiple_of(block * sw, sw), sw), :]
    total = mm_nt(both[...], jnp.concatenate([w, w_other_ref[r]], 1)).astype(BF)
    part = count // 2
    leaves = (r % 2 == 1) if low_first else (r >= part)

    @pl.when(leaves)
    def _():
        send_ref[r // 2 if low_first else r - part] = total

    @pl.when(jnp.logical_not(leaves))
    def _():
        keep_ref[r // 2 if low_first else r] = total


def grad_part(place, dp, other, w_in, w_other, low_first):
    half, width = dp.shape
    count, sw = w_other.shape[:2]
    return pl.pallas_call(
        functools.partial(grad_kernel, count, low_first),
        grid_spec=pltpu.PrefetchScalarGridSpec(
            num_scalar_prefetch=1,
            grid=(count,),
            in_specs=[KEPT] * 4,
            out_specs=[KEPT] * 2,
            scratch_shapes=[pltpu.VMEM((half, 2 * width), BF)],
        ),
        out_shape=[kept((count // 2, half, sw), BF)] * 2,
        compiler_params=params(),
        cost_estimate=LIGHT,
        name="grad_part",
    )(place, *map(keep, (dp, other, w_in, w_other)))


def halves_kernel(x_ref, y_ref, x_top_ref, y_low_ref):
    half = x_top_ref.shape[0]
    x_top_ref[...] = x_ref[:half, :]
    y_low_ref[...] = y_ref[half:, :]


def halves(x_got, y_got):
    rows, wide = x_got.shape
    return pl.pallas_call(
        halves_kernel,
        in_specs=[KEPT] * 2,
        out_specs=[KEPT] * 2,
        out_shape=[kept((rows // 2, wide), BF)] * 2,
        compiler_params=pltpu.CompilerParams(vmem_limit_bytes=VMEM),
        cost_estimate=LIGHT,
        name="halves",
    )(keep(x_got), keep(y_got))


def swapped(array, distance):
    count = lax.axis_size("tp")
    return lax.ppermute(array, "tp", [(i, i ^ distance) for i in range(count)])


def summed(a, b):
    return a.astype(F32) + b.astype(F32)


def passing_kernel(first, stride, keep_ref, got_ref, out_ref):
    for i in range(out_ref.shape[0]):
        out_ref[i] = summed(keep_ref[first + stride * i], got_ref[first + stride * i]).astype(BF)


def passing(kept_sum, got, first, stride):
    left, half, sw = got.shape
    return pl.pallas_call(
        functools.partial(passing_kernel, first, stride),
        in_specs=[KEPT] * 2,
        out_specs=KEPT,
        out_shape=kept((left // 2, half, sw), BF),
        compiler_params=pltpu.CompilerParams(vmem_limit_bytes=VMEM),
        cost_estimate=LIGHT,
        name="passing",
    )(keep(kept_sum), keep(got))


def reduce_both(a_send, a_keep, b_send, b_keep, a_own, b_own, meanwhile):
    pairs = lax.axis_size("tp") // 2
    a_step, b_step = 1, pairs // 2
    while True:
        a_got = swapped(a_send, 2 * a_step)
        b_got = swapped(b_send, 2 * b_step)
        left = a_keep.shape[0]
        a_keep, b_keep = meanwhile(a_keep, b_keep)
        if left == 1:
            return a_keep[0], a_got[0], b_keep[0], b_got[0]
        a_send = passing(a_keep, a_got, 1, 2)
        b_send = passing(b_keep, b_got, left // 2, 1)
        a_keep = summed(a_keep[0::2], a_got[0::2])
        b_keep = summed(b_keep[: left // 2], b_got[: left // 2])
        if left == 2:
            a_keep = a_keep + a_own
            b_keep = b_keep + b_own
        a_step, b_step = a_step * 2, b_step // 2


def finish_kernel(half, ak_ref, ag_ref, bk_ref, bg_ref, out_ref):
    out_ref[:half, :] = (ak_ref[...] + ag_ref[...].astype(F32)).astype(BF)
    out_ref[half:, :] = (bk_ref[...] + bg_ref[...].astype(F32)).astype(BF)


def finish(a_keep, a_got, b_keep, b_got):
    half, sw = a_keep.shape
    return pl.pallas_call(
        functools.partial(finish_kernel, half),
        out_shape=jax.ShapeDtypeStruct((2 * half, sw), BF),
        compiler_params=pltpu.CompilerParams(vmem_limit_bytes=VMEM),
        cost_estimate=LIGHT,
        name="finish",
    )(a_keep, a_got, b_keep, b_got)


def per_device(inputs, cotangent, w_in, conv_w, norm_gain, w_out, keep_flags):
    heads = keep_flags.shape[0]
    sel, bias = selectors(heads)
    tp = lax.axis_size("tp")
    pairs = tp // 2
    me = lax.axis_index("tp")
    pair = me // 2
    place = jnp.stack([pair, me % 2]).astype(jnp.int32)
    slice_width = inputs.shape[1] // tp
    column = me * slice_width
    gain = (norm_gain.reshape(heads, DV) * keep_flags.astype(F32)[:, None]).reshape(1, heads * DV)

    half = inputs.shape[0] // 2
    tail, w_other, *near = columns(place, w_out, (1, 2), pairs, inputs, w_in)
    w_other = swapped(w_other, 1)
    halo = shifted(tail, 1)
    near = [swapped(one, 2 * m) for m, one in enumerate(near, 1)]
    far = columns(place, w_out, range(3, pairs), pairs)
    halo, place, gain, far = lax.optimization_barrier((halo, place, gain, far))
    v, pq, pk, fq, fk, loc, state = project(inputs, halo, w_in, conv_w, sel, bias, heads)
    state, w_other = lax.optimization_barrier((state, w_other))
    before = from_others(state, 1)
    v, near, far = lax.optimization_barrier((v, near, far))
    far = [swapped(one, 2 * m) for m, one in enumerate(far, 3)]
    g, num, wt, slope = local_part(cotangent, w_out, gain, v, pq, pk, loc, fq, fk, sel, heads)
    ho, dn, gloc, pre, gstate = norm_part(
        g, num, gain, pq, before, (v, pk, fq, fk, wt, slope, loc, sel), heads
    )
    step = pairs // 2
    got = {r: swapped(ho, 2 * r) for r in range(1, pairs) if r != 1 + step}
    later = from_others(gstate, -1)
    pre, far = lax.optimization_barrier((pre, far))
    dqk, dv, xk = inner_part(v, pq, pk, fq, wt, slope, dn, loc, pre, sel, fk, gloc, heads)
    dp_top, dp, first, last = outer_part(v, pk, fk, dqk, dv, xk, gloc, later, sel, conv_w, heads)
    other_top = swapped(dp_top, 1)
    dp_low = complete(dp, last, shifted(first, -1), conv_w)
    other_low = swapped(dp_low, 1)
    x_top, y_low = halves(got[1], got[step])
    x_top, y_low = swapped(x_top, 2 * step), swapped(y_low, 2)
    a_send, a_keep = grad_part(place, dp_top, other_top, w_in, w_other, True)
    b_send, b_keep = grad_part(place, dp_low, other_low, w_in, w_other, False)
    tops = [(ho, 0)] + [(got.get(r, x_top), 0) for r in range(1, pairs)]
    lows = [(ho, half)] + [(got[r], half) if r in got else (y_low, 0) for r in range(1, pairs)]
    w_cols = [w_out] + near + far
    x_own = lax.dynamic_slice_in_dim(inputs, column, slice_width, 1).astype(F32)
    c_own = lax.dynamic_slice_in_dim(cotangent, column, slice_width, 1).astype(F32)
    stage = []

    def meanwhile(a, b):
        if not stage:
            out_send, out_keep = out_part(place, tops, lows, w_cols)
            stage.append(x_own + out_keep)
            stage.append(out_send)
            a, b, stage[1] = lax.optimization_barrier((a, b, stage[1]))
            stage.append(swapped(stage[1], 1))
        elif len(stage) == 3:
            stage.append((stage[0] + stage[2].astype(F32)).astype(BF))
            a, b, stage[3] = lax.optimization_barrier((a, b, stage[3]))
        return a, b

    sums = reduce_both(a_send, a_keep, b_send, b_keep, c_own[None, :half], c_own[None, half:], meanwhile)
    return stage[3], finish(*sums)


def solution(mesh):
    placed = (
        P("seq", None),
        P("seq", None),
        P(None, "tp"),
        P(None, "tp"),
        P("tp"),
        P("tp", None),
        P("tp"),
    )
    return jax.shard_map(
        per_device,
        mesh=mesh,
        in_specs=placed,
        out_specs=(P("seq", "tp"), P("seq", "tp")),
        check_vma=False,
    )
```

time: 149 us -> 137 us (0.919)
  waiting for transfers between devices: 33.8 us -> 26.5 us
  Pallas kernels: 73.1 us -> 67.7 us
  local copies, waits for them, and re-layouts: 3.45 us -> 5.24 us
    ppermute x14 -> x15, waiting for transfers between devices: 30.6 us -> 22.3 us  [swapped(): return lax.ppermute(array, 'tp', [(i, i ^ distance) for i in range(count)])]
    unnamed x28 -> x38, local copies, waits for them, and re-layouts: 2.53 us -> 5.24 us
    pallas_call x1, Pallas kernels: 10.2 us -> 7.71 us  [inner_part(): pl.pallas_call(functools.partial(inner_kernel, heads), grid=(n,), in_spec...]
    convert_element_type x1 -> x0, other arithmetic: 2.3 us -> none  [reduce_both(): b_send = summed(b_keep[left // 2:], b_got[left // 2:]).astype(BF)]
    pallas_call x6 -> x9, Pallas kernels: 24.5 us -> 22.7 us  [the longest x2 10.8 us: grad_part(): pl.pallas_call(functools.partial(grad_kernel, count, low_first), grid_spe...]
    ppermute x14 -> x15, starting transfers between devices: 12.2 us -> 12.5 us  [swapped(): return lax.ppermute(array, 'tp', [(i, i ^ distance) for i in range(count)])]
  transfers between devices with their start and end apart: 22 -> 23, of which waited for: 10 -> 8; matrix products, arithmetic and copies ran while one was open for 5% -> 4% of each run, Pallas kernels for 48% -> 47%
where the time goes in v2:
time: 137 us
  Pallas kernels  67.7 us (49%)
  starting transfers between devices  30.5 us (22%)
  waiting for transfers between devices  26.5 us (19%)
  other arithmetic  5.79 us (4%)
  local copies, waits for them, and re-layouts  5.24 us (4%)
    ppermute x15, waiting for transfers between devices, swapped(): return lax.ppermute(array, 'tp', [(i, i ^ distance) for i in range(count)])  22.3 us
    ppermute x8, starting transfers between devices, shifted(): return lax.ppermute(array, 'seq', pairs)  18 us
    pallas_call x1, Pallas kernels, project(): pl.pallas_call(functools.partial(project_kernel, heads), grid=(n,), in_sp...  15 us
    ppermute x15, starting transfers between devices, swapped(): return lax.ppermute(array, 'tp', [(i, i ^ distance) for i in range(count)])  12.5 us
    pallas_call x2, Pallas kernels, grad_part(): pl.pallas_call(functools.partial(grad_kernel, count, low_first), grid_spe...  10.8 us
    pallas_call x1, Pallas kernels, local_part(): pl.pallas_call(functools.partial(local_kernel, heads), grid=(n,), in_spec...  8.93 us
    pallas_call x1, Pallas kernels, out_part(): pl.pallas_call(functools.partial(out_kernel, count, sw), grid_spec=pltpu....  8.62 us
    pallas_call x1, Pallas kernels, inner_part(): pl.pallas_call(functools.partial(inner_kernel, heads), grid=(n,), in_spec...  7.71 us
  transfers between devices with their start and end apart: 23, of which 8 were waited for; matrix products, arithmetic and copies ran while one was open for 4% of the time, Pallas kernels for 47%

profile of v2, /device:TPU:0, one launch (start us, length us, event | category | flops | bytes accessed | tf_op | source)
XLA Modules:
  0.0 136.8 jit_solution(12389987466041252396)
XLA Ops:
  0.6 0.1 pad_add_fusion.place_ref
  0.7 3.0 %columns.2 = (bf16[16,4096]{1,0:T(8,128)(2,1)S(1)}, bf16[4,512,640]{2,1,0:T(8,128)(2,1)S(1)}, bf16[512,1024]{1,0:T(8,128)(2,1)S(1)}, bf16[512,1024]{1,0:T(8,128)(2,1)S(1)}) custom-call(s32[2]{0:T(128)S(1)} %pad_add_fusion.place_ref, bf16[512,4096]{1,0:T(8,128)(2,1)} %refs_8_.1, bf16[1024,4096]{1,0:T(8,128)(2,1)} %x_ref.1, bf16[4096,640]{1,0:T(8,128)(2,1)} %w_ref.9), custom_call_target="tpu_custom_call" | custom-call | flops 1000 | bytes 1048576 | tf_op jit(solution)/shard_map/columns/pallas_call | solution.py:477
  3.7 4.9 %collective-permute-start = (bf16[16,4096]{1,0:T(8,128)(2,1)S(1)}, bf16[16,4096]{1,0:T(8,128)(2,1)S(1)}, u32[]{:S(2)}, u32[]{:S(2)}) collective-permute-start(bf16[16,4096]{1,0:T(8,128)(2,1)S(1)} %get-tuple-element.55), channel_id=1, source_target_pairs={{0,8},{8,16},{16,24},{1,9},{9,17},{17,25},{2,10},{10,18},{18,26},{... | collective-permute-start | bytes 393224 | tf_op jit(solution)/shard_map/ppermute | solution.py:496
  8.7 1.6 %collective-permute-start.1 = (bf16[512,1024]{1,0:T(8,128)(2,1)S(1)}, bf16[512,1024]{1,0:T(8,128)(2,1)S(1)}, u32[]{:S(2)}, u32[]{:S(2)}) collective-permute-start(bf16[512,1024]{1,0:T(8,128)(2,1)S(1)} %get-tuple-element.59), channel_id=1, source_target_pairs={{0,2},{1,3},{2,0},{3,1},{4,6},{5,7},{6,4},{7,5},{8,10},{9,11},{10,... | collective-permute-start | bytes 3145736 | tf_op jit(solution)/shard_map/ppermute | solution.py:652
  10.2 1.5 %collective-permute-start.2 = (bf16[512,1024]{1,0:T(8,128)(2,1)S(1)}, bf16[512,1024]{1,0:T(8,128)(2,1)S(1)}, u32[]{:S(2)}, u32[]{:S(2)}) collective-permute-start(bf16[512,1024]{1,0:T(8,128)(2,1)S(1)} %get-tuple-element.60), channel_id=1, source_target_pairs={{0,4},{1,5},{2,6},{3,7},{4,0},{5,1},{6,2},{7,3},{8,12},{9,13},{10,... | collective-permute-start | bytes 3145736 | tf_op jit(solution)/shard_map/ppermute | solution.py:652
  11.7 2.1 %columns.3 = bf16[512,1024]{1,0:T(8,128)(2,1)S(1)} custom-call(s32[2]{0:T(128)S(1)} %pad_add_fusion.place_ref, bf16[512,4096]{1,0:T(8,128)(2,1)} %refs_8_.1), custom_call_target="tpu_custom_call" | custom-call | flops 1000 | bytes 1048576 | tf_op jit(solution)/shard_map/columns/pallas_call | solution.py:477
  13.9 0.1 bitcast_multiply_fusion
  13.9 0.0 collective-permute-done.halo_ref
  14.0 0.6 copy-done
  14.6 15.0 %project.1 = (bf16[1024,512]{1,0:T(8,128)(2,1)S(1)}, bf16[4,1024,256]{2,1,0:T(8,128)(2,1)S(1)}, bf16[4,1024,256]{2,1,0:T(8,128)(2,1)S(1)}, bf16[4,1024,512]{2,1,...) custom-call(bf16[1024,4096]{1,0:T(8,128)(2,1)} %x_ref.1, ...), custom_call_target="tpu_custom_call" | custom-call | flops 107374182400 | bytes 1048576 | tf_op jit(solution)/shard_map/project/pallas_call | solution.py:173
  29.6 0.0 collective-permute-done.3.w_other_ref
  29.6 3.5 %collective-permute-start.4 = (bf16[4,160,128]{2,1,0:T(8,128)(2,1)S(1)}, bf16[4,160,128]{2,1,0:T(8,128)(2,1)S(1)}, u32[]{:S(2)}, u32[]{:S(2)}) collective-permute-start(bf16[4,160,128]{2,1,0:T(8,128)(2,1)S(1)} %get-tuple-element.75), channel_id=1, source_target_pairs={{0,8},{8,16},{16,24},{1,9},{9,17},{17,25},{2,10},{10,18},{18,26},{... | collective-permute-start | bytes 491528 | tf_op jit(solution)/shard_map/ppermute | solution.py:496
  33.1 2.9 %collective-permute-start.5 = (bf16[4,160,128]{2,1,0:T(8,128)(2,1)S(1)}, bf16[4,160,128]{2,1,0:T(8,128)(2,1)S(1)}, u32[]{:S(2)}, u32[]{:S(2)}) collective-permute-start(bf16[4,160,128]{2,1,0:T(8,128)(2,1)S(1)} %get-tuple-element.75), channel_id=1, source_target_pairs={{0,16},{8,24},{1,17},{9,25},{2,18},{10,26},{3,19},{11,27},{4,20},{... | collective-permute-start | bytes 491528 | tf_op jit(solution)/shard_map/ppermute | solution.py:496
  36.0 1.3 collective-permute-start.6
  37.3 0.0 copy-start.15
  37.3 0.0 collective-permute-done.2.refs_10_
  37.4 0.0 copy-start.16
  37.4 1.8 %collective-permute-start.7 = (bf16[512,1024]{1,0:T(8,128)(2,1)S(1)}, bf16[512,1024]{1,0:T(8,128)(2,1)S(1)}, u32[]{:S(2)}, u32[]{:S(2)}) collective-permute-start(bf16[512,1024]{1,0:T(8,128)(2,1)S(1)} %columns.3), channel_id=1, source_target_pairs={{0,6},{1,7},{2,4},{3,5},{4,2},{5,3},{6,0},{7,1},{8,14},{9,15},{10,... | collective-permute-start | bytes 3145736 | tf_op jit(solution)/shard_map/ppermute | solution.py:652
  39.2 8.9 %local_part.1 = (f32[1024,512]{1,0:T(8,128)S(1)}, f32[1024,512]{1,0:T(8,128)S(1)}, bf16[4,1024,256]{2,1,0:T(8,128)(2,1)S(1)}, bf16[4,1024,256]{2,1,0:T(8,128)(2,1)S(1)}) custom-call(bf16[1024,4096]{1,0:T(8,128)(2,1)} %ct_ref.1, bf16[512,4096]{1,0:T(8,128)(2,1)S(1)} %copy-done.1, f32[1,512]{1,0:T(1,128)S(1)} %bitcast.21, ...), custom_call_target="tpu_custom_call" | custom-call | flops 1000 | bytes 1048576 | tf_op jit(solution)/shard_map/local_part/pallas_call | solution.py:222
  48.2 0.0 collective-permute-done.5.refs_1_
  48.2 0.0 collective-permute-done.6.refs_2_
  48.2 5.2 %norm_part.1 = (bf16[1024,512]{1,0:T(8,128)(2,1)S(1)}, bf16[1024,512]{1,0:T(8,128)(2,1)S(1)}, bf16[4,4,128,256]{3,2,1,0:T(8,128)(2,1)S(1)}, bf16[4,160,128]{2,1,0:T(8,128)(2,1)S(1)}, bf16[4,160,128]{2,1,0:T(8,128)(2,1)S(1)}) custom-call(f32[1024,512]{1,0:T(8,128)S(1)} %get-tuple-element.71.g_ref, f32[1024,512]{1,0:T(8,128)S(1)} %get-tuple-element.72.num_ref, ...), custom_call_target="tpu_custom_call" | custom-call | flops 17179869184 | bytes 1048576 | tf_op jit(solution)/shard_map/norm_part/pallas_call | solution.py:275
  53.4 1.3 collective-permute-start.10
  54.7 1.3 collective-permute-start.8
  56.0 1.3 collective-permute-start.9
  57.3 0.6 collective-permute-start.14
  57.9 6.5 %collective-permute-done.7.refs_11_ = bf16[512,1024]{1,0:T(8,128)(2,1)S(1)} collective-permute-done((bf16[512,1024]{1,0:T(8,128)(2,1)S(1)}, bf16[512,1024]{1,0:T(8,128)(2,1)S(1)}, u32[]{:S(2)}, u32[]{:S(2)}) %collective-permute-start.7) | collective-permute-done | bytes 1048608 | tf_op jit(solution)/shard_map/ppermute | solution.py:652
  64.4 0.8 collective-permute-start.15
  65.3 7.7 %inner_part.1 = (f32[1024,128]{1,0:T(8,128)S(1)}, f32[1024,512]{1,0:T(8,128)S(1)}, f32[4,1024,128]{2,1,0:T(8,128)S(1)}) custom-call(bf16[1024,512]{1,0:T(8,128)(2,1)S(1)} %get-tuple-element.62.v_ref.refs_3_, bf16[4,1024,256]{2,1,0:T(8,128)(2,1)S(1)} %get-tuple-element.65.pq_ref, bf16[4,1024,256]{2,1,0:T(8,128)(2,1)S(1)} %get-tuple-element.63.pk_ref.refs_4_, ...), custom_call_target="tpu_custom_call" | custom-call | flops 1000 | bytes 1048576 | tf_op jit(solution)/shard_map/inner_part/pallas_call | solution.py:330
  73.0 0.0 collective-permute-done.9.refs_1_
  73.1 1.6 %copy-done.3 = bf16[4,1024,256]{2,1,0:T(8,128)(2,1)S(1)} copy-done((bf16[4,1024,256]{2,1,0:T(8,128)(2,1)S(1)}, bf16[4,1024,256]{2,1,0:T(8,128)(2,1)}, u32[]{:S(2)}) %copy-start.3) | copy-done | bytes 2097176
  74.6 3.7 %outer_part.1 = (bf16[512,640]{1,0:T(8,128)(2,1)S(1)}, bf16[1024,640]{1,0:T(8,128)(2,1)S(1)}, f32[8,640]{1,0:T(8,128)S(1)}, f32[16,640]{1,0:T(8,128)S(1)}) custom-call(bf16[1024,512]{1,0:T(8,128)(2,1)S(1)} %get-tuple-element.62.v_ref.refs_3_, bf16[4,1024,256]{2,1,0:T(8,128)(2,1)S(1)} %copy-done.3, ...), custom_call_target="tpu_custom_call" | custom-call | flops 17179869184 | bytes 1048576 | tf_op jit(solution)/shard_map/outer_part/pallas_call | solution.py:419
  78.3 1.5 %collective-permute-start.12 = (f32[8,640]{1,0:T(8,128)S(1)}, f32[8,640]{1,0:T(8,128)S(1)}, u32[]{:S(2)}, u32[]{:S(2)}) collective-permute-start(f32[8,640]{1,0:T(8,128)S(1)} %get-tuple-element.90), channel_id=1, source_target_pairs={{8,0},{16,8},{24,16},{9,1},{17,9},{25,17},{10,2},{18,10},{26,18},{... | collective-permute-start | bytes 61448 | tf_op jit(solution)/shard_map/ppermute | solution.py:496
  79.8 0.1 collective-permute-start.11
  79.9 4.1 %collective-permute-done.12.after_ref = f32[8,640]{1,0:T(8,128)S(1)} collective-permute-done((f32[8,640]{1,0:T(8,128)S(1)}, f32[8,640]{1,0:T(8,128)S(1)}, u32[]{:S(2)}, u32[]{:S(2)}) %collective-permute-start.12) | collective-permute-done | bytes 20512 | tf_op jit(solution)/shard_map/ppermute | solution.py:496
  84.0 0.1 complete.1.dp_ref
  84.1 0.1 collective-permute-start.13
  84.1 0.2 collective-permute-done.14.x_ref.refs_1_.refs_5_
  84.3 2.3 %collective-permute-done.15.y_ref.refs_2_.refs_6_ = bf16[1024,512]{1,0:T(8,128)(2,1)S(1)} collective-permute-done((bf16[1024,512]{1,0:T(8,128)(2,1)S(1)}, bf16[1024,512]{1,0:T(8,128)(2,1)S(1)}, u32[]{:S(2)}, u32[]{:S(2)}) %collective-permute-start.15) | collective-permute-done | bytes 1048608 | tf_op jit(solution)/shard_map/ppermute | solution.py:652
  86.6 0.1 halves.1
  86.7 0.6 collective-permute-start.16
  87.3 0.9 collective-permute-start.17
  88.2 0.0 collective-permute-done.11.other_ref
  88.2 5.4 %grad_part.2 = (bf16[2,512,512]{2,1,0:T(8,128)(2,1)}, bf16[2,512,512]{2,1,0:T(8,128)(2,1)S(1)}) custom-call(s32[2]{0:T(128)S(1)} %pad_add_fusion.place_ref, bf16[512,640]{1,0:T(8,128)(2,1)S(1)} %get-tuple-element.85.dp_ref, bf16[512,640]{1,0:T(8,128)(2,1)S(1)} %collective-permute-done.11.other_ref, bf16[4096,640]{1,0:T(8,128)(2,1)S(1)} %copy-done, ...), custom_call_target="tpu_custom_call" | custom-call | flops 1000 | bytes 1048576 | tf_op jit(solution)/shard_map/grad_part/pallas_call | solution.py:615
  93.6 1.1 collective-permute-start.18
  94.8 5.4 %grad_part.3 = (bf16[2,512,512]{2,1,0:T(8,128)(2,1)}, bf16[2,512,512]{2,1,0:T(8,128)(2,1)S(1)}) custom-call(s32[2]{0:T(128)S(1)} %pad_add_fusion.place_ref, bf16[512,640]{1,0:T(8,128)(2,1)S(1)} %complete.1.dp_ref, bf16[512,640]{1,0:T(8,128)(2,1)S(1)} %collective-permute-done.13.other_ref, bf16[4096,640]{1,0:T(8,128)(2,1)S(1)} %copy-done, ...), custom_call_target="tpu_custom_call" | custom-call | flops 1000 | bytes 1048576 | tf_op jit(solution)/shard_map/grad_part/pallas_call | solution.py:615
  100.2 1.0 copy-done.5
  101.2 1.5 %collective-permute-start.19 = (bf16[2,512,512]{2,1,0:T(8,128)(2,1)}, bf16[2,512,512]{2,1,0:T(8,128)(2,1)S(1)}, u32[]{:S(2)}, u32[]{:S(2)}) collective-permute-start(bf16[2,512,512]{2,1,0:T(8,128)(2,1)} %get-tuple-element.102), channel_id=1, source_target_pairs={{0,4},{1,5},{2,6},{3,7},{4,0},{5,1},{6,2},{7,3},{8,12},{9,13},{10,... | collective-permute-start | bytes 3145736 | tf_op jit(solution)/shard_map/ppermute | solution.py:652
  102.7 0.0 collective-permute-done.16.refs_3_
  102.7 0.6 copy-done.11
  103.3 8.6 %out_part.1 = (bf16[1024,512]{1,0:T(8,128)(2,1)}, f32[1024,512]{1,0:T(8,128)S(1)}) custom-call(s32[2]{0:T(128)S(1)} %copy-done.11, bf16[1024,512]{1,0:T(8,128)(2,1)S(1)} %get-tuple-element.92.refs_0_.refs_4_, bf16[1024,512]{1,0:T(8,128)(2,1)S(1)} %collective-permute-done.14.x_ref.refs_1_.refs_5_, ...), custom_call_target="tpu_custom_call" | custom-call | flops 17179869184 | bytes 1048576 | tf_op jit(solution)/shard_map/out_part/pallas_call | solution.py:546
  111.9 1.3 copy-done.7
  113.3 1.5 %dynamic-slice_convert_fusion = f32[1024,512]{1,0:T(8,128)S(1)} fusion(bf16[1024,4096]{1,0:T(8,128)(2,1)} %ct_ref.1, s32[]{:T(128)S(6)} %select_n.17), kind=kLoop, calls=%fused_computation.5 | loop fusion | flops 524288 | bytes 3145732 | tf_op jit(solution)/shard_map/convert_element_type | solution.py:758
  114.8 7.3 %collective-permute-done.18.got_ref = bf16[2,512,512]{2,1,0:T(8,128)(2,1)} collective-permute-done((bf16[2,512,512]{2,1,0:T(8,128)(2,1)}, bf16[2,512,512]{2,1,0:T(8,128)(2,1)}, u32[]{:S(2)}, u32[]{:S(2)}) %collective-permute-start.18) | collective-permute-done | bytes 1048608 | tf_op jit(solution)/shard_map/ppermute | solution.py:652
  122.1 1.3 passing.2
  123.4 0.9 collective-permute-start.21
  124.3 0.6 collective-permute-done.19.got_ref
  125.0 0.1 passing.3
  125.1 0.9 collective-permute-start.22
  126.0 1.5 %fusion = (f32[1,512,512]{2,1,0:T(8,128)S(1)}, f32[1,512,512]{2,1,0:T(8,128)S(1)}) fusion(f32[1024,512]{1,0:T(8,128)S(1)} %dynamic-slice_convert_fusion, bf16[2,512,512]{2,1,0:T(8,128)(2,1)S(1)} %collective-permute-done.19.got_ref, bf16[2,512,512]{2,1,0:T(8,128)(2,1)S(1)} %copy-done.6, bf16[2,512,512]{2,1,0:T(8,128)(2,1)} %collective-permute-done.18.got_ref, ...), kind=kLoop, calls=%fused_computation.2 | loop fusion | flops 2097152 | bytes 6291456 | tf_op jit(solution)/shard_map/add | solution.py:693
  127.6 2.7 %add_convert_fusion = bf16[1024,512]{1,0:T(8,128)(2,1)} fusion(bf16[1024,512]{1,0:T(8,128)(2,1)S(1)} %collective-permute-done.20, f32[1024,512]{1,0:T(8,128)S(1)} %copy-done.8, bf16[1024,4096]{1,0:T(8,128)(2,1)} %x_ref.1, s32[]{:T(128)S(6)} %select_n.17), kind=kLoop, calls=%fused_computation | loop fusion | flops 2621440 | bytes 5242884 | tf_op jit(solution)/shard_map/convert_element_type | solution.py:769
  130.2 5.3 %collective-permute-done.21 = bf16[1,512,512]{2,1,0:T(8,128)(2,1)S(1)} collective-permute-done((bf16[1,512,512]{2,1,0:T(8,128)(2,1)S(1)}, bf16[1,512,512]{2,1,0:T(8,128)(2,1)S(1)}, u32[]{:S(2)}, u32[]{:S(2)}) %collective-permute-start.21) | collective-permute-done | bytes 524320 | tf_op jit(solution)/shard_map/ppermute | solution.py:652
  135.5 0.1 collective-permute-done.22
  135.6 1.1 finish.1
  (41 shorter events, 0.1 us)
Async XLA Ops:
  0.7 94.1 %copy-start.10 = (s32[2]{0:T(128)}, s32[2]{0:T(128)S(1)}, u32[]{:S(2)}) copy-start(s32[2]{0:T(128)S(1)} %pad_add_fusion.place_ref) | copy-start | bytes 28
  0.7 13.1 %copy-start.14 = (f32[512]{0:T(512)S(1)}, f32[512]{0:T(512)}, u32[]{:S(2)}) copy-start(f32[512]{0:T(512)} %param.14) | copy-start | bytes 6148
  0.7 13.2 %copy-start.4 = (bf16[4,128,1024]{2,1,0:T(8,128)(2,1)S(1)}, bf16[4,128,1024]{2,1,0:T(8,128)(2,1)}, u32[]{:S(2)}) copy-start(bf16[4,128,1024]{2,1,0:T(8,128)(2,1)} %constant.39.clone.sel_ref.refs_10_) | copy-start | bytes 3145732
  0.7 13.2 %copy-start.13 = (f32[8,256]{1,0:T(8,128)S(1)}, f32[8,256]{1,0:T(8,128)}, u32[]{:S(2)}) copy-start(f32[8,256]{1,0:T(8,128)} %constant.40.clone.bias_ref) | copy-start | bytes 24580
  3.7 10.2 %collective-permute-start = (bf16[16,4096]{1,0:T(8,128)(2,1)S(1)}, bf16[16,4096]{1,0:T(8,128)(2,1)S(1)}, u32[]{:S(2)}, u32[]{:S(2)}) collective-permute-start(bf16[16,4096]{1,0:T(8,128)(2,1)S(1)} %get-tuple-element.55), channel_id=1, source_target_pairs={{0,8},{8,16},{16,24},{1,9},{9,17},{17,25},{2,10},{10,18},{18,26},{... | collective-permute-start | bytes 393224 | tf_op jit(solution)/shard_map/ppermute | solution.py:496
  8.7 28.7 %collective-permute-start.1 = (bf16[512,1024]{1,0:T(8,128)(2,1)S(1)}, bf16[512,1024]{1,0:T(8,128)(2,1)S(1)}, u32[]{:S(2)}, u32[]{:S(2)}) collective-permute-start(bf16[512,1024]{1,0:T(8,128)(2,1)S(1)} %get-tuple-element.59), channel_id=1, source_target_pairs={{0,2},{1,3},{2,0},{3,1},{4,6},{5,7},{6,4},{7,5},{8,10},{9,11},{10,... | collective-permute-start | bytes 3145736 | tf_op jit(solution)/shard_map/ppermute | solution.py:652
  10.2 27.1 %collective-permute-start.2 = (bf16[512,1024]{1,0:T(8,128)(2,1)S(1)}, bf16[512,1024]{1,0:T(8,128)(2,1)S(1)}, u32[]{:S(2)}, u32[]{:S(2)}) collective-permute-start(bf16[512,1024]{1,0:T(8,128)(2,1)S(1)} %get-tuple-element.60), channel_id=1, source_target_pairs={{0,4},{1,5},{2,6},{3,7},{4,0},{5,1},{6,2},{7,3},{8,12},{9,13},{10,... | collective-permute-start | bytes 3145736 | tf_op jit(solution)/shard_map/ppermute | solution.py:652
  11.7 2.1 %copy-start.18 = (s32[4]{0:T(128)S(1)}, s32[4]{0:T(128)}, u32[]{:S(2)}) copy-start(s32[4]{0:T(128)} %param.16) | copy-start | bytes 52
  11.7 2.2 %copy-start.9 = (f32[3,640]{1,0:T(4,128)S(1)}, f32[3,640]{1,0:T(4,128)}, u32[]{:S(2)}) copy-start(f32[3,640]{1,0:T(4,128)} %cw_ref.5) | copy-start | bytes 23044
  11.7 2.8 %copy-start = (bf16[4096,640]{1,0:T(8,128)(2,1)S(1)}, bf16[4096,640]{1,0:T(8,128)(2,1)}, u32[]{:S(2)}) copy-start(bf16[4096,640]{1,0:T(8,128)(2,1)} %w_ref.9) | copy-start | bytes 15728644
  11.7 17.8 %collective-permute-start.3 = (bf16[4,512,640]{2,1,0:T(8,128)(2,1)S(1)}, bf16[4,512,640]{2,1,0:T(8,128)(2,1)S(1)}, u32[]{:S(2)}, u32[]{:S(2)}) collective-permute-start(bf16[4,512,640]{2,1,0:T(8,128)(2,1)S(1)} %get-tuple-element.74), channel_id=1, source_target_pairs={{0,1},{1,0},{2,3},{3,2},{4,5},{5,4},{6,7},{7,6},{8,9},{9,8},{10,11... | collective-permute-start | bytes 7864328 | tf_op jit(solution)/shard_map/ppermute | solution.py:652
  14.6 24.6 %copy-start.1 = (bf16[512,4096]{1,0:T(8,128)(2,1)S(1)}, bf16[512,4096]{1,0:T(8,128)(2,1)}, u32[]{:S(2)}) copy-start(bf16[512,4096]{1,0:T(8,128)(2,1)} %refs_8_.1) | copy-start | bytes 12582916
  29.6 35.7 %copy-start.2 = (bf16[4,1024,256]{2,1,0:T(8,128)(2,1)}, bf16[4,1024,256]{2,1,0:T(8,128)(2,1)S(1)}, u32[]{:S(2)}) copy-start(bf16[4,1024,256]{2,1,0:T(8,128)(2,1)S(1)} %get-tuple-element.63.pk_ref.refs_4_) | copy-start | bytes 6291460
  29.6 18.6 %collective-permute-start.4 = (bf16[4,160,128]{2,1,0:T(8,128)(2,1)S(1)}, bf16[4,160,128]{2,1,0:T(8,128)(2,1)S(1)}, u32[]{:S(2)}, u32[]{:S(2)}) collective-permute-start(bf16[4,160,128]{2,1,0:T(8,128)(2,1)S(1)} %get-tuple-element.75), channel_id=1, source_target_pairs={{0,8},{8,16},{16,24},{1,9},{9,17},{17,25},{2,10},{10,18},{18,26},{... | collective-permute-start | bytes 491528 | tf_op jit(solution)/shard_map/ppermute | solution.py:496
  33.1 15.1 %collective-permute-start.5 = (bf16[4,160,128]{2,1,0:T(8,128)(2,1)S(1)}, bf16[4,160,128]{2,1,0:T(8,128)(2,1)S(1)}, u32[]{:S(2)}, u32[]{:S(2)}) collective-permute-start(bf16[4,160,128]{2,1,0:T(8,128)(2,1)S(1)} %get-tuple-element.75), channel_id=1, source_target_pairs={{0,16},{8,24},{1,17},{9,25},{2,18},{10,26},{3,19},{11,27},{4,20},{... | collective-permute-start | bytes 491528 | tf_op jit(solution)/shard_map/ppermute | solution.py:496
  36.0 12.2 %collective-permute-start.6 = (bf16[4,160,128]{2,1,0:T(8,128)(2,1)S(1)}, bf16[4,160,128]{2,1,0:T(8,128)(2,1)S(1)}, u32[]{:S(2)}, u32[]{:S(2)}) collective-permute-start(bf16[4,160,128]{2,1,0:T(8,128)(2,1)S(1)} %get-tuple-element.75), channel_id=1, source_target_pairs={{0,24},{1,25},{2,26},{3,27},{4,28},{5,29},{6,30},{7,31}} | collective-permute-start | bytes 491528 | tf_op jit(solution)/shard_map/ppermute | solution.py:496
  37.3 10.8 %copy-start.15 = (bf16[512,1024]{1,0:T(8,128)(2,1)}, bf16[512,1024]{1,0:T(8,128)(2,1)S(1)}, u32[]{:S(2)}) copy-start(bf16[512,1024]{1,0:T(8,128)(2,1)S(1)} %collective-permute-done.1.refs_9_) | copy-start | bytes 3145732
  37.4 10.8 %copy-start.16 = (bf16[512,1024]{1,0:T(8,128)(2,1)}, bf16[512,1024]{1,0:T(8,128)(2,1)S(1)}, u32[]{:S(2)}) copy-start(bf16[512,1024]{1,0:T(8,128)(2,1)S(1)} %collective-permute-done.2.refs_10_) | copy-start | bytes 3145732
  37.4 27.1 %collective-permute-start.7 = (bf16[512,1024]{1,0:T(8,128)(2,1)S(1)}, bf16[512,1024]{1,0:T(8,128)(2,1)S(1)}, u32[]{:S(2)}, u32[]{:S(2)}) collective-permute-start(bf16[512,1024]{1,0:T(8,128)(2,1)S(1)} %columns.3), channel_id=1, source_target_pairs={{0,6},{1,7},{2,4},{3,5},{4,2},{5,3},{6,0},{7,1},{8,14},{9,15},{10,... | collective-permute-start | bytes 3145736 | tf_op jit(solution)/shard_map/ppermute | solution.py:652
  39.2 9.0 %copy-start.12 = (bf16[256,256]{1,0:T(8,128)(2,1)S(1)}, bf16[256,256]{1,0:T(8,128)(2,1)}, u32[]{:S(2)}) copy-start(bf16[256,256]{1,0:T(8,128)(2,1)} %constant.41.clone.ones_ref) | copy-start | bytes 393220
  53.4 19.6 %collective-permute-start.10 = (bf16[4,160,128]{2,1,0:T(8,128)(2,1)S(1)}, bf16[4,160,128]{2,1,0:T(8,128)(2,1)S(1)}, u32[]{:S(2)}, u32[]{:S(2)}) collective-permute-start(bf16[4,160,128]{2,1,0:T(8,128)(2,1)S(1)} %get-tuple-element.84), channel_id=1, source_target_pairs={{24,0},{25,1},{26,2},{27,3},{28,4},{29,5},{30,6},{31,7}} | collective-permute-start | bytes 491528 | tf_op jit(solution)/shard_map/ppermute | solution.py:496
  54.7 18.3 %collective-permute-start.8 = (bf16[4,160,128]{2,1,0:T(8,128)(2,1)S(1)}, bf16[4,160,128]{2,1,0:T(8,128)(2,1)S(1)}, u32[]{:S(2)}, u32[]{:S(2)}) collective-permute-start(bf16[4,160,128]{2,1,0:T(8,128)(2,1)S(1)} %get-tuple-element.84), channel_id=1, source_target_pairs={{8,0},{16,8},{24,16},{9,1},{17,9},{25,17},{10,2},{18,10},{26,18},{... | collective-permute-start | bytes 491528 | tf_op jit(solution)/shard_map/ppermute | solution.py:496
  56.0 17.0 %collective-permute-start.9 = (bf16[4,160,128]{2,1,0:T(8,128)(2,1)S(1)}, bf16[4,160,128]{2,1,0:T(8,128)(2,1)S(1)}, u32[]{:S(2)}, u32[]{:S(2)}) collective-permute-start(bf16[4,160,128]{2,1,0:T(8,128)(2,1)S(1)} %get-tuple-element.84), channel_id=1, source_target_pairs={{16,0},{24,8},{17,1},{25,9},{18,2},{26,10},{19,3},{27,11},{20,4},{... | collective-permute-start | bytes 491528 | tf_op jit(solution)/shard_map/ppermute | solution.py:496
  57.3 27.0 %collective-permute-start.14 = (bf16[1024,512]{1,0:T(8,128)(2,1)S(1)}, bf16[1024,512]{1,0:T(8,128)(2,1)S(1)}, u32[]{:S(2)}, u32[]{:S(2)}) collective-permute-start(bf16[1024,512]{1,0:T(8,128)(2,1)S(1)} %get-tuple-element.92.refs_0_.refs_4_), channel_id=1, source_target_pairs={{0,2},{1,3},{2,0},{3,1},{4,6},{5,7},{6,4},{7,5},{8,10},{9,11},{10,... | collective-permute-start | bytes 3145736 | tf_op jit(solution)/shard_map/ppermute | solution.py:652
  64.4 8.6 %copy-start.17 = (bf16[512,1024]{1,0:T(8,128)(2,1)}, bf16[512,1024]{1,0:T(8,128)(2,1)S(1)}, u32[]{:S(2)}) copy-start(bf16[512,1024]{1,0:T(8,128)(2,1)S(1)} %collective-permute-done.7.refs_11_) | copy-start | bytes 3145732
  64.4 22.2 %collective-permute-start.15 = (bf16[1024,512]{1,0:T(8,128)(2,1)S(1)}, bf16[1024,512]{1,0:T(8,128)(2,1)S(1)}, u32[]{:S(2)}, u32[]{:S(2)}) collective-permute-start(bf16[1024,512]{1,0:T(8,128)(2,1)S(1)} %get-tuple-element.92.refs_0_.refs_4_), channel_id=1, source_target_pairs={{0,4},{1,5},{2,6},{3,7},{4,0},{5,1},{6,2},{7,3},{8,12},{9,13},{10,... | collective-permute-start | bytes 3145736 | tf_op jit(solution)/shard_map/ppermute | solution.py:652
  73.0 1.6 %copy-start.3 = (bf16[4,1024,256]{2,1,0:T(8,128)(2,1)S(1)}, bf16[4,1024,256]{2,1,0:T(8,128)(2,1)}, u32[]{:S(2)}) copy-start(bf16[4,1024,256]{2,1,0:T(8,128)(2,1)} %copy-done.2) | copy-start | bytes 6291460
  78.3 5.7 %collective-permute-start.12 = (f32[8,640]{1,0:T(8,128)S(1)}, f32[8,640]{1,0:T(8,128)S(1)}, u32[]{:S(2)}, u32[]{:S(2)}) collective-permute-start(f32[8,640]{1,0:T(8,128)S(1)} %get-tuple-element.90), channel_id=1, source_target_pairs={{8,0},{16,8},{24,16},{9,1},{17,9},{25,17},{10,2},{18,10},{26,18},{... | collective-permute-start | bytes 61448 | tf_op jit(solution)/shard_map/ppermute | solution.py:496
  79.8 8.4 %collective-permute-start.11 = (bf16[512,640]{1,0:T(8,128)(2,1)S(1)}, bf16[512,640]{1,0:T(8,128)(2,1)S(1)}, u32[]{:S(2)}, u32[]{:S(2)}) collective-permute-start(bf16[512,640]{1,0:T(8,128)(2,1)S(1)} %get-tuple-element.85.dp_ref), channel_id=1, source_target_pairs={{0,1},{1,0},{2,3},{3,2},{4,5},{5,4},{6,7},{7,6},{8,9},{9,8},{10,11... | collective-permute-start | bytes 1966088 | tf_op jit(solution)/shard_map/ppermute | solution.py:652
  84.1 10.7 %collective-permute-start.13 = (bf16[512,640]{1,0:T(8,128)(2,1)S(1)}, bf16[512,640]{1,0:T(8,128)(2,1)S(1)}, u32[]{:S(2)}, u32[]{:S(2)}) collective-permute-start(bf16[512,640]{1,0:T(8,128)(2,1)S(1)} %complete.1.dp_ref), channel_id=1, source_target_pairs={{0,1},{1,0},{2,3},{3,2},{4,5},{5,4},{6,7},{7,6},{8,9},{9,8},{10,11... | collective-permute-start | bytes 1966088 | tf_op jit(solution)/shard_map/ppermute | solution.py:652
  86.7 16.0 %collective-permute-start.16 = (bf16[512,512]{1,0:T(8,128)(2,1)S(1)}, bf16[512,512]{1,0:T(8,128)(2,1)S(1)}, u32[]{:S(2)}, u32[]{:S(2)}) collective-permute-start(bf16[512,512]{1,0:T(8,128)(2,1)S(1)} %get-tuple-element.93), channel_id=1, source_target_pairs={{0,4},{1,5},{2,6},{3,7},{4,0},{5,1},{6,2},{7,3},{8,12},{9,13},{10,... | collective-permute-start | bytes 1572872 | tf_op jit(solution)/shard_map/ppermute | solution.py:652
  87.3 15.4 %collective-permute-start.17 = (bf16[512,512]{1,0:T(8,128)(2,1)S(1)}, bf16[512,512]{1,0:T(8,128)(2,1)S(1)}, u32[]{:S(2)}, u32[]{:S(2)}) collective-permute-start(bf16[512,512]{1,0:T(8,128)(2,1)S(1)} %get-tuple-element.94), channel_id=1, source_target_pairs={{0,2},{1,3},{2,0},{3,1},{4,6},{5,7},{6,4},{7,5},{8,10},{9,11},{10,... | collective-permute-start | bytes 1572872 | tf_op jit(solution)/shard_map/ppermute | solution.py:652
  93.6 28.5 %collective-permute-start.18 = (bf16[2,512,512]{2,1,0:T(8,128)(2,1)}, bf16[2,512,512]{2,1,0:T(8,128)(2,1)}, u32[]{:S(2)}, u32[]{:S(2)}) collective-permute-start(bf16[2,512,512]{2,1,0:T(8,128)(2,1)} %get-tuple-element.100), channel_id=1, source_target_pairs={{0,2},{1,3},{2,0},{3,1},{4,6},{5,7},{6,4},{7,5},{8,10},{9,11},{10,... | collective-permute-start | bytes 3145736 | tf_op jit(solution)/shard_map/ppermute | solution.py:652
  100.2 1.0 copy-start.5
  101.2 23.8 %collective-permute-start.19 = (bf16[2,512,512]{2,1,0:T(8,128)(2,1)}, bf16[2,512,512]{2,1,0:T(8,128)(2,1)S(1)}, u32[]{:S(2)}, u32[]{:S(2)}) collective-permute-start(bf16[2,512,512]{2,1,0:T(8,128)(2,1)} %get-tuple-element.102), channel_id=1, source_target_pairs={{0,4},{1,5},{2,6},{3,7},{4,0},{5,1},{6,2},{7,3},{8,12},{9,13},{10,... | collective-permute-start | bytes 3145736 | tf_op jit(solution)/shard_map/ppermute | solution.py:652
  102.7 0.6 copy-start.11
  111.9 1.3 copy-start.7
  113.3 14.3 %collective-permute-start.20 = (bf16[1024,512]{1,0:T(8,128)(2,1)}, bf16[1024,512]{1,0:T(8,128)(2,1)S(1)}, u32[]{:S(2)}, u32[]{:S(2)}) collective-permute-start(bf16[1024,512]{1,0:T(8,128)(2,1)} %get-tuple-element.104), channel_id=1, source_target_pairs={{0,1},{1,0},{2,3},{3,2},{4,5},{5,4},{6,7},{7,6},{8,9},{9,8},{10,11... | collective-permute-start | bytes 3145736 | tf_op jit(solution)/shard_map/ppermute | solution.py:652
  114.8 10.2 %copy-start.6 = (bf16[2,512,512]{2,1,0:T(8,128)(2,1)S(1)}, bf16[2,512,512]{2,1,0:T(8,128)(2,1)}, u32[]{:S(2)}) copy-start(bf16[2,512,512]{2,1,0:T(8,128)(2,1)} %copy-done.5) | copy-start | bytes 3145732
  123.4 12.1 %collective-permute-start.21 = (bf16[1,512,512]{2,1,0:T(8,128)(2,1)S(1)}, bf16[1,512,512]{2,1,0:T(8,128)(2,1)S(1)}, u32[]{:S(2)}, u32[]{:S(2)}) collective-permute-start(bf16[1,512,512]{2,1,0:T(8,128)(2,1)S(1)} %passing.2), channel_id=1, source_target_pairs={{0,4},{1,5},{2,6},{3,7},{4,0},{5,1},{6,2},{7,3},{8,12},{9,13},{10,... | collective-permute-start | bytes 1572872 | tf_op jit(solution)/shard_map/ppermute | solution.py:652
  125.1 2.5 %copy-start.8 = (f32[1024,512]{1,0:T(8,128)S(1)}, f32[1024,512]{1,0:T(8,128)}, u32[]{:S(2)}) copy-start(f32[1024,512]{1,0:T(8,128)} %copy-done.7) | copy-start | bytes 6291460
  125.1 10.5 %collective-permute-start.22 = (bf16[1,512,512]{2,1,0:T(8,128)(2,1)S(1)}, bf16[1,512,512]{2,1,0:T(8,128)(2,1)S(1)}, u32[]{:S(2)}, u32[]{:S(2)}) collective-permute-start(bf16[1,512,512]{2,1,0:T(8,128)(2,1)S(1)} %passing.3), channel_id=1, source_target_pairs={{0,2},{1,3},{2,0},{3,1},{4,6},{5,7},{6,4},{7,5},{8,10},{9,11},{10,... | collective-permute-start | bytes 1572872 | tf_op jit(solution)/shard_map/ppermute | solution.py:652

commit v3 on v2

--- a/solution.py
+++ b/solution.py
@@ -17,7 +17,7 @@
 EPS = 1e-06
 BF = jnp.bfloat16
 F32 = jnp.float32
-VMEM = 16 * 1024 * 1024
+MIB = 1024 * 1024
 
 
 def mm(a, b):
@@ -87,8 +87,8 @@
     return r >= c
 
 
-def params():
-    return pltpu.CompilerParams(dimension_semantics=("arbitrary",), vmem_limit_bytes=VMEM)
+def params(mib):
+    return pltpu.CompilerParams(dimension_semantics=("arbitrary",), vmem_limit_bytes=mib * MIB)
 
 
 def whole(shape):
@@ -192,7 +192,7 @@
             jax.ShapeDtypeStruct((heads, ES, DV), BF),
         ],
         scratch_shapes=[pltpu.VMEM((CH + 8, width), F32), pltpu.VMEM((heads, DV, EP), F32)],
-        compiler_params=params(),
+        compiler_params=params(12),
         cost_estimate=cost(100 << 30),
         name="project",
     )(stay(x), halo, keep(w_in), conv_w, keep(sel), bias)
@@ -225,7 +225,7 @@
         in_specs=[pl.BlockSpec((CH, d), lambda c: (c, 0)), KEPT, whole((1, wide))] + [KEPT] * 7,
         out_specs=[KEPT] * 4,
         out_shape=[kept((rows, wide), F32)] * 2 + [kept((heads, rows, CH), BF)] * 2,
-        compiler_params=params(),
+        compiler_params=params(12),
         cost_estimate=LIGHT,
         name="local_part",
     )(stay(ct), keep(w_out), gain, *map(keep, (v, pq, pk, loc, fq, fk, sel)))
@@ -287,7 +287,7 @@
             jax.ShapeDtypeStruct((heads, ES, DV), BF),
         ],
         scratch_shapes=[pltpu.VMEM((heads, DV, EP), F32)],
-        compiler_params=params(),
+        compiler_params=params(8),
         cost_estimate=cost(16 << 30),
         name="norm_part",
     )(keep(g), keep(num), gain, keep(pq), ones, *got, *map(keep, later))
@@ -338,7 +338,7 @@
             kept((heads, rows, 128), F32),
         ],
         scratch_shapes=[pltpu.VMEM((heads, DV, EP), F32)],
-        compiler_params=params(),
+        compiler_params=params(8),
         cost_estimate=LIGHT,
         name="inner_part",
     )(*map(keep, (v, pq, pk, fq, wt, slope, dn, loc, pre, sel, fk, gloc)))
@@ -428,7 +428,7 @@
             kept((16, width), F32),
         ],
         scratch_shapes=[pltpu.VMEM((CH + 8, width), F32), pltpu.VMEM((heads, DV, EP), F32)],
-        compiler_params=params(),
+        compiler_params=params(8),
         cost_estimate=cost(16 << 30),
         name="outer_part",
     )(*map(keep, (v, pk, fk, dqk, dv, xk, loc, sel)), conv_w, *got)
@@ -484,7 +484,7 @@
             scratch_shapes=[pltpu.SemaphoreType.DMA((len(which) + 1 + count,))],
         ),
         out_shape=out_shape,
-        compiler_params=pltpu.CompilerParams(vmem_limit_bytes=VMEM),
+        compiler_params=pltpu.CompilerParams(vmem_limit_bytes=4 * MIB),
         cost_estimate=LIGHT,
         name="columns",
     )(place, *args)
@@ -554,7 +554,7 @@
             out_specs=[row, row],
         ),
         out_shape=[jax.ShapeDtypeStruct((rows, sw), BF), jax.ShapeDtypeStruct((rows, sw), F32)],
-        compiler_params=params(),
+        compiler_params=params(16),
         cost_estimate=cost(16 << 30),
         name="out_part",
     )(place, *operands, *map(stay, ws))
@@ -578,7 +578,7 @@
         in_specs=[KEPT] * 4,
         out_specs=KEPT,
         out_shape=kept((rows // 2, width), BF),
-        compiler_params=pltpu.CompilerParams(vmem_limit_bytes=VMEM),
+        compiler_params=pltpu.CompilerParams(vmem_limit_bytes=4 * MIB),
         cost_estimate=LIGHT,
         name="complete",
     )(keep(dp), keep(last), after, conv_w)
@@ -622,7 +622,7 @@
             scratch_shapes=[pltpu.VMEM((half, 2 * width), BF)],
         ),
         out_shape=[kept((count // 2, half, sw), BF)] * 2,
-        compiler_params=params(),
+        compiler_params=params(8),
         cost_estimate=LIGHT,
         name="grad_part",
     )(place, *map(keep, (dp, other, w_in, w_other)))
@@ -641,7 +641,7 @@
         in_specs=[KEPT] * 2,
         out_specs=[KEPT] * 2,
         out_shape=[kept((rows // 2, wide), BF)] * 2,
-        compiler_params=pltpu.CompilerParams(vmem_limit_bytes=VMEM),
+        compiler_params=pltpu.CompilerParams(vmem_limit_bytes=4 * MIB),
         cost_estimate=LIGHT,
         name="halves",
     )(keep(x_got), keep(y_got))
@@ -668,7 +668,7 @@
         in_specs=[KEPT] * 2,
         out_specs=KEPT,
         out_shape=kept((left // 2, half, sw), BF),
-        compiler_params=pltpu.CompilerParams(vmem_limit_bytes=VMEM),
+        compiler_params=pltpu.CompilerParams(vmem_limit_bytes=4 * MIB),
         cost_estimate=LIGHT,
         name="passing",
     )(keep(kept_sum), keep(got))
@@ -704,7 +704,7 @@
     return pl.pallas_call(
         functools.partial(finish_kernel, half),
         out_shape=jax.ShapeDtypeStruct((2 * half, sw), BF),
-        compiler_params=pltpu.CompilerParams(vmem_limit_bytes=VMEM),
+        compiler_params=pltpu.CompilerParams(vmem_limit_bytes=4 * MIB),
         cost_estimate=LIGHT,
         name="finish",
     )(a_keep, a_got, b_keep, b_got)

time: 137 us -> 136 us (level)
  local copies, waits for them, and re-layouts: 5.24 us -> 1.97 us
  waiting for transfers between devices: 26.5 us -> 28.3 us
    unnamed x38 -> x30, local copies, waits for them, and re-layouts: 5.24 us -> 1.97 us
    ppermute x15, waiting for transfers between devices: 22.3 us -> 24.1 us  [swapped(): return lax.ppermute(array, 'tp', [(i, i ^ distance) for i in range(count)])]
  transfers between devices with their start and end apart: 23 -> 23, of which waited for: 8 -> 9; matrix products, arithmetic and copies ran while one was open for 4% -> 4% of each run, Pallas kernels for 47% -> 47%
where the time goes in v3:
time: 136 us
  Pallas kernels  67.8 us (50%)
  starting transfers between devices  30.3 us (22%)
  waiting for transfers between devices  28.3 us (21%)
  other arithmetic  6.08 us (4%)
  local copies, waits for them, and re-layouts  1.97 us (1%)
    ppermute x15, waiting for transfers between devices, swapped(): return lax.ppermute(array, 'tp', [(i, i ^ distance) for i in range(count)])  24.1 us
    ppermute x8, starting transfers between devices, shifted(): return lax.ppermute(array, 'seq', pairs)  18 us
    pallas_call x1, Pallas kernels, project(): pl.pallas_call(functools.partial(project_kernel, heads), grid=(n,), in_sp...  14.6 us
    ppermute x15, starting transfers between devices, swapped(): return lax.ppermute(array, 'tp', [(i, i ^ distance) for i in range(count)])  12.3 us
    pallas_call x2, Pallas kernels, grad_part(): pl.pallas_call(functools.partial(grad_kernel, count, low_first), grid_spe...  10.8 us
    pallas_call x1, Pallas kernels, local_part(): pl.pallas_call(functools.partial(local_kernel, heads), grid=(n,), in_spec...  9.01 us
    pallas_call x1, Pallas kernels, out_part(): pl.pallas_call(functools.partial(out_kernel, count, sw), grid_spec=pltpu....  8.81 us
    pallas_call x1, Pallas kernels, inner_part(): pl.pallas_call(functools.partial(inner_kernel, heads), grid=(n,), in_spec...  7.75 us
  transfers between devices with their start and end apart: 23, of which 9 were waited for; matrix products, arithmetic and copies ran while one was open for 4% of the time, Pallas kernels for 47%

profile of v3, /device:TPU:0, one launch (start us, length us, event | category | flops | bytes accessed | tf_op | source)
XLA Modules:
  0.0 135.5 jit_solution(15707005578337946723)
XLA Ops:
  0.6 0.1 pad_add_fusion.place_ref
  0.7 3.0 %columns.2 = (bf16[16,4096]{1,0:T(8,128)(2,1)S(1)}, bf16[4,512,640]{2,1,0:T(8,128)(2,1)S(1)}, bf16[512,1024]{1,0:T(8,128)(2,1)S(1)}, bf16[512,1024]{1,0:T(8,128)(2,1)S(1)}) custom-call(s32[2]{0:T(128)S(1)} %pad_add_fusion.place_ref, bf16[512,4096]{1,0:T(8,128)(2,1)} %refs_8_.1, bf16[1024,4096]{1,0:T(8,128)(2,1)} %x_ref.1, bf16[4096,640]{1,0:T(8,128)(2,1)} %w_ref.9), custom_call_target="tpu_custom_call" | custom-call | flops 1000 | bytes 1048576 | tf_op jit(solution)/shard_map/columns/pallas_call | solution.py:477
  3.7 4.9 %collective-permute-start = (bf16[16,4096]{1,0:T(8,128)(2,1)S(1)}, bf16[16,4096]{1,0:T(8,128)(2,1)S(1)}, u32[]{:S(2)}, u32[]{:S(2)}) collective-permute-start(bf16[16,4096]{1,0:T(8,128)(2,1)S(1)} %get-tuple-element.55), channel_id=1, source_target_pairs={{0,8},{8,16},{16,24},{1,9},{9,17},{17,25},{2,10},{10,18},{18,26},{... | collective-permute-start | bytes 393224 | tf_op jit(solution)/shard_map/ppermute | solution.py:496
  8.7 1.6 %collective-permute-start.1 = (bf16[512,1024]{1,0:T(8,128)(2,1)S(1)}, bf16[512,1024]{1,0:T(8,128)(2,1)S(1)}, u32[]{:S(2)}, u32[]{:S(2)}) collective-permute-start(bf16[512,1024]{1,0:T(8,128)(2,1)S(1)} %get-tuple-element.59), channel_id=1, source_target_pairs={{0,2},{1,3},{2,0},{3,1},{4,6},{5,7},{6,4},{7,5},{8,10},{9,11},{10,... | collective-permute-start | bytes 3145736 | tf_op jit(solution)/shard_map/ppermute | solution.py:652
  10.2 1.5 %collective-permute-start.2 = (bf16[512,1024]{1,0:T(8,128)(2,1)S(1)}, bf16[512,1024]{1,0:T(8,128)(2,1)S(1)}, u32[]{:S(2)}, u32[]{:S(2)}) collective-permute-start(bf16[512,1024]{1,0:T(8,128)(2,1)S(1)} %get-tuple-element.60), channel_id=1, source_target_pairs={{0,4},{1,5},{2,6},{3,7},{4,0},{5,1},{6,2},{7,3},{8,12},{9,13},{10,... | collective-permute-start | bytes 3145736 | tf_op jit(solution)/shard_map/ppermute | solution.py:652
  11.7 0.0 collective-permute-start.3
  11.8 2.1 %columns.3 = bf16[512,1024]{1,0:T(8,128)(2,1)S(1)} custom-call(s32[2]{0:T(128)S(1)} %pad_add_fusion.place_ref, bf16[512,4096]{1,0:T(8,128)(2,1)} %refs_8_.1), custom_call_target="tpu_custom_call" | custom-call | flops 1000 | bytes 1048576 | tf_op jit(solution)/shard_map/columns/pallas_call | solution.py:477
  13.9 0.1 bitcast_multiply_fusion
  14.0 0.0 collective-permute-done.halo_ref
  14.0 0.6 copy-done
  14.6 14.6 %project.1 = (bf16[1024,512]{1,0:T(8,128)(2,1)S(1)}, bf16[4,1024,256]{2,1,0:T(8,128)(2,1)S(1)}, bf16[4,1024,256]{2,1,0:T(8,128)(2,1)S(1)}, bf16[4,1024,512]{2,1,...) custom-call(bf16[1024,4096]{1,0:T(8,128)(2,1)} %x_ref.1, ...), custom_call_target="tpu_custom_call" | custom-call | flops 107374182400 | bytes 1048576 | tf_op jit(solution)/shard_map/project/pallas_call | solution.py:173
  29.2 0.0 collective-permute-done.3.w_other_ref
  29.2 3.5 %collective-permute-start.4 = (bf16[4,160,128]{2,1,0:T(8,128)(2,1)S(1)}, bf16[4,160,128]{2,1,0:T(8,128)(2,1)S(1)}, u32[]{:S(2)}, u32[]{:S(2)}) collective-permute-start(bf16[4,160,128]{2,1,0:T(8,128)(2,1)S(1)} %get-tuple-element.75), channel_id=1, source_target_pairs={{0,8},{8,16},{16,24},{1,9},{9,17},{17,25},{2,10},{10,18},{18,26},{... | collective-permute-start | bytes 491528 | tf_op jit(solution)/shard_map/ppermute | solution.py:496
  32.7 2.9 %collective-permute-start.5 = (bf16[4,160,128]{2,1,0:T(8,128)(2,1)S(1)}, bf16[4,160,128]{2,1,0:T(8,128)(2,1)S(1)}, u32[]{:S(2)}, u32[]{:S(2)}) collective-permute-start(bf16[4,160,128]{2,1,0:T(8,128)(2,1)S(1)} %get-tuple-element.75), channel_id=1, source_target_pairs={{0,16},{8,24},{1,17},{9,25},{2,18},{10,26},{3,19},{11,27},{4,20},{... | collective-permute-start | bytes 491528 | tf_op jit(solution)/shard_map/ppermute | solution.py:496
  35.7 1.3 collective-permute-start.6
  37.0 0.0 collective-permute-done.1.refs_9_
  37.0 0.0 copy-start.11
  37.0 0.0 collective-permute-done.2.refs_10_
  37.0 0.0 copy-start.12
  37.0 1.8 %collective-permute-start.7 = (bf16[512,1024]{1,0:T(8,128)(2,1)S(1)}, bf16[512,1024]{1,0:T(8,128)(2,1)S(1)}, u32[]{:S(2)}, u32[]{:S(2)}) collective-permute-start(bf16[512,1024]{1,0:T(8,128)(2,1)S(1)} %columns.3), channel_id=1, source_target_pairs={{0,6},{1,7},{2,4},{3,5},{4,2},{5,3},{6,0},{7,1},{8,14},{9,15},{10,... | collective-permute-start | bytes 3145736 | tf_op jit(solution)/shard_map/ppermute | solution.py:652
  38.9 9.0 %local_part.1 = (f32[1024,512]{1,0:T(8,128)S(1)}, f32[1024,512]{1,0:T(8,128)S(1)}, bf16[4,1024,256]{2,1,0:T(8,128)(2,1)S(1)}, bf16[4,1024,256]{2,1,0:T(8,128)(2,1)S(1)}) custom-call(bf16[1024,4096]{1,0:T(8,128)(2,1)} %ct_ref.1, bf16[512,4096]{1,0:T(8,128)(2,1)S(1)} %copy-done.1, f32[1,512]{1,0:T(1,128)S(1)} %bitcast.21, ...), custom_call_target="tpu_custom_call" | custom-call | flops 1000 | bytes 1048576 | tf_op jit(solution)/shard_map/local_part/pallas_call | solution.py:222
  47.9 0.0 collective-permute-done.5.refs_1_
  47.9 5.2 %norm_part.1 = (bf16[1024,512]{1,0:T(8,128)(2,1)S(1)}, bf16[1024,512]{1,0:T(8,128)(2,1)S(1)}, bf16[4,4,128,256]{3,2,1,0:T(8,128)(2,1)S(1)}, bf16[4,160,128]{2,1,0:T(8,128)(2,1)S(1)}, bf16[4,160,128]{2,1,0:T(8,128)(2,1)S(1)}) custom-call(f32[1024,512]{1,0:T(8,128)S(1)} %get-tuple-element.71.g_ref, f32[1024,512]{1,0:T(8,128)S(1)} %get-tuple-element.72.num_ref, ...), custom_call_target="tpu_custom_call" | custom-call | flops 17179869184 | bytes 1048576 | tf_op jit(solution)/shard_map/norm_part/pallas_call | solution.py:275
  53.1 1.3 collective-permute-start.10
  54.4 1.3 collective-permute-start.8
  55.7 1.3 collective-permute-start.9
  57.0 0.6 collective-permute-start.14
  57.6 6.4 %collective-permute-done.7.refs_11_ = bf16[512,1024]{1,0:T(8,128)(2,1)S(1)} collective-permute-done((bf16[512,1024]{1,0:T(8,128)(2,1)S(1)}, bf16[512,1024]{1,0:T(8,128)(2,1)S(1)}, u32[]{:S(2)}, u32[]{:S(2)}) %collective-permute-start.7) | collective-permute-done | bytes 1048608 | tf_op jit(solution)/shard_map/ppermute | solution.py:652
  64.1 0.9 collective-permute-start.15
  64.9 7.8 %inner_part.1 = (f32[1024,128]{1,0:T(8,128)S(1)}, f32[1024,512]{1,0:T(8,128)S(1)}, f32[4,1024,128]{2,1,0:T(8,128)S(1)}) custom-call(bf16[1024,512]{1,0:T(8,128)(2,1)S(1)} %get-tuple-element.62.v_ref.refs_3_, bf16[4,1024,256]{2,1,0:T(8,128)(2,1)S(1)} %get-tuple-element.65.pq_ref, bf16[4,1024,256]{2,1,0:T(8,128)(2,1)S(1)} %get-tuple-element.63.pk_ref.refs_4_, ...), custom_call_target="tpu_custom_call" | custom-call | flops 1000 | bytes 1048576 | tf_op jit(solution)/shard_map/inner_part/pallas_call | solution.py:330
  72.7 0.0 collective-permute-done.9.refs_1_
  72.7 3.9 %outer_part.1 = (bf16[512,640]{1,0:T(8,128)(2,1)S(1)}, bf16[1024,640]{1,0:T(8,128)(2,1)S(1)}, f32[8,640]{1,0:T(8,128)S(1)}, f32[16,640]{1,0:T(8,128)S(1)}) custom-call(bf16[1024,512]{1,0:T(8,128)(2,1)S(1)} %get-tuple-element.62.v_ref.refs_3_, bf16[4,1024,256]{2,1,0:T(8,128)(2,1)S(1)} %get-tuple-element.63.pk_ref.refs_4_, ...), custom_call_target="tpu_custom_call" | custom-call | flops 17179869184 | bytes 1048576 | tf_op jit(solution)/shard_map/outer_part/pallas_call | solution.py:419
  76.6 1.5 %collective-permute-start.12 = (f32[8,640]{1,0:T(8,128)S(1)}, f32[8,640]{1,0:T(8,128)S(1)}, u32[]{:S(2)}, u32[]{:S(2)}) collective-permute-start(f32[8,640]{1,0:T(8,128)S(1)} %get-tuple-element.90), channel_id=1, source_target_pairs={{8,0},{16,8},{24,16},{9,1},{17,9},{25,17},{10,2},{18,10},{26,18},{... | collective-permute-start | bytes 61448 | tf_op jit(solution)/shard_map/ppermute | solution.py:496
  78.1 0.1 collective-permute-start.11
  78.2 4.1 %collective-permute-done.12.after_ref = f32[8,640]{1,0:T(8,128)S(1)} collective-permute-done((f32[8,640]{1,0:T(8,128)S(1)}, f32[8,640]{1,0:T(8,128)S(1)}, u32[]{:S(2)}, u32[]{:S(2)}) %collective-permute-start.12) | collective-permute-done | bytes 20512 | tf_op jit(solution)/shard_map/ppermute | solution.py:496
  82.3 0.1 complete.1.dp_ref
  82.4 0.1 collective-permute-start.13
  82.5 1.5 %collective-permute-done.14.x_ref.refs_1_.refs_5_ = bf16[1024,512]{1,0:T(8,128)(2,1)S(1)} collective-permute-done((bf16[1024,512]{1,0:T(8,128)(2,1)S(1)}, bf16[1024,512]{1,0:T(8,128)(2,1)S(1)}, u32[]{:S(2)}, u32[]{:S(2)}) %collective-permute-start.14) | collective-permute-done | bytes 1048608 | tf_op jit(solution)/shard_map/ppermute | solution.py:652
  84.0 2.8 %collective-permute-done.15.y_ref.refs_2_.refs_6_ = bf16[1024,512]{1,0:T(8,128)(2,1)S(1)} collective-permute-done((bf16[1024,512]{1,0:T(8,128)(2,1)S(1)}, bf16[1024,512]{1,0:T(8,128)(2,1)S(1)}, u32[]{:S(2)}, u32[]{:S(2)}) %collective-permute-start.15) | collective-permute-done | bytes 1048608 | tf_op jit(solution)/shard_map/ppermute | solution.py:652
  86.8 0.1 halves.1
  86.8 0.1 collective-permute-start.16
  87.0 0.9 collective-permute-start.17
  87.9 0.0 collective-permute-done.11.other_ref
  87.9 5.4 %grad_part.2 = (bf16[2,512,512]{2,1,0:T(8,128)(2,1)}, bf16[2,512,512]{2,1,0:T(8,128)(2,1)S(1)}) custom-call(s32[2]{0:T(128)S(1)} %copy-done.7, bf16[512,640]{1,0:T(8,128)(2,1)S(1)} %get-tuple-element.85.dp_ref, bf16[512,640]{1,0:T(8,128)(2,1)S(1)} %collective-permute-done.11.other_ref, bf16[4096,640]{1,0:T(8,128)(2,1)S(1)} %copy-done, ...), custom_call_target="tpu_custom_call" | custom-call | flops 1000 | bytes 1048576 | tf_op jit(solution)/shard_map/grad_part/pallas_call | solution.py:615
  93.2 1.1 collective-permute-start.18
  94.4 0.0 collective-permute-done.13.other_ref
  94.4 5.4 %grad_part.3 = (bf16[2,512,512]{2,1,0:T(8,128)(2,1)}, bf16[2,512,512]{2,1,0:T(8,128)(2,1)S(1)}) custom-call(s32[2]{0:T(128)S(1)} %copy-done.7, bf16[512,640]{1,0:T(8,128)(2,1)S(1)} %complete.1.dp_ref, bf16[512,640]{1,0:T(8,128)(2,1)S(1)} %collective-permute-done.13.other_ref, bf16[4096,640]{1,0:T(8,128)(2,1)S(1)} %copy-done, ...), custom_call_target="tpu_custom_call" | custom-call | flops 1000 | bytes 1048576 | tf_op jit(solution)/shard_map/grad_part/pallas_call | solution.py:615
  99.8 1.9 %collective-permute-start.19 = (bf16[2,512,512]{2,1,0:T(8,128)(2,1)}, bf16[2,512,512]{2,1,0:T(8,128)(2,1)}, u32[]{:S(2)}, u32[]{:S(2)}) collective-permute-start(bf16[2,512,512]{2,1,0:T(8,128)(2,1)} %get-tuple-element.102), channel_id=1, source_target_pairs={{0,4},{1,5},{2,6},{3,7},{4,0},{5,1},{6,2},{7,3},{8,12},{9,13},{10,... | collective-permute-start | bytes 3145736 | tf_op jit(solution)/shard_map/ppermute | solution.py:652
  101.7 0.0 collective-permute-done.16.refs_3_
  101.7 0.1 collective-permute-done.17.refs_7_
  101.8 8.8 %out_part.1 = (bf16[1024,512]{1,0:T(8,128)(2,1)}, f32[1024,512]{1,0:T(8,128)S(1)}) custom-call(s32[2]{0:T(128)S(1)} %copy-done.7, bf16[1024,512]{1,0:T(8,128)(2,1)S(1)} %get-tuple-element.92.refs_0_.refs_4_, bf16[1024,512]{1,0:T(8,128)(2,1)S(1)} %collective-permute-done.14.x_ref.refs_1_.refs_5_, ...), custom_call_target="tpu_custom_call" | custom-call | flops 17179869184 | bytes 1048576 | tf_op jit(solution)/shard_map/out_part/pallas_call | solution.py:546
  110.6 1.3 copy-done.3
  112.0 1.5 %dynamic-slice_convert_fusion = f32[1024,512]{1,0:T(8,128)S(1)} fusion(bf16[1024,4096]{1,0:T(8,128)(2,1)} %ct_ref.1, s32[]{:T(128)S(6)} %select_n.17), kind=kLoop, calls=%fused_computation.5 | loop fusion | flops 524288 | bytes 3145732 | tf_op jit(solution)/shard_map/convert_element_type | solution.py:758
  113.5 6.8 %collective-permute-done.18.got_ref = bf16[2,512,512]{2,1,0:T(8,128)(2,1)S(1)} collective-permute-done((bf16[2,512,512]{2,1,0:T(8,128)(2,1)}, bf16[2,512,512]{2,1,0:T(8,128)(2,1)S(1)}, u32[]{:S(2)}, u32[]{:S(2)}) %collective-permute-start.18) | collective-permute-done | bytes 1048608 | tf_op jit(solution)/shard_map/ppermute | solution.py:652
  120.3 0.1 passing.2
  120.4 0.9 collective-permute-start.21
  121.3 2.4 %collective-permute-done.19.got_ref = bf16[2,512,512]{2,1,0:T(8,128)(2,1)} collective-permute-done((bf16[2,512,512]{2,1,0:T(8,128)(2,1)}, bf16[2,512,512]{2,1,0:T(8,128)(2,1)}, u32[]{:S(2)}, u32[]{:S(2)}) %collective-permute-start.19) | collective-permute-done | bytes 1048608 | tf_op jit(solution)/shard_map/ppermute | solution.py:652
  123.8 1.3 passing.3
  125.1 0.8 collective-permute-start.22
  125.9 1.5 %fusion = (f32[1,512,512]{2,1,0:T(8,128)S(1)}, f32[1,512,512]{2,1,0:T(8,128)S(1)}) fusion(f32[1024,512]{1,0:T(8,128)S(1)} %dynamic-slice_convert_fusion, bf16[2,512,512]{2,1,0:T(8,128)(2,1)} %collective-permute-done.19.got_ref, bf16[2,512,512]{2,1,0:T(8,128)(2,1)S(1)} %get-tuple-element.101.keep_ref, ...), kind=kLoop, calls=%fused_computation.2 | loop fusion | flops 2097152 | bytes 6291456 | tf_op jit(solution)/shard_map/add | solution.py:693
  127.4 3.0 %add_convert_fusion = bf16[1024,512]{1,0:T(8,128)(2,1)} fusion(bf16[1024,512]{1,0:T(8,128)(2,1)} %collective-permute-done.20, f32[1024,512]{1,0:T(8,128)S(1)} %copy-done.4, bf16[1024,4096]{1,0:T(8,128)(2,1)} %x_ref.1, s32[]{:T(128)S(6)} %select_n.17), kind=kLoop, calls=%fused_computation | loop fusion | flops 2621440 | bytes 5242884 | tf_op jit(solution)/shard_map/convert_element_type | solution.py:769
  130.4 2.4 %collective-permute-done.21 = bf16[1,512,512]{2,1,0:T(8,128)(2,1)S(1)} collective-permute-done((bf16[1,512,512]{2,1,0:T(8,128)(2,1)S(1)}, bf16[1,512,512]{2,1,0:T(8,128)(2,1)S(1)}, u32[]{:S(2)}, u32[]{:S(2)}) %collective-permute-start.21) | collective-permute-done | bytes 524320 | tf_op jit(solution)/shard_map/ppermute | solution.py:652
  132.7 1.6 %collective-permute-done.22 = bf16[1,512,512]{2,1,0:T(8,128)(2,1)S(1)} collective-permute-done((bf16[1,512,512]{2,1,0:T(8,128)(2,1)S(1)}, bf16[1,512,512]{2,1,0:T(8,128)(2,1)S(1)}, u32[]{:S(2)}, u32[]{:S(2)}) %collective-permute-start.22) | collective-permute-done | bytes 524320 | tf_op jit(solution)/shard_map/ppermute | solution.py:652
  134.4 1.1 finish.1
  (33 shorter events, 0.1 us)
Async XLA Ops:
  0.7 11.0 %copy-start.6 = (s32[2]{0:T(128)}, s32[2]{0:T(128)S(1)}, u32[]{:S(2)}) copy-start(s32[2]{0:T(128)S(1)} %pad_add_fusion.place_ref) | copy-start | bytes 28
  0.7 13.2 %copy-start.10 = (f32[512]{0:T(512)S(1)}, f32[512]{0:T(512)}, u32[]{:S(2)}) copy-start(f32[512]{0:T(512)} %param.14) | copy-start | bytes 6148
  0.7 13.2 %copy-start.2 = (bf16[4,128,1024]{2,1,0:T(8,128)(2,1)S(1)}, bf16[4,128,1024]{2,1,0:T(8,128)(2,1)}, u32[]{:S(2)}) copy-start(bf16[4,128,1024]{2,1,0:T(8,128)(2,1)} %constant.39.clone.sel_ref.refs_10_) | copy-start | bytes 3145732
  0.7 13.2 %copy-start.9 = (f32[8,256]{1,0:T(8,128)S(1)}, f32[8,256]{1,0:T(8,128)}, u32[]{:S(2)}) copy-start(f32[8,256]{1,0:T(8,128)} %constant.40.clone.bias_ref) | copy-start | bytes 24580
  3.7 10.3 %collective-permute-start = (bf16[16,4096]{1,0:T(8,128)(2,1)S(1)}, bf16[16,4096]{1,0:T(8,128)(2,1)S(1)}, u32[]{:S(2)}, u32[]{:S(2)}) collective-permute-start(bf16[16,4096]{1,0:T(8,128)(2,1)S(1)} %get-tuple-element.55), channel_id=1, source_target_pairs={{0,8},{8,16},{16,24},{1,9},{9,17},{17,25},{2,10},{10,18},{18,26},{... | collective-permute-start | bytes 393224 | tf_op jit(solution)/shard_map/ppermute | solution.py:496
  8.7 28.3 %collective-permute-start.1 = (bf16[512,1024]{1,0:T(8,128)(2,1)S(1)}, bf16[512,1024]{1,0:T(8,128)(2,1)S(1)}, u32[]{:S(2)}, u32[]{:S(2)}) collective-permute-start(bf16[512,1024]{1,0:T(8,128)(2,1)S(1)} %get-tuple-element.59), channel_id=1, source_target_pairs={{0,2},{1,3},{2,0},{3,1},{4,6},{5,7},{6,4},{7,5},{8,10},{9,11},{10,... | collective-permute-start | bytes 3145736 | tf_op jit(solution)/shard_map/ppermute | solution.py:652
  10.2 26.8 %collective-permute-start.2 = (bf16[512,1024]{1,0:T(8,128)(2,1)S(1)}, bf16[512,1024]{1,0:T(8,128)(2,1)S(1)}, u32[]{:S(2)}, u32[]{:S(2)}) collective-permute-start(bf16[512,1024]{1,0:T(8,128)(2,1)S(1)} %get-tuple-element.60), channel_id=1, source_target_pairs={{0,4},{1,5},{2,6},{3,7},{4,0},{5,1},{6,2},{7,3},{8,12},{9,13},{10,... | collective-permute-start | bytes 3145736 | tf_op jit(solution)/shard_map/ppermute | solution.py:652
  11.7 2.1 %copy-start.14 = (s32[4]{0:T(128)S(1)}, s32[4]{0:T(128)}, u32[]{:S(2)}) copy-start(s32[4]{0:T(128)} %param.16) | copy-start | bytes 52
  11.7 2.3 %copy-start.5 = (f32[3,640]{1,0:T(4,128)S(1)}, f32[3,640]{1,0:T(4,128)}, u32[]{:S(2)}) copy-start(f32[3,640]{1,0:T(4,128)} %cw_ref.5) | copy-start | bytes 23044
  11.7 2.8 %copy-start = (bf16[4096,640]{1,0:T(8,128)(2,1)S(1)}, bf16[4096,640]{1,0:T(8,128)(2,1)}, u32[]{:S(2)}) copy-start(bf16[4096,640]{1,0:T(8,128)(2,1)} %w_ref.9) | copy-start | bytes 15728644
  11.7 17.5 %collective-permute-start.3 = (bf16[4,512,640]{2,1,0:T(8,128)(2,1)S(1)}, bf16[4,512,640]{2,1,0:T(8,128)(2,1)S(1)}, u32[]{:S(2)}, u32[]{:S(2)}) collective-permute-start(bf16[4,512,640]{2,1,0:T(8,128)(2,1)S(1)} %get-tuple-element.74), channel_id=1, source_target_pairs={{0,1},{1,0},{2,3},{3,2},{4,5},{5,4},{6,7},{7,6},{8,9},{9,8},{10,11... | collective-permute-start | bytes 7864328 | tf_op jit(solution)/shard_map/ppermute | solution.py:652
  14.6 24.3 %copy-start.1 = (bf16[512,4096]{1,0:T(8,128)(2,1)S(1)}, bf16[512,4096]{1,0:T(8,128)(2,1)}, u32[]{:S(2)}) copy-start(bf16[512,4096]{1,0:T(8,128)(2,1)} %refs_8_.1) | copy-start | bytes 12582916
  29.2 18.7 %collective-permute-start.4 = (bf16[4,160,128]{2,1,0:T(8,128)(2,1)S(1)}, bf16[4,160,128]{2,1,0:T(8,128)(2,1)S(1)}, u32[]{:S(2)}, u32[]{:S(2)}) collective-permute-start(bf16[4,160,128]{2,1,0:T(8,128)(2,1)S(1)} %get-tuple-element.75), channel_id=1, source_target_pairs={{0,8},{8,16},{16,24},{1,9},{9,17},{17,25},{2,10},{10,18},{18,26},{... | collective-permute-start | bytes 491528 | tf_op jit(solution)/shard_map/ppermute | solution.py:496
  32.7 15.2 %collective-permute-start.5 = (bf16[4,160,128]{2,1,0:T(8,128)(2,1)S(1)}, bf16[4,160,128]{2,1,0:T(8,128)(2,1)S(1)}, u32[]{:S(2)}, u32[]{:S(2)}) collective-permute-start(bf16[4,160,128]{2,1,0:T(8,128)(2,1)S(1)} %get-tuple-element.75), channel_id=1, source_target_pairs={{0,16},{8,24},{1,17},{9,25},{2,18},{10,26},{3,19},{11,27},{4,20},{... | collective-permute-start | bytes 491528 | tf_op jit(solution)/shard_map/ppermute | solution.py:496
  35.7 12.3 %collective-permute-start.6 = (bf16[4,160,128]{2,1,0:T(8,128)(2,1)S(1)}, bf16[4,160,128]{2,1,0:T(8,128)(2,1)S(1)}, u32[]{:S(2)}, u32[]{:S(2)}) collective-permute-start(bf16[4,160,128]{2,1,0:T(8,128)(2,1)S(1)} %get-tuple-element.75), channel_id=1, source_target_pairs={{0,24},{1,25},{2,26},{3,27},{4,28},{5,29},{6,30},{7,31}} | collective-permute-start | bytes 491528 | tf_op jit(solution)/shard_map/ppermute | solution.py:496
  37.0 10.9 %copy-start.11 = (bf16[512,1024]{1,0:T(8,128)(2,1)}, bf16[512,1024]{1,0:T(8,128)(2,1)S(1)}, u32[]{:S(2)}) copy-start(bf16[512,1024]{1,0:T(8,128)(2,1)S(1)} %collective-permute-done.1.refs_9_) | copy-start | bytes 3145732
  37.0 10.9 %copy-start.12 = (bf16[512,1024]{1,0:T(8,128)(2,1)}, bf16[512,1024]{1,0:T(8,128)(2,1)S(1)}, u32[]{:S(2)}) copy-start(bf16[512,1024]{1,0:T(8,128)(2,1)S(1)} %collective-permute-done.2.refs_10_) | copy-start | bytes 3145732
  37.0 27.1 %collective-permute-start.7 = (bf16[512,1024]{1,0:T(8,128)(2,1)S(1)}, bf16[512,1024]{1,0:T(8,128)(2,1)S(1)}, u32[]{:S(2)}, u32[]{:S(2)}) collective-permute-start(bf16[512,1024]{1,0:T(8,128)(2,1)S(1)} %columns.3), channel_id=1, source_target_pairs={{0,6},{1,7},{2,4},{3,5},{4,2},{5,3},{6,0},{7,1},{8,14},{9,15},{10,... | collective-permute-start | bytes 3145736 | tf_op jit(solution)/shard_map/ppermute | solution.py:652
  38.9 9.1 %copy-start.8 = (bf16[256,256]{1,0:T(8,128)(2,1)S(1)}, bf16[256,256]{1,0:T(8,128)(2,1)}, u32[]{:S(2)}) copy-start(bf16[256,256]{1,0:T(8,128)(2,1)} %constant.41.clone.ones_ref) | copy-start | bytes 393220
  53.1 19.6 %collective-permute-start.10 = (bf16[4,160,128]{2,1,0:T(8,128)(2,1)S(1)}, bf16[4,160,128]{2,1,0:T(8,128)(2,1)S(1)}, u32[]{:S(2)}, u32[]{:S(2)}) collective-permute-start(bf16[4,160,128]{2,1,0:T(8,128)(2,1)S(1)} %get-tuple-element.84), channel_id=1, source_target_pairs={{24,0},{25,1},{26,2},{27,3},{28,4},{29,5},{30,6},{31,7}} | collective-permute-start | bytes 491528 | tf_op jit(solution)/shard_map/ppermute | solution.py:496
  54.4 18.3 %collective-permute-start.8 = (bf16[4,160,128]{2,1,0:T(8,128)(2,1)S(1)}, bf16[4,160,128]{2,1,0:T(8,128)(2,1)S(1)}, u32[]{:S(2)}, u32[]{:S(2)}) collective-permute-start(bf16[4,160,128]{2,1,0:T(8,128)(2,1)S(1)} %get-tuple-element.84), channel_id=1, source_target_pairs={{8,0},{16,8},{24,16},{9,1},{17,9},{25,17},{10,2},{18,10},{26,18},{... | collective-permute-start | bytes 491528 | tf_op jit(solution)/shard_map/ppermute | solution.py:496
  55.7 17.0 %collective-permute-start.9 = (bf16[4,160,128]{2,1,0:T(8,128)(2,1)S(1)}, bf16[4,160,128]{2,1,0:T(8,128)(2,1)S(1)}, u32[]{:S(2)}, u32[]{:S(2)}) collective-permute-start(bf16[4,160,128]{2,1,0:T(8,128)(2,1)S(1)} %get-tuple-element.84), channel_id=1, source_target_pairs={{16,0},{24,8},{17,1},{25,9},{18,2},{26,10},{19,3},{27,11},{20,4},{... | collective-permute-start | bytes 491528 | tf_op jit(solution)/shard_map/ppermute | solution.py:496
  57.0 26.9 %collective-permute-start.14 = (bf16[1024,512]{1,0:T(8,128)(2,1)S(1)}, bf16[1024,512]{1,0:T(8,128)(2,1)S(1)}, u32[]{:S(2)}, u32[]{:S(2)}) collective-permute-start(bf16[1024,512]{1,0:T(8,128)(2,1)S(1)} %get-tuple-element.92.refs_0_.refs_4_), channel_id=1, source_target_pairs={{0,2},{1,3},{2,0},{3,1},{4,6},{5,7},{6,4},{7,5},{8,10},{9,11},{10,... | collective-permute-start | bytes 3145736 | tf_op jit(solution)/shard_map/ppermute | solution.py:652
  64.1 8.6 %copy-start.13 = (bf16[512,1024]{1,0:T(8,128)(2,1)}, bf16[512,1024]{1,0:T(8,128)(2,1)S(1)}, u32[]{:S(2)}) copy-start(bf16[512,1024]{1,0:T(8,128)(2,1)S(1)} %collective-permute-done.7.refs_11_) | copy-start | bytes 3145732
  64.1 22.7 %collective-permute-start.15 = (bf16[1024,512]{1,0:T(8,128)(2,1)S(1)}, bf16[1024,512]{1,0:T(8,128)(2,1)S(1)}, u32[]{:S(2)}, u32[]{:S(2)}) collective-permute-start(bf16[1024,512]{1,0:T(8,128)(2,1)S(1)} %get-tuple-element.92.refs_0_.refs_4_), channel_id=1, source_target_pairs={{0,4},{1,5},{2,6},{3,7},{4,0},{5,1},{6,2},{7,3},{8,12},{9,13},{10,... | collective-permute-start | bytes 3145736 | tf_op jit(solution)/shard_map/ppermute | solution.py:652
  76.6 11.2 %copy-start.7 = (s32[2]{0:T(128)S(1)}, s32[2]{0:T(128)}, u32[]{:S(2)}) copy-start(s32[2]{0:T(128)} %copy-done.6) | copy-start | bytes 28
  76.6 5.7 %collective-permute-start.12 = (f32[8,640]{1,0:T(8,128)S(1)}, f32[8,640]{1,0:T(8,128)S(1)}, u32[]{:S(2)}, u32[]{:S(2)}) collective-permute-start(f32[8,640]{1,0:T(8,128)S(1)} %get-tuple-element.90), channel_id=1, source_target_pairs={{8,0},{16,8},{24,16},{9,1},{17,9},{25,17},{10,2},{18,10},{26,18},{... | collective-permute-start | bytes 61448 | tf_op jit(solution)/shard_map/ppermute | solution.py:496
  78.1 9.7 %collective-permute-start.11 = (bf16[512,640]{1,0:T(8,128)(2,1)S(1)}, bf16[512,640]{1,0:T(8,128)(2,1)S(1)}, u32[]{:S(2)}, u32[]{:S(2)}) collective-permute-start(bf16[512,640]{1,0:T(8,128)(2,1)S(1)} %get-tuple-element.85.dp_ref), channel_id=1, source_target_pairs={{0,1},{1,0},{2,3},{3,2},{4,5},{5,4},{6,7},{7,6},{8,9},{9,8},{10,11... | collective-permute-start | bytes 1966088 | tf_op jit(solution)/shard_map/ppermute | solution.py:652
  82.4 12.0 %collective-permute-start.13 = (bf16[512,640]{1,0:T(8,128)(2,1)S(1)}, bf16[512,640]{1,0:T(8,128)(2,1)S(1)}, u32[]{:S(2)}, u32[]{:S(2)}) collective-permute-start(bf16[512,640]{1,0:T(8,128)(2,1)S(1)} %complete.1.dp_ref), channel_id=1, source_target_pairs={{0,1},{1,0},{2,3},{3,2},{4,5},{5,4},{6,7},{7,6},{8,9},{9,8},{10,11... | collective-permute-start | bytes 1966088 | tf_op jit(solution)/shard_map/ppermute | solution.py:652
  86.8 14.9 %collective-permute-start.16 = (bf16[512,512]{1,0:T(8,128)(2,1)S(1)}, bf16[512,512]{1,0:T(8,128)(2,1)S(1)}, u32[]{:S(2)}, u32[]{:S(2)}) collective-permute-start(bf16[512,512]{1,0:T(8,128)(2,1)S(1)} %get-tuple-element.93), channel_id=1, source_target_pairs={{0,4},{1,5},{2,6},{3,7},{4,0},{5,1},{6,2},{7,3},{8,12},{9,13},{10,... | collective-permute-start | bytes 1572872 | tf_op jit(solution)/shard_map/ppermute | solution.py:652
  87.0 14.9 %collective-permute-start.17 = (bf16[512,512]{1,0:T(8,128)(2,1)S(1)}, bf16[512,512]{1,0:T(8,128)(2,1)S(1)}, u32[]{:S(2)}, u32[]{:S(2)}) collective-permute-start(bf16[512,512]{1,0:T(8,128)(2,1)S(1)} %get-tuple-element.94), channel_id=1, source_target_pairs={{0,2},{1,3},{2,0},{3,1},{4,6},{5,7},{6,4},{7,5},{8,10},{9,11},{10,... | collective-permute-start | bytes 1572872 | tf_op jit(solution)/shard_map/ppermute | solution.py:652
  93.2 27.0 %collective-permute-start.18 = (bf16[2,512,512]{2,1,0:T(8,128)(2,1)}, bf16[2,512,512]{2,1,0:T(8,128)(2,1)S(1)}, u32[]{:S(2)}, u32[]{:S(2)}) collective-permute-start(bf16[2,512,512]{2,1,0:T(8,128)(2,1)} %get-tuple-element.100), channel_id=1, source_target_pairs={{0,2},{1,3},{2,0},{3,1},{4,6},{5,7},{6,4},{7,5},{8,10},{9,11},{10,... | collective-permute-start | bytes 3145736 | tf_op jit(solution)/shard_map/ppermute | solution.py:652
  99.8 24.0 %collective-permute-start.19 = (bf16[2,512,512]{2,1,0:T(8,128)(2,1)}, bf16[2,512,512]{2,1,0:T(8,128)(2,1)}, u32[]{:S(2)}, u32[]{:S(2)}) collective-permute-start(bf16[2,512,512]{2,1,0:T(8,128)(2,1)} %get-tuple-element.102), channel_id=1, source_target_pairs={{0,4},{1,5},{2,6},{3,7},{4,0},{5,1},{6,2},{7,3},{8,12},{9,13},{10,... | collective-permute-start | bytes 3145736 | tf_op jit(solution)/shard_map/ppermute | solution.py:652
  110.6 1.3 copy-start.3
  112.0 15.4 %collective-permute-start.20 = (bf16[1024,512]{1,0:T(8,128)(2,1)}, bf16[1024,512]{1,0:T(8,128)(2,1)}, u32[]{:S(2)}, u32[]{:S(2)}) collective-permute-start(bf16[1024,512]{1,0:T(8,128)(2,1)} %get-tuple-element.104), channel_id=1, source_target_pairs={{0,1},{1,0},{2,3},{3,2},{4,5},{5,4},{6,7},{7,6},{8,9},{9,8},{10,11... | collective-permute-start | bytes 3145736 | tf_op jit(solution)/shard_map/ppermute | solution.py:652
  120.4 12.3 %collective-permute-start.21 = (bf16[1,512,512]{2,1,0:T(8,128)(2,1)S(1)}, bf16[1,512,512]{2,1,0:T(8,128)(2,1)S(1)}, u32[]{:S(2)}, u32[]{:S(2)}) collective-permute-start(bf16[1,512,512]{2,1,0:T(8,128)(2,1)S(1)} %passing.2), channel_id=1, source_target_pairs={{0,4},{1,5},{2,6},{3,7},{4,0},{5,1},{6,2},{7,3},{8,12},{9,13},{10,... | collective-permute-start | bytes 1572872 | tf_op jit(solution)/shard_map/ppermute | solution.py:652
  125.1 2.3 %copy-start.4 = (f32[1024,512]{1,0:T(8,128)S(1)}, f32[1024,512]{1,0:T(8,128)}, u32[]{:S(2)}) copy-start(f32[1024,512]{1,0:T(8,128)} %copy-done.3) | copy-start | bytes 6291460
  125.1 9.2 %collective-permute-start.22 = (bf16[1,512,512]{2,1,0:T(8,128)(2,1)S(1)}, bf16[1,512,512]{2,1,0:T(8,128)(2,1)S(1)}, u32[]{:S(2)}, u32[]{:S(2)}) collective-permute-start(bf16[1,512,512]{2,1,0:T(8,128)(2,1)S(1)} %passing.3), channel_id=1, source_target_pairs={{0,2},{1,3},{2,0},{3,1},{4,6},{5,7},{6,4},{7,5},{8,10},{9,11},{10,... | collective-permute-start | bytes 1572872 | tf_op jit(solution)/shard_map/ppermute | solution.py:652

commit v4 on v3

--- a/solution.py
+++ b/solution.py
@@ -125,10 +125,35 @@
     return jnp.concatenate([u[:, :128] + bias[:, :128], u[:, 128:]], 1)
 
 
-def project_kernel(heads, x_ref, halo_ref, w_ref, cw_ref, sel_ref, bias_ref,
-                   v_ref, pq_ref, pk_ref, fq_ref, fk_ref, loc_ref, state_ref, ext, run):
+def with_rows(hbm_ref, first_ref, buf, sems, use):
+    c = pl.program_id(0)
+
+    def fetch(k):
+        slot = lax.rem(k, 2)
+        return pltpu.make_async_copy(hbm_ref.at[rows_at(k), :], buf.at[slot], sems.at[slot])
+
+    @pl.when(c == 0)
+    def _():
+        fetch(1).start()
+        use(first_ref[...])
+
+    @pl.when(c >= 1)
+    def _():
+        fetch(c).wait()
+
+        @pl.when(c + 1 < pl.num_programs(0))
+        def _():
+            fetch(c + 1).start()
+
+        use(buf[lax.rem(c, 2)])
+
+
+def project_kernel(heads, x_ref, x_first_ref, ct_ref, halo_ref, w_ref, cw_ref, sel_ref, bias_ref,
+                   v_ref, pq_ref, pk_ref, fq_ref, fk_ref, loc_ref, ct_first_ref, state_ref, ext, run, buf, sems):
     c = pl.program_id(0)
     at = rows_at(c)
+    last = pl.num_programs(0) - 1
+    ct_copy = pltpu.make_async_copy(ct_ref.at[pl.ds(0, CH), :], ct_first_ref, sems.at[2])
 
     @pl.when(c == 0)
     def _():
@@ -136,7 +161,14 @@
         ext[0:8, :] = before[8:16]
         run[...] = jnp.zeros_like(run)
 
-    ext[8:, :] = mm(x_ref[...], w_ref[...]).astype(BF).astype(F32)
+    @pl.when(c == last)
+    def _():
+        ct_copy.start()
+
+    def product(rows):
+        ext[8:, :] = mm(rows, w_ref[...]).astype(BF).astype(F32)
+
+    with_rows(x_ref, x_first_ref, buf, sems, product)
     conv = (cw_ref[0:1] * ext[8 : 8 + CH, :] + cw_ref[1:2] * ext[7 : 7 + CH, :]
             + cw_ref[2:3] * ext[6 : 6 + CH, :])
     ext[0:8, :] = ext[CH : CH + 8, :]
@@ -160,13 +192,14 @@
         loc_ref[c, h] = run[h].astype(BF)
         run[h] = run[h] + mm_tn(v, pk)
 
-    @pl.when(c == pl.num_programs(0) - 1)
+    @pl.when(c == last)
     def _():
         for h in range(heads):
             state_ref[h] = run[h].T[:ES].astype(BF)
-
-
-def project(x, halo, w_in, conv_w, sel, bias, heads):
+        ct_copy.wait()
+
+
+def project(x, x_first, ct, halo, w_in, conv_w, sel, bias, heads):
     rows, d = x.shape
     width = w_in.shape[1]
     n = rows // CH
@@ -174,14 +207,16 @@
         functools.partial(project_kernel, heads),
         grid=(n,),
         in_specs=[
-            pl.BlockSpec((CH, d), lambda c: (c, 0)),
+            pl.BlockSpec(memory_space=pltpu.HBM),
+            KEPT,
+            pl.BlockSpec(memory_space=pltpu.HBM),
             whole((16, d)),
             KEPT,
             whole((3, width)),
             KEPT,
             whole(bias.shape),
         ],
-        out_specs=[KEPT] * 6 + [whole((heads, ES, DV))],
+        out_specs=[KEPT] * 7 + [whole((heads, ES, DV))],
         out_shape=[
             kept((rows, heads * DV), BF),
             kept((heads, rows, EP), BF),
@@ -189,20 +224,30 @@
             kept((heads, rows, 2 * EP), BF),
             kept((heads, rows, 2 * EP), BF),
             kept((n, heads, DV, EP), BF),
+            kept((CH, d), BF),
             jax.ShapeDtypeStruct((heads, ES, DV), BF),
         ],
-        scratch_shapes=[pltpu.VMEM((CH + 8, width), F32), pltpu.VMEM((heads, DV, EP), F32)],
-        compiler_params=params(12),
+        scratch_shapes=[
+            pltpu.VMEM((CH + 8, width), F32),
+            pltpu.VMEM((heads, DV, EP), F32),
+            pltpu.VMEM((2, CH, d), BF),
+            pltpu.SemaphoreType.DMA((3,)),
+        ],
+        compiler_params=params(9),
         cost_estimate=cost(100 << 30),
         name="project",
-    )(stay(x), halo, keep(w_in), conv_w, keep(sel), bias)
-
-
-def local_kernel(heads, ct_ref, wo_ref, gain_ref, v_ref, pq_ref, pk_ref, loc_ref, fq_ref, fk_ref, sel_ref,
-                 g_ref, num_ref, wt_ref, slope_ref):
+    )(stay(x), keep(x_first), stay(ct), halo, keep(w_in), conv_w, keep(sel), bias)
+
+
+def local_kernel(heads, ct_ref, ct_first_ref, wo_ref, gain_ref, v_ref, pq_ref, pk_ref, loc_ref, fq_ref, fk_ref, sel_ref,
+                 g_ref, num_ref, wt_ref, slope_ref, buf, sems):
     c = pl.program_id(0)
     at = rows_at(c)
-    g_ref[at, :] = mm_nt(ct_ref[...], wo_ref[...]) * gain_ref[...]
+
+    def product(rows):
+        g_ref[at, :] = mm_nt(rows, wo_ref[...]) * gain_ref[...]
+
+    with_rows(ct_ref, ct_first_ref, buf, sems, product)
     mask = causal()
     for h in range(heads):
         pq = pq_ref[h, at, :]
@@ -215,20 +260,21 @@
         num_ref[at, lanes] = mm(weights, v_ref[at, lanes]) + mm_nt(pq, loc_ref[c, h])
 
 
-def local_part(ct, w_out, gain, v, pq, pk, loc, fq, fk, sel, heads):
+def local_part(ct, ct_first, w_out, gain, v, pq, pk, loc, fq, fk, sel, heads):
     rows, d = ct.shape
     n = rows // CH
     wide = heads * DV
     return pl.pallas_call(
         functools.partial(local_kernel, heads),
         grid=(n,),
-        in_specs=[pl.BlockSpec((CH, d), lambda c: (c, 0)), KEPT, whole((1, wide))] + [KEPT] * 7,
+        in_specs=[pl.BlockSpec(memory_space=pltpu.HBM), KEPT, KEPT, whole((1, wide))] + [KEPT] * 7,
         out_specs=[KEPT] * 4,
         out_shape=[kept((rows, wide), F32)] * 2 + [kept((heads, rows, CH), BF)] * 2,
-        compiler_params=params(12),
+        scratch_shapes=[pltpu.VMEM((2, CH, d), BF), pltpu.SemaphoreType.DMA((2,))],
+        compiler_params=params(8),
         cost_estimate=LIGHT,
         name="local_part",
-    )(stay(ct), keep(w_out), gain, *map(keep, (v, pq, pk, loc, fq, fk, sel)))
+    )(stay(ct), keep(ct_first), keep(w_out), gain, *map(keep, (v, pq, pk, loc, fq, fk, sel)))
 
 
 def norm_kernel(heads, parts, passed, g_ref, num_ref, gain_ref, pq_ref, ones_ref, *refs):
@@ -287,7 +333,7 @@
             jax.ShapeDtypeStruct((heads, ES, DV), BF),
         ],
         scratch_shapes=[pltpu.VMEM((heads, DV, EP), F32)],
-        compiler_params=params(8),
+        compiler_params=params(5),
         cost_estimate=cost(16 << 30),
         name="norm_part",
     )(keep(g), keep(num), gain, keep(pq), ones, *got, *map(keep, later))
@@ -338,7 +384,7 @@
             kept((heads, rows, 128), F32),
         ],
         scratch_shapes=[pltpu.VMEM((heads, DV, EP), F32)],
-        compiler_params=params(8),
+        compiler_params=params(5),
         cost_estimate=LIGHT,
         name="inner_part",
     )(*map(keep, (v, pq, pk, fq, wt, slope, dn, loc, pre, sel, fk, gloc)))
@@ -428,66 +474,79 @@
             kept((16, width), F32),
         ],
         scratch_shapes=[pltpu.VMEM((CH + 8, width), F32), pltpu.VMEM((heads, DV, EP), F32)],
-        compiler_params=params(8),
+        compiler_params=params(5),
         cost_estimate=cost(16 << 30),
         name="outer_part",
     )(*map(keep, (v, pk, fk, dqk, dv, xk, loc, sel)), conv_w, *got)
 
 
-def columns_kernel(which, place_ref, w_ref, *refs):
-    outs, sems = refs[-1 - len(which) : -1], refs[-1]
-    wide = outs[0].shape[1]
-    copies = []
-    for i, m in enumerate(which):
-        start = pl.multiple_of(lax.bitwise_xor(place_ref[0], m) * wide, wide)
-        copies.append(pltpu.make_async_copy(w_ref.at[:, pl.ds(start, wide)], outs[i], sems.at[i]))
-    if len(refs) > len(which) + 1:
-        x_ref, wi_ref, tail_ref, wi_out_ref = refs[:4]
-        rows = tail_ref.shape[0]
-        copies.append(
-            pltpu.make_async_copy(x_ref.at[pl.ds(x_ref.shape[0] - rows, rows), :], tail_ref, sems.at[len(which)])
-        )
-        count, sw = wi_out_ref.shape[:2]
-        for r in range(count):
-            block = 2 * lax.bitwise_xor(place_ref[0], r) + 1 - place_ref[1]
-            copies.append(
-                pltpu.make_async_copy(
-                    wi_ref.at[pl.ds(pl.multiple_of(block * sw, sw), sw), :],
-                    wi_out_ref.at[r],
-                    sems.at[len(which) + 1 + r],
-                )
-            )
+def run_copies(copies, sems):
+    copies = [pltpu.make_async_copy(*one, sems.at[i]) for i, one in enumerate(copies)]
     for copy in copies:
         copy.start()
     for copy in copies:
         copy.wait()
 
 
-def columns(place, w_out, which, count, x=None, w_in=None):
-    rows, d = w_out.shape
+def column_copies(which, place_ref, w_ref, outs):
+    wide = outs[0].shape[1]
+    for m, out in zip(which, outs):
+        start = pl.multiple_of(lax.bitwise_xor(place_ref[0], m) * wide, wide)
+        yield w_ref.at[:, pl.ds(start, wide)], out
+
+
+def near_kernel(which, place_ref, w_ref, x_ref, tail_ref, *refs):
+    rows = tail_ref.shape[0]
+    copies = list(column_copies(which, place_ref, w_ref, refs[:-1]))
+    copies.append((x_ref.at[pl.ds(x_ref.shape[0] - rows, rows), :], tail_ref))
+    run_copies(copies, refs[-1])
+
+
+def rest_kernel(which, place_ref, w_ref, wi_ref, x_ref, blocks_ref, first_ref, *refs):
+    copies = list(column_copies(which, place_ref, w_ref, refs[:-1]))
+    count, sw = blocks_ref.shape[:2]
+    for r in range(count):
+        block = 2 * lax.bitwise_xor(place_ref[0], r) + 1 - place_ref[1]
+        copies.append((wi_ref.at[pl.ds(pl.multiple_of(block * sw, sw), sw), :], blocks_ref.at[r]))
+    copies.append((x_ref.at[pl.ds(0, CH), :], first_ref))
+    run_copies(copies, refs[-1])
+
+
+def copied(kernel, which, place, arrays, extra, specs, copies, name):
+    rows, d = arrays[0].shape
     anywhere = pl.BlockSpec(memory_space=pltpu.HBM)
-    out_shape = [jax.ShapeDtypeStruct((rows, d // count), w_out.dtype)] * len(which)
-    args = [stay(w_out)]
-    if x is not None:
-        args += [stay(x), stay(w_in)]
-        out_shape = [
-            jax.ShapeDtypeStruct((16, x.shape[1]), x.dtype),
-            jax.ShapeDtypeStruct((count, w_in.shape[0] // (2 * count), w_in.shape[1]), w_in.dtype),
-        ] + out_shape
-    return pl.pallas_call(
-        functools.partial(columns_kernel, which),
+    pairs = lax.axis_size("tp") // 2
+    return pl.pallas_call(
+        functools.partial(kernel, which),
         grid_spec=pltpu.PrefetchScalarGridSpec(
             num_scalar_prefetch=1,
             grid=(1,),
-            in_specs=[anywhere] * len(args),
-            out_specs=[anywhere] * len(out_shape),
-            scratch_shapes=[pltpu.SemaphoreType.DMA((len(which) + 1 + count,))],
+            in_specs=[anywhere] * len(arrays),
+            out_specs=specs + [anywhere] * len(which),
+            scratch_shapes=[pltpu.SemaphoreType.DMA((copies,))],
         ),
-        out_shape=out_shape,
+        out_shape=extra + [jax.ShapeDtypeStruct((rows, d // pairs), arrays[0].dtype)] * len(which),
         compiler_params=pltpu.CompilerParams(vmem_limit_bytes=4 * MIB),
         cost_estimate=LIGHT,
-        name="columns",
-    )(place, *args)
+        name=name,
+    )(place, *map(stay, arrays))
+
+
+def near_sends(place, w_out, x):
+    tail = jax.ShapeDtypeStruct((16, x.shape[1]), x.dtype)
+    spec = pl.BlockSpec(memory_space=pltpu.HBM)
+    return copied(near_kernel, (1, 2), place, (w_out, x), [tail], [spec], 3, "near_sends")
+
+
+def rest_sends(place, w_out, w_in, x):
+    pairs = lax.axis_size("tp") // 2
+    which = tuple(range(3, pairs))
+    blocks = jax.ShapeDtypeStruct((pairs, w_in.shape[0] // (2 * pairs), w_in.shape[1]), w_in.dtype)
+    specs = [pl.BlockSpec(memory_space=pltpu.HBM), KEPT]
+    extra = [blocks, kept((CH, x.shape[1]), x.dtype)]
+    return copied(
+        rest_kernel, which, place, (w_out, w_in, x), extra, specs, len(which) + pairs + 1, "rest_sends"
+    )
 
 
 def shifted(array, by):
@@ -513,8 +572,8 @@
             one = mm(part[...], w[...])
             total = one if total is None else total + one
         first, second = total[:, :sw], total[:, sw:]
-        send_ref[...] = jnp.where(odd, first, second).astype(BF)
-        keep_ref[...] = jnp.where(odd, second, first)
+        send_ref[rows_at(c), :] = jnp.where(odd, first, second).astype(BF)
+        keep_ref[rows_at(c), :] = jnp.where(odd, second, first)
 
     @pl.when(c < half_chunks)
     def _():
@@ -531,7 +590,6 @@
     wide = tops[0][0].shape[1]
     sw = ws[1].shape[1] // 2
     part = rows // (2 * CH)
-    row = pl.BlockSpec((CH, sw), lambda c, place: (c, 0))
     operands, specs = [], []
     for array, start in tops:
         operands.append(array)
@@ -551,9 +609,9 @@
             in_specs=specs
             + [pl.BlockSpec((wide, 2 * sw), lambda c, place: (0, place[0]))]
             + [pl.BlockSpec((wide, 2 * sw), lambda c, place: (0, 0))] * (count - 1),
-            out_specs=[row, row],
+            out_specs=[KEPT, KEPT],
         ),
-        out_shape=[jax.ShapeDtypeStruct((rows, sw), BF), jax.ShapeDtypeStruct((rows, sw), F32)],
+        out_shape=[kept((rows, sw), BF), kept((rows, sw), F32)],
         compiler_params=params(16),
         cost_estimate=cost(16 << 30),
         name="out_part",
@@ -622,7 +680,7 @@
             scratch_shapes=[pltpu.VMEM((half, 2 * width), BF)],
         ),
         out_shape=[kept((count // 2, half, sw), BF)] * 2,
-        compiler_params=params(8),
+        compiler_params=params(5),
         cost_estimate=LIGHT,
         name="grad_part",
     )(place, *map(keep, (dp, other, w_in, w_other)))
@@ -656,58 +714,119 @@
     return a.astype(F32) + b.astype(F32)
 
 
-def passing_kernel(first, stride, keep_ref, got_ref, out_ref):
+def passing_kernel(places, *refs):
+    ins, out_ref = refs[:-1], refs[-1]
     for i in range(out_ref.shape[0]):
-        out_ref[i] = summed(keep_ref[first + stride * i], got_ref[first + stride * i]).astype(BF)
-
-
-def passing(kept_sum, got, first, stride):
-    left, half, sw = got.shape
-    return pl.pallas_call(
-        functools.partial(passing_kernel, first, stride),
-        in_specs=[KEPT] * 2,
+        total = None
+        for ref, place in zip(ins, places):
+            one = ref[place[i]].astype(F32)
+            total = one if total is None else total + one
+        out_ref[i] = total.astype(BF)
+
+
+def passing(terms, blocks):
+    places = [[place[i] for i in blocks] for _, place in terms]
+    return pl.pallas_call(
+        functools.partial(passing_kernel, places),
+        in_specs=[KEPT] * len(terms),
         out_specs=KEPT,
-        out_shape=kept((left // 2, half, sw), BF),
+        out_shape=kept((len(blocks),) + terms[0][0].shape[1:], BF),
         compiler_params=pltpu.CompilerParams(vmem_limit_bytes=4 * MIB),
         cost_estimate=LIGHT,
         name="passing",
-    )(keep(kept_sum), keep(got))
-
-
-def reduce_both(a_send, a_keep, b_send, b_keep, a_own, b_own, meanwhile):
+    )(*[keep(array) for array, _ in terms])
+
+
+def reduce_both(a_send, a_keep, b_send, b_keep, meanwhile):
     pairs = lax.axis_size("tp") // 2
     a_step, b_step = 1, pairs // 2
+    left = pairs // 2
+    a_terms, b_terms = [(a_keep, list(range(left)))], [(b_keep, list(range(left)))]
     while True:
-        a_got = swapped(a_send, 2 * a_step)
-        b_got = swapped(b_send, 2 * b_step)
-        left = a_keep.shape[0]
-        a_keep, b_keep = meanwhile(a_keep, b_keep)
+        a_got, b_got = swapped(a_send, 2 * a_step), swapped(b_send, 2 * b_step)
+        a_got, b_got = meanwhile(a_got, b_got)
+        a_terms.append((a_got, list(range(left))))
+        b_terms.append((b_got, list(range(left))))
         if left == 1:
-            return a_keep[0], a_got[0], b_keep[0], b_got[0]
-        a_send = passing(a_keep, a_got, 1, 2)
-        b_send = passing(b_keep, b_got, left // 2, 1)
-        a_keep = summed(a_keep[0::2], a_got[0::2])
-        b_keep = summed(b_keep[: left // 2], b_got[: left // 2])
-        if left == 2:
-            a_keep = a_keep + a_own
-            b_keep = b_keep + b_own
+            return a_terms, b_terms
+        half = left // 2
+        a_send = passing(a_terms, list(range(1, left, 2)))
+        b_send = passing(b_terms, list(range(half, left)))
+        a_terms = [(array, place[0::2]) for array, place in a_terms]
+        b_terms = [(array, place[:half]) for array, place in b_terms]
+        left = half
         a_step, b_step = a_step * 2, b_step // 2
 
 
-def finish_kernel(half, ak_ref, ag_ref, bk_ref, bg_ref, out_ref):
-    out_ref[:half, :] = (ak_ref[...] + ag_ref[...].astype(F32)).astype(BF)
-    out_ref[half:, :] = (bk_ref[...] + bg_ref[...].astype(F32)).astype(BF)
-
-
-def finish(a_keep, a_got, b_keep, b_got):
-    half, sw = a_keep.shape
-    return pl.pallas_call(
-        functools.partial(finish_kernel, half),
-        out_shape=jax.ShapeDtypeStruct((2 * half, sw), BF),
+def own_kernel(place_ref, x_ref, ct_ref, x_own_ref, ct_own_ref, sems):
+    sw = x_own_ref.shape[1]
+    at = pl.ds(pl.multiple_of(place_ref[2] * sw, sw), sw)
+    copies = [
+        pltpu.make_async_copy(x_ref.at[:, at], x_own_ref, sems.at[0]),
+        pltpu.make_async_copy(ct_ref.at[:, at], ct_own_ref, sems.at[1]),
+    ]
+    for copy in copies:
+        copy.start()
+    for copy in copies:
+        copy.wait()
+
+
+def own_columns(place, x, ct, sw):
+    rows = x.shape[0]
+    anywhere = pl.BlockSpec(memory_space=pltpu.HBM)
+    return pl.pallas_call(
+        own_kernel,
+        grid_spec=pltpu.PrefetchScalarGridSpec(
+            num_scalar_prefetch=1,
+            grid=(1,),
+            in_specs=[anywhere] * 2,
+            out_specs=[KEPT] * 2,
+            scratch_shapes=[pltpu.SemaphoreType.DMA((2,))],
+        ),
+        out_shape=[kept((rows, sw), x.dtype)] * 2,
         compiler_params=pltpu.CompilerParams(vmem_limit_bytes=4 * MIB),
         cost_estimate=LIGHT,
+        name="own_columns",
+    )(place, stay(x), stay(ct))
+
+
+def finish_kernel(places, own_ref, *refs):
+    tops, lows, out_ref = refs[: len(places)], refs[len(places) : -1], refs[-1]
+    half = out_ref.shape[0] // 2
+    for first, ins in ((0, tops), (half, lows)):
+        total = own_ref[first : first + half, :].astype(F32)
+        for ref, place in zip(ins, places):
+            total = total + ref[place].astype(F32)
+        out_ref[first : first + half, :] = total.astype(BF)
+
+
+def finish(own, a_terms, b_terms):
+    places = [index[0] for _, index in a_terms]
+    assert places == [index[0] for _, index in b_terms]
+    terms = [array for array, _ in a_terms + b_terms]
+    return pl.pallas_call(
+        functools.partial(finish_kernel, places),
+        in_specs=[KEPT] * (1 + len(terms)),
+        out_shape=jax.ShapeDtypeStruct(own.shape, BF),
+        compiler_params=pltpu.CompilerParams(vmem_limit_bytes=6 * MIB),
+        cost_estimate=LIGHT,
         name="finish",
-    )(a_keep, a_got, b_keep, b_got)
+    )(*map(keep, [own] + terms))
+
+
+def finish_out_kernel(own_ref, keep_ref, got_ref, out_ref):
+    out_ref[...] = (own_ref[...].astype(F32) + keep_ref[...] + got_ref[...].astype(F32)).astype(BF)
+
+
+def finish_out(own, kept_part, got):
+    return pl.pallas_call(
+        finish_out_kernel,
+        in_specs=[KEPT] * 3,
+        out_shape=jax.ShapeDtypeStruct(own.shape, BF),
+        compiler_params=pltpu.CompilerParams(vmem_limit_bytes=6 * MIB),
+        cost_estimate=LIGHT,
+        name="finish_out",
+    )(*map(keep, (own, kept_part, got)))
 
 
 def per_device(inputs, cotangent, w_in, conv_w, norm_gain, w_out, keep_flags):
@@ -717,24 +836,23 @@
     pairs = tp // 2
     me = lax.axis_index("tp")
     pair = me // 2
-    place = jnp.stack([pair, me % 2]).astype(jnp.int32)
-    slice_width = inputs.shape[1] // tp
-    column = me * slice_width
+    place = jnp.stack([pair, me % 2, me]).astype(jnp.int32)
     gain = (norm_gain.reshape(heads, DV) * keep_flags.astype(F32)[:, None]).reshape(1, heads * DV)
 
     half = inputs.shape[0] // 2
-    tail, w_other, *near = columns(place, w_out, (1, 2), pairs, inputs, w_in)
-    w_other = swapped(w_other, 1)
+    tail, *near = near_sends(place, w_out, inputs)
     halo = shifted(tail, 1)
     near = [swapped(one, 2 * m) for m, one in enumerate(near, 1)]
-    far = columns(place, w_out, range(3, pairs), pairs)
+    w_other, x_first, *far = rest_sends(place, w_out, w_in, inputs)
+    w_other = swapped(w_other, 1)
     halo, place, gain, far = lax.optimization_barrier((halo, place, gain, far))
-    v, pq, pk, fq, fk, loc, state = project(inputs, halo, w_in, conv_w, sel, bias, heads)
+    v, pq, pk, fq, fk, loc, ct_first, state = project(
+        inputs, x_first, cotangent, halo, w_in, conv_w, sel, bias, heads)
     state, w_other = lax.optimization_barrier((state, w_other))
     before = from_others(state, 1)
     v, near, far = lax.optimization_barrier((v, near, far))
     far = [swapped(one, 2 * m) for m, one in enumerate(far, 3)]
-    g, num, wt, slope = local_part(cotangent, w_out, gain, v, pq, pk, loc, fq, fk, sel, heads)
+    g, num, wt, slope = local_part(cotangent, ct_first, w_out, gain, v, pq, pk, loc, fq, fk, sel, heads)
     ho, dn, gloc, pre, gstate = norm_part(
         g, num, gain, pq, before, (v, pk, fq, fk, wt, slope, loc, sel), heads
     )
@@ -745,33 +863,33 @@
     dqk, dv, xk = inner_part(v, pq, pk, fq, wt, slope, dn, loc, pre, sel, fk, gloc, heads)
     dp_top, dp, first, last = outer_part(v, pk, fk, dqk, dv, xk, gloc, later, sel, conv_w, heads)
     other_top = swapped(dp_top, 1)
-    dp_low = complete(dp, last, shifted(first, -1), conv_w)
+    after = shifted(first, -1)
+    a_send, a_keep = grad_part(place, dp_top, other_top, w_in, w_other, True)
+    dp_low = complete(dp, last, after, conv_w)
     other_low = swapped(dp_low, 1)
     x_top, y_low = halves(got[1], got[step])
     x_top, y_low = swapped(x_top, 2 * step), swapped(y_low, 2)
-    a_send, a_keep = grad_part(place, dp_top, other_top, w_in, w_other, True)
     b_send, b_keep = grad_part(place, dp_low, other_low, w_in, w_other, False)
     tops = [(ho, 0)] + [(got.get(r, x_top), 0) for r in range(1, pairs)]
     lows = [(ho, half)] + [(got[r], half) if r in got else (y_low, 0) for r in range(1, pairs)]
     w_cols = [w_out] + near + far
-    x_own = lax.dynamic_slice_in_dim(inputs, column, slice_width, 1).astype(F32)
-    c_own = lax.dynamic_slice_in_dim(cotangent, column, slice_width, 1).astype(F32)
+    place_, b_keep = lax.optimization_barrier((place, b_keep))
     stage = []
 
-    def meanwhile(a, b):
+    def meanwhile(a_got, b_got):
         if not stage:
             out_send, out_keep = out_part(place, tops, lows, w_cols)
-            stage.append(x_own + out_keep)
-            stage.append(out_send)
-            a, b, stage[1] = lax.optimization_barrier((a, b, stage[1]))
-            stage.append(swapped(stage[1], 1))
-        elif len(stage) == 3:
-            stage.append((stage[0] + stage[2].astype(F32)).astype(BF))
-            a, b, stage[3] = lax.optimization_barrier((a, b, stage[3]))
-        return a, b
-
-    sums = reduce_both(a_send, a_keep, b_send, b_keep, c_own[None, :half], c_own[None, half:], meanwhile)
-    return stage[3], finish(*sums)
+            own = own_columns(place_, inputs, cotangent, inputs.shape[1] // tp)
+            out_got = swapped(out_send, 1)
+            a_got, b_got, out_keep = lax.optimization_barrier((a_got, b_got, out_keep))
+            stage.extend([*own, out_keep, out_got])
+        elif len(stage) == 4:
+            stage.append(finish_out(stage[0], *stage[2:]))
+            a_got, b_got, stage[4] = lax.optimization_barrier((a_got, b_got, stage[4]))
+        return a_got, b_got
+
+    a_terms, b_terms = reduce_both(a_send, a_keep, b_send, b_keep, meanwhile)
+    return stage[4], finish(stage[1], a_terms, b_terms)
 
 
 def solution(mesh):

time: 136 us -> 135 us (level)
  waiting for transfers between devices: 28.3 us -> 37.5 us
  other arithmetic: 6.08 us -> 0.15 us
  local copies, waits for them, and re-layouts: 1.97 us -> 0.07 us
  Pallas kernels: 67.8 us -> 66.1 us
    ppermute x15, waiting for transfers between devices: 24.1 us -> 33.2 us  [swapped(): return lax.ppermute(array, 'tp', [(i, i ^ distance) for i in range(count)])]
    convert_element_type x2 -> x0, other arithmetic: 4.46 us -> none  [the longest x1 2.96 us: meanwhile(): stage.append((stage[0] + stage[2].astype(F32)).astype(BF))]
    pallas_call x5 -> x7, Pallas kernels: 7.68 us -> 10.6 us  [the longest x2 5.43 us: copied(): pl.pallas_call(functools.partial(kernel, which), grid_spec=pltpu.Prefetch...]
    pallas_call x2, Pallas kernels: 10.8 us -> 8.86 us  [grad_part(): pl.pallas_call(functools.partial(grad_kernel, count, low_first), grid_spe...]
    unnamed x30 -> x28, local copies, waits for them, and re-layouts: 1.97 us -> 0.07 us
    add x1 -> x0, other arithmetic: 1.47 us -> none  [reduce_both(): b_keep = b_keep + b_own]
  transfers between devices with their start and end apart: 23 -> 23, of which waited for: 9 -> 8; matrix products, arithmetic and copies ran while one was open for 4% -> 0% of each run, Pallas kernels for 47% -> 47%
where the time goes in v4:
time: 135 us; the launch traced here: 134 us
  Pallas kernels  66.1 us (49%)
  waiting for transfers between devices  37.5 us (28%)
  starting transfers between devices  29.4 us (22%)
    ppermute x15, waiting for transfers between devices, swapped(): return lax.ppermute(array, 'tp', [(i, i ^ distance) for i in range(count)])  33.2 us
    ppermute x8, starting transfers between devices, shifted(): return lax.ppermute(array, 'seq', pairs)  17.4 us
    pallas_call x1, Pallas kernels, project(): pl.pallas_call(functools.partial(project_kernel, heads), grid=(n,), in_sp...  13.6 us
    ppermute x15, starting transfers between devices, swapped(): return lax.ppermute(array, 'tp', [(i, i ^ distance) for i in range(count)])  12 us
    pallas_call x2, Pallas kernels, grad_part(): pl.pallas_call(functools.partial(grad_kernel, count, low_first), grid_spe...  8.86 us
    pallas_call x1, Pallas kernels, local_part(): pl.pallas_call(functools.partial(local_kernel, heads), grid=(n,), in_spec...  7.99 us
    pallas_call x1, Pallas kernels, out_part(): pl.pallas_call(functools.partial(out_kernel, count, sw), grid_spec=pltpu....  7.99 us
    pallas_call x1, Pallas kernels, inner_part(): pl.pallas_call(functools.partial(inner_kernel, heads), grid=(n,), in_spec...  7.78 us
  transfers between devices with their start and end apart: 23, of which 8 were waited for; matrix products, arithmetic and copies ran while one was open for 0% of the time, Pallas kernels for 47%

profile of v4, /device:TPU:0, one launch (start us, length us, event | category | flops | bytes accessed | tf_op | source)
XLA Modules:
  0.0 134.3 jit_solution(17948213774556813899)
XLA Ops:
  0.6 0.1 pad_add_fusion.place_ref
  0.7 2.1 %near_sends.1 = (bf16[16,4096]{1,0:T(8,128)(2,1)S(1)}, bf16[512,1024]{1,0:T(8,128)(2,1)S(1)}, bf16[512,1024]{1,0:T(8,128)(2,1)S(1)}) custom-call(s32[3]{0:T(128)S(1)} %pad_add_fusion.place_ref, bf16[512,4096]{1,0:T(8,128)(2,1)} %refs_8_.1, bf16[1024,4096]{1,0:T(8,128)(2,1)} %x_ref.7), custom_call_target="tpu_custom_call" | custom-call | flops 1000 | bytes 1048576 | tf_op jit(solution)/shard_map/near_sends/pallas_call | solution.py:519
  2.9 4.9 %collective-permute-start = (bf16[16,4096]{1,0:T(8,128)(2,1)S(1)}, bf16[16,4096]{1,0:T(8,128)(2,1)S(1)}, u32[]{:S(2)}, u32[]{:S(2)}) collective-permute-start(bf16[16,4096]{1,0:T(8,128)(2,1)S(1)} %get-tuple-element.62), channel_id=1, source_target_pairs={{0,8},{8,16},{16,24},{1,9},{9,17},{17,25},{2,10},{10,18},{18,26},{... | collective-permute-start | bytes 393224 | tf_op jit(solution)/shard_map/ppermute | solution.py:555
  7.8 1.6 %collective-permute-start.1 = (bf16[512,1024]{1,0:T(8,128)(2,1)S(1)}, bf16[512,1024]{1,0:T(8,128)(2,1)S(1)}, u32[]{:S(2)}, u32[]{:S(2)}) collective-permute-start(bf16[512,1024]{1,0:T(8,128)(2,1)S(1)} %get-tuple-element.68), channel_id=1, source_target_pairs={{0,2},{1,3},{2,0},{3,1},{4,6},{5,7},{6,4},{7,5},{8,10},{9,11},{10,... | collective-permute-start | bytes 3145736 | tf_op jit(solution)/shard_map/ppermute | solution.py:710
  9.4 0.0 copy-start.1
  9.4 0.0 copy-start.4
  9.4 0.0 copy-start.6
  9.4 1.6 %collective-permute-start.2 = (bf16[512,1024]{1,0:T(8,128)(2,1)S(1)}, bf16[512,1024]{1,0:T(8,128)(2,1)S(1)}, u32[]{:S(2)}, u32[]{:S(2)}) collective-permute-start(bf16[512,1024]{1,0:T(8,128)(2,1)S(1)} %get-tuple-element.69), channel_id=1, source_target_pairs={{0,4},{1,5},{2,6},{3,7},{4,0},{5,1},{6,2},{7,3},{8,12},{9,13},{10,... | collective-permute-start | bytes 3145736 | tf_op jit(solution)/shard_map/ppermute | solution.py:710
  11.0 3.3 %rest_sends.1 = (bf16[4,512,640]{2,1,0:T(8,128)(2,1)S(1)}, bf16[256,4096]{1,0:T(8,128)(2,1)S(1)}, bf16[512,1024]{1,0:T(8,128)(2,1)S(1)}) custom-call(s32[3]{0:T(128)S(1)} %pad_add_fusion.place_ref, bf16[512,4096]{1,0:T(8,128)(2,1)} %refs_8_.1, bf16[4096,640]{1,0:T(8,128)(2,1)} %w_ref.9, bf16[1024,4096]{1,0:T(8,128)(2,1)} %x_ref.7), custom_call_target="tpu_custom_call" | custom-call | flops 1000 | bytes 1048576 | tf_op jit(solution)/shard_map/rest_sends/pallas_call | solution.py:519
  14.3 0.1 collective-permute-start.3
  14.4 0.1 bitcast_multiply_fusion
  14.5 0.0 collective-permute-done.halo_ref
  14.5 0.0 copy-start
  14.6 13.6 %project.1 = (bf16[1024,512]{1,0:T(8,128)(2,1)S(1)}, bf16[4,1024,256]{2,1,0:T(8,128)(2,1)S(1)}, bf16[4,1024,256]{2,1,0:T(8,128)(2,1)S(1)}, bf16[4,1024,512]{2,1,...) custom-call(bf16[1024,4096]{1,0:T(8,128)(2,1)} %x_ref.7, ...), custom_call_target="tpu_custom_call" | custom-call | flops 107374182400 | bytes 1048576 | tf_op jit(solution)/shard_map/project/pallas_call | solution.py:206
  28.2 0.0 collective-permute-done.3.w_other_ref
  28.2 3.3 %collective-permute-start.6 = (bf16[4,160,128]{2,1,0:T(8,128)(2,1)S(1)}, bf16[4,160,128]{2,1,0:T(8,128)(2,1)S(1)}, u32[]{:S(2)}, u32[]{:S(2)}) collective-permute-start(bf16[4,160,128]{2,1,0:T(8,128)(2,1)S(1)} %get-tuple-element.85), channel_id=1, source_target_pairs={{0,24},{1,25},{2,26},{3,27},{4,28},{5,29},{6,30},{7,31}} | collective-permute-start | bytes 491528 | tf_op jit(solution)/shard_map/ppermute | solution.py:555
  31.5 1.8 %collective-permute-start.5 = (bf16[4,160,128]{2,1,0:T(8,128)(2,1)S(1)}, bf16[4,160,128]{2,1,0:T(8,128)(2,1)S(1)}, u32[]{:S(2)}, u32[]{:S(2)}) collective-permute-start(bf16[4,160,128]{2,1,0:T(8,128)(2,1)S(1)} %get-tuple-element.85), channel_id=1, source_target_pairs={{0,16},{8,24},{1,17},{9,25},{2,18},{10,26},{3,19},{11,27},{4,20},{... | collective-permute-start | bytes 491528 | tf_op jit(solution)/shard_map/ppermute | solution.py:555
  33.4 1.9 %collective-permute-start.4 = (bf16[4,160,128]{2,1,0:T(8,128)(2,1)S(1)}, bf16[4,160,128]{2,1,0:T(8,128)(2,1)S(1)}, u32[]{:S(2)}, u32[]{:S(2)}) collective-permute-start(bf16[4,160,128]{2,1,0:T(8,128)(2,1)S(1)} %get-tuple-element.85), channel_id=1, source_target_pairs={{0,8},{8,16},{16,24},{1,9},{9,17},{17,25},{2,10},{10,18},{18,26},{... | collective-permute-start | bytes 491528 | tf_op jit(solution)/shard_map/ppermute | solution.py:555
  35.3 0.0 collective-permute-done.1.refs_9_
  35.3 0.0 copy-start.8
  35.4 0.0 copy-start.9
  35.4 1.6 %collective-permute-start.7 = (bf16[512,1024]{1,0:T(8,128)(2,1)S(1)}, bf16[512,1024]{1,0:T(8,128)(2,1)S(1)}, u32[]{:S(2)}, u32[]{:S(2)}) collective-permute-start(bf16[512,1024]{1,0:T(8,128)(2,1)S(1)} %get-tuple-element.88), channel_id=1, source_target_pairs={{0,6},{1,7},{2,4},{3,5},{4,2},{5,3},{6,0},{7,1},{8,14},{9,15},{10,... | collective-permute-start | bytes 3145736 | tf_op jit(solution)/shard_map/ppermute | solution.py:710
  37.0 8.0 %local_part.1 = (f32[1024,512]{1,0:T(8,128)S(1)}, f32[1024,512]{1,0:T(8,128)S(1)}, bf16[4,1024,256]{2,1,0:T(8,128)(2,1)S(1)}, bf16[4,1024,256]{2,1,0:T(8,128)(2,1)S(1)}) custom-call(bf16[1024,4096]{1,0:T(8,128)(2,1)} %ct_ref.5, bf16[256,4096]{1,0:T(8,128)(2,1)S(1)} %get-tuple-element.76.ct_first_ref, bf16[512,4096]{1,0:T(8,128)(2,1)S(1)} %copy-done, ...), custom_call_target="tpu_custom_call" | custom-call | flops 1000 | bytes 1048576 | tf_op jit(solution)/shard_map/local_part/pallas_call | solution.py:267
  45.0 0.0 collective-permute-done.6.refs_2_
  45.1 0.0 collective-permute-done.4.refs_0_
  45.1 5.2 %norm_part.1 = (bf16[1024,512]{1,0:T(8,128)(2,1)S(1)}, bf16[1024,512]{1,0:T(8,128)(2,1)S(1)}, bf16[4,4,128,256]{3,2,1,0:T(8,128)(2,1)S(1)}, bf16[4,160,128]{2,1,0:T(8,128)(2,1)S(1)}, bf16[4,160,128]{2,1,0:T(8,128)(2,1)S(1)}) custom-call(f32[1024,512]{1,0:T(8,128)S(1)} %get-tuple-element.81.g_ref, f32[1024,512]{1,0:T(8,128)S(1)} %get-tuple-element.82.num_ref, ...), custom_call_target="tpu_custom_call" | custom-call | flops 17179869184 | bytes 1048576 | tf_op jit(solution)/shard_map/norm_part/pallas_call | solution.py:321
  50.3 1.3 collective-permute-start.10
  51.6 1.3 collective-permute-start.9
  52.9 1.5 %collective-permute-start.8 = (bf16[4,160,128]{2,1,0:T(8,128)(2,1)S(1)}, bf16[4,160,128]{2,1,0:T(8,128)(2,1)S(1)}, u32[]{:S(2)}, u32[]{:S(2)}) collective-permute-start(bf16[4,160,128]{2,1,0:T(8,128)(2,1)S(1)} %get-tuple-element.94), channel_id=1, source_target_pairs={{8,0},{16,8},{24,16},{9,1},{17,9},{25,17},{10,2},{18,10},{26,18},{... | collective-permute-start | bytes 491528 | tf_op jit(solution)/shard_map/ppermute | solution.py:555
  54.3 0.6 collective-permute-start.17
  55.0 6.5 %collective-permute-done.7.refs_11_ = bf16[512,1024]{1,0:T(8,128)(2,1)S(1)} collective-permute-done((bf16[512,1024]{1,0:T(8,128)(2,1)S(1)}, bf16[512,1024]{1,0:T(8,128)(2,1)S(1)}, u32[]{:S(2)}, u32[]{:S(2)}) %collective-permute-start.7) | collective-permute-done | bytes 1048608 | tf_op jit(solution)/shard_map/ppermute | solution.py:710
  61.4 0.5 collective-permute-start.16
  62.0 7.8 %inner_part.1 = (f32[1024,128]{1,0:T(8,128)S(1)}, f32[1024,512]{1,0:T(8,128)S(1)}, f32[4,1024,128]{2,1,0:T(8,128)S(1)}) custom-call(bf16[1024,512]{1,0:T(8,128)(2,1)S(1)} %get-tuple-element.71.v_ref.refs_3_, bf16[4,1024,256]{2,1,0:T(8,128)(2,1)S(1)} %get-tuple-element.74.pq_ref, bf16[4,1024,256]{2,1,0:T(8,128)(2,1)S(1)} %get-tuple-element.72.pk_ref.refs_4_, ...), custom_call_target="tpu_custom_call" | custom-call | flops 1000 | bytes 1048576 | tf_op jit(solution)/shard_map/inner_part/pallas_call | solution.py:376
  69.8 0.0 collective-permute-done.9.refs_1_
  69.8 0.0 collective-permute-done.8.refs_0_
  69.8 3.9 %outer_part.1 = (bf16[512,640]{1,0:T(8,128)(2,1)S(1)}, bf16[1024,640]{1,0:T(8,128)(2,1)S(1)}, f32[8,640]{1,0:T(8,128)S(1)}, f32[16,640]{1,0:T(8,128)S(1)}) custom-call(bf16[1024,512]{1,0:T(8,128)(2,1)S(1)} %get-tuple-element.71.v_ref.refs_3_, bf16[4,1024,256]{2,1,0:T(8,128)(2,1)S(1)} %get-tuple-element.72.pk_ref.refs_4_, ...), custom_call_target="tpu_custom_call" | custom-call | flops 17179869184 | bytes 1048576 | tf_op jit(solution)/shard_map/outer_part/pallas_call | solution.py:465
  73.7 1.3 collective-permute-start.13
  75.0 0.1 collective-permute-start.11
  75.1 4.3 %collective-permute-done.13.after_ref = f32[8,640]{1,0:T(8,128)S(1)} collective-permute-done((f32[8,640]{1,0:T(8,128)S(1)}, f32[8,640]{1,0:T(8,128)S(1)}, u32[]{:S(2)}, u32[]{:S(2)}) %collective-permute-start.13) | collective-permute-done | bytes 20512 | tf_op jit(solution)/shard_map/ppermute | solution.py:555
  79.4 0.1 complete.1.dp_ref
  79.4 0.1 collective-permute-start.14
  79.5 4.3 %collective-permute-done.17.y_ref.refs_2_.refs_6_ = bf16[1024,512]{1,0:T(8,128)(2,1)S(1)} collective-permute-done((bf16[1024,512]{1,0:T(8,128)(2,1)S(1)}, bf16[1024,512]{1,0:T(8,128)(2,1)S(1)}, u32[]{:S(2)}, u32[]{:S(2)}) %collective-permute-start.17) | collective-permute-done | bytes 1048608 | tf_op jit(solution)/shard_map/ppermute | solution.py:710
  83.8 1.7 %collective-permute-done.16.x_ref.refs_1_.refs_5_ = bf16[1024,512]{1,0:T(8,128)(2,1)S(1)} collective-permute-done((bf16[1024,512]{1,0:T(8,128)(2,1)S(1)}, bf16[1024,512]{1,0:T(8,128)(2,1)S(1)}, u32[]{:S(2)}, u32[]{:S(2)}) %collective-permute-start.16) | collective-permute-done | bytes 1048608 | tf_op jit(solution)/shard_map/ppermute | solution.py:710
  85.5 0.1 halves.1
  85.5 1.1 collective-permute-start.18
  86.7 0.3 collective-permute-start.19
  87.0 0.0 collective-permute-done.11.other_ref
  87.0 4.4 %grad_part.2 = (bf16[2,512,512]{2,1,0:T(8,128)(2,1)S(1)}, bf16[2,512,512]{2,1,0:T(8,128)(2,1)S(1)}) custom-call(s32[3]{0:T(128)S(1)} %copy-done.3, bf16[512,640]{1,0:T(8,128)(2,1)S(1)} %get-tuple-element.95.dp_ref, bf16[512,640]{1,0:T(8,128)(2,1)S(1)} %collective-permute-done.11.other_ref, bf16[4096,640]{1,0:T(8,128)(2,1)S(1)} %bitcast.7, ...), custom_call_target="tpu_custom_call" | custom-call | flops 1000 | bytes 1048576 | tf_op jit(solution)/shard_map/grad_part/pallas_call | solution.py:673
  91.4 1.8 %collective-permute-start.12 = (bf16[2,512,512]{2,1,0:T(8,128)(2,1)S(1)}, bf16[2,512,512]{2,1,0:T(8,128)(2,1)S(1)}, u32[]{:S(2)}, u32[]{:S(2)}) collective-permute-start(bf16[2,512,512]{2,1,0:T(8,128)(2,1)S(1)} %get-tuple-element.98), channel_id=1, source_target_pairs={{0,2},{1,3},{2,0},{3,1},{4,6},{5,7},{6,4},{7,5},{8,10},{9,11},{10,... | collective-permute-start | bytes 3145736 | tf_op jit(solution)/shard_map/ppermute | solution.py:710
  93.2 4.4 %grad_part.3 = (bf16[2,512,512]{2,1,0:T(8,128)(2,1)S(1)}, bf16[2,512,512]{2,1,0:T(8,128)(2,1)S(1)}) custom-call(s32[3]{0:T(128)S(1)} %copy-done.3, bf16[512,640]{1,0:T(8,128)(2,1)S(1)} %complete.1.dp_ref, bf16[512,640]{1,0:T(8,128)(2,1)S(1)} %collective-permute-done.14.other_ref, bf16[4096,640]{1,0:T(8,128)(2,1)S(1)} %bitcast.7, ...), custom_call_target="tpu_custom_call" | custom-call | flops 1000 | bytes 1048576 | tf_op jit(solution)/shard_map/grad_part/pallas_call | solution.py:673
  97.7 1.0 collective-permute-start.15
  98.7 2.9 %collective-permute-done.19.refs_7_ = bf16[512,512]{1,0:T(8,128)(2,1)S(1)} collective-permute-done((bf16[512,512]{1,0:T(8,128)(2,1)S(1)}, bf16[512,512]{1,0:T(8,128)(2,1)S(1)}, u32[]{:S(2)}, u32[]{:S(2)}) %collective-permute-start.19) | collective-permute-done | bytes 524320 | tf_op jit(solution)/shard_map/ppermute | solution.py:710
  101.5 8.0 %out_part.1 = (bf16[1024,512]{1,0:T(8,128)(2,1)S(1)}, f32[1024,512]{1,0:T(8,128)S(1)}) custom-call(s32[3]{0:T(128)S(1)} %copy-done.3, bf16[1024,512]{1,0:T(8,128)(2,1)S(1)} %get-tuple-element.103.refs_0_.refs_4_, bf16[1024,512]{1,0:T(8,128)(2,1)S(1)} %collective-permute-done.16.x_ref.refs_1_.refs_5_, ...), custom_call_target="tpu_custom_call" | custom-call | flops 17179869184 | bytes 1048576 | tf_op jit(solution)/shard_map/out_part/pallas_call | solution.py:604
  109.5 0.1 collective-permute-start.22
  109.6 11.4 %collective-permute-done.12.refs_1_ = bf16[2,512,512]{2,1,0:T(8,128)(2,1)S(1)} collective-permute-done((bf16[2,512,512]{2,1,0:T(8,128)(2,1)S(1)}, bf16[2,512,512]{2,1,0:T(8,128)(2,1)S(1)}, u32[]{:S(2)}, u32[]{:S(2)}) %collective-permute-start.12) | collective-permute-done | bytes 1048608 | tf_op jit(solution)/shard_map/ppermute | solution.py:710
  121.1 0.1 passing.3
  121.2 0.6 collective-permute-start.21
  121.8 0.1 passing.2
  121.9 1.0 collective-permute-start.20
  122.9 2.1 %own_columns.1 = (bf16[1024,512]{1,0:T(8,128)(2,1)S(1)}, bf16[1024,512]{1,0:T(8,128)(2,1)S(1)}) custom-call(s32[3]{0:T(128)S(1)} %copy-done.3, bf16[1024,4096]{1,0:T(8,128)(2,1)} %x_ref.7, bf16[1024,4096]{1,0:T(8,128)(2,1)} %ct_ref.5), custom_call_target="tpu_custom_call" | custom-call | flops 1000 | bytes 1048576 | tf_op jit(solution)/shard_map/own_columns/pallas_call | solution.py:777
  125.0 1.4 %finish_out.1 = bf16[1024,512]{1,0:T(8,128)(2,1)} custom-call(bf16[1024,512]{1,0:T(8,128)(2,1)S(1)} %get-tuple-element.115.own_ref, f32[1024,512]{1,0:T(8,128)S(1)} %get-tuple-element.116.keep_ref, bf16[1024,512]{1,0:T(8,128)(2,1)S(1)} %collective-permute-done.22.got_ref), custom_call_target="tpu_custom_call" | custom-call | flops 1000 | bytes 1048576 | tf_op jit(solution)/shard_map/finish_out/pallas_call | solution.py:822
  126.4 5.9 %collective-permute-done.21.refs_5_ = bf16[1,512,512]{2,1,0:T(8,128)(2,1)S(1)} collective-permute-done((bf16[1,512,512]{2,1,0:T(8,128)(2,1)S(1)}, bf16[1,512,512]{2,1,0:T(8,128)(2,1)S(1)}, u32[]{:S(2)}, u32[]{:S(2)}) %collective-permute-start.21) | collective-permute-done | bytes 524320 | tf_op jit(solution)/shard_map/ppermute | solution.py:710
  132.3 0.6 collective-permute-done.20.refs_2_
  132.9 1.5 %finish.1 = bf16[1024,512]{1,0:T(8,128)(2,1)} custom-call(bf16[1024,512]{1,0:T(8,128)(2,1)S(1)} %get-tuple-element.119.own_ref, bf16[2,512,512]{2,1,0:T(8,128)(2,1)S(1)} %get-tuple-element.97.refs_0_, bf16[2,512,512]{2,1,0:T(8,128)(2,1)S(1)} %collective-permute-done.12.refs_1_, bf16[1,512,512]{2,1,0:T(8,128)(2,1)S(1)} %collective-permute-done.20.refs_2_, ...), custom_call_target="tpu_custom_call" | custom-call | flops 1000 | bytes 1048576 | tf_op jit(solution)/shard_map/finish/pallas_call | solution.py:807
  (31 shorter events, 0.1 us)
Async XLA Ops:
  0.7 10.3 %copy-start.2 = (s32[3]{0:T(128)}, s32[3]{0:T(128)S(1)}, u32[]{:S(2)}) copy-start(s32[3]{0:T(128)S(1)} %pad_add_fusion.place_ref) | copy-start | bytes 40
  2.9 11.6 %collective-permute-start = (bf16[16,4096]{1,0:T(8,128)(2,1)S(1)}, bf16[16,4096]{1,0:T(8,128)(2,1)S(1)}, u32[]{:S(2)}, u32[]{:S(2)}) collective-permute-start(bf16[16,4096]{1,0:T(8,128)(2,1)S(1)} %get-tuple-element.62), channel_id=1, source_target_pairs={{0,8},{8,16},{16,24},{1,9},{9,17},{17,25},{2,10},{10,18},{18,26},{... | collective-permute-start | bytes 393224 | tf_op jit(solution)/shard_map/ppermute | solution.py:555
  7.8 27.5 %collective-permute-start.1 = (bf16[512,1024]{1,0:T(8,128)(2,1)S(1)}, bf16[512,1024]{1,0:T(8,128)(2,1)S(1)}, u32[]{:S(2)}, u32[]{:S(2)}) collective-permute-start(bf16[512,1024]{1,0:T(8,128)(2,1)S(1)} %get-tuple-element.68), channel_id=1, source_target_pairs={{0,2},{1,3},{2,0},{3,1},{4,6},{5,7},{6,4},{7,5},{8,10},{9,11},{10,... | collective-permute-start | bytes 3145736 | tf_op jit(solution)/shard_map/ppermute | solution.py:710
  9.4 5.1 %slice-start = ((s8[5242880]{0:T(1024)(128)(4,1)}), s8[4194304]{0:T(1024)(128)(4,1)S(1)}, s32[]{:S(2)}) async-start(s8[5242880]{0:T(1024)(128)(4,1)} %bitcast.6), calls=%async_computation | async-start | bytes 8388608
  9.4 5.0 %copy-start.11 = (s32[4]{0:T(128)S(1)}, s32[4]{0:T(128)}, u32[]{:S(2)}) copy-start(s32[4]{0:T(128)} %param.16) | copy-start | bytes 52
  9.4 5.1 %copy-start.7 = (f32[512]{0:T(512)S(1)}, f32[512]{0:T(512)}, u32[]{:S(2)}) copy-start(f32[512]{0:T(512)} %param.14) | copy-start | bytes 6148
  9.4 5.1 %slice-start.1 = ((s8[5242880]{0:T(1024)(128)(4,1)}), s8[1048576]{0:T(1024)(128)(4,1)S(1)}, s32[]{:S(2)}) async-start(s8[5242880]{0:T(1024)(128)(4,1)} %bitcast.6), calls=%async_computation.1 | async-start | bytes 2097152
  9.4 5.1 %copy-start.1 = (bf16[4,128,1024]{2,1,0:T(8,128)(2,1)S(1)}, bf16[4,128,1024]{2,1,0:T(8,128)(2,1)}, u32[]{:S(2)}) copy-start(bf16[4,128,1024]{2,1,0:T(8,128)(2,1)} %constant.34.clone.sel_ref.refs_10_) | copy-start | bytes 3145732
  9.4 5.1 %copy-start.4 = (f32[3,640]{1,0:T(4,128)S(1)}, f32[3,640]{1,0:T(4,128)}, u32[]{:S(2)}) copy-start(f32[3,640]{1,0:T(4,128)} %cw_ref.5) | copy-start | bytes 23044
  9.4 5.1 %copy-start.6 = (f32[8,256]{1,0:T(8,128)S(1)}, f32[8,256]{1,0:T(8,128)}, u32[]{:S(2)}) copy-start(f32[8,256]{1,0:T(8,128)} %constant.35.clone.bias_ref) | copy-start | bytes 24580
  9.4 25.9 %collective-permute-start.2 = (bf16[512,1024]{1,0:T(8,128)(2,1)S(1)}, bf16[512,1024]{1,0:T(8,128)(2,1)S(1)}, u32[]{:S(2)}, u32[]{:S(2)}) collective-permute-start(bf16[512,1024]{1,0:T(8,128)(2,1)S(1)} %get-tuple-element.69), channel_id=1, source_target_pairs={{0,4},{1,5},{2,6},{3,7},{4,0},{5,1},{6,2},{7,3},{8,12},{9,13},{10,... | collective-permute-start | bytes 3145736 | tf_op jit(solution)/shard_map/ppermute | solution.py:710
  14.3 13.9 %collective-permute-start.3 = (bf16[4,512,640]{2,1,0:T(8,128)(2,1)S(1)}, bf16[4,512,640]{2,1,0:T(8,128)(2,1)S(1)}, u32[]{:S(2)}, u32[]{:S(2)}) collective-permute-start(bf16[4,512,640]{2,1,0:T(8,128)(2,1)S(1)} %get-tuple-element.84), channel_id=1, source_target_pairs={{0,1},{1,0},{2,3},{3,2},{4,5},{5,4},{6,7},{7,6},{8,9},{9,8},{10,11... | collective-permute-start | bytes 7864328 | tf_op jit(solution)/shard_map/ppermute | solution.py:710
  14.5 22.5 %copy-start = (bf16[512,4096]{1,0:T(8,128)(2,1)S(1)}, bf16[512,4096]{1,0:T(8,128)(2,1)}, u32[]{:S(2)}) copy-start(bf16[512,4096]{1,0:T(8,128)(2,1)} %refs_8_.1) | copy-start | bytes 12582916
  28.2 16.8 %collective-permute-start.6 = (bf16[4,160,128]{2,1,0:T(8,128)(2,1)S(1)}, bf16[4,160,128]{2,1,0:T(8,128)(2,1)S(1)}, u32[]{:S(2)}, u32[]{:S(2)}) collective-permute-start(bf16[4,160,128]{2,1,0:T(8,128)(2,1)S(1)} %get-tuple-element.85), channel_id=1, source_target_pairs={{0,24},{1,25},{2,26},{3,27},{4,28},{5,29},{6,30},{7,31}} | collective-permute-start | bytes 491528 | tf_op jit(solution)/shard_map/ppermute | solution.py:555
  31.5 13.5 %collective-permute-start.5 = (bf16[4,160,128]{2,1,0:T(8,128)(2,1)S(1)}, bf16[4,160,128]{2,1,0:T(8,128)(2,1)S(1)}, u32[]{:S(2)}, u32[]{:S(2)}) collective-permute-start(bf16[4,160,128]{2,1,0:T(8,128)(2,1)S(1)} %get-tuple-element.85), channel_id=1, source_target_pairs={{0,16},{8,24},{1,17},{9,25},{2,18},{10,26},{3,19},{11,27},{4,20},{... | collective-permute-start | bytes 491528 | tf_op jit(solution)/shard_map/ppermute | solution.py:555
  33.4 11.7 %collective-permute-start.4 = (bf16[4,160,128]{2,1,0:T(8,128)(2,1)S(1)}, bf16[4,160,128]{2,1,0:T(8,128)(2,1)S(1)}, u32[]{:S(2)}, u32[]{:S(2)}) collective-permute-start(bf16[4,160,128]{2,1,0:T(8,128)(2,1)S(1)} %get-tuple-element.85), channel_id=1, source_target_pairs={{0,8},{8,16},{16,24},{1,9},{9,17},{17,25},{2,10},{10,18},{18,26},{... | collective-permute-start | bytes 491528 | tf_op jit(solution)/shard_map/ppermute | solution.py:555
  35.3 9.7 %copy-start.8 = (bf16[512,1024]{1,0:T(8,128)(2,1)}, bf16[512,1024]{1,0:T(8,128)(2,1)S(1)}, u32[]{:S(2)}) copy-start(bf16[512,1024]{1,0:T(8,128)(2,1)S(1)} %collective-permute-done.1.refs_9_) | copy-start | bytes 3145732
  35.4 9.7 %copy-start.9 = (bf16[512,1024]{1,0:T(8,128)(2,1)}, bf16[512,1024]{1,0:T(8,128)(2,1)S(1)}, u32[]{:S(2)}) copy-start(bf16[512,1024]{1,0:T(8,128)(2,1)S(1)} %collective-permute-done.2.refs_10_) | copy-start | bytes 3145732
  35.4 26.0 %collective-permute-start.7 = (bf16[512,1024]{1,0:T(8,128)(2,1)S(1)}, bf16[512,1024]{1,0:T(8,128)(2,1)S(1)}, u32[]{:S(2)}, u32[]{:S(2)}) collective-permute-start(bf16[512,1024]{1,0:T(8,128)(2,1)S(1)} %get-tuple-element.88), channel_id=1, source_target_pairs={{0,6},{1,7},{2,4},{3,5},{4,2},{5,3},{6,0},{7,1},{8,14},{9,15},{10,... | collective-permute-start | bytes 3145736 | tf_op jit(solution)/shard_map/ppermute | solution.py:710
  37.0 8.1 %copy-start.5 = (bf16[256,256]{1,0:T(8,128)(2,1)S(1)}, bf16[256,256]{1,0:T(8,128)(2,1)}, u32[]{:S(2)}) copy-start(bf16[256,256]{1,0:T(8,128)(2,1)} %constant.36.clone.ones_ref) | copy-start | bytes 393220
  50.3 19.5 %collective-permute-start.10 = (bf16[4,160,128]{2,1,0:T(8,128)(2,1)S(1)}, bf16[4,160,128]{2,1,0:T(8,128)(2,1)S(1)}, u32[]{:S(2)}, u32[]{:S(2)}) collective-permute-start(bf16[4,160,128]{2,1,0:T(8,128)(2,1)S(1)} %get-tuple-element.94), channel_id=1, source_target_pairs={{24,0},{25,1},{26,2},{27,3},{28,4},{29,5},{30,6},{31,7}} | collective-permute-start | bytes 491528 | tf_op jit(solution)/shard_map/ppermute | solution.py:555
  51.6 18.2 %collective-permute-start.9 = (bf16[4,160,128]{2,1,0:T(8,128)(2,1)S(1)}, bf16[4,160,128]{2,1,0:T(8,128)(2,1)S(1)}, u32[]{:S(2)}, u32[]{:S(2)}) collective-permute-start(bf16[4,160,128]{2,1,0:T(8,128)(2,1)S(1)} %get-tuple-element.94), channel_id=1, source_target_pairs={{16,0},{24,8},{17,1},{25,9},{18,2},{26,10},{19,3},{27,11},{20,4},{... | collective-permute-start | bytes 491528 | tf_op jit(solution)/shard_map/ppermute | solution.py:555
  52.9 16.9 %collective-permute-start.8 = (bf16[4,160,128]{2,1,0:T(8,128)(2,1)S(1)}, bf16[4,160,128]{2,1,0:T(8,128)(2,1)S(1)}, u32[]{:S(2)}, u32[]{:S(2)}) collective-permute-start(bf16[4,160,128]{2,1,0:T(8,128)(2,1)S(1)} %get-tuple-element.94), channel_id=1, source_target_pairs={{8,0},{16,8},{24,16},{9,1},{17,9},{25,17},{10,2},{18,10},{26,18},{... | collective-permute-start | bytes 491528 | tf_op jit(solution)/shard_map/ppermute | solution.py:555
  54.3 29.4 %collective-permute-start.17 = (bf16[1024,512]{1,0:T(8,128)(2,1)S(1)}, bf16[1024,512]{1,0:T(8,128)(2,1)S(1)}, u32[]{:S(2)}, u32[]{:S(2)}) collective-permute-start(bf16[1024,512]{1,0:T(8,128)(2,1)S(1)} %get-tuple-element.103.refs_0_.refs_4_), channel_id=1, source_target_pairs={{0,4},{1,5},{2,6},{3,7},{4,0},{5,1},{6,2},{7,3},{8,12},{9,13},{10,... | collective-permute-start | bytes 3145736 | tf_op jit(solution)/shard_map/ppermute | solution.py:710
  61.4 8.3 %copy-start.10 = (bf16[512,1024]{1,0:T(8,128)(2,1)}, bf16[512,1024]{1,0:T(8,128)(2,1)S(1)}, u32[]{:S(2)}) copy-start(bf16[512,1024]{1,0:T(8,128)(2,1)S(1)} %collective-permute-done.7.refs_11_) | copy-start | bytes 3145732
  61.4 24.1 %collective-permute-start.16 = (bf16[1024,512]{1,0:T(8,128)(2,1)S(1)}, bf16[1024,512]{1,0:T(8,128)(2,1)S(1)}, u32[]{:S(2)}, u32[]{:S(2)}) collective-permute-start(bf16[1024,512]{1,0:T(8,128)(2,1)S(1)} %get-tuple-element.103.refs_0_.refs_4_), channel_id=1, source_target_pairs={{0,2},{1,3},{2,0},{3,1},{4,6},{5,7},{6,4},{7,5},{8,10},{9,11},{10,... | collective-permute-start | bytes 3145736 | tf_op jit(solution)/shard_map/ppermute | solution.py:710
  73.7 13.3 %copy-start.3 = (s32[3]{0:T(128)S(1)}, s32[3]{0:T(128)}, u32[]{:S(2)}) copy-start(s32[3]{0:T(128)} %copy-done.2) | copy-start | bytes 40
  73.7 5.7 %collective-permute-start.13 = (f32[8,640]{1,0:T(8,128)S(1)}, f32[8,640]{1,0:T(8,128)S(1)}, u32[]{:S(2)}, u32[]{:S(2)}) collective-permute-start(f32[8,640]{1,0:T(8,128)S(1)} %get-tuple-element.101), channel_id=1, source_target_pairs={{8,0},{16,8},{24,16},{9,1},{17,9},{25,17},{10,2},{18,10},{26,18},{... | collective-permute-start | bytes 61448 | tf_op jit(solution)/shard_map/ppermute | solution.py:555
  75.0 12.0 %collective-permute-start.11 = (bf16[512,640]{1,0:T(8,128)(2,1)S(1)}, bf16[512,640]{1,0:T(8,128)(2,1)S(1)}, u32[]{:S(2)}, u32[]{:S(2)}) collective-permute-start(bf16[512,640]{1,0:T(8,128)(2,1)S(1)} %get-tuple-element.95.dp_ref), channel_id=1, source_target_pairs={{0,1},{1,0},{2,3},{3,2},{4,5},{5,4},{6,7},{7,6},{8,9},{9,8},{10,11... | collective-permute-start | bytes 1966088 | tf_op jit(solution)/shard_map/ppermute | solution.py:710
  79.4 13.8 %collective-permute-start.14 = (bf16[512,640]{1,0:T(8,128)(2,1)S(1)}, bf16[512,640]{1,0:T(8,128)(2,1)S(1)}, u32[]{:S(2)}, u32[]{:S(2)}) collective-permute-start(bf16[512,640]{1,0:T(8,128)(2,1)S(1)} %complete.1.dp_ref), channel_id=1, source_target_pairs={{0,1},{1,0},{2,3},{3,2},{4,5},{5,4},{6,7},{7,6},{8,9},{9,8},{10,11... | collective-permute-start | bytes 1966088 | tf_op jit(solution)/shard_map/ppermute | solution.py:710
  85.5 13.1 %collective-permute-start.18 = (bf16[512,512]{1,0:T(8,128)(2,1)S(1)}, bf16[512,512]{1,0:T(8,128)(2,1)S(1)}, u32[]{:S(2)}, u32[]{:S(2)}) collective-permute-start(bf16[512,512]{1,0:T(8,128)(2,1)S(1)} %get-tuple-element.104), channel_id=1, source_target_pairs={{0,4},{1,5},{2,6},{3,7},{4,0},{5,1},{6,2},{7,3},{8,12},{9,13},{10,... | collective-permute-start | bytes 1572872 | tf_op jit(solution)/shard_map/ppermute | solution.py:710
  86.7 14.9 %collective-permute-start.19 = (bf16[512,512]{1,0:T(8,128)(2,1)S(1)}, bf16[512,512]{1,0:T(8,128)(2,1)S(1)}, u32[]{:S(2)}, u32[]{:S(2)}) collective-permute-start(bf16[512,512]{1,0:T(8,128)(2,1)S(1)} %get-tuple-element.105), channel_id=1, source_target_pairs={{0,2},{1,3},{2,0},{3,1},{4,6},{5,7},{6,4},{7,5},{8,10},{9,11},{10,... | collective-permute-start | bytes 1572872 | tf_op jit(solution)/shard_map/ppermute | solution.py:710
  91.4 29.6 %collective-permute-start.12 = (bf16[2,512,512]{2,1,0:T(8,128)(2,1)S(1)}, bf16[2,512,512]{2,1,0:T(8,128)(2,1)S(1)}, u32[]{:S(2)}, u32[]{:S(2)}) collective-permute-start(bf16[2,512,512]{2,1,0:T(8,128)(2,1)S(1)} %get-tuple-element.98), channel_id=1, source_target_pairs={{0,2},{1,3},{2,0},{3,1},{4,6},{5,7},{6,4},{7,5},{8,10},{9,11},{10,... | collective-permute-start | bytes 3145736 | tf_op jit(solution)/shard_map/ppermute | solution.py:710
  97.7 23.4 %collective-permute-start.15 = (bf16[2,512,512]{2,1,0:T(8,128)(2,1)S(1)}, bf16[2,512,512]{2,1,0:T(8,128)(2,1)S(1)}, u32[]{:S(2)}, u32[]{:S(2)}) collective-permute-start(bf16[2,512,512]{2,1,0:T(8,128)(2,1)S(1)} %get-tuple-element.102), channel_id=1, source_target_pairs={{0,4},{1,5},{2,6},{3,7},{4,0},{5,1},{6,2},{7,3},{8,12},{9,13},{10,... | collective-permute-start | bytes 3145736 | tf_op jit(solution)/shard_map/ppermute | solution.py:710
  109.5 15.5 %collective-permute-start.22 = (bf16[1024,512]{1,0:T(8,128)(2,1)S(1)}, bf16[1024,512]{1,0:T(8,128)(2,1)S(1)}, u32[]{:S(2)}, u32[]{:S(2)}) collective-permute-start(bf16[1024,512]{1,0:T(8,128)(2,1)S(1)} %get-tuple-element.117), channel_id=1, source_target_pairs={{0,1},{1,0},{2,3},{3,2},{4,5},{5,4},{6,7},{7,6},{8,9},{9,8},{10,11... | collective-permute-start | bytes 3145736 | tf_op jit(solution)/shard_map/ppermute | solution.py:710
  121.2 11.1 %collective-permute-start.21 = (bf16[1,512,512]{2,1,0:T(8,128)(2,1)S(1)}, bf16[1,512,512]{2,1,0:T(8,128)(2,1)S(1)}, u32[]{:S(2)}, u32[]{:S(2)}) collective-permute-start(bf16[1,512,512]{2,1,0:T(8,128)(2,1)S(1)} %passing.3), channel_id=1, source_target_pairs={{0,2},{1,3},{2,0},{3,1},{4,6},{5,7},{6,4},{7,5},{8,10},{9,11},{10,... | collective-permute-start | bytes 1572872 | tf_op jit(solution)/shard_map/ppermute | solution.py:710
  121.9 11.0 %collective-permute-start.20 = (bf16[1,512,512]{2,1,0:T(8,128)(2,1)S(1)}, bf16[1,512,512]{2,1,0:T(8,128)(2,1)S(1)}, u32[]{:S(2)}, u32[]{:S(2)}) collective-permute-start(bf16[1,512,512]{2,1,0:T(8,128)(2,1)S(1)} %passing.2), channel_id=1, source_target_pairs={{0,4},{1,5},{2,6},{3,7},{4,0},{5,1},{6,2},{7,3},{8,12},{9,13},{10,... | collective-permute-start | bytes 1572872 | tf_op jit(solution)/shard_map/ppermute | solution.py:710

commit v5 on v4

--- a/solution.py
+++ b/solution.py
@@ -798,6 +798,30 @@
         for ref, place in zip(ins, places):
             total = total + ref[place].astype(F32)
         out_ref[first : first + half, :] = total.astype(BF)
+
+
+def partial_kernel(places, own_ref, *refs):
+    tops, lows, out_ref = refs[: len(places)], refs[len(places) : -1], refs[-1]
+    half = out_ref.shape[0] // 2
+    for first, ins in ((0, tops), (half, lows)):
+        total = own_ref[first : first + half, :].astype(F32)
+        for ref, place in zip(ins, places):
+            total = total + ref[place].astype(F32)
+        out_ref[first : first + half, :] = total
+
+
+def partial_sum(own, a_terms, b_terms):
+    places = [index[0] for _, index in a_terms]
+    terms = [array for array, _ in a_terms + b_terms]
+    return pl.pallas_call(
+        functools.partial(partial_kernel, places),
+        in_specs=[KEPT] * (1 + len(terms)),
+        out_specs=KEPT,
+        out_shape=kept(own.shape, F32),
+        compiler_params=pltpu.CompilerParams(vmem_limit_bytes=6 * MIB),
+        cost_estimate=LIGHT,
+        name="partial_sum",
+    )(*map(keep, [own] + terms))
 
 
 def finish(own, a_terms, b_terms):
@@ -889,7 +913,9 @@
         return a_got, b_got
 
     a_terms, b_terms = reduce_both(a_send, a_keep, b_send, b_keep, meanwhile)
-    return stage[4], finish(stage[1], a_terms, b_terms)
+    rest = partial_sum(stage[1], a_terms[:-1], b_terms[:-1])
+    rest, a_got, b_got = lax.optimization_barrier((rest, a_terms[-1][0], b_terms[-1][0]))
+    return stage[4], finish(rest, [(a_got, a_terms[-1][1])], [(b_got, b_terms[-1][1])])
 
 
 def solution(mesh):

time: 135 us -> 134 us (level)
  no operation moved by 1% of the time
where the time goes in v5:
time: 134 us
  Pallas kernels  66.2 us (49%)
  waiting for transfers between devices  37 us (28%)
  starting transfers between devices  29.4 us (22%)
    ppermute x15, waiting for transfers between devices, swapped(): return lax.ppermute(array, 'tp', [(i, i ^ distance) for i in range(count)])  32.7 us
    ppermute x8, starting transfers between devices, shifted(): return lax.ppermute(array, 'seq', pairs)  17.4 us
    pallas_call x1, Pallas kernels, project(): pl.pallas_call(functools.partial(project_kernel, heads), grid=(n,), in_sp...  13.6 us
    ppermute x15, starting transfers between devices, swapped(): return lax.ppermute(array, 'tp', [(i, i ^ distance) for i in range(count)])  12 us
    pallas_call x2, Pallas kernels, grad_part(): pl.pallas_call(functools.partial(grad_kernel, count, low_first), grid_spe...  8.86 us
    pallas_call x1, Pallas kernels, local_part(): pl.pallas_call(functools.partial(local_kernel, heads), grid=(n,), in_spec...  7.99 us
    pallas_call x1, Pallas kernels, out_part(): pl.pallas_call(functools.partial(out_kernel, count, sw), grid_spec=pltpu....  7.99 us
    pallas_call x1, Pallas kernels, inner_part(): pl.pallas_call(functools.partial(inner_kernel, heads), grid=(n,), in_spec...  7.78 us
  transfers between devices with their start and end apart: 23, of which 8 were waited for; matrix products, arithmetic and copies ran while one was open for 0% of the time, Pallas kernels for 47%

profile of v5, /device:TPU:0, one launch (start us, length us, event | category | flops | bytes accessed | tf_op | source)
XLA Modules:
  0.0 134.0 jit_solution(7037193824583518356)
XLA Ops:
  0.6 0.1 pad_add_fusion.place_ref
  0.7 2.1 %near_sends.1 = (bf16[16,4096]{1,0:T(8,128)(2,1)S(1)}, bf16[512,1024]{1,0:T(8,128)(2,1)S(1)}, bf16[512,1024]{1,0:T(8,128)(2,1)S(1)}) custom-call(s32[3]{0:T(128)S(1)} %pad_add_fusion.place_ref, bf16[512,4096]{1,0:T(8,128)(2,1)} %refs_8_.1, bf16[1024,4096]{1,0:T(8,128)(2,1)} %x_ref.7), custom_call_target="tpu_custom_call" | custom-call | flops 1000 | bytes 1048576 | tf_op jit(solution)/shard_map/near_sends/pallas_call | solution.py:519
  2.9 4.9 %collective-permute-start = (bf16[16,4096]{1,0:T(8,128)(2,1)S(1)}, bf16[16,4096]{1,0:T(8,128)(2,1)S(1)}, u32[]{:S(2)}, u32[]{:S(2)}) collective-permute-start(bf16[16,4096]{1,0:T(8,128)(2,1)S(1)} %get-tuple-element.65), channel_id=1, source_target_pairs={{0,8},{8,16},{16,24},{1,9},{9,17},{17,25},{2,10},{10,18},{18,26},{... | collective-permute-start | bytes 393224 | tf_op jit(solution)/shard_map/ppermute | solution.py:555
  7.8 1.6 %collective-permute-start.1 = (bf16[512,1024]{1,0:T(8,128)(2,1)S(1)}, bf16[512,1024]{1,0:T(8,128)(2,1)S(1)}, u32[]{:S(2)}, u32[]{:S(2)}) collective-permute-start(bf16[512,1024]{1,0:T(8,128)(2,1)S(1)} %get-tuple-element.71), channel_id=1, source_target_pairs={{0,2},{1,3},{2,0},{3,1},{4,6},{5,7},{6,4},{7,5},{8,10},{9,11},{10,... | collective-permute-start | bytes 3145736 | tf_op jit(solution)/shard_map/ppermute | solution.py:710
  9.4 0.0 copy-start.1
  9.4 0.0 copy-start.4
  9.4 0.0 copy-start.6
  9.4 1.6 %collective-permute-start.2 = (bf16[512,1024]{1,0:T(8,128)(2,1)S(1)}, bf16[512,1024]{1,0:T(8,128)(2,1)S(1)}, u32[]{:S(2)}, u32[]{:S(2)}) collective-permute-start(bf16[512,1024]{1,0:T(8,128)(2,1)S(1)} %get-tuple-element.72), channel_id=1, source_target_pairs={{0,4},{1,5},{2,6},{3,7},{4,0},{5,1},{6,2},{7,3},{8,12},{9,13},{10,... | collective-permute-start | bytes 3145736 | tf_op jit(solution)/shard_map/ppermute | solution.py:710
  11.0 3.3 %rest_sends.1 = (bf16[4,512,640]{2,1,0:T(8,128)(2,1)S(1)}, bf16[256,4096]{1,0:T(8,128)(2,1)S(1)}, bf16[512,1024]{1,0:T(8,128)(2,1)S(1)}) custom-call(s32[3]{0:T(128)S(1)} %pad_add_fusion.place_ref, bf16[512,4096]{1,0:T(8,128)(2,1)} %refs_8_.1, bf16[4096,640]{1,0:T(8,128)(2,1)} %w_ref.9, bf16[1024,4096]{1,0:T(8,128)(2,1)} %x_ref.7), custom_call_target="tpu_custom_call" | custom-call | flops 1000 | bytes 1048576 | tf_op jit(solution)/shard_map/rest_sends/pallas_call | solution.py:519
  14.3 0.1 collective-permute-start.3
  14.4 0.1 bitcast_multiply_fusion
  14.5 0.0 collective-permute-done.halo_ref
  14.5 0.0 copy-start
  14.6 13.6 %project.1 = (bf16[1024,512]{1,0:T(8,128)(2,1)S(1)}, bf16[4,1024,256]{2,1,0:T(8,128)(2,1)S(1)}, bf16[4,1024,256]{2,1,0:T(8,128)(2,1)S(1)}, bf16[4,1024,512]{2,1,...) custom-call(bf16[1024,4096]{1,0:T(8,128)(2,1)} %x_ref.7, ...), custom_call_target="tpu_custom_call" | custom-call | flops 107374182400 | bytes 1048576 | tf_op jit(solution)/shard_map/project/pallas_call | solution.py:206
  28.2 0.0 collective-permute-done.3.w_other_ref
  28.2 3.3 %collective-permute-start.6 = (bf16[4,160,128]{2,1,0:T(8,128)(2,1)S(1)}, bf16[4,160,128]{2,1,0:T(8,128)(2,1)S(1)}, u32[]{:S(2)}, u32[]{:S(2)}) collective-permute-start(bf16[4,160,128]{2,1,0:T(8,128)(2,1)S(1)} %get-tuple-element.88), channel_id=1, source_target_pairs={{0,24},{1,25},{2,26},{3,27},{4,28},{5,29},{6,30},{7,31}} | collective-permute-start | bytes 491528 | tf_op jit(solution)/shard_map/ppermute | solution.py:555
  31.5 1.8 %collective-permute-start.5 = (bf16[4,160,128]{2,1,0:T(8,128)(2,1)S(1)}, bf16[4,160,128]{2,1,0:T(8,128)(2,1)S(1)}, u32[]{:S(2)}, u32[]{:S(2)}) collective-permute-start(bf16[4,160,128]{2,1,0:T(8,128)(2,1)S(1)} %get-tuple-element.88), channel_id=1, source_target_pairs={{0,16},{8,24},{1,17},{9,25},{2,18},{10,26},{3,19},{11,27},{4,20},{... | collective-permute-start | bytes 491528 | tf_op jit(solution)/shard_map/ppermute | solution.py:555
  33.4 1.9 %collective-permute-start.4 = (bf16[4,160,128]{2,1,0:T(8,128)(2,1)S(1)}, bf16[4,160,128]{2,1,0:T(8,128)(2,1)S(1)}, u32[]{:S(2)}, u32[]{:S(2)}) collective-permute-start(bf16[4,160,128]{2,1,0:T(8,128)(2,1)S(1)} %get-tuple-element.88), channel_id=1, source_target_pairs={{0,8},{8,16},{16,24},{1,9},{9,17},{17,25},{2,10},{10,18},{18,26},{... | collective-permute-start | bytes 491528 | tf_op jit(solution)/shard_map/ppermute | solution.py:555
  35.3 0.0 collective-permute-done.1.refs_9_
  35.3 0.0 copy-start.8
  35.4 0.0 copy-start.9
  35.4 1.6 %collective-permute-start.7 = (bf16[512,1024]{1,0:T(8,128)(2,1)S(1)}, bf16[512,1024]{1,0:T(8,128)(2,1)S(1)}, u32[]{:S(2)}, u32[]{:S(2)}) collective-permute-start(bf16[512,1024]{1,0:T(8,128)(2,1)S(1)} %get-tuple-element.91), channel_id=1, source_target_pairs={{0,6},{1,7},{2,4},{3,5},{4,2},{5,3},{6,0},{7,1},{8,14},{9,15},{10,... | collective-permute-start | bytes 3145736 | tf_op jit(solution)/shard_map/ppermute | solution.py:710
  37.0 8.0 %local_part.1 = (f32[1024,512]{1,0:T(8,128)S(1)}, f32[1024,512]{1,0:T(8,128)S(1)}, bf16[4,1024,256]{2,1,0:T(8,128)(2,1)S(1)}, bf16[4,1024,256]{2,1,0:T(8,128)(2,1)S(1)}) custom-call(bf16[1024,4096]{1,0:T(8,128)(2,1)} %ct_ref.5, bf16[256,4096]{1,0:T(8,128)(2,1)S(1)} %get-tuple-element.79.ct_first_ref, bf16[512,4096]{1,0:T(8,128)(2,1)S(1)} %copy-done, ...), custom_call_target="tpu_custom_call" | custom-call | flops 1000 | bytes 1048576 | tf_op jit(solution)/shard_map/local_part/pallas_call | solution.py:267
  45.0 0.0 collective-permute-done.6.refs_2_
  45.1 0.0 collective-permute-done.4.refs_0_
  45.1 5.2 %norm_part.1 = (bf16[1024,512]{1,0:T(8,128)(2,1)S(1)}, bf16[1024,512]{1,0:T(8,128)(2,1)S(1)}, bf16[4,4,128,256]{3,2,1,0:T(8,128)(2,1)S(1)}, bf16[4,160,128]{2,1,0:T(8,128)(2,1)S(1)}, bf16[4,160,128]{2,1,0:T(8,128)(2,1)S(1)}) custom-call(f32[1024,512]{1,0:T(8,128)S(1)} %get-tuple-element.84.g_ref, f32[1024,512]{1,0:T(8,128)S(1)} %get-tuple-element.85.num_ref, ...), custom_call_target="tpu_custom_call" | custom-call | flops 17179869184 | bytes 1048576 | tf_op jit(solution)/shard_map/norm_part/pallas_call | solution.py:321
  50.3 1.3 collective-permute-start.10
  51.6 1.3 collective-permute-start.9
  52.9 1.5 %collective-permute-start.8 = (bf16[4,160,128]{2,1,0:T(8,128)(2,1)S(1)}, bf16[4,160,128]{2,1,0:T(8,128)(2,1)S(1)}, u32[]{:S(2)}, u32[]{:S(2)}) collective-permute-start(bf16[4,160,128]{2,1,0:T(8,128)(2,1)S(1)} %get-tuple-element.97), channel_id=1, source_target_pairs={{8,0},{16,8},{24,16},{9,1},{17,9},{25,17},{10,2},{18,10},{26,18},{... | collective-permute-start | bytes 491528 | tf_op jit(solution)/shard_map/ppermute | solution.py:555
  54.3 0.6 collective-permute-start.17
  55.0 6.5 %collective-permute-done.7.refs_11_ = bf16[512,1024]{1,0:T(8,128)(2,1)S(1)} collective-permute-done((bf16[512,1024]{1,0:T(8,128)(2,1)S(1)}, bf16[512,1024]{1,0:T(8,128)(2,1)S(1)}, u32[]{:S(2)}, u32[]{:S(2)}) %collective-permute-start.7) | collective-permute-done | bytes 1048608 | tf_op jit(solution)/shard_map/ppermute | solution.py:710
  61.4 0.5 collective-permute-start.16
  62.0 7.8 %inner_part.1 = (f32[1024,128]{1,0:T(8,128)S(1)}, f32[1024,512]{1,0:T(8,128)S(1)}, f32[4,1024,128]{2,1,0:T(8,128)S(1)}) custom-call(bf16[1024,512]{1,0:T(8,128)(2,1)S(1)} %get-tuple-element.74.v_ref.refs_3_, bf16[4,1024,256]{2,1,0:T(8,128)(2,1)S(1)} %get-tuple-element.77.pq_ref, bf16[4,1024,256]{2,1,0:T(8,128)(2,1)S(1)} %get-tuple-element.75.pk_ref.refs_4_, ...), custom_call_target="tpu_custom_call" | custom-call | flops 1000 | bytes 1048576 | tf_op jit(solution)/shard_map/inner_part/pallas_call | solution.py:376
  69.8 0.0 collective-permute-done.9.refs_1_
  69.8 0.0 collective-permute-done.8.refs_0_
  69.8 3.9 %outer_part.1 = (bf16[512,640]{1,0:T(8,128)(2,1)S(1)}, bf16[1024,640]{1,0:T(8,128)(2,1)S(1)}, f32[8,640]{1,0:T(8,128)S(1)}, f32[16,640]{1,0:T(8,128)S(1)}) custom-call(bf16[1024,512]{1,0:T(8,128)(2,1)S(1)} %get-tuple-element.74.v_ref.refs_3_, bf16[4,1024,256]{2,1,0:T(8,128)(2,1)S(1)} %get-tuple-element.75.pk_ref.refs_4_, ...), custom_call_target="tpu_custom_call" | custom-call | flops 17179869184 | bytes 1048576 | tf_op jit(solution)/shard_map/outer_part/pallas_call | solution.py:465
  73.7 1.3 collective-permute-start.13
  75.0 0.1 collective-permute-start.11
  75.1 4.3 %collective-permute-done.13.after_ref = f32[8,640]{1,0:T(8,128)S(1)} collective-permute-done((f32[8,640]{1,0:T(8,128)S(1)}, f32[8,640]{1,0:T(8,128)S(1)}, u32[]{:S(2)}, u32[]{:S(2)}) %collective-permute-start.13) | collective-permute-done | bytes 20512 | tf_op jit(solution)/shard_map/ppermute | solution.py:555
  79.4 0.1 complete.1.dp_ref
  79.4 0.1 collective-permute-start.14
  79.5 4.3 %collective-permute-done.17.y_ref.refs_2_.refs_6_ = bf16[1024,512]{1,0:T(8,128)(2,1)S(1)} collective-permute-done((bf16[1024,512]{1,0:T(8,128)(2,1)S(1)}, bf16[1024,512]{1,0:T(8,128)(2,1)S(1)}, u32[]{:S(2)}, u32[]{:S(2)}) %collective-permute-start.17) | collective-permute-done | bytes 1048608 | tf_op jit(solution)/shard_map/ppermute | solution.py:710
  83.8 1.7 %collective-permute-done.16.x_ref.refs_1_.refs_5_ = bf16[1024,512]{1,0:T(8,128)(2,1)S(1)} collective-permute-done((bf16[1024,512]{1,0:T(8,128)(2,1)S(1)}, bf16[1024,512]{1,0:T(8,128)(2,1)S(1)}, u32[]{:S(2)}, u32[]{:S(2)}) %collective-permute-start.16) | collective-permute-done | bytes 1048608 | tf_op jit(solution)/shard_map/ppermute | solution.py:710
  85.5 0.1 halves.1
  85.5 1.1 collective-permute-start.18
  86.7 0.3 collective-permute-start.19
  87.0 4.4 %grad_part.2 = (bf16[2,512,512]{2,1,0:T(8,128)(2,1)S(1)}, bf16[2,512,512]{2,1,0:T(8,128)(2,1)S(1)}) custom-call(s32[3]{0:T(128)S(1)} %copy-done.3, bf16[512,640]{1,0:T(8,128)(2,1)S(1)} %get-tuple-element.98.dp_ref, bf16[512,640]{1,0:T(8,128)(2,1)S(1)} %collective-permute-done.11.other_ref, bf16[4096,640]{1,0:T(8,128)(2,1)S(1)} %bitcast.7, ...), custom_call_target="tpu_custom_call" | custom-call | flops 1000 | bytes 1048576 | tf_op jit(solution)/shard_map/grad_part/pallas_call | solution.py:673
  91.4 1.8 %collective-permute-start.12 = (bf16[2,512,512]{2,1,0:T(8,128)(2,1)S(1)}, bf16[2,512,512]{2,1,0:T(8,128)(2,1)S(1)}, u32[]{:S(2)}, u32[]{:S(2)}) collective-permute-start(bf16[2,512,512]{2,1,0:T(8,128)(2,1)S(1)} %get-tuple-element.101), channel_id=1, source_target_pairs={{0,2},{1,3},{2,0},{3,1},{4,6},{5,7},{6,4},{7,5},{8,10},{9,11},{10,... | collective-permute-start | bytes 3145736 | tf_op jit(solution)/shard_map/ppermute | solution.py:710
  93.2 4.4 %grad_part.3 = (bf16[2,512,512]{2,1,0:T(8,128)(2,1)S(1)}, bf16[2,512,512]{2,1,0:T(8,128)(2,1)S(1)}) custom-call(s32[3]{0:T(128)S(1)} %copy-done.3, bf16[512,640]{1,0:T(8,128)(2,1)S(1)} %complete.1.dp_ref, bf16[512,640]{1,0:T(8,128)(2,1)S(1)} %collective-permute-done.14.other_ref, bf16[4096,640]{1,0:T(8,128)(2,1)S(1)} %bitcast.7, ...), custom_call_target="tpu_custom_call" | custom-call | flops 1000 | bytes 1048576 | tf_op jit(solution)/shard_map/grad_part/pallas_call | solution.py:673
  97.7 1.0 collective-permute-start.15
  98.7 2.9 %collective-permute-done.19.refs_7_ = bf16[512,512]{1,0:T(8,128)(2,1)S(1)} collective-permute-done((bf16[512,512]{1,0:T(8,128)(2,1)S(1)}, bf16[512,512]{1,0:T(8,128)(2,1)S(1)}, u32[]{:S(2)}, u32[]{:S(2)}) %collective-permute-start.19) | collective-permute-done | bytes 524320 | tf_op jit(solution)/shard_map/ppermute | solution.py:710
  101.5 8.0 %out_part.1 = (bf16[1024,512]{1,0:T(8,128)(2,1)S(1)}, f32[1024,512]{1,0:T(8,128)S(1)}) custom-call(s32[3]{0:T(128)S(1)} %copy-done.3, bf16[1024,512]{1,0:T(8,128)(2,1)S(1)} %get-tuple-element.106.refs_0_.refs_4_, bf16[1024,512]{1,0:T(8,128)(2,1)S(1)} %collective-permute-done.16.x_ref.refs_1_.refs_5_, ...), custom_call_target="tpu_custom_call" | custom-call | flops 17179869184 | bytes 1048576 | tf_op jit(solution)/shard_map/out_part/pallas_call | solution.py:604
  109.5 0.1 collective-permute-start.22
  109.6 11.4 %collective-permute-done.12.refs_1_ = bf16[2,512,512]{2,1,0:T(8,128)(2,1)S(1)} collective-permute-done((bf16[2,512,512]{2,1,0:T(8,128)(2,1)S(1)}, bf16[2,512,512]{2,1,0:T(8,128)(2,1)S(1)}, u32[]{:S(2)}, u32[]{:S(2)}) %collective-permute-start.12) | collective-permute-done | bytes 1048608 | tf_op jit(solution)/shard_map/ppermute | solution.py:710
  121.1 0.1 passing.3
  121.2 0.6 collective-permute-start.21
  121.8 0.1 passing.2
  121.9 1.0 collective-permute-start.20
  122.9 2.1 %own_columns.1 = (bf16[1024,512]{1,0:T(8,128)(2,1)S(1)}, bf16[1024,512]{1,0:T(8,128)(2,1)S(1)}) custom-call(s32[3]{0:T(128)S(1)} %copy-done.3, bf16[1024,4096]{1,0:T(8,128)(2,1)} %x_ref.7, bf16[1024,4096]{1,0:T(8,128)(2,1)} %ct_ref.5), custom_call_target="tpu_custom_call" | custom-call | flops 1000 | bytes 1048576 | tf_op jit(solution)/shard_map/own_columns/pallas_call | solution.py:777
  125.0 0.5 partial_sum.1.own_ref
  125.5 1.4 %finish_out.1 = bf16[1024,512]{1,0:T(8,128)(2,1)} custom-call(bf16[1024,512]{1,0:T(8,128)(2,1)S(1)} %get-tuple-element.118.own_ref, f32[1024,512]{1,0:T(8,128)S(1)} %get-tuple-element.119.keep_ref, bf16[1024,512]{1,0:T(8,128)(2,1)S(1)} %collective-permute-done.22.got_ref), custom_call_target="tpu_custom_call" | custom-call | flops 1000 | bytes 1048576 | tf_op jit(solution)/shard_map/finish_out/pallas_call | solution.py:846
  126.9 5.4 %collective-permute-done.21.refs_1_ = bf16[1,512,512]{2,1,0:T(8,128)(2,1)S(1)} collective-permute-done((bf16[1,512,512]{2,1,0:T(8,128)(2,1)S(1)}, bf16[1,512,512]{2,1,0:T(8,128)(2,1)S(1)}, u32[]{:S(2)}, u32[]{:S(2)}) %collective-permute-start.21) | collective-permute-done | bytes 524320 | tf_op jit(solution)/shard_map/ppermute | solution.py:710
  132.3 0.6 collective-permute-done.20.refs_0_
  132.9 1.1 finish.1
  (32 shorter events, 0.1 us)
Async XLA Ops:
  0.7 10.3 %copy-start.2 = (s32[3]{0:T(128)}, s32[3]{0:T(128)S(1)}, u32[]{:S(2)}) copy-start(s32[3]{0:T(128)S(1)} %pad_add_fusion.place_ref) | copy-start | bytes 40
  2.9 11.6 %collective-permute-start = (bf16[16,4096]{1,0:T(8,128)(2,1)S(1)}, bf16[16,4096]{1,0:T(8,128)(2,1)S(1)}, u32[]{:S(2)}, u32[]{:S(2)}) collective-permute-start(bf16[16,4096]{1,0:T(8,128)(2,1)S(1)} %get-tuple-element.65), channel_id=1, source_target_pairs={{0,8},{8,16},{16,24},{1,9},{9,17},{17,25},{2,10},{10,18},{18,26},{... | collective-permute-start | bytes 393224 | tf_op jit(solution)/shard_map/ppermute | solution.py:555
  7.8 27.5 %collective-permute-start.1 = (bf16[512,1024]{1,0:T(8,128)(2,1)S(1)}, bf16[512,1024]{1,0:T(8,128)(2,1)S(1)}, u32[]{:S(2)}, u32[]{:S(2)}) collective-permute-start(bf16[512,1024]{1,0:T(8,128)(2,1)S(1)} %get-tuple-element.71), channel_id=1, source_target_pairs={{0,2},{1,3},{2,0},{3,1},{4,6},{5,7},{6,4},{7,5},{8,10},{9,11},{10,... | collective-permute-start | bytes 3145736 | tf_op jit(solution)/shard_map/ppermute | solution.py:710
  9.4 5.1 %slice-start = ((s8[5242880]{0:T(1024)(128)(4,1)}), s8[4194304]{0:T(1024)(128)(4,1)S(1)}, s32[]{:S(2)}) async-start(s8[5242880]{0:T(1024)(128)(4,1)} %bitcast.6), calls=%async_computation | async-start | bytes 8388608
  9.4 5.0 %copy-start.11 = (s32[4]{0:T(128)S(1)}, s32[4]{0:T(128)}, u32[]{:S(2)}) copy-start(s32[4]{0:T(128)} %param.16) | copy-start | bytes 52
  9.4 5.1 %copy-start.7 = (f32[512]{0:T(512)S(1)}, f32[512]{0:T(512)}, u32[]{:S(2)}) copy-start(f32[512]{0:T(512)} %param.14) | copy-start | bytes 6148
  9.4 5.1 %slice-start.1 = ((s8[5242880]{0:T(1024)(128)(4,1)}), s8[1048576]{0:T(1024)(128)(4,1)S(1)}, s32[]{:S(2)}) async-start(s8[5242880]{0:T(1024)(128)(4,1)} %bitcast.6), calls=%async_computation.1 | async-start | bytes 2097152
  9.4 5.1 %copy-start.1 = (bf16[4,128,1024]{2,1,0:T(8,128)(2,1)S(1)}, bf16[4,128,1024]{2,1,0:T(8,128)(2,1)}, u32[]{:S(2)}) copy-start(bf16[4,128,1024]{2,1,0:T(8,128)(2,1)} %constant.34.clone.sel_ref.refs_10_) | copy-start | bytes 3145732
  9.4 5.1 %copy-start.4 = (f32[3,640]{1,0:T(4,128)S(1)}, f32[3,640]{1,0:T(4,128)}, u32[]{:S(2)}) copy-start(f32[3,640]{1,0:T(4,128)} %cw_ref.5) | copy-start | bytes 23044
  9.4 5.1 %copy-start.6 = (f32[8,256]{1,0:T(8,128)S(1)}, f32[8,256]{1,0:T(8,128)}, u32[]{:S(2)}) copy-start(f32[8,256]{1,0:T(8,128)} %constant.35.clone.bias_ref) | copy-start | bytes 24580
  9.4 25.9 %collective-permute-start.2 = (bf16[512,1024]{1,0:T(8,128)(2,1)S(1)}, bf16[512,1024]{1,0:T(8,128)(2,1)S(1)}, u32[]{:S(2)}, u32[]{:S(2)}) collective-permute-start(bf16[512,1024]{1,0:T(8,128)(2,1)S(1)} %get-tuple-element.72), channel_id=1, source_target_pairs={{0,4},{1,5},{2,6},{3,7},{4,0},{5,1},{6,2},{7,3},{8,12},{9,13},{10,... | collective-permute-start | bytes 3145736 | tf_op jit(solution)/shard_map/ppermute | solution.py:710
  14.3 13.9 %collective-permute-start.3 = (bf16[4,512,640]{2,1,0:T(8,128)(2,1)S(1)}, bf16[4,512,640]{2,1,0:T(8,128)(2,1)S(1)}, u32[]{:S(2)}, u32[]{:S(2)}) collective-permute-start(bf16[4,512,640]{2,1,0:T(8,128)(2,1)S(1)} %get-tuple-element.87), channel_id=1, source_target_pairs={{0,1},{1,0},{2,3},{3,2},{4,5},{5,4},{6,7},{7,6},{8,9},{9,8},{10,11... | collective-permute-start | bytes 7864328 | tf_op jit(solution)/shard_map/ppermute | solution.py:710
  14.5 22.5 %copy-start = (bf16[512,4096]{1,0:T(8,128)(2,1)S(1)}, bf16[512,4096]{1,0:T(8,128)(2,1)}, u32[]{:S(2)}) copy-start(bf16[512,4096]{1,0:T(8,128)(2,1)} %refs_8_.1) | copy-start | bytes 12582916
  28.2 16.8 %collective-permute-start.6 = (bf16[4,160,128]{2,1,0:T(8,128)(2,1)S(1)}, bf16[4,160,128]{2,1,0:T(8,128)(2,1)S(1)}, u32[]{:S(2)}, u32[]{:S(2)}) collective-permute-start(bf16[4,160,128]{2,1,0:T(8,128)(2,1)S(1)} %get-tuple-element.88), channel_id=1, source_target_pairs={{0,24},{1,25},{2,26},{3,27},{4,28},{5,29},{6,30},{7,31}} | collective-permute-start | bytes 491528 | tf_op jit(solution)/shard_map/ppermute | solution.py:555
  31.5 13.5 %collective-permute-start.5 = (bf16[4,160,128]{2,1,0:T(8,128)(2,1)S(1)}, bf16[4,160,128]{2,1,0:T(8,128)(2,1)S(1)}, u32[]{:S(2)}, u32[]{:S(2)}) collective-permute-start(bf16[4,160,128]{2,1,0:T(8,128)(2,1)S(1)} %get-tuple-element.88), channel_id=1, source_target_pairs={{0,16},{8,24},{1,17},{9,25},{2,18},{10,26},{3,19},{11,27},{4,20},{... | collective-permute-start | bytes 491528 | tf_op jit(solution)/shard_map/ppermute | solution.py:555
  33.4 11.7 %collective-permute-start.4 = (bf16[4,160,128]{2,1,0:T(8,128)(2,1)S(1)}, bf16[4,160,128]{2,1,0:T(8,128)(2,1)S(1)}, u32[]{:S(2)}, u32[]{:S(2)}) collective-permute-start(bf16[4,160,128]{2,1,0:T(8,128)(2,1)S(1)} %get-tuple-element.88), channel_id=1, source_target_pairs={{0,8},{8,16},{16,24},{1,9},{9,17},{17,25},{2,10},{10,18},{18,26},{... | collective-permute-start | bytes 491528 | tf_op jit(solution)/shard_map/ppermute | solution.py:555
  35.3 9.7 %copy-start.8 = (bf16[512,1024]{1,0:T(8,128)(2,1)}, bf16[512,1024]{1,0:T(8,128)(2,1)S(1)}, u32[]{:S(2)}) copy-start(bf16[512,1024]{1,0:T(8,128)(2,1)S(1)} %collective-permute-done.1.refs_9_) | copy-start | bytes 3145732
  35.4 9.7 %copy-start.9 = (bf16[512,1024]{1,0:T(8,128)(2,1)}, bf16[512,1024]{1,0:T(8,128)(2,1)S(1)}, u32[]{:S(2)}) copy-start(bf16[512,1024]{1,0:T(8,128)(2,1)S(1)} %collective-permute-done.2.refs_10_) | copy-start | bytes 3145732
  35.4 26.0 %collective-permute-start.7 = (bf16[512,1024]{1,0:T(8,128)(2,1)S(1)}, bf16[512,1024]{1,0:T(8,128)(2,1)S(1)}, u32[]{:S(2)}, u32[]{:S(2)}) collective-permute-start(bf16[512,1024]{1,0:T(8,128)(2,1)S(1)} %get-tuple-element.91), channel_id=1, source_target_pairs={{0,6},{1,7},{2,4},{3,5},{4,2},{5,3},{6,0},{7,1},{8,14},{9,15},{10,... | collective-permute-start | bytes 3145736 | tf_op jit(solution)/shard_map/ppermute | solution.py:710
  37.0 8.1 %copy-start.5 = (bf16[256,256]{1,0:T(8,128)(2,1)S(1)}, bf16[256,256]{1,0:T(8,128)(2,1)}, u32[]{:S(2)}) copy-start(bf16[256,256]{1,0:T(8,128)(2,1)} %constant.36.clone.ones_ref) | copy-start | bytes 393220
  50.3 19.5 %collective-permute-start.10 = (bf16[4,160,128]{2,1,0:T(8,128)(2,1)S(1)}, bf16[4,160,128]{2,1,0:T(8,128)(2,1)S(1)}, u32[]{:S(2)}, u32[]{:S(2)}) collective-permute-start(bf16[4,160,128]{2,1,0:T(8,128)(2,1)S(1)} %get-tuple-element.97), channel_id=1, source_target_pairs={{24,0},{25,1},{26,2},{27,3},{28,4},{29,5},{30,6},{31,7}} | collective-permute-start | bytes 491528 | tf_op jit(solution)/shard_map/ppermute | solution.py:555
  51.6 18.2 %collective-permute-start.9 = (bf16[4,160,128]{2,1,0:T(8,128)(2,1)S(1)}, bf16[4,160,128]{2,1,0:T(8,128)(2,1)S(1)}, u32[]{:S(2)}, u32[]{:S(2)}) collective-permute-start(bf16[4,160,128]{2,1,0:T(8,128)(2,1)S(1)} %get-tuple-element.97), channel_id=1, source_target_pairs={{16,0},{24,8},{17,1},{25,9},{18,2},{26,10},{19,3},{27,11},{20,4},{... | collective-permute-start | bytes 491528 | tf_op jit(solution)/shard_map/ppermute | solution.py:555
  52.9 16.9 %collective-permute-start.8 = (bf16[4,160,128]{2,1,0:T(8,128)(2,1)S(1)}, bf16[4,160,128]{2,1,0:T(8,128)(2,1)S(1)}, u32[]{:S(2)}, u32[]{:S(2)}) collective-permute-start(bf16[4,160,128]{2,1,0:T(8,128)(2,1)S(1)} %get-tuple-element.97), channel_id=1, source_target_pairs={{8,0},{16,8},{24,16},{9,1},{17,9},{25,17},{10,2},{18,10},{26,18},{... | collective-permute-start | bytes 491528 | tf_op jit(solution)/shard_map/ppermute | solution.py:555
  54.3 29.4 %collective-permute-start.17 = (bf16[1024,512]{1,0:T(8,128)(2,1)S(1)}, bf16[1024,512]{1,0:T(8,128)(2,1)S(1)}, u32[]{:S(2)}, u32[]{:S(2)}) collective-permute-start(bf16[1024,512]{1,0:T(8,128)(2,1)S(1)} %get-tuple-element.106.refs_0_.refs_4_), channel_id=1, source_target_pairs={{0,4},{1,5},{2,6},{3,7},{4,0},{5,1},{6,2},{7,3},{8,12},{9,13},{10,... | collective-permute-start | bytes 3145736 | tf_op jit(solution)/shard_map/ppermute | solution.py:710
  61.4 8.3 %copy-start.10 = (bf16[512,1024]{1,0:T(8,128)(2,1)}, bf16[512,1024]{1,0:T(8,128)(2,1)S(1)}, u32[]{:S(2)}) copy-start(bf16[512,1024]{1,0:T(8,128)(2,1)S(1)} %collective-permute-done.7.refs_11_) | copy-start | bytes 3145732
  61.4 24.1 %collective-permute-start.16 = (bf16[1024,512]{1,0:T(8,128)(2,1)S(1)}, bf16[1024,512]{1,0:T(8,128)(2,1)S(1)}, u32[]{:S(2)}, u32[]{:S(2)}) collective-permute-start(bf16[1024,512]{1,0:T(8,128)(2,1)S(1)} %get-tuple-element.106.refs_0_.refs_4_), channel_id=1, source_target_pairs={{0,2},{1,3},{2,0},{3,1},{4,6},{5,7},{6,4},{7,5},{8,10},{9,11},{10,... | collective-permute-start | bytes 3145736 | tf_op jit(solution)/shard_map/ppermute | solution.py:710
  73.7 13.3 %copy-start.3 = (s32[3]{0:T(128)S(1)}, s32[3]{0:T(128)}, u32[]{:S(2)}) copy-start(s32[3]{0:T(128)} %copy-done.2) | copy-start | bytes 40
  73.7 5.7 %collective-permute-start.13 = (f32[8,640]{1,0:T(8,128)S(1)}, f32[8,640]{1,0:T(8,128)S(1)}, u32[]{:S(2)}, u32[]{:S(2)}) collective-permute-start(f32[8,640]{1,0:T(8,128)S(1)} %get-tuple-element.104), channel_id=1, source_target_pairs={{8,0},{16,8},{24,16},{9,1},{17,9},{25,17},{10,2},{18,10},{26,18},{... | collective-permute-start | bytes 61448 | tf_op jit(solution)/shard_map/ppermute | solution.py:555
  75.0 12.0 %collective-permute-start.11 = (bf16[512,640]{1,0:T(8,128)(2,1)S(1)}, bf16[512,640]{1,0:T(8,128)(2,1)S(1)}, u32[]{:S(2)}, u32[]{:S(2)}) collective-permute-start(bf16[512,640]{1,0:T(8,128)(2,1)S(1)} %get-tuple-element.98.dp_ref), channel_id=1, source_target_pairs={{0,1},{1,0},{2,3},{3,2},{4,5},{5,4},{6,7},{7,6},{8,9},{9,8},{10,11... | collective-permute-start | bytes 1966088 | tf_op jit(solution)/shard_map/ppermute | solution.py:710
  79.4 13.8 %collective-permute-start.14 = (bf16[512,640]{1,0:T(8,128)(2,1)S(1)}, bf16[512,640]{1,0:T(8,128)(2,1)S(1)}, u32[]{:S(2)}, u32[]{:S(2)}) collective-permute-start(bf16[512,640]{1,0:T(8,128)(2,1)S(1)} %complete.1.dp_ref), channel_id=1, source_target_pairs={{0,1},{1,0},{2,3},{3,2},{4,5},{5,4},{6,7},{7,6},{8,9},{9,8},{10,11... | collective-permute-start | bytes 1966088 | tf_op jit(solution)/shard_map/ppermute | solution.py:710
  85.5 13.1 %collective-permute-start.18 = (bf16[512,512]{1,0:T(8,128)(2,1)S(1)}, bf16[512,512]{1,0:T(8,128)(2,1)S(1)}, u32[]{:S(2)}, u32[]{:S(2)}) collective-permute-start(bf16[512,512]{1,0:T(8,128)(2,1)S(1)} %get-tuple-element.107), channel_id=1, source_target_pairs={{0,4},{1,5},{2,6},{3,7},{4,0},{5,1},{6,2},{7,3},{8,12},{9,13},{10,... | collective-permute-start | bytes 1572872 | tf_op jit(solution)/shard_map/ppermute | solution.py:710
  86.7 14.9 %collective-permute-start.19 = (bf16[512,512]{1,0:T(8,128)(2,1)S(1)}, bf16[512,512]{1,0:T(8,128)(2,1)S(1)}, u32[]{:S(2)}, u32[]{:S(2)}) collective-permute-start(bf16[512,512]{1,0:T(8,128)(2,1)S(1)} %get-tuple-element.108), channel_id=1, source_target_pairs={{0,2},{1,3},{2,0},{3,1},{4,6},{5,7},{6,4},{7,5},{8,10},{9,11},{10,... | collective-permute-start | bytes 1572872 | tf_op jit(solution)/shard_map/ppermute | solution.py:710
  91.4 29.6 %collective-permute-start.12 = (bf16[2,512,512]{2,1,0:T(8,128)(2,1)S(1)}, bf16[2,512,512]{2,1,0:T(8,128)(2,1)S(1)}, u32[]{:S(2)}, u32[]{:S(2)}) collective-permute-start(bf16[2,512,512]{2,1,0:T(8,128)(2,1)S(1)} %get-tuple-element.101), channel_id=1, source_target_pairs={{0,2},{1,3},{2,0},{3,1},{4,6},{5,7},{6,4},{7,5},{8,10},{9,11},{10,... | collective-permute-start | bytes 3145736 | tf_op jit(solution)/shard_map/ppermute | solution.py:710
  97.7 23.4 %collective-permute-start.15 = (bf16[2,512,512]{2,1,0:T(8,128)(2,1)S(1)}, bf16[2,512,512]{2,1,0:T(8,128)(2,1)S(1)}, u32[]{:S(2)}, u32[]{:S(2)}) collective-permute-start(bf16[2,512,512]{2,1,0:T(8,128)(2,1)S(1)} %get-tuple-element.105), channel_id=1, source_target_pairs={{0,4},{1,5},{2,6},{3,7},{4,0},{5,1},{6,2},{7,3},{8,12},{9,13},{10,... | collective-permute-start | bytes 3145736 | tf_op jit(solution)/shard_map/ppermute | solution.py:710
  109.5 15.9 %collective-permute-start.22 = (bf16[1024,512]{1,0:T(8,128)(2,1)S(1)}, bf16[1024,512]{1,0:T(8,128)(2,1)S(1)}, u32[]{:S(2)}, u32[]{:S(2)}) collective-permute-start(bf16[1024,512]{1,0:T(8,128)(2,1)S(1)} %get-tuple-element.120), channel_id=1, source_target_pairs={{0,1},{1,0},{2,3},{3,2},{4,5},{5,4},{6,7},{7,6},{8,9},{9,8},{10,11... | collective-permute-start | bytes 3145736 | tf_op jit(solution)/shard_map/ppermute | solution.py:710
  121.2 11.1 %collective-permute-start.21 = (bf16[1,512,512]{2,1,0:T(8,128)(2,1)S(1)}, bf16[1,512,512]{2,1,0:T(8,128)(2,1)S(1)}, u32[]{:S(2)}, u32[]{:S(2)}) collective-permute-start(bf16[1,512,512]{2,1,0:T(8,128)(2,1)S(1)} %passing.3), channel_id=1, source_target_pairs={{0,2},{1,3},{2,0},{3,1},{4,6},{5,7},{6,4},{7,5},{8,10},{9,11},{10,... | collective-permute-start | bytes 1572872 | tf_op jit(solution)/shard_map/ppermute | solution.py:710
  121.9 11.0 %collective-permute-start.20 = (bf16[1,512,512]{2,1,0:T(8,128)(2,1)S(1)}, bf16[1,512,512]{2,1,0:T(8,128)(2,1)S(1)}, u32[]{:S(2)}, u32[]{:S(2)}) collective-permute-start(bf16[1,512,512]{2,1,0:T(8,128)(2,1)S(1)} %passing.2), channel_id=1, source_target_pairs={{0,4},{1,5},{2,6},{3,7},{4,0},{5,1},{6,2},{7,3},{8,12},{9,13},{10,... | collective-permute-start | bytes 1572872 | tf_op jit(solution)/shard_map/ppermute | solution.py:710

commit v6 on v5

--- a/solution.py
+++ b/solution.py
@@ -556,7 +556,8 @@
 
 
 def from_others(part, sign):
-    return [shifted(part, sign * step) for step in range(1, lax.axis_size("seq"))]
+    steps = range(1, lax.axis_size("seq"))
+    return [shifted(part, sign * step) for step in (steps if sign > 0 else reversed(steps))]
 
 
 def out_kernel(count, sw, place_ref, *refs):

time: 134 us -> 134 us (level)
    ppermute x8, waiting for transfers between devices: 4.32 us -> 6.17 us  [shifted(): return lax.ppermute(array, 'seq', pairs)]
    ppermute x15, waiting for transfers between devices: 32.7 us -> 30.9 us  [swapped(): return lax.ppermute(array, 'tp', [(i, i ^ distance) for i in range(count)])]
  transfers between devices with their start and end apart: 23 -> 23, of which waited for: 8 -> 9; matrix products, arithmetic and copies ran while one was open for 0% -> 0% of each run, Pallas kernels for 47% -> 47%
where the time goes in v6:
time: 134 us
  Pallas kernels  66.2 us (49%)
  waiting for transfers between devices  37.1 us (28%)
  starting transfers between devices  29.4 us (22%)
    ppermute x15, waiting for transfers between devices, swapped(): return lax.ppermute(array, 'tp', [(i, i ^ distance) for i in range(count)])  30.9 us
    ppermute x8, starting transfers between devices, shifted(): return lax.ppermute(array, 'seq', pairs)  17.4 us
    pallas_call x1, Pallas kernels, project(): pl.pallas_call(functools.partial(project_kernel, heads), grid=(n,), in_sp...  13.6 us
    ppermute x15, starting transfers between devices, swapped(): return lax.ppermute(array, 'tp', [(i, i ^ distance) for i in range(count)])  12 us
    pallas_call x2, Pallas kernels, grad_part(): pl.pallas_call(functools.partial(grad_kernel, count, low_first), grid_spe...  8.86 us
    pallas_call x1, Pallas kernels, local_part(): pl.pallas_call(functools.partial(local_kernel, heads), grid=(n,), in_spec...  7.99 us
    pallas_call x1, Pallas kernels, out_part(): pl.pallas_call(functools.partial(out_kernel, count, sw), grid_spec=pltpu....  7.99 us
    pallas_call x1, Pallas kernels, inner_part(): pl.pallas_call(functools.partial(inner_kernel, heads), grid=(n,), in_spec...  7.78 us
  transfers between devices with their start and end apart: 23, of which 9 were waited for; matrix products, arithmetic and copies ran while one was open for 0% of the time, Pallas kernels for 47%

profile of v6, /device:TPU:0, one launch (start us, length us, event | category | flops | bytes accessed | tf_op | source)
XLA Modules:
  0.0 134.0 jit_solution(12056153623895665081)
XLA Ops:
  0.6 0.1 pad_add_fusion.place_ref
  0.7 2.1 %near_sends.1 = (bf16[16,4096]{1,0:T(8,128)(2,1)S(1)}, bf16[512,1024]{1,0:T(8,128)(2,1)S(1)}, bf16[512,1024]{1,0:T(8,128)(2,1)S(1)}) custom-call(s32[3]{0:T(128)S(1)} %pad_add_fusion.place_ref, bf16[512,4096]{1,0:T(8,128)(2,1)} %refs_8_.1, bf16[1024,4096]{1,0:T(8,128)(2,1)} %x_ref.7), custom_call_target="tpu_custom_call" | custom-call | flops 1000 | bytes 1048576 | tf_op jit(solution)/shard_map/near_sends/pallas_call | solution.py:519
  2.9 4.9 %collective-permute-start = (bf16[16,4096]{1,0:T(8,128)(2,1)S(1)}, bf16[16,4096]{1,0:T(8,128)(2,1)S(1)}, u32[]{:S(2)}, u32[]{:S(2)}) collective-permute-start(bf16[16,4096]{1,0:T(8,128)(2,1)S(1)} %get-tuple-element.65), channel_id=1, source_target_pairs={{0,8},{8,16},{16,24},{1,9},{9,17},{17,25},{2,10},{10,18},{18,26},{... | collective-permute-start | bytes 393224 | tf_op jit(solution)/shard_map/ppermute | solution.py:555
  7.8 1.6 %collective-permute-start.1 = (bf16[512,1024]{1,0:T(8,128)(2,1)S(1)}, bf16[512,1024]{1,0:T(8,128)(2,1)S(1)}, u32[]{:S(2)}, u32[]{:S(2)}) collective-permute-start(bf16[512,1024]{1,0:T(8,128)(2,1)S(1)} %get-tuple-element.71), channel_id=1, source_target_pairs={{0,2},{1,3},{2,0},{3,1},{4,6},{5,7},{6,4},{7,5},{8,10},{9,11},{10,... | collective-permute-start | bytes 3145736 | tf_op jit(solution)/shard_map/ppermute | solution.py:711
  9.4 0.0 copy-start.1
  9.4 0.0 copy-start.4
  9.4 0.0 copy-start.6
  9.4 1.6 %collective-permute-start.2 = (bf16[512,1024]{1,0:T(8,128)(2,1)S(1)}, bf16[512,1024]{1,0:T(8,128)(2,1)S(1)}, u32[]{:S(2)}, u32[]{:S(2)}) collective-permute-start(bf16[512,1024]{1,0:T(8,128)(2,1)S(1)} %get-tuple-element.72), channel_id=1, source_target_pairs={{0,4},{1,5},{2,6},{3,7},{4,0},{5,1},{6,2},{7,3},{8,12},{9,13},{10,... | collective-permute-start | bytes 3145736 | tf_op jit(solution)/shard_map/ppermute | solution.py:711
  11.0 3.3 %rest_sends.1 = (bf16[4,512,640]{2,1,0:T(8,128)(2,1)S(1)}, bf16[256,4096]{1,0:T(8,128)(2,1)S(1)}, bf16[512,1024]{1,0:T(8,128)(2,1)S(1)}) custom-call(s32[3]{0:T(128)S(1)} %pad_add_fusion.place_ref, bf16[512,4096]{1,0:T(8,128)(2,1)} %refs_8_.1, bf16[4096,640]{1,0:T(8,128)(2,1)} %w_ref.9, bf16[1024,4096]{1,0:T(8,128)(2,1)} %x_ref.7), custom_call_target="tpu_custom_call" | custom-call | flops 1000 | bytes 1048576 | tf_op jit(solution)/shard_map/rest_sends/pallas_call | solution.py:519
  14.3 0.1 collective-permute-start.3
  14.4 0.1 bitcast_multiply_fusion
  14.5 0.0 collective-permute-done.halo_ref
  14.5 0.0 copy-start
  14.6 13.6 %project.1 = (bf16[1024,512]{1,0:T(8,128)(2,1)S(1)}, bf16[4,1024,256]{2,1,0:T(8,128)(2,1)S(1)}, bf16[4,1024,256]{2,1,0:T(8,128)(2,1)S(1)}, bf16[4,1024,512]{2,1,...) custom-call(bf16[1024,4096]{1,0:T(8,128)(2,1)} %x_ref.7, ...), custom_call_target="tpu_custom_call" | custom-call | flops 107374182400 | bytes 1048576 | tf_op jit(solution)/shard_map/project/pallas_call | solution.py:206
  28.2 0.0 collective-permute-done.3.w_other_ref
  28.2 3.3 %collective-permute-start.6 = (bf16[4,160,128]{2,1,0:T(8,128)(2,1)S(1)}, bf16[4,160,128]{2,1,0:T(8,128)(2,1)S(1)}, u32[]{:S(2)}, u32[]{:S(2)}) collective-permute-start(bf16[4,160,128]{2,1,0:T(8,128)(2,1)S(1)} %get-tuple-element.88), channel_id=1, source_target_pairs={{0,24},{1,25},{2,26},{3,27},{4,28},{5,29},{6,30},{7,31}} | collective-permute-start | bytes 491528 | tf_op jit(solution)/shard_map/ppermute | solution.py:555
  31.5 1.8 %collective-permute-start.5 = (bf16[4,160,128]{2,1,0:T(8,128)(2,1)S(1)}, bf16[4,160,128]{2,1,0:T(8,128)(2,1)S(1)}, u32[]{:S(2)}, u32[]{:S(2)}) collective-permute-start(bf16[4,160,128]{2,1,0:T(8,128)(2,1)S(1)} %get-tuple-element.88), channel_id=1, source_target_pairs={{0,16},{8,24},{1,17},{9,25},{2,18},{10,26},{3,19},{11,27},{4,20},{... | collective-permute-start | bytes 491528 | tf_op jit(solution)/shard_map/ppermute | solution.py:555
  33.4 1.9 %collective-permute-start.4 = (bf16[4,160,128]{2,1,0:T(8,128)(2,1)S(1)}, bf16[4,160,128]{2,1,0:T(8,128)(2,1)S(1)}, u32[]{:S(2)}, u32[]{:S(2)}) collective-permute-start(bf16[4,160,128]{2,1,0:T(8,128)(2,1)S(1)} %get-tuple-element.88), channel_id=1, source_target_pairs={{0,8},{8,16},{16,24},{1,9},{9,17},{17,25},{2,10},{10,18},{18,26},{... | collective-permute-start | bytes 491528 | tf_op jit(solution)/shard_map/ppermute | solution.py:555
  35.3 0.0 collective-permute-done.1.refs_9_
  35.3 0.0 copy-start.8
  35.4 0.0 copy-start.9
  35.4 1.6 %collective-permute-start.7 = (bf16[512,1024]{1,0:T(8,128)(2,1)S(1)}, bf16[512,1024]{1,0:T(8,128)(2,1)S(1)}, u32[]{:S(2)}, u32[]{:S(2)}) collective-permute-start(bf16[512,1024]{1,0:T(8,128)(2,1)S(1)} %get-tuple-element.91), channel_id=1, source_target_pairs={{0,6},{1,7},{2,4},{3,5},{4,2},{5,3},{6,0},{7,1},{8,14},{9,15},{10,... | collective-permute-start | bytes 3145736 | tf_op jit(solution)/shard_map/ppermute | solution.py:711
  37.0 8.0 %local_part.1 = (f32[1024,512]{1,0:T(8,128)S(1)}, f32[1024,512]{1,0:T(8,128)S(1)}, bf16[4,1024,256]{2,1,0:T(8,128)(2,1)S(1)}, bf16[4,1024,256]{2,1,0:T(8,128)(2,1)S(1)}) custom-call(bf16[1024,4096]{1,0:T(8,128)(2,1)} %ct_ref.5, bf16[256,4096]{1,0:T(8,128)(2,1)S(1)} %get-tuple-element.79.ct_first_ref, bf16[512,4096]{1,0:T(8,128)(2,1)S(1)} %copy-done, ...), custom_call_target="tpu_custom_call" | custom-call | flops 1000 | bytes 1048576 | tf_op jit(solution)/shard_map/local_part/pallas_call | solution.py:267
  45.0 0.0 collective-permute-done.6.refs_2_
  45.1 0.0 collective-permute-done.4.refs_0_
  45.1 5.2 %norm_part.1 = (bf16[1024,512]{1,0:T(8,128)(2,1)S(1)}, bf16[1024,512]{1,0:T(8,128)(2,1)S(1)}, bf16[4,4,128,256]{3,2,1,0:T(8,128)(2,1)S(1)}, bf16[4,160,128]{2,1,0:T(8,128)(2,1)S(1)}, bf16[4,160,128]{2,1,0:T(8,128)(2,1)S(1)}) custom-call(f32[1024,512]{1,0:T(8,128)S(1)} %get-tuple-element.84.g_ref, f32[1024,512]{1,0:T(8,128)S(1)} %get-tuple-element.85.num_ref, ...), custom_call_target="tpu_custom_call" | custom-call | flops 17179869184 | bytes 1048576 | tf_op jit(solution)/shard_map/norm_part/pallas_call | solution.py:321
  50.3 1.3 collective-permute-start.10
  51.6 1.3 collective-permute-start.9
  52.9 1.5 %collective-permute-start.8 = (bf16[4,160,128]{2,1,0:T(8,128)(2,1)S(1)}, bf16[4,160,128]{2,1,0:T(8,128)(2,1)S(1)}, u32[]{:S(2)}, u32[]{:S(2)}) collective-permute-start(bf16[4,160,128]{2,1,0:T(8,128)(2,1)S(1)} %get-tuple-element.97), channel_id=1, source_target_pairs={{24,0},{25,1},{26,2},{27,3},{28,4},{29,5},{30,6},{31,7}} | collective-permute-start | bytes 491528 | tf_op jit(solution)/shard_map/ppermute | solution.py:555
  54.3 0.6 collective-permute-start.17
  55.0 6.5 %collective-permute-done.7.refs_11_ = bf16[512,1024]{1,0:T(8,128)(2,1)S(1)} collective-permute-done((bf16[512,1024]{1,0:T(8,128)(2,1)S(1)}, bf16[512,1024]{1,0:T(8,128)(2,1)S(1)}, u32[]{:S(2)}, u32[]{:S(2)}) %collective-permute-start.7) | collective-permute-done | bytes 1048608 | tf_op jit(solution)/shard_map/ppermute | solution.py:711
  61.4 0.5 collective-permute-start.16
  62.0 7.8 %inner_part.1 = (f32[1024,128]{1,0:T(8,128)S(1)}, f32[1024,512]{1,0:T(8,128)S(1)}, f32[4,1024,128]{2,1,0:T(8,128)S(1)}) custom-call(bf16[1024,512]{1,0:T(8,128)(2,1)S(1)} %get-tuple-element.74.v_ref.refs_3_, bf16[4,1024,256]{2,1,0:T(8,128)(2,1)S(1)} %get-tuple-element.77.pq_ref, bf16[4,1024,256]{2,1,0:T(8,128)(2,1)S(1)} %get-tuple-element.75.pk_ref.refs_4_, ...), custom_call_target="tpu_custom_call" | custom-call | flops 1000 | bytes 1048576 | tf_op jit(solution)/shard_map/inner_part/pallas_call | solution.py:376
  69.8 1.9 %collective-permute-done.9.refs_1_ = bf16[4,160,128]{2,1,0:T(8,128)(2,1)S(1)} collective-permute-done((bf16[4,160,128]{2,1,0:T(8,128)(2,1)S(1)}, bf16[4,160,128]{2,1,0:T(8,128)(2,1)S(1)}, u32[]{:S(2)}, u32[]{:S(2)}) %collective-permute-start.9) | collective-permute-done | bytes 163872 | tf_op jit(solution)/shard_map/ppermute | solution.py:555
  71.6 3.9 %outer_part.1 = (bf16[512,640]{1,0:T(8,128)(2,1)S(1)}, bf16[1024,640]{1,0:T(8,128)(2,1)S(1)}, f32[8,640]{1,0:T(8,128)S(1)}, f32[16,640]{1,0:T(8,128)S(1)}) custom-call(bf16[1024,512]{1,0:T(8,128)(2,1)S(1)} %get-tuple-element.74.v_ref.refs_3_, bf16[4,1024,256]{2,1,0:T(8,128)(2,1)S(1)} %get-tuple-element.75.pk_ref.refs_4_, ...), custom_call_target="tpu_custom_call" | custom-call | flops 17179869184 | bytes 1048576 | tf_op jit(solution)/shard_map/outer_part/pallas_call | solution.py:465
  75.5 1.3 collective-permute-start.13
  76.8 0.1 collective-permute-start.11
  76.9 4.3 %collective-permute-done.13.after_ref = f32[8,640]{1,0:T(8,128)S(1)} collective-permute-done((f32[8,640]{1,0:T(8,128)S(1)}, f32[8,640]{1,0:T(8,128)S(1)}, u32[]{:S(2)}, u32[]{:S(2)}) %collective-permute-start.13) | collective-permute-done | bytes 20512 | tf_op jit(solution)/shard_map/ppermute | solution.py:555
  81.2 0.1 complete.1.dp_ref
  81.3 0.1 collective-permute-start.14
  81.3 2.5 %collective-permute-done.17.y_ref.refs_2_.refs_6_ = bf16[1024,512]{1,0:T(8,128)(2,1)S(1)} collective-permute-done((bf16[1024,512]{1,0:T(8,128)(2,1)S(1)}, bf16[1024,512]{1,0:T(8,128)(2,1)S(1)}, u32[]{:S(2)}, u32[]{:S(2)}) %collective-permute-start.17) | collective-permute-done | bytes 1048608 | tf_op jit(solution)/shard_map/ppermute | solution.py:711
  83.8 1.7 %collective-permute-done.16.x_ref.refs_1_.refs_5_ = bf16[1024,512]{1,0:T(8,128)(2,1)S(1)} collective-permute-done((bf16[1024,512]{1,0:T(8,128)(2,1)S(1)}, bf16[1024,512]{1,0:T(8,128)(2,1)S(1)}, u32[]{:S(2)}, u32[]{:S(2)}) %collective-permute-start.16) | collective-permute-done | bytes 1048608 | tf_op jit(solution)/shard_map/ppermute | solution.py:711
  85.5 0.1 halves.1
  85.5 1.1 collective-permute-start.18
  86.7 0.3 collective-permute-start.19
  87.0 0.0 collective-permute-done.11.other_ref
  87.0 4.4 %grad_part.2 = (bf16[2,512,512]{2,1,0:T(8,128)(2,1)S(1)}, bf16[2,512,512]{2,1,0:T(8,128)(2,1)S(1)}) custom-call(s32[3]{0:T(128)S(1)} %copy-done.3, bf16[512,640]{1,0:T(8,128)(2,1)S(1)} %get-tuple-element.98.dp_ref, bf16[512,640]{1,0:T(8,128)(2,1)S(1)} %collective-permute-done.11.other_ref, bf16[4096,640]{1,0:T(8,128)(2,1)S(1)} %bitcast.7, ...), custom_call_target="tpu_custom_call" | custom-call | flops 1000 | bytes 1048576 | tf_op jit(solution)/shard_map/grad_part/pallas_call | solution.py:674
  91.4 1.8 %collective-permute-start.12 = (bf16[2,512,512]{2,1,0:T(8,128)(2,1)S(1)}, bf16[2,512,512]{2,1,0:T(8,128)(2,1)S(1)}, u32[]{:S(2)}, u32[]{:S(2)}) collective-permute-start(bf16[2,512,512]{2,1,0:T(8,128)(2,1)S(1)} %get-tuple-element.101), channel_id=1, source_target_pairs={{0,2},{1,3},{2,0},{3,1},{4,6},{5,7},{6,4},{7,5},{8,10},{9,11},{10,... | collective-permute-start | bytes 3145736 | tf_op jit(solution)/shard_map/ppermute | solution.py:711
  93.2 4.4 %grad_part.3 = (bf16[2,512,512]{2,1,0:T(8,128)(2,1)S(1)}, bf16[2,512,512]{2,1,0:T(8,128)(2,1)S(1)}) custom-call(s32[3]{0:T(128)S(1)} %copy-done.3, bf16[512,640]{1,0:T(8,128)(2,1)S(1)} %complete.1.dp_ref, bf16[512,640]{1,0:T(8,128)(2,1)S(1)} %collective-permute-done.14.other_ref, bf16[4096,640]{1,0:T(8,128)(2,1)S(1)} %bitcast.7, ...), custom_call_target="tpu_custom_call" | custom-call | flops 1000 | bytes 1048576 | tf_op jit(solution)/shard_map/grad_part/pallas_call | solution.py:674
  97.7 1.0 collective-permute-start.15
  98.7 2.9 %collective-permute-done.19.refs_7_ = bf16[512,512]{1,0:T(8,128)(2,1)S(1)} collective-permute-done((bf16[512,512]{1,0:T(8,128)(2,1)S(1)}, bf16[512,512]{1,0:T(8,128)(2,1)S(1)}, u32[]{:S(2)}, u32[]{:S(2)}) %collective-permute-start.19) | collective-permute-done | bytes 524320 | tf_op jit(solution)/shard_map/ppermute | solution.py:711
  101.5 8.0 %out_part.1 = (bf16[1024,512]{1,0:T(8,128)(2,1)S(1)}, f32[1024,512]{1,0:T(8,128)S(1)}) custom-call(s32[3]{0:T(128)S(1)} %copy-done.3, bf16[1024,512]{1,0:T(8,128)(2,1)S(1)} %get-tuple-element.106.refs_0_.refs_4_, bf16[1024,512]{1,0:T(8,128)(2,1)S(1)} %collective-permute-done.16.x_ref.refs_1_.refs_5_, ...), custom_call_target="tpu_custom_call" | custom-call | flops 17179869184 | bytes 1048576 | tf_op jit(solution)/shard_map/out_part/pallas_call | solution.py:605
  109.5 0.1 collective-permute-start.22
  109.6 11.4 %collective-permute-done.12.refs_1_ = bf16[2,512,512]{2,1,0:T(8,128)(2,1)S(1)} collective-permute-done((bf16[2,512,512]{2,1,0:T(8,128)(2,1)S(1)}, bf16[2,512,512]{2,1,0:T(8,128)(2,1)S(1)}, u32[]{:S(2)}, u32[]{:S(2)}) %collective-permute-start.12) | collective-permute-done | bytes 1048608 | tf_op jit(solution)/shard_map/ppermute | solution.py:711
  121.1 0.1 passing.3
  121.2 0.6 collective-permute-start.21
  121.8 0.1 passing.2
  121.9 1.0 collective-permute-start.20
  122.9 2.1 %own_columns.1 = (bf16[1024,512]{1,0:T(8,128)(2,1)S(1)}, bf16[1024,512]{1,0:T(8,128)(2,1)S(1)}) custom-call(s32[3]{0:T(128)S(1)} %copy-done.3, bf16[1024,4096]{1,0:T(8,128)(2,1)} %x_ref.7, bf16[1024,4096]{1,0:T(8,128)(2,1)} %ct_ref.5), custom_call_target="tpu_custom_call" | custom-call | flops 1000 | bytes 1048576 | tf_op jit(solution)/shard_map/own_columns/pallas_call | solution.py:778
  125.0 0.5 partial_sum.1.own_ref
  125.5 1.4 %finish_out.1 = bf16[1024,512]{1,0:T(8,128)(2,1)} custom-call(bf16[1024,512]{1,0:T(8,128)(2,1)S(1)} %get-tuple-element.118.own_ref, f32[1024,512]{1,0:T(8,128)S(1)} %get-tuple-element.119.keep_ref, bf16[1024,512]{1,0:T(8,128)(2,1)S(1)} %collective-permute-done.22.got_ref), custom_call_target="tpu_custom_call" | custom-call | flops 1000 | bytes 1048576 | tf_op jit(solution)/shard_map/finish_out/pallas_call | solution.py:847
  126.9 5.4 %collective-permute-done.21.refs_1_ = bf16[1,512,512]{2,1,0:T(8,128)(2,1)S(1)} collective-permute-done((bf16[1,512,512]{2,1,0:T(8,128)(2,1)S(1)}, bf16[1,512,512]{2,1,0:T(8,128)(2,1)S(1)}, u32[]{:S(2)}, u32[]{:S(2)}) %collective-permute-start.21) | collective-permute-done | bytes 524320 | tf_op jit(solution)/shard_map/ppermute | solution.py:711
  132.3 0.6 collective-permute-done.20.refs_0_
  132.9 1.1 finish.1
  (32 shorter events, 0.1 us)
Async XLA Ops:
  0.7 10.3 %copy-start.2 = (s32[3]{0:T(128)}, s32[3]{0:T(128)S(1)}, u32[]{:S(2)}) copy-start(s32[3]{0:T(128)S(1)} %pad_add_fusion.place_ref) | copy-start | bytes 40
  2.9 11.6 %collective-permute-start = (bf16[16,4096]{1,0:T(8,128)(2,1)S(1)}, bf16[16,4096]{1,0:T(8,128)(2,1)S(1)}, u32[]{:S(2)}, u32[]{:S(2)}) collective-permute-start(bf16[16,4096]{1,0:T(8,128)(2,1)S(1)} %get-tuple-element.65), channel_id=1, source_target_pairs={{0,8},{8,16},{16,24},{1,9},{9,17},{17,25},{2,10},{10,18},{18,26},{... | collective-permute-start | bytes 393224 | tf_op jit(solution)/shard_map/ppermute | solution.py:555
  7.8 27.5 %collective-permute-start.1 = (bf16[512,1024]{1,0:T(8,128)(2,1)S(1)}, bf16[512,1024]{1,0:T(8,128)(2,1)S(1)}, u32[]{:S(2)}, u32[]{:S(2)}) collective-permute-start(bf16[512,1024]{1,0:T(8,128)(2,1)S(1)} %get-tuple-element.71), channel_id=1, source_target_pairs={{0,2},{1,3},{2,0},{3,1},{4,6},{5,7},{6,4},{7,5},{8,10},{9,11},{10,... | collective-permute-start | bytes 3145736 | tf_op jit(solution)/shard_map/ppermute | solution.py:711
  9.4 5.1 %slice-start = ((s8[5242880]{0:T(1024)(128)(4,1)}), s8[4194304]{0:T(1024)(128)(4,1)S(1)}, s32[]{:S(2)}) async-start(s8[5242880]{0:T(1024)(128)(4,1)} %bitcast.6), calls=%async_computation | async-start | bytes 8388608
  9.4 5.0 %copy-start.11 = (s32[4]{0:T(128)S(1)}, s32[4]{0:T(128)}, u32[]{:S(2)}) copy-start(s32[4]{0:T(128)} %param.16) | copy-start | bytes 52
  9.4 5.1 %copy-start.7 = (f32[512]{0:T(512)S(1)}, f32[512]{0:T(512)}, u32[]{:S(2)}) copy-start(f32[512]{0:T(512)} %param.14) | copy-start | bytes 6148
  9.4 5.1 %slice-start.1 = ((s8[5242880]{0:T(1024)(128)(4,1)}), s8[1048576]{0:T(1024)(128)(4,1)S(1)}, s32[]{:S(2)}) async-start(s8[5242880]{0:T(1024)(128)(4,1)} %bitcast.6), calls=%async_computation.1 | async-start | bytes 2097152
  9.4 5.1 %copy-start.1 = (bf16[4,128,1024]{2,1,0:T(8,128)(2,1)S(1)}, bf16[4,128,1024]{2,1,0:T(8,128)(2,1)}, u32[]{:S(2)}) copy-start(bf16[4,128,1024]{2,1,0:T(8,128)(2,1)} %constant.34.clone.sel_ref.refs_10_) | copy-start | bytes 3145732
  9.4 5.1 %copy-start.4 = (f32[3,640]{1,0:T(4,128)S(1)}, f32[3,640]{1,0:T(4,128)}, u32[]{:S(2)}) copy-start(f32[3,640]{1,0:T(4,128)} %cw_ref.5) | copy-start | bytes 23044
  9.4 5.1 %copy-start.6 = (f32[8,256]{1,0:T(8,128)S(1)}, f32[8,256]{1,0:T(8,128)}, u32[]{:S(2)}) copy-start(f32[8,256]{1,0:T(8,128)} %constant.35.clone.bias_ref) | copy-start | bytes 24580
  9.4 25.9 %collective-permute-start.2 = (bf16[512,1024]{1,0:T(8,128)(2,1)S(1)}, bf16[512,1024]{1,0:T(8,128)(2,1)S(1)}, u32[]{:S(2)}, u32[]{:S(2)}) collective-permute-start(bf16[512,1024]{1,0:T(8,128)(2,1)S(1)} %get-tuple-element.72), channel_id=1, source_target_pairs={{0,4},{1,5},{2,6},{3,7},{4,0},{5,1},{6,2},{7,3},{8,12},{9,13},{10,... | collective-permute-start | bytes 3145736 | tf_op jit(solution)/shard_map/ppermute | solution.py:711
  14.3 13.9 %collective-permute-start.3 = (bf16[4,512,640]{2,1,0:T(8,128)(2,1)S(1)}, bf16[4,512,640]{2,1,0:T(8,128)(2,1)S(1)}, u32[]{:S(2)}, u32[]{:S(2)}) collective-permute-start(bf16[4,512,640]{2,1,0:T(8,128)(2,1)S(1)} %get-tuple-element.87), channel_id=1, source_target_pairs={{0,1},{1,0},{2,3},{3,2},{4,5},{5,4},{6,7},{7,6},{8,9},{9,8},{10,11... | collective-permute-start | bytes 7864328 | tf_op jit(solution)/shard_map/ppermute | solution.py:711
  14.5 22.5 %copy-start = (bf16[512,4096]{1,0:T(8,128)(2,1)S(1)}, bf16[512,4096]{1,0:T(8,128)(2,1)}, u32[]{:S(2)}) copy-start(bf16[512,4096]{1,0:T(8,128)(2,1)} %refs_8_.1) | copy-start | bytes 12582916
  28.2 16.8 %collective-permute-start.6 = (bf16[4,160,128]{2,1,0:T(8,128)(2,1)S(1)}, bf16[4,160,128]{2,1,0:T(8,128)(2,1)S(1)}, u32[]{:S(2)}, u32[]{:S(2)}) collective-permute-start(bf16[4,160,128]{2,1,0:T(8,128)(2,1)S(1)} %get-tuple-element.88), channel_id=1, source_target_pairs={{0,24},{1,25},{2,26},{3,27},{4,28},{5,29},{6,30},{7,31}} | collective-permute-start | bytes 491528 | tf_op jit(solution)/shard_map/ppermute | solution.py:555
  31.5 13.5 %collective-permute-start.5 = (bf16[4,160,128]{2,1,0:T(8,128)(2,1)S(1)}, bf16[4,160,128]{2,1,0:T(8,128)(2,1)S(1)}, u32[]{:S(2)}, u32[]{:S(2)}) collective-permute-start(bf16[4,160,128]{2,1,0:T(8,128)(2,1)S(1)} %get-tuple-element.88), channel_id=1, source_target_pairs={{0,16},{8,24},{1,17},{9,25},{2,18},{10,26},{3,19},{11,27},{4,20},{... | collective-permute-start | bytes 491528 | tf_op jit(solution)/shard_map/ppermute | solution.py:555
  33.4 11.7 %collective-permute-start.4 = (bf16[4,160,128]{2,1,0:T(8,128)(2,1)S(1)}, bf16[4,160,128]{2,1,0:T(8,128)(2,1)S(1)}, u32[]{:S(2)}, u32[]{:S(2)}) collective-permute-start(bf16[4,160,128]{2,1,0:T(8,128)(2,1)S(1)} %get-tuple-element.88), channel_id=1, source_target_pairs={{0,8},{8,16},{16,24},{1,9},{9,17},{17,25},{2,10},{10,18},{18,26},{... | collective-permute-start | bytes 491528 | tf_op jit(solution)/shard_map/ppermute | solution.py:555
  35.3 9.7 %copy-start.8 = (bf16[512,1024]{1,0:T(8,128)(2,1)}, bf16[512,1024]{1,0:T(8,128)(2,1)S(1)}, u32[]{:S(2)}) copy-start(bf16[512,1024]{1,0:T(8,128)(2,1)S(1)} %collective-permute-done.1.refs_9_) | copy-start | bytes 3145732
  35.4 9.7 %copy-start.9 = (bf16[512,1024]{1,0:T(8,128)(2,1)}, bf16[512,1024]{1,0:T(8,128)(2,1)S(1)}, u32[]{:S(2)}) copy-start(bf16[512,1024]{1,0:T(8,128)(2,1)S(1)} %collective-permute-done.2.refs_10_) | copy-start | bytes 3145732
  35.4 26.0 %collective-permute-start.7 = (bf16[512,1024]{1,0:T(8,128)(2,1)S(1)}, bf16[512,1024]{1,0:T(8,128)(2,1)S(1)}, u32[]{:S(2)}, u32[]{:S(2)}) collective-permute-start(bf16[512,1024]{1,0:T(8,128)(2,1)S(1)} %get-tuple-element.91), channel_id=1, source_target_pairs={{0,6},{1,7},{2,4},{3,5},{4,2},{5,3},{6,0},{7,1},{8,14},{9,15},{10,... | collective-permute-start | bytes 3145736 | tf_op jit(solution)/shard_map/ppermute | solution.py:711
  37.0 8.1 %copy-start.5 = (bf16[256,256]{1,0:T(8,128)(2,1)S(1)}, bf16[256,256]{1,0:T(8,128)(2,1)}, u32[]{:S(2)}) copy-start(bf16[256,256]{1,0:T(8,128)(2,1)} %constant.36.clone.ones_ref) | copy-start | bytes 393220
  50.3 19.5 %collective-permute-start.10 = (bf16[4,160,128]{2,1,0:T(8,128)(2,1)S(1)}, bf16[4,160,128]{2,1,0:T(8,128)(2,1)S(1)}, u32[]{:S(2)}, u32[]{:S(2)}) collective-permute-start(bf16[4,160,128]{2,1,0:T(8,128)(2,1)S(1)} %get-tuple-element.97), channel_id=1, source_target_pairs={{8,0},{16,8},{24,16},{9,1},{17,9},{25,17},{10,2},{18,10},{26,18},{... | collective-permute-start | bytes 491528 | tf_op jit(solution)/shard_map/ppermute | solution.py:555
  51.6 20.0 %collective-permute-start.9 = (bf16[4,160,128]{2,1,0:T(8,128)(2,1)S(1)}, bf16[4,160,128]{2,1,0:T(8,128)(2,1)S(1)}, u32[]{:S(2)}, u32[]{:S(2)}) collective-permute-start(bf16[4,160,128]{2,1,0:T(8,128)(2,1)S(1)} %get-tuple-element.97), channel_id=1, source_target_pairs={{16,0},{24,8},{17,1},{25,9},{18,2},{26,10},{19,3},{27,11},{20,4},{... | collective-permute-start | bytes 491528 | tf_op jit(solution)/shard_map/ppermute | solution.py:555
  52.9 18.8 %collective-permute-start.8 = (bf16[4,160,128]{2,1,0:T(8,128)(2,1)S(1)}, bf16[4,160,128]{2,1,0:T(8,128)(2,1)S(1)}, u32[]{:S(2)}, u32[]{:S(2)}) collective-permute-start(bf16[4,160,128]{2,1,0:T(8,128)(2,1)S(1)} %get-tuple-element.97), channel_id=1, source_target_pairs={{24,0},{25,1},{26,2},{27,3},{28,4},{29,5},{30,6},{31,7}} | collective-permute-start | bytes 491528 | tf_op jit(solution)/shard_map/ppermute | solution.py:555
  54.3 29.4 %collective-permute-start.17 = (bf16[1024,512]{1,0:T(8,128)(2,1)S(1)}, bf16[1024,512]{1,0:T(8,128)(2,1)S(1)}, u32[]{:S(2)}, u32[]{:S(2)}) collective-permute-start(bf16[1024,512]{1,0:T(8,128)(2,1)S(1)} %get-tuple-element.106.refs_0_.refs_4_), channel_id=1, source_target_pairs={{0,4},{1,5},{2,6},{3,7},{4,0},{5,1},{6,2},{7,3},{8,12},{9,13},{10,... | collective-permute-start | bytes 3145736 | tf_op jit(solution)/shard_map/ppermute | solution.py:711
  61.4 8.3 %copy-start.10 = (bf16[512,1024]{1,0:T(8,128)(2,1)}, bf16[512,1024]{1,0:T(8,128)(2,1)S(1)}, u32[]{:S(2)}) copy-start(bf16[512,1024]{1,0:T(8,128)(2,1)S(1)} %collective-permute-done.7.refs_11_) | copy-start | bytes 3145732
  61.4 24.1 %collective-permute-start.16 = (bf16[1024,512]{1,0:T(8,128)(2,1)S(1)}, bf16[1024,512]{1,0:T(8,128)(2,1)S(1)}, u32[]{:S(2)}, u32[]{:S(2)}) collective-permute-start(bf16[1024,512]{1,0:T(8,128)(2,1)S(1)} %get-tuple-element.106.refs_0_.refs_4_), channel_id=1, source_target_pairs={{0,2},{1,3},{2,0},{3,1},{4,6},{5,7},{6,4},{7,5},{8,10},{9,11},{10,... | collective-permute-start | bytes 3145736 | tf_op jit(solution)/shard_map/ppermute | solution.py:711
  75.5 11.5 %copy-start.3 = (s32[3]{0:T(128)S(1)}, s32[3]{0:T(128)}, u32[]{:S(2)}) copy-start(s32[3]{0:T(128)} %copy-done.2) | copy-start | bytes 40
  75.5 5.7 %collective-permute-start.13 = (f32[8,640]{1,0:T(8,128)S(1)}, f32[8,640]{1,0:T(8,128)S(1)}, u32[]{:S(2)}, u32[]{:S(2)}) collective-permute-start(f32[8,640]{1,0:T(8,128)S(1)} %get-tuple-element.104), channel_id=1, source_target_pairs={{8,0},{16,8},{24,16},{9,1},{17,9},{25,17},{10,2},{18,10},{26,18},{... | collective-permute-start | bytes 61448 | tf_op jit(solution)/shard_map/ppermute | solution.py:555
  76.8 10.2 %collective-permute-start.11 = (bf16[512,640]{1,0:T(8,128)(2,1)S(1)}, bf16[512,640]{1,0:T(8,128)(2,1)S(1)}, u32[]{:S(2)}, u32[]{:S(2)}) collective-permute-start(bf16[512,640]{1,0:T(8,128)(2,1)S(1)} %get-tuple-element.98.dp_ref), channel_id=1, source_target_pairs={{0,1},{1,0},{2,3},{3,2},{4,5},{5,4},{6,7},{7,6},{8,9},{9,8},{10,11... | collective-permute-start | bytes 1966088 | tf_op jit(solution)/shard_map/ppermute | solution.py:711
  81.3 12.0 %collective-permute-start.14 = (bf16[512,640]{1,0:T(8,128)(2,1)S(1)}, bf16[512,640]{1,0:T(8,128)(2,1)S(1)}, u32[]{:S(2)}, u32[]{:S(2)}) collective-permute-start(bf16[512,640]{1,0:T(8,128)(2,1)S(1)} %complete.1.dp_ref), channel_id=1, source_target_pairs={{0,1},{1,0},{2,3},{3,2},{4,5},{5,4},{6,7},{7,6},{8,9},{9,8},{10,11... | collective-permute-start | bytes 1966088 | tf_op jit(solution)/shard_map/ppermute | solution.py:711
  85.5 13.1 %collective-permute-start.18 = (bf16[512,512]{1,0:T(8,128)(2,1)S(1)}, bf16[512,512]{1,0:T(8,128)(2,1)S(1)}, u32[]{:S(2)}, u32[]{:S(2)}) collective-permute-start(bf16[512,512]{1,0:T(8,128)(2,1)S(1)} %get-tuple-element.107), channel_id=1, source_target_pairs={{0,4},{1,5},{2,6},{3,7},{4,0},{5,1},{6,2},{7,3},{8,12},{9,13},{10,... | collective-permute-start | bytes 1572872 | tf_op jit(solution)/shard_map/ppermute | solution.py:711
  86.7 14.9 %collective-permute-start.19 = (bf16[512,512]{1,0:T(8,128)(2,1)S(1)}, bf16[512,512]{1,0:T(8,128)(2,1)S(1)}, u32[]{:S(2)}, u32[]{:S(2)}) collective-permute-start(bf16[512,512]{1,0:T(8,128)(2,1)S(1)} %get-tuple-element.108), channel_id=1, source_target_pairs={{0,2},{1,3},{2,0},{3,1},{4,6},{5,7},{6,4},{7,5},{8,10},{9,11},{10,... | collective-permute-start | bytes 1572872 | tf_op jit(solution)/shard_map/ppermute | solution.py:711
  91.4 29.6 %collective-permute-start.12 = (bf16[2,512,512]{2,1,0:T(8,128)(2,1)S(1)}, bf16[2,512,512]{2,1,0:T(8,128)(2,1)S(1)}, u32[]{:S(2)}, u32[]{:S(2)}) collective-permute-start(bf16[2,512,512]{2,1,0:T(8,128)(2,1)S(1)} %get-tuple-element.101), channel_id=1, source_target_pairs={{0,2},{1,3},{2,0},{3,1},{4,6},{5,7},{6,4},{7,5},{8,10},{9,11},{10,... | collective-permute-start | bytes 3145736 | tf_op jit(solution)/shard_map/ppermute | solution.py:711
  97.7 23.4 %collective-permute-start.15 = (bf16[2,512,512]{2,1,0:T(8,128)(2,1)S(1)}, bf16[2,512,512]{2,1,0:T(8,128)(2,1)S(1)}, u32[]{:S(2)}, u32[]{:S(2)}) collective-permute-start(bf16[2,512,512]{2,1,0:T(8,128)(2,1)S(1)} %get-tuple-element.105), channel_id=1, source_target_pairs={{0,4},{1,5},{2,6},{3,7},{4,0},{5,1},{6,2},{7,3},{8,12},{9,13},{10,... | collective-permute-start | bytes 3145736 | tf_op jit(solution)/shard_map/ppermute | solution.py:711
  109.5 15.9 %collective-permute-start.22 = (bf16[1024,512]{1,0:T(8,128)(2,1)S(1)}, bf16[1024,512]{1,0:T(8,128)(2,1)S(1)}, u32[]{:S(2)}, u32[]{:S(2)}) collective-permute-start(bf16[1024,512]{1,0:T(8,128)(2,1)S(1)} %get-tuple-element.120), channel_id=1, source_target_pairs={{0,1},{1,0},{2,3},{3,2},{4,5},{5,4},{6,7},{7,6},{8,9},{9,8},{10,11... | collective-permute-start | bytes 3145736 | tf_op jit(solution)/shard_map/ppermute | solution.py:711
  121.2 11.1 %collective-permute-start.21 = (bf16[1,512,512]{2,1,0:T(8,128)(2,1)S(1)}, bf16[1,512,512]{2,1,0:T(8,128)(2,1)S(1)}, u32[]{:S(2)}, u32[]{:S(2)}) collective-permute-start(bf16[1,512,512]{2,1,0:T(8,128)(2,1)S(1)} %passing.3), channel_id=1, source_target_pairs={{0,2},{1,3},{2,0},{3,1},{4,6},{5,7},{6,4},{7,5},{8,10},{9,11},{10,... | collective-permute-start | bytes 1572872 | tf_op jit(solution)/shard_map/ppermute | solution.py:711
  121.9 11.0 %collective-permute-start.20 = (bf16[1,512,512]{2,1,0:T(8,128)(2,1)S(1)}, bf16[1,512,512]{2,1,0:T(8,128)(2,1)S(1)}, u32[]{:S(2)}, u32[]{:S(2)}) collective-permute-start(bf16[1,512,512]{2,1,0:T(8,128)(2,1)S(1)} %passing.2), channel_id=1, source_target_pairs={{0,4},{1,5},{2,6},{3,7},{4,0},{5,1},{6,2},{7,3},{8,12},{9,13},{10,... | collective-permute-start | bytes 1572872 | tf_op jit(solution)/shard_map/ppermute | solution.py:711

commit v7 on v5

--- a/solution.py
+++ b/solution.py
@@ -556,7 +556,7 @@
 
 
 def from_others(part, sign):
-    return [shifted(part, sign * step) for step in range(1, lax.axis_size("seq"))]
+    return [shifted(part, sign * step) for step in reversed(range(1, lax.axis_size("seq")))]
 
 
 def out_kernel(count, sw, place_ref, *refs):

time: 134 us -> 135 us (level)
  transfers between devices with their start and end apart: 23 -> 23, of which waited for: 8 -> 9; matrix products, arithmetic and copies ran while one was open for 0% -> 0% of each run, Pallas kernels for 47% -> 47%
where the time goes in v7:
time: 135 us
  Pallas kernels  66.2 us (49%)
  waiting for transfers between devices  37.7 us (28%)
  starting transfers between devices  30 us (22%)
    ppermute x15, waiting for transfers between devices, swapped(): return lax.ppermute(array, 'tp', [(i, i ^ distance) for i in range(count)])  33.3 us
    ppermute x8, starting transfers between devices, shifted(): return lax.ppermute(array, 'seq', pairs)  18 us
    pallas_call x1, Pallas kernels, project(): pl.pallas_call(functools.partial(project_kernel, heads), grid=(n,), in_sp...  13.6 us
    ppermute x15, starting transfers between devices, swapped(): return lax.ppermute(array, 'tp', [(i, i ^ distance) for i in range(count)])  12 us
    pallas_call x2, Pallas kernels, grad_part(): pl.pallas_call(functools.partial(grad_kernel, count, low_first), grid_spe...  8.85 us
    pallas_call x1, Pallas kernels, local_part(): pl.pallas_call(functools.partial(local_kernel, heads), grid=(n,), in_spec...  8 us
    pallas_call x1, Pallas kernels, out_part(): pl.pallas_call(functools.partial(out_kernel, count, sw), grid_spec=pltpu....  7.99 us
    pallas_call x1, Pallas kernels, inner_part(): pl.pallas_call(functools.partial(inner_kernel, heads), grid=(n,), in_spec...  7.78 us
  transfers between devices with their start and end apart: 23, of which 9 were waited for; matrix products, arithmetic and copies ran while one was open for 0% of the time, Pallas kernels for 47%

profile of v7, /device:TPU:0, one launch (start us, length us, event | category | flops | bytes accessed | tf_op | source)
XLA Modules:
  0.0 135.1 jit_solution(4770015449324277946)
XLA Ops:
  0.6 0.1 pad_add_fusion.place_ref
  0.7 2.1 %near_sends.1 = (bf16[16,4096]{1,0:T(8,128)(2,1)S(1)}, bf16[512,1024]{1,0:T(8,128)(2,1)S(1)}, bf16[512,1024]{1,0:T(8,128)(2,1)S(1)}) custom-call(s32[3]{0:T(128)S(1)} %pad_add_fusion.place_ref, bf16[512,4096]{1,0:T(8,128)(2,1)} %refs_8_.1, bf16[1024,4096]{1,0:T(8,128)(2,1)} %x_ref.7), custom_call_target="tpu_custom_call" | custom-call | flops 1000 | bytes 1048576 | tf_op jit(solution)/shard_map/near_sends/pallas_call | solution.py:519
  2.9 4.9 %collective-permute-start = (bf16[16,4096]{1,0:T(8,128)(2,1)S(1)}, bf16[16,4096]{1,0:T(8,128)(2,1)S(1)}, u32[]{:S(2)}, u32[]{:S(2)}) collective-permute-start(bf16[16,4096]{1,0:T(8,128)(2,1)S(1)} %get-tuple-element.65), channel_id=1, source_target_pairs={{0,8},{8,16},{16,24},{1,9},{9,17},{17,25},{2,10},{10,18},{18,26},{... | collective-permute-start | bytes 393224 | tf_op jit(solution)/shard_map/ppermute | solution.py:555
  7.8 1.6 %collective-permute-start.1 = (bf16[512,1024]{1,0:T(8,128)(2,1)S(1)}, bf16[512,1024]{1,0:T(8,128)(2,1)S(1)}, u32[]{:S(2)}, u32[]{:S(2)}) collective-permute-start(bf16[512,1024]{1,0:T(8,128)(2,1)S(1)} %get-tuple-element.71), channel_id=1, source_target_pairs={{0,2},{1,3},{2,0},{3,1},{4,6},{5,7},{6,4},{7,5},{8,10},{9,11},{10,... | collective-permute-start | bytes 3145736 | tf_op jit(solution)/shard_map/ppermute | solution.py:710
  9.4 0.0 copy-start.1
  9.4 0.0 copy-start.4
  9.4 0.0 copy-start.6
  9.4 1.6 %collective-permute-start.2 = (bf16[512,1024]{1,0:T(8,128)(2,1)S(1)}, bf16[512,1024]{1,0:T(8,128)(2,1)S(1)}, u32[]{:S(2)}, u32[]{:S(2)}) collective-permute-start(bf16[512,1024]{1,0:T(8,128)(2,1)S(1)} %get-tuple-element.72), channel_id=1, source_target_pairs={{0,4},{1,5},{2,6},{3,7},{4,0},{5,1},{6,2},{7,3},{8,12},{9,13},{10,... | collective-permute-start | bytes 3145736 | tf_op jit(solution)/shard_map/ppermute | solution.py:710
  11.0 3.3 %rest_sends.1 = (bf16[4,512,640]{2,1,0:T(8,128)(2,1)S(1)}, bf16[256,4096]{1,0:T(8,128)(2,1)S(1)}, bf16[512,1024]{1,0:T(8,128)(2,1)S(1)}) custom-call(s32[3]{0:T(128)S(1)} %pad_add_fusion.place_ref, bf16[512,4096]{1,0:T(8,128)(2,1)} %refs_8_.1, bf16[4096,640]{1,0:T(8,128)(2,1)} %w_ref.9, bf16[1024,4096]{1,0:T(8,128)(2,1)} %x_ref.7), custom_call_target="tpu_custom_call" | custom-call | flops 1000 | bytes 1048576 | tf_op jit(solution)/shard_map/rest_sends/pallas_call | solution.py:519
  14.3 0.1 collective-permute-start.3
  14.4 0.1 bitcast_multiply_fusion
  14.5 0.0 collective-permute-done.halo_ref
  14.5 0.0 copy-start
  14.6 13.6 %project.1 = (bf16[1024,512]{1,0:T(8,128)(2,1)S(1)}, bf16[4,1024,256]{2,1,0:T(8,128)(2,1)S(1)}, bf16[4,1024,256]{2,1,0:T(8,128)(2,1)S(1)}, bf16[4,1024,512]{2,1,...) custom-call(bf16[1024,4096]{1,0:T(8,128)(2,1)} %x_ref.7, ...), custom_call_target="tpu_custom_call" | custom-call | flops 107374182400 | bytes 1048576 | tf_op jit(solution)/shard_map/project/pallas_call | solution.py:206
  28.2 0.0 collective-permute-done.3.w_other_ref
  28.2 3.5 %collective-permute-start.6 = (bf16[4,160,128]{2,1,0:T(8,128)(2,1)S(1)}, bf16[4,160,128]{2,1,0:T(8,128)(2,1)S(1)}, u32[]{:S(2)}, u32[]{:S(2)}) collective-permute-start(bf16[4,160,128]{2,1,0:T(8,128)(2,1)S(1)} %get-tuple-element.88), channel_id=1, source_target_pairs={{0,8},{8,16},{16,24},{1,9},{9,17},{17,25},{2,10},{10,18},{18,26},{... | collective-permute-start | bytes 491528 | tf_op jit(solution)/shard_map/ppermute | solution.py:555
  31.7 2.9 %collective-permute-start.5 = (bf16[4,160,128]{2,1,0:T(8,128)(2,1)S(1)}, bf16[4,160,128]{2,1,0:T(8,128)(2,1)S(1)}, u32[]{:S(2)}, u32[]{:S(2)}) collective-permute-start(bf16[4,160,128]{2,1,0:T(8,128)(2,1)S(1)} %get-tuple-element.88), channel_id=1, source_target_pairs={{0,16},{8,24},{1,17},{9,25},{2,18},{10,26},{3,19},{11,27},{4,20},{... | collective-permute-start | bytes 491528 | tf_op jit(solution)/shard_map/ppermute | solution.py:555
  34.6 1.3 collective-permute-start.4
  35.9 0.0 collective-permute-done.1.refs_9_
  36.0 0.0 copy-start.8
  36.0 0.0 collective-permute-done.2.refs_10_
  36.0 0.0 copy-start.9
  36.0 1.1 collective-permute-start.7
  37.1 8.0 %local_part.1 = (f32[1024,512]{1,0:T(8,128)S(1)}, f32[1024,512]{1,0:T(8,128)S(1)}, bf16[4,1024,256]{2,1,0:T(8,128)(2,1)S(1)}, bf16[4,1024,256]{2,1,0:T(8,128)(2,1)S(1)}) custom-call(bf16[1024,4096]{1,0:T(8,128)(2,1)} %ct_ref.5, bf16[256,4096]{1,0:T(8,128)(2,1)S(1)} %get-tuple-element.79.ct_first_ref, bf16[512,4096]{1,0:T(8,128)(2,1)S(1)} %copy-done, ...), custom_call_target="tpu_custom_call" | custom-call | flops 1000 | bytes 1048576 | tf_op jit(solution)/shard_map/local_part/pallas_call | solution.py:267
  45.1 0.0 collective-permute-done.5.refs_1_
  45.2 0.0 collective-permute-done.4.refs_0_
  45.2 5.2 %norm_part.1 = (bf16[1024,512]{1,0:T(8,128)(2,1)S(1)}, bf16[1024,512]{1,0:T(8,128)(2,1)S(1)}, bf16[4,4,128,256]{3,2,1,0:T(8,128)(2,1)S(1)}, bf16[4,160,128]{2,1,0:T(8,128)(2,1)S(1)}, bf16[4,160,128]{2,1,0:T(8,128)(2,1)S(1)}) custom-call(f32[1024,512]{1,0:T(8,128)S(1)} %get-tuple-element.84.g_ref, f32[1024,512]{1,0:T(8,128)S(1)} %get-tuple-element.85.num_ref, ...), custom_call_target="tpu_custom_call" | custom-call | flops 17179869184 | bytes 1048576 | tf_op jit(solution)/shard_map/norm_part/pallas_call | solution.py:321
  50.4 1.3 collective-permute-start.10
  51.7 1.3 collective-permute-start.9
  53.0 1.5 %collective-permute-start.8 = (bf16[4,160,128]{2,1,0:T(8,128)(2,1)S(1)}, bf16[4,160,128]{2,1,0:T(8,128)(2,1)S(1)}, u32[]{:S(2)}, u32[]{:S(2)}) collective-permute-start(bf16[4,160,128]{2,1,0:T(8,128)(2,1)S(1)} %get-tuple-element.97), channel_id=1, source_target_pairs={{24,0},{25,1},{26,2},{27,3},{28,4},{29,5},{30,6},{31,7}} | collective-permute-start | bytes 491528 | tf_op jit(solution)/shard_map/ppermute | solution.py:555
  54.5 1.0 collective-permute-start.17
  55.5 6.9 %collective-permute-done.7.refs_11_ = bf16[512,1024]{1,0:T(8,128)(2,1)S(1)} collective-permute-done((bf16[512,1024]{1,0:T(8,128)(2,1)S(1)}, bf16[512,1024]{1,0:T(8,128)(2,1)S(1)}, u32[]{:S(2)}, u32[]{:S(2)}) %collective-permute-start.7) | collective-permute-done | bytes 1048608 | tf_op jit(solution)/shard_map/ppermute | solution.py:710
  62.3 0.5 collective-permute-start.16
  62.9 7.8 %inner_part.1 = (f32[1024,128]{1,0:T(8,128)S(1)}, f32[1024,512]{1,0:T(8,128)S(1)}, f32[4,1024,128]{2,1,0:T(8,128)S(1)}) custom-call(bf16[1024,512]{1,0:T(8,128)(2,1)S(1)} %get-tuple-element.74.v_ref.refs_3_, bf16[4,1024,256]{2,1,0:T(8,128)(2,1)S(1)} %get-tuple-element.77.pq_ref, bf16[4,1024,256]{2,1,0:T(8,128)(2,1)S(1)} %get-tuple-element.75.pk_ref.refs_4_, ...), custom_call_target="tpu_custom_call" | custom-call | flops 1000 | bytes 1048576 | tf_op jit(solution)/shard_map/inner_part/pallas_call | solution.py:376
  70.7 0.1 collective-permute-done.9.refs_1_
  70.7 3.9 %outer_part.1 = (bf16[512,640]{1,0:T(8,128)(2,1)S(1)}, bf16[1024,640]{1,0:T(8,128)(2,1)S(1)}, f32[8,640]{1,0:T(8,128)S(1)}, f32[16,640]{1,0:T(8,128)S(1)}) custom-call(bf16[1024,512]{1,0:T(8,128)(2,1)S(1)} %get-tuple-element.74.v_ref.refs_3_, bf16[4,1024,256]{2,1,0:T(8,128)(2,1)S(1)} %get-tuple-element.75.pk_ref.refs_4_, ...), custom_call_target="tpu_custom_call" | custom-call | flops 17179869184 | bytes 1048576 | tf_op jit(solution)/shard_map/outer_part/pallas_call | solution.py:465
  74.6 1.3 collective-permute-start.13
  75.9 0.1 collective-permute-start.11
  76.0 4.3 %collective-permute-done.13.after_ref = f32[8,640]{1,0:T(8,128)S(1)} collective-permute-done((f32[8,640]{1,0:T(8,128)S(1)}, f32[8,640]{1,0:T(8,128)S(1)}, u32[]{:S(2)}, u32[]{:S(2)}) %collective-permute-start.13) | collective-permute-done | bytes 20512 | tf_op jit(solution)/shard_map/ppermute | solution.py:555
  80.3 0.1 complete.1.dp_ref
  80.4 0.1 collective-permute-start.14
  80.5 4.2 %collective-permute-done.17.y_ref.refs_2_.refs_6_ = bf16[1024,512]{1,0:T(8,128)(2,1)S(1)} collective-permute-done((bf16[1024,512]{1,0:T(8,128)(2,1)S(1)}, bf16[1024,512]{1,0:T(8,128)(2,1)S(1)}, u32[]{:S(2)}, u32[]{:S(2)}) %collective-permute-start.17) | collective-permute-done | bytes 1048608 | tf_op jit(solution)/shard_map/ppermute | solution.py:710
  84.7 2.0 %collective-permute-done.16.x_ref.refs_1_.refs_5_ = bf16[1024,512]{1,0:T(8,128)(2,1)S(1)} collective-permute-done((bf16[1024,512]{1,0:T(8,128)(2,1)S(1)}, bf16[1024,512]{1,0:T(8,128)(2,1)S(1)}, u32[]{:S(2)}, u32[]{:S(2)}) %collective-permute-start.16) | collective-permute-done | bytes 1048608 | tf_op jit(solution)/shard_map/ppermute | solution.py:710
  86.7 0.1 halves.1
  86.8 1.1 collective-permute-start.18
  87.9 0.5 collective-permute-start.19
  88.5 4.4 %grad_part.2 = (bf16[2,512,512]{2,1,0:T(8,128)(2,1)S(1)}, bf16[2,512,512]{2,1,0:T(8,128)(2,1)S(1)}) custom-call(s32[3]{0:T(128)S(1)} %copy-done.3, bf16[512,640]{1,0:T(8,128)(2,1)S(1)} %get-tuple-element.98.dp_ref, bf16[512,640]{1,0:T(8,128)(2,1)S(1)} %collective-permute-done.11.other_ref, bf16[4096,640]{1,0:T(8,128)(2,1)S(1)} %bitcast.7, ...), custom_call_target="tpu_custom_call" | custom-call | flops 1000 | bytes 1048576 | tf_op jit(solution)/shard_map/grad_part/pallas_call | solution.py:673
  92.9 1.6 %collective-permute-start.12 = (bf16[2,512,512]{2,1,0:T(8,128)(2,1)S(1)}, bf16[2,512,512]{2,1,0:T(8,128)(2,1)S(1)}, u32[]{:S(2)}, u32[]{:S(2)}) collective-permute-start(bf16[2,512,512]{2,1,0:T(8,128)(2,1)S(1)} %get-tuple-element.101), channel_id=1, source_target_pairs={{0,2},{1,3},{2,0},{3,1},{4,6},{5,7},{6,4},{7,5},{8,10},{9,11},{10,... | collective-permute-start | bytes 3145736 | tf_op jit(solution)/shard_map/ppermute | solution.py:710
  94.5 4.4 %grad_part.3 = (bf16[2,512,512]{2,1,0:T(8,128)(2,1)S(1)}, bf16[2,512,512]{2,1,0:T(8,128)(2,1)S(1)}) custom-call(s32[3]{0:T(128)S(1)} %copy-done.3, bf16[512,640]{1,0:T(8,128)(2,1)S(1)} %complete.1.dp_ref, bf16[512,640]{1,0:T(8,128)(2,1)S(1)} %collective-permute-done.14.other_ref, bf16[4096,640]{1,0:T(8,128)(2,1)S(1)} %bitcast.7, ...), custom_call_target="tpu_custom_call" | custom-call | flops 1000 | bytes 1048576 | tf_op jit(solution)/shard_map/grad_part/pallas_call | solution.py:673
  98.9 1.0 collective-permute-start.15
  99.9 2.9 %collective-permute-done.19.refs_7_ = bf16[512,512]{1,0:T(8,128)(2,1)S(1)} collective-permute-done((bf16[512,512]{1,0:T(8,128)(2,1)S(1)}, bf16[512,512]{1,0:T(8,128)(2,1)S(1)}, u32[]{:S(2)}, u32[]{:S(2)}) %collective-permute-start.19) | collective-permute-done | bytes 524320 | tf_op jit(solution)/shard_map/ppermute | solution.py:710
  102.8 8.0 %out_part.1 = (bf16[1024,512]{1,0:T(8,128)(2,1)S(1)}, f32[1024,512]{1,0:T(8,128)S(1)}) custom-call(s32[3]{0:T(128)S(1)} %copy-done.3, bf16[1024,512]{1,0:T(8,128)(2,1)S(1)} %get-tuple-element.106.refs_0_.refs_4_, bf16[1024,512]{1,0:T(8,128)(2,1)S(1)} %collective-permute-done.16.x_ref.refs_1_.refs_5_, ...), custom_call_target="tpu_custom_call" | custom-call | flops 17179869184 | bytes 1048576 | tf_op jit(solution)/shard_map/out_part/pallas_call | solution.py:604
  110.8 0.1 collective-permute-start.22
  110.8 11.5 %collective-permute-done.12.refs_1_ = bf16[2,512,512]{2,1,0:T(8,128)(2,1)S(1)} collective-permute-done((bf16[2,512,512]{2,1,0:T(8,128)(2,1)S(1)}, bf16[2,512,512]{2,1,0:T(8,128)(2,1)S(1)}, u32[]{:S(2)}, u32[]{:S(2)}) %collective-permute-start.12) | collective-permute-done | bytes 1048608 | tf_op jit(solution)/shard_map/ppermute | solution.py:710
  122.3 0.1 passing.3
  122.4 0.6 collective-permute-start.21
  123.0 0.1 passing.2
  123.2 1.0 collective-permute-start.20
  124.2 2.1 %own_columns.1 = (bf16[1024,512]{1,0:T(8,128)(2,1)S(1)}, bf16[1024,512]{1,0:T(8,128)(2,1)S(1)}) custom-call(s32[3]{0:T(128)S(1)} %copy-done.3, bf16[1024,4096]{1,0:T(8,128)(2,1)} %x_ref.7, bf16[1024,4096]{1,0:T(8,128)(2,1)} %ct_ref.5), custom_call_target="tpu_custom_call" | custom-call | flops 1000 | bytes 1048576 | tf_op jit(solution)/shard_map/own_columns/pallas_call | solution.py:777
  126.3 0.5 partial_sum.1.own_ref
  126.8 1.4 %finish_out.1 = bf16[1024,512]{1,0:T(8,128)(2,1)} custom-call(bf16[1024,512]{1,0:T(8,128)(2,1)S(1)} %get-tuple-element.118.own_ref, f32[1024,512]{1,0:T(8,128)S(1)} %get-tuple-element.119.keep_ref, bf16[1024,512]{1,0:T(8,128)(2,1)S(1)} %collective-permute-done.22.got_ref), custom_call_target="tpu_custom_call" | custom-call | flops 1000 | bytes 1048576 | tf_op jit(solution)/shard_map/finish_out/pallas_call | solution.py:846
  128.2 5.4 %collective-permute-done.21.refs_1_ = bf16[1,512,512]{2,1,0:T(8,128)(2,1)S(1)} collective-permute-done((bf16[1,512,512]{2,1,0:T(8,128)(2,1)S(1)}, bf16[1,512,512]{2,1,0:T(8,128)(2,1)S(1)}, u32[]{:S(2)}, u32[]{:S(2)}) %collective-permute-start.21) | collective-permute-done | bytes 524320 | tf_op jit(solution)/shard_map/ppermute | solution.py:710
  133.6 0.4 collective-permute-done.20.refs_0_
  134.0 1.1 finish.1
  (32 shorter events, 0.1 us)
Async XLA Ops:
  0.7 10.3 %copy-start.2 = (s32[3]{0:T(128)}, s32[3]{0:T(128)S(1)}, u32[]{:S(2)}) copy-start(s32[3]{0:T(128)S(1)} %pad_add_fusion.place_ref) | copy-start | bytes 40
  2.9 11.6 %collective-permute-start = (bf16[16,4096]{1,0:T(8,128)(2,1)S(1)}, bf16[16,4096]{1,0:T(8,128)(2,1)S(1)}, u32[]{:S(2)}, u32[]{:S(2)}) collective-permute-start(bf16[16,4096]{1,0:T(8,128)(2,1)S(1)} %get-tuple-element.65), channel_id=1, source_target_pairs={{0,8},{8,16},{16,24},{1,9},{9,17},{17,25},{2,10},{10,18},{18,26},{... | collective-permute-start | bytes 393224 | tf_op jit(solution)/shard_map/ppermute | solution.py:555
  7.8 28.2 %collective-permute-start.1 = (bf16[512,1024]{1,0:T(8,128)(2,1)S(1)}, bf16[512,1024]{1,0:T(8,128)(2,1)S(1)}, u32[]{:S(2)}, u32[]{:S(2)}) collective-permute-start(bf16[512,1024]{1,0:T(8,128)(2,1)S(1)} %get-tuple-element.71), channel_id=1, source_target_pairs={{0,2},{1,3},{2,0},{3,1},{4,6},{5,7},{6,4},{7,5},{8,10},{9,11},{10,... | collective-permute-start | bytes 3145736 | tf_op jit(solution)/shard_map/ppermute | solution.py:710
  9.4 5.1 %slice-start = ((s8[5242880]{0:T(1024)(128)(4,1)}), s8[4194304]{0:T(1024)(128)(4,1)S(1)}, s32[]{:S(2)}) async-start(s8[5242880]{0:T(1024)(128)(4,1)} %bitcast.6), calls=%async_computation | async-start | bytes 8388608
  9.4 5.0 %copy-start.11 = (s32[4]{0:T(128)S(1)}, s32[4]{0:T(128)}, u32[]{:S(2)}) copy-start(s32[4]{0:T(128)} %param.16) | copy-start | bytes 52
  9.4 5.1 %copy-start.7 = (f32[512]{0:T(512)S(1)}, f32[512]{0:T(512)}, u32[]{:S(2)}) copy-start(f32[512]{0:T(512)} %param.14) | copy-start | bytes 6148
  9.4 5.1 %slice-start.1 = ((s8[5242880]{0:T(1024)(128)(4,1)}), s8[1048576]{0:T(1024)(128)(4,1)S(1)}, s32[]{:S(2)}) async-start(s8[5242880]{0:T(1024)(128)(4,1)} %bitcast.6), calls=%async_computation.1 | async-start | bytes 2097152
  9.4 5.1 %copy-start.1 = (bf16[4,128,1024]{2,1,0:T(8,128)(2,1)S(1)}, bf16[4,128,1024]{2,1,0:T(8,128)(2,1)}, u32[]{:S(2)}) copy-start(bf16[4,128,1024]{2,1,0:T(8,128)(2,1)} %constant.34.clone.sel_ref.refs_10_) | copy-start | bytes 3145732
  9.4 5.1 %copy-start.4 = (f32[3,640]{1,0:T(4,128)S(1)}, f32[3,640]{1,0:T(4,128)}, u32[]{:S(2)}) copy-start(f32[3,640]{1,0:T(4,128)} %cw_ref.5) | copy-start | bytes 23044
  9.4 5.1 %copy-start.6 = (f32[8,256]{1,0:T(8,128)S(1)}, f32[8,256]{1,0:T(8,128)}, u32[]{:S(2)}) copy-start(f32[8,256]{1,0:T(8,128)} %constant.35.clone.bias_ref) | copy-start | bytes 24580
  9.4 26.6 %collective-permute-start.2 = (bf16[512,1024]{1,0:T(8,128)(2,1)S(1)}, bf16[512,1024]{1,0:T(8,128)(2,1)S(1)}, u32[]{:S(2)}, u32[]{:S(2)}) collective-permute-start(bf16[512,1024]{1,0:T(8,128)(2,1)S(1)} %get-tuple-element.72), channel_id=1, source_target_pairs={{0,4},{1,5},{2,6},{3,7},{4,0},{5,1},{6,2},{7,3},{8,12},{9,13},{10,... | collective-permute-start | bytes 3145736 | tf_op jit(solution)/shard_map/ppermute | solution.py:710
  14.3 13.9 %collective-permute-start.3 = (bf16[4,512,640]{2,1,0:T(8,128)(2,1)S(1)}, bf16[4,512,640]{2,1,0:T(8,128)(2,1)S(1)}, u32[]{:S(2)}, u32[]{:S(2)}) collective-permute-start(bf16[4,512,640]{2,1,0:T(8,128)(2,1)S(1)} %get-tuple-element.87), channel_id=1, source_target_pairs={{0,1},{1,0},{2,3},{3,2},{4,5},{5,4},{6,7},{7,6},{8,9},{9,8},{10,11... | collective-permute-start | bytes 7864328 | tf_op jit(solution)/shard_map/ppermute | solution.py:710
  14.5 22.6 %copy-start = (bf16[512,4096]{1,0:T(8,128)(2,1)S(1)}, bf16[512,4096]{1,0:T(8,128)(2,1)}, u32[]{:S(2)}) copy-start(bf16[512,4096]{1,0:T(8,128)(2,1)} %refs_8_.1) | copy-start | bytes 12582916
  28.2 16.9 %collective-permute-start.6 = (bf16[4,160,128]{2,1,0:T(8,128)(2,1)S(1)}, bf16[4,160,128]{2,1,0:T(8,128)(2,1)S(1)}, u32[]{:S(2)}, u32[]{:S(2)}) collective-permute-start(bf16[4,160,128]{2,1,0:T(8,128)(2,1)S(1)} %get-tuple-element.88), channel_id=1, source_target_pairs={{0,8},{8,16},{16,24},{1,9},{9,17},{17,25},{2,10},{10,18},{18,26},{... | collective-permute-start | bytes 491528 | tf_op jit(solution)/shard_map/ppermute | solution.py:555
  31.7 13.4 %collective-permute-start.5 = (bf16[4,160,128]{2,1,0:T(8,128)(2,1)S(1)}, bf16[4,160,128]{2,1,0:T(8,128)(2,1)S(1)}, u32[]{:S(2)}, u32[]{:S(2)}) collective-permute-start(bf16[4,160,128]{2,1,0:T(8,128)(2,1)S(1)} %get-tuple-element.88), channel_id=1, source_target_pairs={{0,16},{8,24},{1,17},{9,25},{2,18},{10,26},{3,19},{11,27},{4,20},{... | collective-permute-start | bytes 491528 | tf_op jit(solution)/shard_map/ppermute | solution.py:555
  34.6 10.5 %collective-permute-start.4 = (bf16[4,160,128]{2,1,0:T(8,128)(2,1)S(1)}, bf16[4,160,128]{2,1,0:T(8,128)(2,1)S(1)}, u32[]{:S(2)}, u32[]{:S(2)}) collective-permute-start(bf16[4,160,128]{2,1,0:T(8,128)(2,1)S(1)} %get-tuple-element.88), channel_id=1, source_target_pairs={{0,24},{1,25},{2,26},{3,27},{4,28},{5,29},{6,30},{7,31}} | collective-permute-start | bytes 491528 | tf_op jit(solution)/shard_map/ppermute | solution.py:555
  36.0 9.2 %copy-start.8 = (bf16[512,1024]{1,0:T(8,128)(2,1)}, bf16[512,1024]{1,0:T(8,128)(2,1)S(1)}, u32[]{:S(2)}) copy-start(bf16[512,1024]{1,0:T(8,128)(2,1)S(1)} %collective-permute-done.1.refs_9_) | copy-start | bytes 3145732
  36.0 9.2 %copy-start.9 = (bf16[512,1024]{1,0:T(8,128)(2,1)}, bf16[512,1024]{1,0:T(8,128)(2,1)S(1)}, u32[]{:S(2)}) copy-start(bf16[512,1024]{1,0:T(8,128)(2,1)S(1)} %collective-permute-done.2.refs_10_) | copy-start | bytes 3145732
  36.0 26.3 %collective-permute-start.7 = (bf16[512,1024]{1,0:T(8,128)(2,1)S(1)}, bf16[512,1024]{1,0:T(8,128)(2,1)S(1)}, u32[]{:S(2)}, u32[]{:S(2)}) collective-permute-start(bf16[512,1024]{1,0:T(8,128)(2,1)S(1)} %get-tuple-element.91), channel_id=1, source_target_pairs={{0,6},{1,7},{2,4},{3,5},{4,2},{5,3},{6,0},{7,1},{8,14},{9,15},{10,... | collective-permute-start | bytes 3145736 | tf_op jit(solution)/shard_map/ppermute | solution.py:710
  37.1 8.1 %copy-start.5 = (bf16[256,256]{1,0:T(8,128)(2,1)S(1)}, bf16[256,256]{1,0:T(8,128)(2,1)}, u32[]{:S(2)}) copy-start(bf16[256,256]{1,0:T(8,128)(2,1)} %constant.36.clone.ones_ref) | copy-start | bytes 393220
  50.4 20.3 %collective-permute-start.10 = (bf16[4,160,128]{2,1,0:T(8,128)(2,1)S(1)}, bf16[4,160,128]{2,1,0:T(8,128)(2,1)S(1)}, u32[]{:S(2)}, u32[]{:S(2)}) collective-permute-start(bf16[4,160,128]{2,1,0:T(8,128)(2,1)S(1)} %get-tuple-element.97), channel_id=1, source_target_pairs={{8,0},{16,8},{24,16},{9,1},{17,9},{25,17},{10,2},{18,10},{26,18},{... | collective-permute-start | bytes 491528 | tf_op jit(solution)/shard_map/ppermute | solution.py:555
  51.7 19.1 %collective-permute-start.9 = (bf16[4,160,128]{2,1,0:T(8,128)(2,1)S(1)}, bf16[4,160,128]{2,1,0:T(8,128)(2,1)S(1)}, u32[]{:S(2)}, u32[]{:S(2)}) collective-permute-start(bf16[4,160,128]{2,1,0:T(8,128)(2,1)S(1)} %get-tuple-element.97), channel_id=1, source_target_pairs={{16,0},{24,8},{17,1},{25,9},{18,2},{26,10},{19,3},{27,11},{20,4},{... | collective-permute-start | bytes 491528 | tf_op jit(solution)/shard_map/ppermute | solution.py:555
  53.0 17.8 %collective-permute-start.8 = (bf16[4,160,128]{2,1,0:T(8,128)(2,1)S(1)}, bf16[4,160,128]{2,1,0:T(8,128)(2,1)S(1)}, u32[]{:S(2)}, u32[]{:S(2)}) collective-permute-start(bf16[4,160,128]{2,1,0:T(8,128)(2,1)S(1)} %get-tuple-element.97), channel_id=1, source_target_pairs={{24,0},{25,1},{26,2},{27,3},{28,4},{29,5},{30,6},{31,7}} | collective-permute-start | bytes 491528 | tf_op jit(solution)/shard_map/ppermute | solution.py:555
  54.5 30.2 %collective-permute-start.17 = (bf16[1024,512]{1,0:T(8,128)(2,1)S(1)}, bf16[1024,512]{1,0:T(8,128)(2,1)S(1)}, u32[]{:S(2)}, u32[]{:S(2)}) collective-permute-start(bf16[1024,512]{1,0:T(8,128)(2,1)S(1)} %get-tuple-element.106.refs_0_.refs_4_), channel_id=1, source_target_pairs={{0,4},{1,5},{2,6},{3,7},{4,0},{5,1},{6,2},{7,3},{8,12},{9,13},{10,... | collective-permute-start | bytes 3145736 | tf_op jit(solution)/shard_map/ppermute | solution.py:710
  62.3 8.3 %copy-start.10 = (bf16[512,1024]{1,0:T(8,128)(2,1)}, bf16[512,1024]{1,0:T(8,128)(2,1)S(1)}, u32[]{:S(2)}) copy-start(bf16[512,1024]{1,0:T(8,128)(2,1)S(1)} %collective-permute-done.7.refs_11_) | copy-start | bytes 3145732
  62.3 24.4 %collective-permute-start.16 = (bf16[1024,512]{1,0:T(8,128)(2,1)S(1)}, bf16[1024,512]{1,0:T(8,128)(2,1)S(1)}, u32[]{:S(2)}, u32[]{:S(2)}) collective-permute-start(bf16[1024,512]{1,0:T(8,128)(2,1)S(1)} %get-tuple-element.106.refs_0_.refs_4_), channel_id=1, source_target_pairs={{0,2},{1,3},{2,0},{3,1},{4,6},{5,7},{6,4},{7,5},{8,10},{9,11},{10,... | collective-permute-start | bytes 3145736 | tf_op jit(solution)/shard_map/ppermute | solution.py:710
  74.6 13.8 %copy-start.3 = (s32[3]{0:T(128)S(1)}, s32[3]{0:T(128)}, u32[]{:S(2)}) copy-start(s32[3]{0:T(128)} %copy-done.2) | copy-start | bytes 40
  74.6 5.7 %collective-permute-start.13 = (f32[8,640]{1,0:T(8,128)S(1)}, f32[8,640]{1,0:T(8,128)S(1)}, u32[]{:S(2)}, u32[]{:S(2)}) collective-permute-start(f32[8,640]{1,0:T(8,128)S(1)} %get-tuple-element.104), channel_id=1, source_target_pairs={{8,0},{16,8},{24,16},{9,1},{17,9},{25,17},{10,2},{18,10},{26,18},{... | collective-permute-start | bytes 61448 | tf_op jit(solution)/shard_map/ppermute | solution.py:555
  75.9 12.5 %collective-permute-start.11 = (bf16[512,640]{1,0:T(8,128)(2,1)S(1)}, bf16[512,640]{1,0:T(8,128)(2,1)S(1)}, u32[]{:S(2)}, u32[]{:S(2)}) collective-permute-start(bf16[512,640]{1,0:T(8,128)(2,1)S(1)} %get-tuple-element.98.dp_ref), channel_id=1, source_target_pairs={{0,1},{1,0},{2,3},{3,2},{4,5},{5,4},{6,7},{7,6},{8,9},{9,8},{10,11... | collective-permute-start | bytes 1966088 | tf_op jit(solution)/shard_map/ppermute | solution.py:710
  80.4 14.1 %collective-permute-start.14 = (bf16[512,640]{1,0:T(8,128)(2,1)S(1)}, bf16[512,640]{1,0:T(8,128)(2,1)S(1)}, u32[]{:S(2)}, u32[]{:S(2)}) collective-permute-start(bf16[512,640]{1,0:T(8,128)(2,1)S(1)} %complete.1.dp_ref), channel_id=1, source_target_pairs={{0,1},{1,0},{2,3},{3,2},{4,5},{5,4},{6,7},{7,6},{8,9},{9,8},{10,11... | collective-permute-start | bytes 1966088 | tf_op jit(solution)/shard_map/ppermute | solution.py:710
  86.8 13.1 %collective-permute-start.18 = (bf16[512,512]{1,0:T(8,128)(2,1)S(1)}, bf16[512,512]{1,0:T(8,128)(2,1)S(1)}, u32[]{:S(2)}, u32[]{:S(2)}) collective-permute-start(bf16[512,512]{1,0:T(8,128)(2,1)S(1)} %get-tuple-element.107), channel_id=1, source_target_pairs={{0,4},{1,5},{2,6},{3,7},{4,0},{5,1},{6,2},{7,3},{8,12},{9,13},{10,... | collective-permute-start | bytes 1572872 | tf_op jit(solution)/shard_map/ppermute | solution.py:710
  87.9 14.9 %collective-permute-start.19 = (bf16[512,512]{1,0:T(8,128)(2,1)S(1)}, bf16[512,512]{1,0:T(8,128)(2,1)S(1)}, u32[]{:S(2)}, u32[]{:S(2)}) collective-permute-start(bf16[512,512]{1,0:T(8,128)(2,1)S(1)} %get-tuple-element.108), channel_id=1, source_target_pairs={{0,2},{1,3},{2,0},{3,1},{4,6},{5,7},{6,4},{7,5},{8,10},{9,11},{10,... | collective-permute-start | bytes 1572872 | tf_op jit(solution)/shard_map/ppermute | solution.py:710
  92.9 29.4 %collective-permute-start.12 = (bf16[2,512,512]{2,1,0:T(8,128)(2,1)S(1)}, bf16[2,512,512]{2,1,0:T(8,128)(2,1)S(1)}, u32[]{:S(2)}, u32[]{:S(2)}) collective-permute-start(bf16[2,512,512]{2,1,0:T(8,128)(2,1)S(1)} %get-tuple-element.101), channel_id=1, source_target_pairs={{0,2},{1,3},{2,0},{3,1},{4,6},{5,7},{6,4},{7,5},{8,10},{9,11},{10,... | collective-permute-start | bytes 3145736 | tf_op jit(solution)/shard_map/ppermute | solution.py:710
  98.9 23.4 %collective-permute-start.15 = (bf16[2,512,512]{2,1,0:T(8,128)(2,1)S(1)}, bf16[2,512,512]{2,1,0:T(8,128)(2,1)S(1)}, u32[]{:S(2)}, u32[]{:S(2)}) collective-permute-start(bf16[2,512,512]{2,1,0:T(8,128)(2,1)S(1)} %get-tuple-element.105), channel_id=1, source_target_pairs={{0,4},{1,5},{2,6},{3,7},{4,0},{5,1},{6,2},{7,3},{8,12},{9,13},{10,... | collective-permute-start | bytes 3145736 | tf_op jit(solution)/shard_map/ppermute | solution.py:710
  110.8 16.0 %collective-permute-start.22 = (bf16[1024,512]{1,0:T(8,128)(2,1)S(1)}, bf16[1024,512]{1,0:T(8,128)(2,1)S(1)}, u32[]{:S(2)}, u32[]{:S(2)}) collective-permute-start(bf16[1024,512]{1,0:T(8,128)(2,1)S(1)} %get-tuple-element.120), channel_id=1, source_target_pairs={{0,1},{1,0},{2,3},{3,2},{4,5},{5,4},{6,7},{7,6},{8,9},{9,8},{10,11... | collective-permute-start | bytes 3145736 | tf_op jit(solution)/shard_map/ppermute | solution.py:710
  122.4 11.1 %collective-permute-start.21 = (bf16[1,512,512]{2,1,0:T(8,128)(2,1)S(1)}, bf16[1,512,512]{2,1,0:T(8,128)(2,1)S(1)}, u32[]{:S(2)}, u32[]{:S(2)}) collective-permute-start(bf16[1,512,512]{2,1,0:T(8,128)(2,1)S(1)} %passing.3), channel_id=1, source_target_pairs={{0,2},{1,3},{2,0},{3,1},{4,6},{5,7},{6,4},{7,5},{8,10},{9,11},{10,... | collective-permute-start | bytes 1572872 | tf_op jit(solution)/shard_map/ppermute | solution.py:710
  123.2 10.8 %collective-permute-start.20 = (bf16[1,512,512]{2,1,0:T(8,128)(2,1)S(1)}, bf16[1,512,512]{2,1,0:T(8,128)(2,1)S(1)}, u32[]{:S(2)}, u32[]{:S(2)}) collective-permute-start(bf16[1,512,512]{2,1,0:T(8,128)(2,1)S(1)} %passing.2), channel_id=1, source_target_pairs={{0,4},{1,5},{2,6},{3,7},{4,0},{5,1},{6,2},{7,3},{8,12},{9,13},{10,... | collective-permute-start | bytes 1572872 | tf_op jit(solution)/shard_map/ppermute | solution.py:710
